TPU v7x, 32 devices: a whole 2x2x4 slice. The times are simulated.
32 devices in a mesh: tok: 8 (over z, y), feat: 4 (over x, core).
Axes of the slice: x: 2, y: 2, z: 4, core: 2. Of those that a mesh axis runs over, the one named last changes fastest.
Arguments:
- activations: bfloat16 [12288, 8192], P('tok', 'feat'), as said below
- start_basis: float32 [32, 8192], P(None, 'feat'), may hold values from -6 to 6
Outputs:
- scores: float32 [12288], P('tok')
- basis: float32 [32, 8192], P(None, 'feat')
Inputs may be any that keep to these rules, and one draw needn't show every extreme that they name: `activations`: token rows carry a feature offset whose size varies along the rows, on top of independent entries.
All inputs are finite; a program needn't handle non-finite values.
Results may differ from a plain program's by a relative error of at most 0.0048.
Values may be sent and summed in bfloat16 or wider, within the bound.
No kernel may reach another device: no remote copies, remote signals or barrier semaphores. Data moves between devices by JAX's collectives and lax.ppermute only.
A program may use at most 64 MiB of HBM per device.

v0:
```python
import jax
import jax.numpy as jnp
from jax import lax
from jax.sharding import PartitionSpec as P

ITERS = 4


def partial_projection(activations, vectors, local_mean):
    shift = jnp.dot(vectors.astype(jnp.float32), local_mean, precision=lax.Precision.HIGHEST)
    product = lax.dot_general(
        vectors, activations, (((1,), (1,)), ((), ())), preferred_element_type=jnp.float32
    )
    return product - shift[:, None]


def project(activations, vectors, local_mean):
    return lax.psum(partial_projection(activations, vectors, local_mean), "feat")


def image_term(weights, rows, local_mean):
    term = jnp.dot(weights, rows, preferred_element_type=jnp.float32)
    counts = jnp.sum(weights.astype(jnp.float32), axis=1)
    return term - counts[:, None] * local_mean[None, :]


def on_device(activations, start_basis):
    total_rows = activations.shape[0] * lax.axis_size("tok")
    column_sums = jnp.sum(activations, axis=0, dtype=jnp.float32)
    local_mean = lax.psum(column_sums, "tok") / total_rows
    basis = start_basis

    def advance(step, basis):
        vectors = basis.astype(jnp.bfloat16)
        projected = project(activations, vectors, local_mean)
        weights = projected.astype(jnp.bfloat16)
        term = image_term(weights, activations, local_mean)
        image = lax.psum(term, "tok")
        partial_gram = jnp.dot(image, image.T, precision=lax.Precision.HIGHEST)
        gram = lax.psum(partial_gram, "feat")
        lower = jnp.linalg.cholesky(gram)
        return jax.scipy.linalg.solve_triangular(lower, image, lower=True)

    basis = lax.fori_loop(0, ITERS, advance, basis)
    projected = project(activations, basis.astype(jnp.bfloat16), local_mean)
    scores = jnp.mean(projected * projected, axis=0)
    return (scores, basis)


def solution(mesh):
    in_specs = (P("tok", "feat"), P(None, "feat"))
    out_specs = (P("tok"), P(None, "feat"))
    return jax.shard_map(
        on_device, mesh=mesh, in_specs=in_specs, out_specs=out_specs, check_vma=False
    )
```

profile of v0, /device:TPU:0, one launch (start us, length us, event | category | flops | bytes accessed | tf_op | source)
XLA Modules:
  0.0 528.0 jit_solution(3952752050595288349)
XLA Ops:
  8.0 4.0 convert_reduce_fusion.1
  12.0 23.4 %psum.35 = f32[2048]{0:T(1024)S(1)} all-reduce(f32[2048]{0:T(1024)S(1)} %convert_reduce_fusion.1), channel_id=1, replica_groups=mesh['tok'=8,'feat'=4] {'tok'}, use_global_device_ids=true, to_apply=%region_1.0 | all-reduce | flops 2048 | bytes 16384 | tf_op jit(solution)/shard_map/psum | solution.py:30
  35.4 447.1 %while.10 = (s32[]{:T(128)}, f32[32,2048]{1,0:T(8,128)S(1)}, bf16[1536,2048]{1,0:T(8,128)(2,1)}, f32[2048]{0:T(1024)S(1)}, s32[]{:T(128)}) while((s32[]{:T(128)}, f32[32,2048]{1,0:T(8,128)S(1)}, bf16[1536,2048]{1,0:T(8,128)(2,1)}, f32[2048]{0:T(1024)S(1)}, s32[]{:T(128)}) %tuple.29), condition=%wide.region_9.10_spmd, body=%wide.region_2.0_spmd.sunk | while | flops 454305792 | bytes 16483175 | solution.py:44
  35.6 4.8 convolution_subtract_fusion.5
  40.4 12.1 %all-reduce.7 = bf16[32,1536]{1,0:T(8,128)(2,1)S(1)} all-reduce(f32[32,1536]{1,0:T(8,128)S(1)} %convolution_subtract_fusion.5), channel_id=1, replica_groups=mesh['tok'=8,'feat'=4] {'feat'}, use_global_device_ids=true, to_apply=%region_3.0 | all-reduce | flops 49152 | bytes 294912 | tf_op jit(solution)/shard_map/while/body/eval_jaxpr/psum | solution.py:18
  52.7 4.7 convolution_subtract_fusion.6
  57.4 68.7 %all-reduce.6.cloned.1.call-done = f32[32,2048]{1,0:T(8,128)} async-done(((f32[32,2048]{1,0:T(8,128)}), f32[32,2048]{1,0:T(8,128)}) %all-reduce.6.cloned.1.call-update) | async-done | bytes 262160 | tf_op jit(solution)/shard_map/while/body/eval_jaxpr/psum | solution.py:38
  127.5 10.1 %psum.42 = f32[32,32]{0,1:T(8,128)S(1)} all-reduce(f32[32,32]{0,1:T(8,128)S(1)} %fusion.43), channel_id=1, replica_groups=mesh['tok'=8,'feat'=4] {'feat'}, use_global_device_ids=true, to_apply=%region_6.0 | all-reduce | flops 1024 | bytes 8192 | tf_op jit(solution)/shard_map/while/body/eval_jaxpr/psum | solution.py:40
  137.7 2.9 cholesky.58
  141.9 2.4 custom-call.8
  146.0 4.8 convolution_subtract_fusion.5
  150.8 12.1 %all-reduce.7 = bf16[32,1536]{1,0:T(8,128)(2,1)S(1)} all-reduce(f32[32,1536]{1,0:T(8,128)S(1)} %convolution_subtract_fusion.5), channel_id=1, replica_groups=mesh['tok'=8,'feat'=4] {'feat'}, use_global_device_ids=true, to_apply=%region_3.0 | all-reduce | flops 49152 | bytes 294912 | tf_op jit(solution)/shard_map/while/body/eval_jaxpr/psum | solution.py:18
  163.0 4.7 convolution_subtract_fusion.6
  167.7 70.6 %all-reduce.6.cloned.1.call-done = f32[32,2048]{1,0:T(8,128)} async-done(((f32[32,2048]{1,0:T(8,128)}), f32[32,2048]{1,0:T(8,128)}) %all-reduce.6.cloned.1.call-update) | async-done | bytes 262160 | tf_op jit(solution)/shard_map/while/body/eval_jaxpr/psum | solution.py:38
  239.7 10.1 %psum.42 = f32[32,32]{0,1:T(8,128)S(1)} all-reduce(f32[32,32]{0,1:T(8,128)S(1)} %fusion.43), channel_id=1, replica_groups=mesh['tok'=8,'feat'=4] {'feat'}, use_global_device_ids=true, to_apply=%region_6.0 | all-reduce | flops 1024 | bytes 8192 | tf_op jit(solution)/shard_map/while/body/eval_jaxpr/psum | solution.py:40
  249.9 2.9 cholesky.58
  254.2 2.4 custom-call.8
  258.2 4.8 convolution_subtract_fusion.5
  263.0 12.1 %all-reduce.7 = bf16[32,1536]{1,0:T(8,128)(2,1)S(1)} all-reduce(f32[32,1536]{1,0:T(8,128)S(1)} %convolution_subtract_fusion.5), channel_id=1, replica_groups=mesh['tok'=8,'feat'=4] {'feat'}, use_global_device_ids=true, to_apply=%region_3.0 | all-reduce | flops 49152 | bytes 294912 | tf_op jit(solution)/shard_map/while/body/eval_jaxpr/psum | solution.py:18
  275.3 4.7 convolution_subtract_fusion.6
  280.0 70.6 %all-reduce.6.cloned.1.call-done = f32[32,2048]{1,0:T(8,128)} async-done(((f32[32,2048]{1,0:T(8,128)}), f32[32,2048]{1,0:T(8,128)}) %all-reduce.6.cloned.1.call-update) | async-done | bytes 262160 | tf_op jit(solution)/shard_map/while/body/eval_jaxpr/psum | solution.py:38
  352.0 10.1 %psum.42 = f32[32,32]{0,1:T(8,128)S(1)} all-reduce(f32[32,32]{0,1:T(8,128)S(1)} %fusion.43), channel_id=1, replica_groups=mesh['tok'=8,'feat'=4] {'feat'}, use_global_device_ids=true, to_apply=%region_6.0 | all-reduce | flops 1024 | bytes 8192 | tf_op jit(solution)/shard_map/while/body/eval_jaxpr/psum | solution.py:40
  362.2 2.9 cholesky.58
  366.4 2.4 custom-call.8
  370.5 4.8 convolution_subtract_fusion.5
  375.3 12.1 %all-reduce.7 = bf16[32,1536]{1,0:T(8,128)(2,1)S(1)} all-reduce(f32[32,1536]{1,0:T(8,128)S(1)} %convolution_subtract_fusion.5), channel_id=1, replica_groups=mesh['tok'=8,'feat'=4] {'feat'}, use_global_device_ids=true, to_apply=%region_3.0 | all-reduce | flops 49152 | bytes 294912 | tf_op jit(solution)/shard_map/while/body/eval_jaxpr/psum | solution.py:18
  387.5 4.7 convolution_subtract_fusion.6
  392.3 70.6 %all-reduce.6.cloned.1.call-done = f32[32,2048]{1,0:T(8,128)} async-done(((f32[32,2048]{1,0:T(8,128)}), f32[32,2048]{1,0:T(8,128)}) %all-reduce.6.cloned.1.call-update) | async-done | bytes 262160 | tf_op jit(solution)/shard_map/while/body/eval_jaxpr/psum | solution.py:38
  464.2 10.1 %psum.42 = f32[32,32]{0,1:T(8,128)S(1)} all-reduce(f32[32,32]{0,1:T(8,128)S(1)} %fusion.43), channel_id=1, replica_groups=mesh['tok'=8,'feat'=4] {'feat'}, use_global_device_ids=true, to_apply=%region_6.0 | all-reduce | flops 1024 | bytes 8192 | tf_op jit(solution)/shard_map/while/body/eval_jaxpr/psum | solution.py:40
  474.4 2.9 cholesky.58
  482.8 5.5 %convolution_subtract_fusion.2 = f32[32,1536]{1,0:T(8,128)} fusion(bf16[1536,2048]{1,0:T(8,128)(2,1)} %get-tuple-element.75, f32[32]{0:T(128)S(1)} %convolution_bitcast_fusion.1, f32[32,2048]{1,0:T(8,128)S(1)} %get-tuple-element.23), kind=kOutput, calls=%fused_computation.18 | convolution fusion | flops 201441280 | bytes 6750336 | tf_op jit(solution)/shard_map/dot_general | solution.py:11
  488.3 31.0 %all-reduce.4.cloned.1.call-done = f32[32,1536]{1,0:T(8,128)} async-done(((f32[32,1536]{1,0:T(8,128)}), f32[32,1536]{1,0:T(8,128)}) %all-reduce.4.cloned.1.call-update) | async-done | bytes 196624 | tf_op jit(solution)/shard_map/psum | solution.py:18
  (55 shorter events, 22.3 us)
Async XLA Ops:
  8.0 27.4 %copy-start.1 = (f32[32,2048]{1,0:T(8,128)S(1)}, f32[32,2048]{1,0:T(8,128)}, u32[]{:S(2)}) copy-start(f32[32,2048]{1,0:T(8,128)} %param.5) | copy-start | bytes 786436
  35.4 90.6 %all-reduce.6.cloned.1.call-start = ((), (), s32[]{:S(2)}) async-start(), calls=%async_computation.1 | async-start | bytes 524288 | tf_op jit(solution)/shard_map/while/body/eval_jaxpr/psum | solution.py:38
  145.8 92.6 %all-reduce.6.cloned.1.call-start = ((), (), s32[]{:S(2)}) async-start(), calls=%async_computation.1 | async-start | bytes 524288 | tf_op jit(solution)/shard_map/while/body/eval_jaxpr/psum | solution.py:38
  258.0 92.6 %all-reduce.6.cloned.1.call-start = ((), (), s32[]{:S(2)}) async-start(), calls=%async_computation.1 | async-start | bytes 524288 | tf_op jit(solution)/shard_map/while/body/eval_jaxpr/psum | solution.py:38
  370.3 92.6 %all-reduce.6.cloned.1.call-start = ((), (), s32[]{:S(2)}) async-start(), calls=%async_computation.1 | async-start | bytes 524288 | tf_op jit(solution)/shard_map/while/body/eval_jaxpr/psum | solution.py:38
  482.5 38.4 %copy-start = (f32[32,2048]{1,0:T(8,128)}, f32[32,2048]{1,0:T(8,128)S(1)}, u32[]{:S(2)}) copy-start(f32[32,2048]{1,0:T(8,128)S(1)} %get-tuple-element.23) | copy-start | bytes 786436
  482.5 36.8 %all-reduce.4.cloned.1.call-start = ((), (), s32[]{:S(2)}) async-start(), calls=%async_computation | async-start | bytes 393216 | tf_op jit(solution)/shard_map/psum | solution.py:18
Sparse Core Ops, SparseCore 0:
  57.5 68.5 all-reduce.5
  167.9 70.4 all-reduce.5
  280.1 70.4 all-reduce.5
  392.4 70.4 all-reduce.5
Sparse Core Ops, SparseCore 1:
  488.4 30.9 all-reduce.3
where the time goes:
time: 529 us; the launch traced here: 528 us
  waiting for transfers between devices  312 us (59%)
  blocking collectives  112 us (21%)
  matrix products  55.3 us (10%)
  other arithmetic  32.8 us (6%)
  between operations  15.2 us (3%)
    psum x4, waiting for transfers between devices, advance(): image = lax.psum(term, 'tok')  280 us
    psum x4, blocking collectives, project(): lax.psum(partial_projection(activations, vectors, local_mean), 'feat')  48.5 us
    psum x4, blocking collectives, advance(): gram = lax.psum(partial_gram, 'feat')  40.5 us
    psum x1, waiting for transfers between devices, project(): lax.psum(partial_projection(activations, vectors, local_mean), 'feat')  31 us
    dot_general x5, matrix products, partial_projection(): lax.dot_general(vectors, activations, (((1,), (1,)), ((), ())), preferred...  24.7 us
    psum x1, blocking collectives, on_device(): local_mean = lax.psum(column_sums, 'tok') / total_rows  23.4 us
    dot_general x4, matrix products, image_term(): term = jnp.dot(weights, rows, preferred_element_type=jnp.float32)  18.7 us
    another operation x12, other arithmetic, advance(): lower = jnp.linalg.cholesky(gram)  14.4 us
  transfers between devices with their start and end apart: 5, of which 5 were waited for; matrix products, arithmetic and copies ran while one was open for 0% of the time, Pallas kernels for 0%

commit v1 on v0

v1 whole, which is shorter than its diff:
```python
import functools

import jax
import jax.numpy as jnp
from jax import lax
from jax.experimental import pallas as pl
from jax.experimental.pallas import tpu as pltpu
from jax.sharding import PartitionSpec as P

ITERS = 4
PEERS = 4
LANES = 128
HIGHEST = lax.Precision.HIGHEST
VMEM = pl.BlockSpec(memory_space=pltpu.VMEM)
SMEM = pl.BlockSpec(memory_space=pltpu.SMEM)
F32 = jnp.float32
BF16 = jnp.bfloat16


def call(kernel, outputs, name, scratch=()):
    def run(*args):
        specs = [SMEM if arg.dtype == jnp.int32 else VMEM for arg in args]
        return pl.pallas_call(
            kernel,
            out_shape=[jax.ShapeDtypeStruct(shape, F32) for shape in outputs],
            in_specs=specs,
            out_specs=[VMEM] * len(outputs),
            scratch_shapes=scratch,
            compiler_params=pltpu.CompilerParams(vmem_limit_bytes=20 * 2**20),
            name=name,
        )(*args)

    return run


def split(value):
    high = value.astype(BF16)
    low = (value - high.astype(F32)).astype(BF16)
    return jnp.concatenate([high, low], axis=0)


def join(value):
    half = value.shape[0] // 2
    return value[:half] + value[half:]


def contract_last(left, right, precision=None):
    return lax.dot_general(
        left, right, (((1,), (1,)), ((), ())), preferred_element_type=F32, precision=precision
    )


def column_sums_kernel(rows_ref, sums_ref):
    ones = jnp.ones((16, rows_ref.shape[0]), BF16)
    sums_ref[...] = jnp.dot(ones, rows_ref[...], preferred_element_type=F32)[:1]


def first_projection_kernel(basis_ref, rows_ref, out_ref):
    tokens = rows_ref.shape[0]
    out_ref[:, :tokens] = join(contract_last(split(basis_ref[...]), rows_ref[...]))
    out_ref[:, tokens:] = jnp.zeros((out_ref.shape[0], LANES), F32)


def projection_kernel(me_ref, c0, c1, c2, c3, mean_ref, rows_ref, out_ref, image_ref):
    tokens = rows_ref.shape[0]
    width = c0.shape[1]
    for distance, chunk in enumerate((c0, c1, c2, c3)):
        place = pl.multiple_of((me_ref[0] ^ distance) * width, width)
        image_ref[:, pl.ds(place, width)] = chunk[...]
    image = image_ref[...]
    shift = jnp.sum(image * mean_ref[...], axis=1, keepdims=True)
    out_ref[:, :tokens] = join(contract_last(split(image), rows_ref[...])) - shift
    out_ref[:, tokens:] = jnp.zeros((out_ref.shape[0], LANES), F32)
    out_ref[:, tokens : tokens + out_ref.shape[0]] = contract_last(image, image, HIGHEST)


def inverse_factor(gram):
    n = gram.shape[0]
    row = lax.broadcasted_iota(jnp.int32, (n, n), 0)
    column = lax.broadcasted_iota(jnp.int32, (n, n), 1)
    work = jnp.concatenate([gram, (row == column).astype(F32)], axis=1)
    below = lax.broadcasted_iota(jnp.int32, (n, 1), 0)
    scale = jnp.zeros((n, 1), F32)
    for k in range(n):
        pivot_row = work[k : k + 1, :]
        pivot = work[k : k + 1, k : k + 1]
        factor = jnp.where(below > k, work[:, k : k + 1] / pivot, 0.0)
        scale = jnp.where(below == k, lax.rsqrt(pivot), scale)
        work = work - factor * pivot_row
    return work[:, n:] * scale


def image_kernel(first, me_ref, own_ref, got_ref, mean_ref, sums_ref, rows_ref, o0, o1, o2, o3):
    tokens = rows_ref.shape[0]
    width = o0.shape[1]
    n = own_ref.shape[0]
    projected = own_ref[:, :tokens] + got_ref[:, :tokens]
    if first:
        centre = jnp.sum(projected, axis=1, keepdims=True) / tokens
        projected = projected - centre
    else:
        gram = own_ref[:, tokens:] + got_ref[:, tokens:]
        lower = inverse_factor(gram[:, :n])
        projected = jnp.dot(lower, projected, preferred_element_type=F32, precision=HIGHEST)
    weights = split(projected)
    counts = join(jnp.sum(weights.astype(F32), axis=1, keepdims=True))
    for distance, out in enumerate((o0, o1, o2, o3)):
        place = pl.ds(pl.multiple_of((me_ref[0] ^ distance) * width, width), width)
        mean = mean_ref[:, place]
        term = join(jnp.dot(weights, rows_ref[:, place], preferred_element_type=F32))
        term = term - counts * mean
        if first:
            term = term + centre * (sums_ref[:, place] - tokens * mean)
        out[...] = term


def last_kernel(own_ref, got_ref, image_ref, scores_ref, basis_ref):
    n = own_ref.shape[0]
    tokens = own_ref.shape[1] - LANES
    total = own_ref[...] + got_ref[...]
    lower = inverse_factor(total[:, tokens : tokens + n])
    projected = jnp.dot(lower, total[:, :tokens], preferred_element_type=F32, precision=HIGHEST)
    scores_ref[...] = jnp.sum(projected * projected, axis=0, keepdims=True) / n
    basis_ref[...] = jnp.dot(lower, image_ref[...], preferred_element_type=F32, precision=HIGHEST)


def add_kernel(*refs):
    terms = [ref[...] for ref in refs[:-1]]
    while len(terms) > 1:
        terms = [sum(terms[i + 1 : i + 2], terms[i]) for i in range(0, len(terms), 2)]
    refs[-1][...] = terms[0]


def add(*terms):
    return call(add_kernel, [terms[0].shape], "add")(*terms)[0]


def swap(value, axis, distance):
    size = lax.axis_size(axis)
    return lax.ppermute(value, axis, [(i, i ^ distance) for i in range(size)])


def distances(axis, start):
    step, size = start, lax.axis_size(axis)
    while step < size:
        yield step
        step *= 2


def sum_but_last(value, axis):
    steps = list(distances(axis, 1))
    for step in steps[:-1]:
        value = add(value, swap(value, axis, step))
    return value, swap(value, axis, steps[-1])


def share(value, axis):
    return [value] + [swap(value, axis, d) for d in range(1, PEERS)]


def on_device(activations, start_basis):
    tokens, features = activations.shape
    n = start_basis.shape[0]
    width = features // PEERS
    me = (lax.axis_index("tok") % PEERS).astype(jnp.int32).reshape(1)
    total_rows = tokens * lax.axis_size("tok")

    sums = call(column_sums_kernel, [(1, features)], "column_sums")(activations)[0]
    all_sums = add(*share(sums, "tok"))
    for step in distances("tok", PEERS):
        all_sums = add(all_sums, swap(all_sums, "tok", step))
    mean = all_sums / total_rows

    packed = (n, tokens + LANES)
    partial = call(first_projection_kernel, [packed], "first_projection")(start_basis, activations)[0]
    for step in range(ITERS):
        own, got = sum_but_last(partial, "feat")
        kernel = functools.partial(image_kernel, step == 0)
        terms = call(kernel, [(n, width)] * PEERS, "image")(me, own, got, mean, sums, activations)
        received = [swap(term, "tok", d) for d, term in enumerate(terms) if d]
        chunk = add(terms[0], *received)
        for distance in distances("tok", PEERS):
            chunk = add(chunk, swap(chunk, "tok", distance))
        partial, image = call(projection_kernel, [packed, (n, features)], "projection")(
            me, *share(chunk, "tok"), mean, activations
        )
    own, got = sum_but_last(partial, "feat")
    scores, basis = call(last_kernel, [(1, tokens), (n, features)], "last")(own, got, image)
    return (scores.reshape(tokens), basis)


def solution(mesh):
    in_specs = (P("tok", "feat"), P(None, "feat"))
    out_specs = (P("tok"), P(None, "feat"))
    return jax.shard_map(
        on_device, mesh=mesh, in_specs=in_specs, out_specs=out_specs, check_vma=False
    )
```

time: 529 us -> 172 us (0.33)
  waiting for transfers between devices: 312 us -> 79.4 us
  blocking collectives: 112 us -> 0 us
  matrix products: 55.3 us -> 0 us
  starting transfers between devices: 0.21 us -> 53.5 us
  other arithmetic: 32.8 us -> 0.63 us
  Pallas kernels: 0 us -> 30.4 us
  between operations: 15.2 us -> 0.76 us
  local copies, waits for them, and re-layouts: 0.31 us -> 6.83 us
    psum x5 -> x0, waiting for transfers between devices: 312 us -> none  [the longest x4 280 us: advance(): image = lax.psum(term, 'tok')]
    psum x9 -> x0, blocking collectives: 112 us -> none  [the longest x4 48.5 us: project(): lax.psum(partial_projection(activations, vectors, local_mean), 'feat')]
    ppermute x0 -> x42, waiting for transfers between devices: none -> 79.4 us  [swap(): return lax.ppermute(value, axis, [(i, i ^ distance) for i in range(size)])]
    ppermute x0 -> x42, starting transfers between devices: none -> 53.5 us  [swap(): return lax.ppermute(value, axis, [(i, i ^ distance) for i in range(size)])]
    dot_general x18 -> x0, matrix products: 49.7 us -> none  [the longest x5 24.7 us: partial_projection(): lax.dot_general(vectors, activations, (((1,), (1,)), ((), ())), preferred...]
    pallas_call x0 -> x26, Pallas kernels: none -> 30.4 us  [run(): pl.pallas_call(kernel, out_shape=[jax.ShapeDtypeStruct(shape, F32) for sh...]
    another operation x20 -> x0, other arithmetic: 26.7 us -> none  [the longest x12 14.4 us: advance(): lower = jnp.linalg.cholesky(gram)]
    unnamed x4 -> x10, local copies, waits for them, and re-layouts: 0.01 us -> 6.83 us
  transfers between devices with their start and end apart: 5 -> 42, of which waited for: 5 -> 40; matrix products, arithmetic and copies ran while one was open for 0% -> 0% of each run, Pallas kernels for 0% -> 1%
where the time goes in v1:
time: 172 us; the launch traced here: 171 us
  waiting for transfers between devices  79.4 us (46%)
  starting transfers between devices  53.5 us (31%)
  Pallas kernels  30.4 us (18%)
  local copies, waits for them, and re-layouts  6.83 us (4%)
    ppermute x42, waiting for transfers between devices, swap(): return lax.ppermute(value, axis, [(i, i ^ distance) for i in range(size)])  79.4 us
    ppermute x42, starting transfers between devices, swap(): return lax.ppermute(value, axis, [(i, i ^ distance) for i in range(size)])  53.5 us
    pallas_call x26, Pallas kernels, run(): pl.pallas_call(kernel, out_shape=[jax.ShapeDtypeStruct(shape, F32) for sh...  30.4 us
    unnamed x10, local copies, waits for them, and re-layouts  6.83 us
  transfers between devices with their start and end apart: 42, of which 40 were waited for; matrix products, arithmetic and copies ran while one was open for 0% of the time, Pallas kernels for 1%

profile of v1, /device:TPU:0, one launch (start us, length us, event | category | flops | bytes accessed | tf_op | source)
XLA Modules:
  0.0 171.5 jit_solution(7445698853824824922)
XLA Ops:
  0.6 2.8 %copy-done = bf16[1536,2048]{1,0:T(8,128)(2,1)S(1)} copy-done((bf16[1536,2048]{1,0:T(8,128)(2,1)S(1)}, bf16[1536,2048]{1,0:T(8,128)(2,1)}, u32[]{:S(2)}) %copy-start) | copy-done | bytes 6291480
  4.4 2.0 %first_projection.1.refs_0_ = f32[32,1664]{1,0:T(8,128)S(1)} custom-call(f32[32,2048]{1,0:T(8,128)S(1)} %copy-done.4, bf16[1536,2048]{1,0:T(8,128)(2,1)S(1)} %copy-done), custom_call_target="tpu_custom_call" | custom-call | tf_op jit(solution)/shard_map/first_projection/pallas_call | solution.py:23
  8.1 4.0 %collective-permute-start.4 = (f32[1,2048]{1,0:T(1,128)S(1)}, f32[1,2048]{1,0:T(1,128)S(1)}, u32[]{:S(2)}, u32[]{:S(2)}) collective-permute-start(f32[1,2048]{1,0:T(1,128)S(1)} %column_sums.1.refs_0_.sums_ref), channel_id=1, source_target_pairs={{0,12},{4,8},{8,4},{12,0},{16,28},{20,24},{24,20},{28,16},{1,13},{... | collective-permute-start | bytes 24584 | tf_op jit(solution)/shard_map/ppermute | solution.py:140
  13.7 2.0 %collective-permute-done.3.refs_2_ = f32[1,2048]{1,0:T(1,128)S(1)} collective-permute-done((f32[1,2048]{1,0:T(1,128)S(1)}, f32[1,2048]{1,0:T(1,128)S(1)}, u32[]{:S(2)}, u32[]{:S(2)}) %collective-permute-start.3) | collective-permute-done | bytes 8224 | tf_op jit(solution)/shard_map/ppermute | solution.py:140
  16.2 2.6 %collective-permute-start.5 = (f32[1,2048]{1,0:T(1,128)S(1)}, f32[1,2048]{1,0:T(1,128)S(1)}, u32[]{:S(2)}, u32[]{:S(2)}) collective-permute-start(f32[1,2048]{1,0:T(1,128)S(1)} %add.22.refs_0_), channel_id=1, source_target_pairs={{0,16},{4,20},{8,24},{12,28},{16,0},{20,4},{24,8},{28,12},{1,17},{... | collective-permute-start | bytes 24584 | tf_op jit(solution)/shard_map/ppermute | solution.py:140
  18.8 2.0 %collective-permute-done.5.refs_1_ = f32[1,2048]{1,0:T(1,128)S(1)} collective-permute-done((f32[1,2048]{1,0:T(1,128)S(1)}, f32[1,2048]{1,0:T(1,128)S(1)}, u32[]{:S(2)}, u32[]{:S(2)}) %collective-permute-start.5) | collective-permute-done | bytes 8224 | tf_op jit(solution)/shard_map/ppermute | solution.py:140
  22.3 4.3 %collective-permute-done.1.got_ref = f32[32,1664]{1,0:T(8,128)S(1)} collective-permute-done((f32[32,1664]{1,0:T(8,128)S(1)}, f32[32,1664]{1,0:T(8,128)S(1)}, u32[]{:S(2)}, u32[]{:S(2)}) %collective-permute-start.1) | collective-permute-done | bytes 213024 | tf_op jit(solution)/shard_map/ppermute | solution.py:140
  26.7 2.8 %copy-done.2 = bf16[1536,2048]{1,0:T(8,128)(2,1)S(1)} copy-done((bf16[1536,2048]{1,0:T(8,128)(2,1)S(1)}, bf16[1536,2048]{1,0:T(8,128)(2,1)}, u32[]{:S(2)}) %copy-start.2) | copy-done | bytes 6291480
  35.3 3.5 %collective-permute-done.8.refs_3_ = f32[32,512]{1,0:T(8,128)S(1)} collective-permute-done((f32[32,512]{1,0:T(8,128)S(1)}, f32[32,512]{1,0:T(8,128)S(1)}, u32[]{:S(2)}, u32[]{:S(2)}) %collective-permute-start.8) | collective-permute-done | bytes 65568 | tf_op jit(solution)/shard_map/ppermute | solution.py:140
  38.8 2.0 %collective-permute-start.9 = (f32[32,512]{1,0:T(8,128)S(1)}, f32[32,512]{1,0:T(8,128)S(1)}, u32[]{:S(2)}, u32[]{:S(2)}) collective-permute-start(f32[32,512]{1,0:T(8,128)S(1)} %add.24.refs_0_), channel_id=1, source_target_pairs={{0,16},{4,20},{8,24},{12,28},{16,0},{20,4},{24,8},{28,12},{1,17},{... | collective-permute-start | bytes 196616 | tf_op jit(solution)/shard_map/ppermute | solution.py:140
  40.8 3.9 %collective-permute-done.9.refs_1_ = f32[32,512]{1,0:T(8,128)S(1)} collective-permute-done((f32[32,512]{1,0:T(8,128)S(1)}, f32[32,512]{1,0:T(8,128)S(1)}, u32[]{:S(2)}, u32[]{:S(2)}) %collective-permute-start.9) | collective-permute-done | bytes 65568 | tf_op jit(solution)/shard_map/ppermute | solution.py:140
  51.4 2.2 %projection.4 = (f32[32,1664]{1,0:T(8,128)S(1)}, f32[32,2048]{1,0:T(8,128)}) custom-call(s32[1]{0:T(128)} %bitcast.me_ref, f32[32,512]{1,0:T(8,128)S(1)} %add.25.c0, f32[32,512]{1,0:T(8,128)S(1)} %collective-permute-done.10.c1, f32[32,512]{1,0:T(8,128)S(1)} %collective-permute-done.11.c2, f32[32,512]{1,0:T(8,128)S(1)} %collective-permute-done.12.c3, ...), custom_call_target="tpu_custom_call" | custom-call | tf_op jit(solution)/shard_map/projection/pallas_call | solution.py:23
  56.7 5.8 %collective-permute-done.14.got_ref = f32[32,1664]{1,0:T(8,128)S(1)} collective-permute-done((f32[32,1664]{1,0:T(8,128)S(1)}, f32[32,1664]{1,0:T(8,128)S(1)}, u32[]{:S(2)}, u32[]{:S(2)}) %collective-permute-start.14) | collective-permute-done | bytes 213024 | tf_op jit(solution)/shard_map/ppermute | solution.py:140
  62.5 4.3 %image.5 = (f32[32,512]{1,0:T(8,128)S(1)}, f32[32,512]{1,0:T(8,128)S(1)}, f32[32,512]{1,0:T(8,128)S(1)}, f32[32,512]{1,0:T(8,128)S(1)}) custom-call(s32[1]{0:T(128)} %bitcast.me_ref, f32[32,1664]{1,0:T(8,128)S(1)} %add.26.own_ref, f32[32,1664]{1,0:T(8,128)S(1)} %collective-permute-done.14.got_ref, f32[1,2048]{1,0:T(1,128)S(1)} %broadcast_multiply_fusion.mean_ref, ...), custom_call_target="tpu_custom_call" | custom-call | tf_op jit(solution)/shard_map/image/pallas_call | solution.py:23
  73.6 2.8 %collective-permute-start.18 = (f32[32,512]{1,0:T(8,128)S(1)}, f32[32,512]{1,0:T(8,128)S(1)}, u32[]{:S(2)}, u32[]{:S(2)}) collective-permute-start(f32[32,512]{1,0:T(8,128)S(1)} %add.27.refs_0_), channel_id=1, source_target_pairs={{0,16},{4,20},{8,24},{12,28},{16,0},{20,4},{24,8},{28,12},{1,17},{... | collective-permute-start | bytes 196616 | tf_op jit(solution)/shard_map/ppermute | solution.py:140
  76.4 2.5 %collective-permute-done.18.refs_1_ = f32[32,512]{1,0:T(8,128)S(1)} collective-permute-done((f32[32,512]{1,0:T(8,128)S(1)}, f32[32,512]{1,0:T(8,128)S(1)}, u32[]{:S(2)}, u32[]{:S(2)}) %collective-permute-start.18) | collective-permute-done | bytes 65568 | tf_op jit(solution)/shard_map/ppermute | solution.py:140
  85.4 2.2 %projection.5 = (f32[32,1664]{1,0:T(8,128)S(1)}, f32[32,2048]{1,0:T(8,128)}) custom-call(s32[1]{0:T(128)} %bitcast.me_ref, f32[32,512]{1,0:T(8,128)S(1)} %add.28.c0, f32[32,512]{1,0:T(8,128)S(1)} %collective-permute-done.19.c1, f32[32,512]{1,0:T(8,128)S(1)} %collective-permute-done.20.c2, f32[32,512]{1,0:T(8,128)S(1)} %collective-permute-done.21.c3, ...), custom_call_target="tpu_custom_call" | custom-call | tf_op jit(solution)/shard_map/projection/pallas_call | solution.py:23
  90.7 5.8 %collective-permute-done.23.got_ref = f32[32,1664]{1,0:T(8,128)S(1)} collective-permute-done((f32[32,1664]{1,0:T(8,128)S(1)}, f32[32,1664]{1,0:T(8,128)S(1)}, u32[]{:S(2)}, u32[]{:S(2)}) %collective-permute-start.23) | collective-permute-done | bytes 213024 | tf_op jit(solution)/shard_map/ppermute | solution.py:140
  96.5 4.3 %image.6 = (f32[32,512]{1,0:T(8,128)S(1)}, f32[32,512]{1,0:T(8,128)S(1)}, f32[32,512]{1,0:T(8,128)S(1)}, f32[32,512]{1,0:T(8,128)S(1)}) custom-call(s32[1]{0:T(128)} %bitcast.me_ref, f32[32,1664]{1,0:T(8,128)S(1)} %add.29.own_ref, f32[32,1664]{1,0:T(8,128)S(1)} %collective-permute-done.23.got_ref, f32[1,2048]{1,0:T(1,128)S(1)} %broadcast_multiply_fusion.mean_ref, ...), custom_call_target="tpu_custom_call" | custom-call | tf_op jit(solution)/shard_map/image/pallas_call | solution.py:23
  106.7 2.1 %collective-permute-done.26.refs_3_ = f32[32,512]{1,0:T(8,128)S(1)} collective-permute-done((f32[32,512]{1,0:T(8,128)S(1)}, f32[32,512]{1,0:T(8,128)S(1)}, u32[]{:S(2)}, u32[]{:S(2)}) %collective-permute-start.26) | collective-permute-done | bytes 65568 | tf_op jit(solution)/shard_map/ppermute | solution.py:140
  110.5 4.3 %collective-permute-done.27.refs_1_ = f32[32,512]{1,0:T(8,128)S(1)} collective-permute-done((f32[32,512]{1,0:T(8,128)S(1)}, f32[32,512]{1,0:T(8,128)S(1)}, u32[]{:S(2)}, u32[]{:S(2)}) %collective-permute-start.27) | collective-permute-done | bytes 65568 | tf_op jit(solution)/shard_map/ppermute | solution.py:140
  114.9 2.1 %collective-permute-start.29 = (f32[32,512]{1,0:T(8,128)S(1)}, f32[32,512]{1,0:T(8,128)S(1)}, u32[]{:S(2)}, u32[]{:S(2)}) collective-permute-start(f32[32,512]{1,0:T(8,128)S(1)} %add.31.c0), channel_id=1, source_target_pairs={{0,8},{4,12},{8,0},{12,4},{16,24},{20,28},{24,16},{28,20},{1,9},{5... | collective-permute-start | bytes 196616 | tf_op jit(solution)/shard_map/ppermute | solution.py:140
  121.3 2.4 %projection.6 = (f32[32,1664]{1,0:T(8,128)S(1)}, f32[32,2048]{1,0:T(8,128)}) custom-call(s32[1]{0:T(128)} %bitcast.me_ref, f32[32,512]{1,0:T(8,128)S(1)} %add.31.c0, f32[32,512]{1,0:T(8,128)S(1)} %collective-permute-done.28.c1, f32[32,512]{1,0:T(8,128)S(1)} %collective-permute-done.29.c2, f32[32,512]{1,0:T(8,128)S(1)} %collective-permute-done.30.c3, ...), custom_call_target="tpu_custom_call" | custom-call | tf_op jit(solution)/shard_map/projection/pallas_call | solution.py:23
  126.7 5.8 %collective-permute-done.32.got_ref = f32[32,1664]{1,0:T(8,128)S(1)} collective-permute-done((f32[32,1664]{1,0:T(8,128)S(1)}, f32[32,1664]{1,0:T(8,128)S(1)}, u32[]{:S(2)}, u32[]{:S(2)}) %collective-permute-start.32) | collective-permute-done | bytes 213024 | tf_op jit(solution)/shard_map/ppermute | solution.py:140
  132.5 4.3 %image.7 = (f32[32,512]{1,0:T(8,128)S(1)}, f32[32,512]{1,0:T(8,128)S(1)}, f32[32,512]{1,0:T(8,128)S(1)}, f32[32,512]{1,0:T(8,128)S(1)}) custom-call(s32[1]{0:T(128)} %bitcast.me_ref, f32[32,1664]{1,0:T(8,128)S(1)} %add.32.own_ref, f32[32,1664]{1,0:T(8,128)S(1)} %collective-permute-done.32.got_ref, f32[1,2048]{1,0:T(1,128)S(1)} %broadcast_multiply_fusion.mean_ref, ...), custom_call_target="tpu_custom_call" | custom-call | tf_op jit(solution)/shard_map/image/pallas_call | solution.py:23
  138.3 2.0 %collective-permute-start.35 = (f32[32,512]{1,0:T(8,128)S(1)}, f32[32,512]{1,0:T(8,128)S(1)}, u32[]{:S(2)}, u32[]{:S(2)}) collective-permute-start(f32[32,512]{1,0:T(8,128)S(1)} %get-tuple-element.43), channel_id=1, source_target_pairs={{0,12},{4,8},{8,4},{12,0},{16,28},{20,24},{24,20},{28,16},{1,13},{... | collective-permute-start | bytes 196616 | tf_op jit(solution)/shard_map/ppermute | solution.py:140
  143.5 3.1 %collective-permute-start.36 = (f32[32,512]{1,0:T(8,128)S(1)}, f32[32,512]{1,0:T(8,128)S(1)}, u32[]{:S(2)}, u32[]{:S(2)}) collective-permute-start(f32[32,512]{1,0:T(8,128)S(1)} %add.33.refs_0_), channel_id=1, source_target_pairs={{0,16},{4,20},{8,24},{12,28},{16,0},{20,4},{24,8},{28,12},{1,17},{... | collective-permute-start | bytes 196616 | tf_op jit(solution)/shard_map/ppermute | solution.py:140
  146.6 2.2 %collective-permute-done.36.refs_1_ = f32[32,512]{1,0:T(8,128)S(1)} collective-permute-done((f32[32,512]{1,0:T(8,128)S(1)}, f32[32,512]{1,0:T(8,128)S(1)}, u32[]{:S(2)}, u32[]{:S(2)}) %collective-permute-start.36) | collective-permute-done | bytes 65568 | tf_op jit(solution)/shard_map/ppermute | solution.py:140
  148.8 2.0 %collective-permute-start.39 = (f32[32,512]{1,0:T(8,128)S(1)}, f32[32,512]{1,0:T(8,128)S(1)}, u32[]{:S(2)}, u32[]{:S(2)}) collective-permute-start(f32[32,512]{1,0:T(8,128)S(1)} %add.34.c0), channel_id=1, source_target_pairs={{0,12},{4,8},{8,4},{12,0},{16,28},{20,24},{24,20},{28,16},{1,13},{... | collective-permute-start | bytes 196616 | tf_op jit(solution)/shard_map/ppermute | solution.py:140
  155.7 2.2 %projection.7 = (f32[32,1664]{1,0:T(8,128)S(1)}, f32[32,2048]{1,0:T(8,128)S(1)}) custom-call(s32[1]{0:T(128)} %bitcast.me_ref, f32[32,512]{1,0:T(8,128)S(1)} %add.34.c0, f32[32,512]{1,0:T(8,128)S(1)} %collective-permute-done.37.c1, f32[32,512]{1,0:T(8,128)S(1)} %collective-permute-done.38.c2, f32[32,512]{1,0:T(8,128)S(1)} %collective-permute-done.39.c3, ...), custom_call_target="tpu_custom_call" | custom-call | tf_op jit(solution)/shard_map/projection/pallas_call | solution.py:23
  161.0 5.8 %collective-permute-done.41.got_ref = f32[32,1664]{1,0:T(8,128)S(1)} collective-permute-done((f32[32,1664]{1,0:T(8,128)S(1)}, f32[32,1664]{1,0:T(8,128)S(1)}, u32[]{:S(2)}, u32[]{:S(2)}) %collective-permute-start.41) | collective-permute-done | bytes 213024 | tf_op jit(solution)/shard_map/ppermute | solution.py:140
  166.8 4.1 %last.1 = (f32[1,1536]{1,0:T(1,128)S(1)}, f32[32,2048]{1,0:T(8,128)}) custom-call(f32[32,1664]{1,0:T(8,128)S(1)} %add.35.own_ref, f32[32,1664]{1,0:T(8,128)S(1)} %collective-permute-done.41.got_ref, f32[32,2048]{1,0:T(8,128)S(1)} %get-tuple-element.45.image_ref), custom_call_target="tpu_custom_call" | custom-call | tf_op jit(solution)/shard_map/last/pallas_call | solution.py:23
  (90 shorter events, 66.7 us)
Async XLA Ops:
  6.4 14.4 %collective-permute-start = (f32[32,1664]{1,0:T(8,128)S(1)}, f32[32,1664]{1,0:T(8,128)S(1)}, u32[]{:S(2)}, u32[]{:S(2)}) collective-permute-start(f32[32,1664]{1,0:T(8,128)S(1)} %first_projection.1.refs_0_), channel_id=1, source_target_pairs={{0,1},{1,0},{2,3},{3,2},{4,5},{5,4},{6,7},{7,6},{8,9},{9,8},{10,11... | collective-permute-start | bytes 638984 | tf_op jit(solution)/shard_map/ppermute | solution.py:140
  8.1 5.6 %collective-permute-start.4 = (f32[1,2048]{1,0:T(1,128)S(1)}, f32[1,2048]{1,0:T(1,128)S(1)}, u32[]{:S(2)}, u32[]{:S(2)}) collective-permute-start(f32[1,2048]{1,0:T(1,128)S(1)} %column_sums.1.refs_0_.sums_ref), channel_id=1, source_target_pairs={{0,12},{4,8},{8,4},{12,0},{16,28},{20,24},{24,20},{28,16},{1,13},{... | collective-permute-start | bytes 24584 | tf_op jit(solution)/shard_map/ppermute | solution.py:140
  16.2 4.5 %collective-permute-start.5 = (f32[1,2048]{1,0:T(1,128)S(1)}, f32[1,2048]{1,0:T(1,128)S(1)}, u32[]{:S(2)}, u32[]{:S(2)}) collective-permute-start(f32[1,2048]{1,0:T(1,128)S(1)} %add.22.refs_0_), channel_id=1, source_target_pairs={{0,16},{4,20},{8,24},{12,28},{16,0},{20,4},{24,8},{28,12},{1,17},{... | collective-permute-start | bytes 24584 | tf_op jit(solution)/shard_map/ppermute | solution.py:140
  20.8 5.9 %collective-permute-start.1 = (f32[32,1664]{1,0:T(8,128)S(1)}, f32[32,1664]{1,0:T(8,128)S(1)}, u32[]{:S(2)}, u32[]{:S(2)}) collective-permute-start(f32[32,1664]{1,0:T(8,128)S(1)} %add.21.own_ref), channel_id=1, source_target_pairs={{0,2},{1,3},{2,0},{3,1},{4,6},{5,7},{6,4},{7,5},{8,10},{9,11},{10,... | collective-permute-start | bytes 638984 | tf_op jit(solution)/shard_map/ppermute | solution.py:140
  30.8 4.3 %collective-permute-start.6 = (f32[32,512]{1,0:T(8,128)S(1)}, f32[32,512]{1,0:T(8,128)S(1)}, u32[]{:S(2)}, u32[]{:S(2)}) collective-permute-start(f32[32,512]{1,0:T(8,128)S(1)} %get-tuple-element.26), channel_id=1, source_target_pairs={{0,4},{4,0},{8,12},{12,8},{16,20},{20,16},{24,28},{28,24},{1,5},{5... | collective-permute-start | bytes 196616 | tf_op jit(solution)/shard_map/ppermute | solution.py:140
  31.0 4.3 %collective-permute-start.7 = (f32[32,512]{1,0:T(8,128)S(1)}, f32[32,512]{1,0:T(8,128)S(1)}, u32[]{:S(2)}, u32[]{:S(2)}) collective-permute-start(f32[32,512]{1,0:T(8,128)S(1)} %get-tuple-element.27), channel_id=1, source_target_pairs={{0,8},{4,12},{8,0},{12,4},{16,24},{20,28},{24,16},{28,20},{1,9},{5... | collective-permute-start | bytes 196616 | tf_op jit(solution)/shard_map/ppermute | solution.py:140
  32.9 5.8 %collective-permute-start.8 = (f32[32,512]{1,0:T(8,128)S(1)}, f32[32,512]{1,0:T(8,128)S(1)}, u32[]{:S(2)}, u32[]{:S(2)}) collective-permute-start(f32[32,512]{1,0:T(8,128)S(1)} %get-tuple-element.28), channel_id=1, source_target_pairs={{0,12},{4,8},{8,4},{12,0},{16,28},{20,24},{24,20},{28,16},{1,13},{... | collective-permute-start | bytes 196616 | tf_op jit(solution)/shard_map/ppermute | solution.py:140
  38.8 5.9 %collective-permute-start.9 = (f32[32,512]{1,0:T(8,128)S(1)}, f32[32,512]{1,0:T(8,128)S(1)}, u32[]{:S(2)}, u32[]{:S(2)}) collective-permute-start(f32[32,512]{1,0:T(8,128)S(1)} %add.24.refs_0_), channel_id=1, source_target_pairs={{0,16},{4,20},{8,24},{12,28},{16,0},{20,4},{24,8},{28,12},{1,17},{... | collective-permute-start | bytes 196616 | tf_op jit(solution)/shard_map/ppermute | solution.py:140
  44.7 5.2 %collective-permute-start.12 = (f32[32,512]{1,0:T(8,128)S(1)}, f32[32,512]{1,0:T(8,128)S(1)}, u32[]{:S(2)}, u32[]{:S(2)}) collective-permute-start(f32[32,512]{1,0:T(8,128)S(1)} %add.25.c0), channel_id=1, source_target_pairs={{0,12},{4,8},{8,4},{12,0},{16,28},{20,24},{24,20},{28,16},{1,13},{... | collective-permute-start | bytes 196616 | tf_op jit(solution)/shard_map/ppermute | solution.py:140
  45.3 4.7 %collective-permute-start.11 = (f32[32,512]{1,0:T(8,128)S(1)}, f32[32,512]{1,0:T(8,128)S(1)}, u32[]{:S(2)}, u32[]{:S(2)}) collective-permute-start(f32[32,512]{1,0:T(8,128)S(1)} %add.25.c0), channel_id=1, source_target_pairs={{0,8},{4,12},{8,0},{12,4},{16,24},{20,28},{24,16},{28,20},{1,9},{5... | collective-permute-start | bytes 196616 | tf_op jit(solution)/shard_map/ppermute | solution.py:140
  47.1 4.3 %collective-permute-start.10 = (f32[32,512]{1,0:T(8,128)S(1)}, f32[32,512]{1,0:T(8,128)S(1)}, u32[]{:S(2)}, u32[]{:S(2)}) collective-permute-start(f32[32,512]{1,0:T(8,128)S(1)} %add.25.c0), channel_id=1, source_target_pairs={{0,4},{4,0},{8,12},{12,8},{16,20},{20,16},{24,28},{28,24},{1,5},{5... | collective-permute-start | bytes 196616 | tf_op jit(solution)/shard_map/ppermute | solution.py:140
  55.1 7.4 %collective-permute-start.14 = (f32[32,1664]{1,0:T(8,128)S(1)}, f32[32,1664]{1,0:T(8,128)S(1)}, u32[]{:S(2)}, u32[]{:S(2)}) collective-permute-start(f32[32,1664]{1,0:T(8,128)S(1)} %add.26.own_ref), channel_id=1, source_target_pairs={{0,2},{1,3},{2,0},{3,1},{4,6},{5,7},{6,4},{7,5},{8,10},{9,11},{10,... | collective-permute-start | bytes 638984 | tf_op jit(solution)/shard_map/ppermute | solution.py:140
  66.8 5.0 %collective-permute-start.15 = (f32[32,512]{1,0:T(8,128)S(1)}, f32[32,512]{1,0:T(8,128)S(1)}, u32[]{:S(2)}, u32[]{:S(2)}) collective-permute-start(f32[32,512]{1,0:T(8,128)S(1)} %get-tuple-element.31), channel_id=1, source_target_pairs={{0,4},{4,0},{8,12},{12,8},{16,20},{20,16},{24,28},{28,24},{1,5},{5... | collective-permute-start | bytes 196616 | tf_op jit(solution)/shard_map/ppermute | solution.py:140
  68.4 5.2 %collective-permute-start.17 = (f32[32,512]{1,0:T(8,128)S(1)}, f32[32,512]{1,0:T(8,128)S(1)}, u32[]{:S(2)}, u32[]{:S(2)}) collective-permute-start(f32[32,512]{1,0:T(8,128)S(1)} %get-tuple-element.33), channel_id=1, source_target_pairs={{0,12},{4,8},{8,4},{12,0},{16,28},{20,24},{24,20},{28,16},{1,13},{... | collective-permute-start | bytes 196616 | tf_op jit(solution)/shard_map/ppermute | solution.py:140
  73.6 5.3 %collective-permute-start.18 = (f32[32,512]{1,0:T(8,128)S(1)}, f32[32,512]{1,0:T(8,128)S(1)}, u32[]{:S(2)}, u32[]{:S(2)}) collective-permute-start(f32[32,512]{1,0:T(8,128)S(1)} %add.27.refs_0_), channel_id=1, source_target_pairs={{0,16},{4,20},{8,24},{12,28},{16,0},{20,4},{24,8},{28,12},{1,17},{... | collective-permute-start | bytes 196616 | tf_op jit(solution)/shard_map/ppermute | solution.py:140
  78.9 5.2 %collective-permute-start.21 = (f32[32,512]{1,0:T(8,128)S(1)}, f32[32,512]{1,0:T(8,128)S(1)}, u32[]{:S(2)}, u32[]{:S(2)}) collective-permute-start(f32[32,512]{1,0:T(8,128)S(1)} %add.28.c0), channel_id=1, source_target_pairs={{0,12},{4,8},{8,4},{12,0},{16,28},{20,24},{24,20},{28,16},{1,13},{... | collective-permute-start | bytes 196616 | tf_op jit(solution)/shard_map/ppermute | solution.py:140
  89.2 7.4 %collective-permute-start.23 = (f32[32,1664]{1,0:T(8,128)S(1)}, f32[32,1664]{1,0:T(8,128)S(1)}, u32[]{:S(2)}, u32[]{:S(2)}) collective-permute-start(f32[32,1664]{1,0:T(8,128)S(1)} %add.29.own_ref), channel_id=1, source_target_pairs={{0,2},{1,3},{2,0},{3,1},{4,6},{5,7},{6,4},{7,5},{8,10},{9,11},{10,... | collective-permute-start | bytes 638984 | tf_op jit(solution)/shard_map/ppermute | solution.py:140
  100.8 4.3 %collective-permute-start.24 = (f32[32,512]{1,0:T(8,128)S(1)}, f32[32,512]{1,0:T(8,128)S(1)}, u32[]{:S(2)}, u32[]{:S(2)}) collective-permute-start(f32[32,512]{1,0:T(8,128)S(1)} %get-tuple-element.36), channel_id=1, source_target_pairs={{0,4},{4,0},{8,12},{12,8},{16,20},{20,16},{24,28},{28,24},{1,5},{5... | collective-permute-start | bytes 196616 | tf_op jit(solution)/shard_map/ppermute | solution.py:140
  102.1 4.6 %collective-permute-start.25 = (f32[32,512]{1,0:T(8,128)S(1)}, f32[32,512]{1,0:T(8,128)S(1)}, u32[]{:S(2)}, u32[]{:S(2)}) collective-permute-start(f32[32,512]{1,0:T(8,128)S(1)} %get-tuple-element.37), channel_id=1, source_target_pairs={{0,8},{4,12},{8,0},{12,4},{16,24},{20,28},{24,16},{28,20},{1,9},{5... | collective-permute-start | bytes 196616 | tf_op jit(solution)/shard_map/ppermute | solution.py:140
  103.6 5.2 %collective-permute-start.26 = (f32[32,512]{1,0:T(8,128)S(1)}, f32[32,512]{1,0:T(8,128)S(1)}, u32[]{:S(2)}, u32[]{:S(2)}) collective-permute-start(f32[32,512]{1,0:T(8,128)S(1)} %get-tuple-element.38), channel_id=1, source_target_pairs={{0,12},{4,8},{8,4},{12,0},{16,28},{20,24},{24,20},{28,16},{1,13},{... | collective-permute-start | bytes 196616 | tf_op jit(solution)/shard_map/ppermute | solution.py:140
  108.8 6.0 %collective-permute-start.27 = (f32[32,512]{1,0:T(8,128)S(1)}, f32[32,512]{1,0:T(8,128)S(1)}, u32[]{:S(2)}, u32[]{:S(2)}) collective-permute-start(f32[32,512]{1,0:T(8,128)S(1)} %add.30.refs_0_), channel_id=1, source_target_pairs={{0,16},{4,20},{8,24},{12,28},{16,0},{20,4},{24,8},{28,12},{1,17},{... | collective-permute-start | bytes 196616 | tf_op jit(solution)/shard_map/ppermute | solution.py:140
  114.8 5.2 %collective-permute-start.30 = (f32[32,512]{1,0:T(8,128)S(1)}, f32[32,512]{1,0:T(8,128)S(1)}, u32[]{:S(2)}, u32[]{:S(2)}) collective-permute-start(f32[32,512]{1,0:T(8,128)S(1)} %add.31.c0), channel_id=1, source_target_pairs={{0,12},{4,8},{8,4},{12,0},{16,28},{20,24},{24,20},{28,16},{1,13},{... | collective-permute-start | bytes 196616 | tf_op jit(solution)/shard_map/ppermute | solution.py:140
  114.9 5.1 %collective-permute-start.29 = (f32[32,512]{1,0:T(8,128)S(1)}, f32[32,512]{1,0:T(8,128)S(1)}, u32[]{:S(2)}, u32[]{:S(2)}) collective-permute-start(f32[32,512]{1,0:T(8,128)S(1)} %add.31.c0), channel_id=1, source_target_pairs={{0,8},{4,12},{8,0},{12,4},{16,24},{20,28},{24,16},{28,20},{1,9},{5... | collective-permute-start | bytes 196616 | tf_op jit(solution)/shard_map/ppermute | solution.py:140
  117.0 4.3 %collective-permute-start.28 = (f32[32,512]{1,0:T(8,128)S(1)}, f32[32,512]{1,0:T(8,128)S(1)}, u32[]{:S(2)}, u32[]{:S(2)}) collective-permute-start(f32[32,512]{1,0:T(8,128)S(1)} %add.31.c0), channel_id=1, source_target_pairs={{0,4},{4,0},{8,12},{12,8},{16,20},{20,16},{24,28},{28,24},{1,5},{5... | collective-permute-start | bytes 196616 | tf_op jit(solution)/shard_map/ppermute | solution.py:140
  125.2 7.4 %collective-permute-start.32 = (f32[32,1664]{1,0:T(8,128)S(1)}, f32[32,1664]{1,0:T(8,128)S(1)}, u32[]{:S(2)}, u32[]{:S(2)}) collective-permute-start(f32[32,1664]{1,0:T(8,128)S(1)} %add.32.own_ref), channel_id=1, source_target_pairs={{0,2},{1,3},{2,0},{3,1},{4,6},{5,7},{6,4},{7,5},{8,10},{9,11},{10,... | collective-permute-start | bytes 638984 | tf_op jit(solution)/shard_map/ppermute | solution.py:140
  136.8 5.0 %collective-permute-start.33 = (f32[32,512]{1,0:T(8,128)S(1)}, f32[32,512]{1,0:T(8,128)S(1)}, u32[]{:S(2)}, u32[]{:S(2)}) collective-permute-start(f32[32,512]{1,0:T(8,128)S(1)} %get-tuple-element.41), channel_id=1, source_target_pairs={{0,4},{4,0},{8,12},{12,8},{16,20},{20,16},{24,28},{28,24},{1,5},{5... | collective-permute-start | bytes 196616 | tf_op jit(solution)/shard_map/ppermute | solution.py:140
  138.2 4.3 %collective-permute-start.34 = (f32[32,512]{1,0:T(8,128)S(1)}, f32[32,512]{1,0:T(8,128)S(1)}, u32[]{:S(2)}, u32[]{:S(2)}) collective-permute-start(f32[32,512]{1,0:T(8,128)S(1)} %get-tuple-element.42), channel_id=1, source_target_pairs={{0,8},{4,12},{8,0},{12,4},{16,24},{20,28},{24,16},{28,20},{1,9},{5... | collective-permute-start | bytes 196616 | tf_op jit(solution)/shard_map/ppermute | solution.py:140
  138.3 5.2 %collective-permute-start.35 = (f32[32,512]{1,0:T(8,128)S(1)}, f32[32,512]{1,0:T(8,128)S(1)}, u32[]{:S(2)}, u32[]{:S(2)}) collective-permute-start(f32[32,512]{1,0:T(8,128)S(1)} %get-tuple-element.43), channel_id=1, source_target_pairs={{0,12},{4,8},{8,4},{12,0},{16,28},{20,24},{24,20},{28,16},{1,13},{... | collective-permute-start | bytes 196616 | tf_op jit(solution)/shard_map/ppermute | solution.py:140
  143.5 5.3 %collective-permute-start.36 = (f32[32,512]{1,0:T(8,128)S(1)}, f32[32,512]{1,0:T(8,128)S(1)}, u32[]{:S(2)}, u32[]{:S(2)}) collective-permute-start(f32[32,512]{1,0:T(8,128)S(1)} %add.33.refs_0_), channel_id=1, source_target_pairs={{0,16},{4,20},{8,24},{12,28},{16,0},{20,4},{24,8},{28,12},{1,17},{... | collective-permute-start | bytes 196616 | tf_op jit(solution)/shard_map/ppermute | solution.py:140
  148.8 5.2 %collective-permute-start.39 = (f32[32,512]{1,0:T(8,128)S(1)}, f32[32,512]{1,0:T(8,128)S(1)}, u32[]{:S(2)}, u32[]{:S(2)}) collective-permute-start(f32[32,512]{1,0:T(8,128)S(1)} %add.34.c0), channel_id=1, source_target_pairs={{0,12},{4,8},{8,4},{12,0},{16,28},{20,24},{24,20},{28,16},{1,13},{... | collective-permute-start | bytes 196616 | tf_op jit(solution)/shard_map/ppermute | solution.py:140
  150.8 4.3 %collective-permute-start.38 = (f32[32,512]{1,0:T(8,128)S(1)}, f32[32,512]{1,0:T(8,128)S(1)}, u32[]{:S(2)}, u32[]{:S(2)}) collective-permute-start(f32[32,512]{1,0:T(8,128)S(1)} %add.34.c0), channel_id=1, source_target_pairs={{0,8},{4,12},{8,0},{12,4},{16,24},{20,28},{24,16},{28,20},{1,9},{5... | collective-permute-start | bytes 196616 | tf_op jit(solution)/shard_map/ppermute | solution.py:140
  159.4 7.4 %collective-permute-start.41 = (f32[32,1664]{1,0:T(8,128)S(1)}, f32[32,1664]{1,0:T(8,128)S(1)}, u32[]{:S(2)}, u32[]{:S(2)}) collective-permute-start(f32[32,1664]{1,0:T(8,128)S(1)} %add.35.own_ref), channel_id=1, source_target_pairs={{0,2},{1,3},{2,0},{3,1},{4,6},{5,7},{6,4},{7,5},{8,10},{9,11},{10,... | collective-permute-start | bytes 638984 | tf_op jit(solution)/shard_map/ppermute | solution.py:140
  (15 other events, 61.6 us)

commit v2 on v0

v2 whole, which is shorter than its diff:
```python
import functools

import jax
import jax.numpy as jnp
from jax import lax
from jax.experimental import pallas as pl
from jax.experimental.pallas import tpu as pltpu
from jax.sharding import PartitionSpec as P

ITERS = 4
PEERS = 4
LANES = 128
EXTRA = 8
LONG = pl.CostEstimate(flops=2**34, bytes_accessed=0, transcendentals=0)
SHORT = pl.CostEstimate(flops=2**29, bytes_accessed=0, transcendentals=0)
HIGHEST = lax.Precision.HIGHEST
VMEM = pl.BlockSpec(memory_space=pltpu.VMEM)
HBM = pl.BlockSpec(memory_space=pltpu.HBM)
F32 = jnp.float32
BF16 = jnp.bfloat16


def call(kernel, outputs, name, scratch=(), in_specs=None, mebibytes=20, cost=None):
    def run(*args):
        specs = in_specs or [VMEM] * len(args)
        return pl.pallas_call(
            kernel,
            out_shape=[jax.ShapeDtypeStruct(shape, dtype) for shape, dtype in outputs],
            in_specs=specs,
            out_specs=[VMEM] * len(outputs),
            scratch_shapes=scratch,
            compiler_params=pltpu.CompilerParams(vmem_limit_bytes=mebibytes * 2**20),
            cost_estimate=cost,
            name=name,
        )(*args)

    return run


def split(value):
    high = value.astype(BF16)
    low = (value - high.astype(F32)).astype(BF16)
    return jnp.concatenate([high, low], axis=0)


def join(value):
    half = value.shape[0] // 2
    return value[:half] + value[half:]


def total(*refs):
    terms = [ref[...].astype(F32) for ref in refs]
    while len(terms) > 1:
        terms = [sum(terms[i + 1 : i + 2], terms[i]) for i in range(0, len(terms), 2)]
    return terms[0]


def contract_last(left, right, precision=None):
    return lax.dot_general(
        left, right, (((1,), (1,)), ((), ())), preferred_element_type=F32, precision=precision
    )


def position():
    return lax.rem(lax.axis_index("tok"), PEERS)


def diagonal(n):
    return lax.broadcasted_iota(jnp.int32, (n, n), 0) == lax.broadcasted_iota(jnp.int32, (n, n), 1)


def first_projection_kernel(blocks, basis_hbm, rows_hbm, out_ref, rows_ref, basis_ref, sems):
    tokens = rows_ref.shape[0]
    height = tokens // blocks
    fetch_basis = pltpu.make_async_copy(basis_hbm, basis_ref, sems.at[blocks])
    fetch_basis.start()
    fetches = []
    for i in range(blocks):
        place = pl.ds(i * height, height)
        fetches.append(
            pltpu.make_async_copy(rows_hbm.at[place, :], rows_ref.at[place, :], sems.at[i])
        )
        fetches[-1].start()
    fetch_basis.wait()
    vectors = split(basis_ref[...])
    for i in range(blocks):
        fetches[i].wait()
        place = pl.ds(i * height, height)
        out_ref[:, place] = join(contract_last(vectors, rows_ref[place, :]))


def projection_kernel(part, first, *refs):
    chunk_ref, rows_ref, *refs = refs
    mean_ref = chunk_ref if first else refs.pop(0)
    n, width = mean_ref.shape[0] - EXTRA, chunk_ref.shape[1]
    place = pl.ds(pl.multiple_of((position() ^ part) * width, width), width)
    chunk = chunk_ref[:n, :]
    shift = jnp.sum(chunk * mean_ref[n : n + 1, :], axis=1, keepdims=True)
    projected = join(contract_last(split(chunk), rows_ref[:, place])) - shift
    gram = contract_last(chunk, chunk, HIGHEST)
    if part > 0:
        projected = refs.pop(0)[...] + projected
    if part == 1:
        gram = refs.pop(0)[...] + gram
    if part < PEERS - 1:
        refs[0][...] = projected
        refs[1][...] = gram
        return
    gram = refs[0][...] + (refs[1][...] + gram)
    out_ref, tokens = refs[2], rows_ref.shape[0]
    out_ref[:, :tokens] = projected
    out_ref[:, tokens:] = jnp.zeros((n, LANES), F32)
    out_ref[:, tokens : tokens + n] = gram


def inverse_factor_kernel(own_ref, got_ref, out_ref):
    n = own_ref.shape[0]
    gram = (own_ref[...] + got_ref[...])[:, :n]
    work = jnp.concatenate([gram, diagonal(n).astype(F32)], axis=1)
    index = lax.broadcasted_iota(jnp.int32, (n, 1), 0)
    scale = jnp.zeros((n, 1), F32)
    for k in range(0, n, 2):
        row0, row1 = work[k : k + 1, :], work[k + 1 : k + 2, :]
        column0, column1 = work[:, k : k + 1], work[:, k + 1 : k + 2]
        pivot0, beside = row0[:, k : k + 1], row0[:, k + 1 : k + 2]
        inverse0 = 1.0 / pivot0
        share0 = beside * inverse0
        pivot1 = row1[:, k + 1 : k + 2] - share0 * beside
        inverse1 = 1.0 / pivot1
        row1 = row1 - share0 * row0
        factor0 = column0 * inverse0
        factor1 = jnp.where(index > k + 1, (column1 - factor0 * beside) * inverse1, 0.0)
        factor0 = jnp.where(index > k, factor0, 0.0)
        scale = jnp.where(index == k, lax.rsqrt(pivot0), scale)
        scale = jnp.where(index == k + 1, lax.rsqrt(pivot1), scale)
        work = work - factor0 * row0 - factor1 * row1
    out_ref[...] = work[:, n:] * scale


def first_term(weights, rows, counts, centre, out_ref):
    n, width = counts.shape[0], out_ref.shape[1]
    term = jnp.dot(weights, rows, preferred_element_type=F32)
    sums = term[2 * n : 2 * n + 1]
    out_ref[:n, :] = join(term[: 2 * n]) + centre * sums
    out_ref[n:, :] = jnp.zeros((EXTRA, width), F32)
    out_ref[n : n + 1, :] = sums
    counts = jnp.where(diagonal(n), counts, 0.0)
    out_ref[n + 1 : n + 2, :n] = jnp.sum(counts, axis=0, keepdims=True)


def first_image_kernel(own_ref, got_ref, rows_ref, *outs):
    *outs, weights_ref, side_ref = outs
    tokens, n, width = rows_ref.shape[0], own_ref.shape[0], outs[0].shape[1]
    projected = total(own_ref, got_ref)[:, :tokens]
    centre = [jnp.sum(ref[:, tokens:].astype(F32), axis=1, keepdims=True) for ref in (own_ref, got_ref)]
    centre = centre[0] + centre[1]
    weights = split(projected)
    counts = join(jnp.sum(weights.astype(F32), axis=1, keepdims=True)) + centre * tokens
    weights = jnp.concatenate([weights, jnp.ones((2 * EXTRA, tokens), BF16)], axis=0)
    for part, out in enumerate(outs, 1):
        place = pl.ds(pl.multiple_of((position() ^ part) * width, width), width)
        first_term(weights, rows_ref[:, place], counts, centre, out)
    weights_ref[...] = weights
    side_ref[...] = jnp.broadcast_to(counts, side_ref.shape)
    side_ref[:, 1:2] = centre


def first_own_image_kernel(weights_ref, side_ref, rows_ref, out_ref):
    width = out_ref.shape[1]
    place = pl.ds(pl.multiple_of(position() * width, width), width)
    first_term(weights_ref[...], rows_ref[:, place], side_ref[:, :1], side_ref[:, 1:2], out_ref)


def first_total_kernel(rows_in_all, own_ref, got_ref, out_ref):
    n = own_ref.shape[0] - EXTRA
    value = own_ref[...] + got_ref[...]
    mean = value[n : n + 1] / rows_in_all
    counts = jnp.where(diagonal(n), value[n + 1 : n + 2, :n], 0.0)
    counts = jnp.sum(counts, axis=1, keepdims=True)
    out_ref[:n, :] = value[:n] - counts * mean
    out_ref[n:, :] = jnp.broadcast_to(mean, (EXTRA, mean.shape[1]))


def image_kernel(own_ref, got_ref, lower_ref, rows_ref, *refs):
    means, outs, (weights_ref, side_ref) = refs[: PEERS - 1], refs[PEERS - 1 : -2], refs[-2:]
    n, width = own_ref.shape[0], outs[0].shape[1]
    projected = total(own_ref, got_ref)
    projected = jnp.dot(lower_ref[...], projected, preferred_element_type=F32, precision=HIGHEST)
    weights = split(projected)
    counts = join(jnp.sum(weights.astype(F32), axis=1, keepdims=True))
    for part, (mean, out) in enumerate(zip(means, outs), 1):
        place = pl.ds(pl.multiple_of((position() ^ part) * width, width), width)
        term = join(jnp.dot(weights, rows_ref[:, place], preferred_element_type=F32))
        out[...] = term - counts * mean[n : n + 1, :]
    weights_ref[...] = weights
    side_ref[...] = jnp.broadcast_to(counts, side_ref.shape)


def own_image_kernel(weights_ref, side_ref, rows_ref, mean_ref, out_ref):
    n, width = out_ref.shape
    place = pl.ds(pl.multiple_of(position() * width, width), width)
    term = join(jnp.dot(weights_ref[...], rows_ref[:, place], preferred_element_type=F32))
    out_ref[...] = term - side_ref[:, :1] * mean_ref[n : n + 1, :]


def assemble_kernel(c0, c1, c2, c3, out_ref):
    n, width = out_ref.shape[0], c0.shape[1]
    for part, chunk in enumerate((c0, c1, c2, c3)):
        place = pl.ds(pl.multiple_of((position() ^ part) * width, width), width)
        out_ref[:, place] = chunk[:n, :]


def last_kernel(own_ref, got_ref, lower_ref, image_ref, scores_ref, basis_ref):
    n = own_ref.shape[0]
    lower = lower_ref[...]
    basis_ref[...] = jnp.dot(lower, image_ref[...], preferred_element_type=F32, precision=HIGHEST)
    projected = total(own_ref, got_ref)
    projected = jnp.dot(lower, projected, preferred_element_type=F32, precision=HIGHEST)
    scores_ref[...] = jnp.sum(projected * projected, axis=0) / n


def add_kernel(*refs):
    refs[-1][...] = total(*refs[:-1])


def add(*terms):
    return call(add_kernel, [(terms[0].shape, F32)], "add")(*terms)[0]


def part_kernel(*refs):
    *terms, projected_ref, gram_ref = refs
    tokens = projected_ref.shape[1]
    value = total(*terms)
    projected_ref[...] = value[:, :tokens].astype(projected_ref.dtype)
    gram_ref[...] = value[:, tokens:]


def first_part_kernel(*refs):
    *terms, out_ref = refs
    tokens = out_ref.shape[1] - LANES
    value = total(*terms)
    centre = jnp.sum(value, axis=1, keepdims=True) / tokens
    out_ref[:, :tokens] = (value - centre).astype(BF16)
    out_ref[:, tokens:] = jnp.zeros((value.shape[0], LANES), BF16)
    for lane in range(3):
        term = centre.astype(BF16)
        out_ref[:, tokens + lane : tokens + lane + 1] = term
        centre = centre - term.astype(F32)


def swap(value, axis, distance):
    size = lax.axis_size(axis)
    return lax.ppermute(value, axis, [(i, i ^ distance) for i in range(size)])


def distances(axis, start):
    step, size = start, lax.axis_size(axis)
    while step < size:
        yield step
        step *= 2


def sum_but_last(value, axis):
    terms = [value]
    for step in list(distances(axis, 1))[:-1]:
        terms = [add(*terms)] if len(terms) > 1 else terms
        terms.append(swap(terms[0], axis, step))
    return terms


def share(value, axis):
    return [value] + [swap(value, axis, d) for d in range(1, PEERS)]


def on_device(activations, start_basis):
    tokens, features = activations.shape
    n = start_basis.shape[0]
    width = features // PEERS
    rows_in_all = tokens * lax.axis_size("tok")
    last_feat = lax.axis_size("feat") // 2

    blocks = 3
    partial, rows = call(
        functools.partial(first_projection_kernel, blocks),
        [((n, tokens), F32), (activations.shape, BF16)],
        "first_projection",
        scratch=[pltpu.VMEM((n, features), F32), pltpu.SemaphoreType.DMA((blocks + 1,))],
        in_specs=[HBM, HBM],
        mebibytes=46,
    )(start_basis, activations)
    terms = sum_but_last(partial, "feat")
    own = call(first_part_kernel, [((n, tokens + LANES), BF16)], "first_part")(*terms)[0]
    got = swap(own, "feat", last_feat)
    packed, side = ((n, tokens + LANES), F32), ((n, LANES), F32)
    for step in range(ITERS):
        first = step == 0
        chunk = ((n + EXTRA if first else n, width), F32)
        weights = ((2 * n + 2 * EXTRA if first else 2 * n, tokens), BF16)
        outputs = [chunk] * (PEERS - 1) + [weights, side]
        if first:
            *terms, weights, sums = call(first_image_kernel, outputs, "first_image")(own, got, rows)
            received = [swap(term, "tok", d) for d, term in enumerate(terms, 1)]
            kept = call(first_own_image_kernel, [chunk], "first_own_image", cost=SHORT)(weights, sums, rows)
        else:
            *terms, weights, sums = call(image_kernel, outputs, "image")(own, got, lower, rows, *means[1:])
            received = [swap(term, "tok", d) for d, term in enumerate(terms, 1)]
            kept = call(own_image_kernel, [chunk], "own_image", cost=SHORT)(weights, sums, rows, means[0])
        image = add(*kept, *received)
        *steps, last_step = distances("tok", PEERS)
        for distance in steps:
            image = add(image, swap(image, "tok", distance))
        kernel = functools.partial(first_total_kernel, rows_in_all) if first else add_kernel
        image = call(kernel, [chunk], "total")(image, swap(image, "tok", last_step))[0]
        images = share(image, "tok")
        if first:
            means = images
        before = []
        for part, image in enumerate(images):
            last = part == PEERS - 1
            operands = [image, rows] + ([] if first else [means[part]])
            operands += [projected] if part else []
            operands += before[:1] if part == 1 else before[1:] if last else []
            projected, *gram = call(
                functools.partial(projection_kernel, part, first),
                [packed] if last else [((n, tokens), F32), ((n, n), F32)],
                "projection",
                cost=SHORT,
            )(*operands)
            before += gram
        terms = sum_but_last(projected, "feat")
        sent = BF16 if step == ITERS - 1 else F32
        own, gram = call(part_kernel, [((n, tokens), sent), side], "part")(*terms)
        got_gram = swap(gram, "feat", last_feat)
        got = swap(own, "feat", last_feat)
        lower = call(inverse_factor_kernel, [((n, n), F32)], "inverse_factor", cost=LONG)(gram, got_gram)[0]
    image = call(assemble_kernel, [((n, features), F32)], "assemble")(*images)[0]
    outputs = [((tokens,), F32), ((n, features), F32)]
    return tuple(call(last_kernel, outputs, "last")(own, got, lower, image))


def solution(mesh):
    in_specs = (P("tok", "feat"), P(None, "feat"))
    out_specs = (P("tok"), P(None, "feat"))
    return jax.shard_map(
        on_device, mesh=mesh, in_specs=in_specs, out_specs=out_specs, check_vma=False
    )
```

time: 529 us -> 142 us (0.27)
  waiting for transfers between devices: 312 us -> 50.3 us
  blocking collectives: 112 us -> 0 us
  matrix products: 55.3 us -> 0 us
  starting transfers between devices: 0.21 us -> 53.9 us
  Pallas kernels: 0 us -> 36 us
  other arithmetic: 32.8 us -> 0 us
  between operations: 15.2 us -> 0.85 us
    psum x5 -> x0, waiting for transfers between devices: 312 us -> none  [the longest x4 280 us: advance(): image = lax.psum(term, 'tok')]
    psum x9 -> x0, blocking collectives: 112 us -> none  [the longest x4 48.5 us: project(): lax.psum(partial_projection(activations, vectors, local_mean), 'feat')]
    ppermute x0 -> x42, starting transfers between devices: none -> 53.9 us  [swap(): return lax.ppermute(value, axis, [(i, i ^ distance) for i in range(size)])]
    ppermute x0 -> x42, waiting for transfers between devices: none -> 50.3 us  [swap(): return lax.ppermute(value, axis, [(i, i ^ distance) for i in range(size)])]
    dot_general x18 -> x0, matrix products: 49.7 us -> none  [the longest x5 24.7 us: partial_projection(): lax.dot_general(vectors, activations, (((1,), (1,)), ((), ())), preferred...]
    pallas_call x0 -> x44, Pallas kernels: none -> 36 us  [run(): pl.pallas_call(kernel, out_shape=[jax.ShapeDtypeStruct(shape, dtype) for...]
    another operation x20 -> x0, other arithmetic: 26.7 us -> none  [the longest x12 14.4 us: advance(): lower = jnp.linalg.cholesky(gram)]
    another operation x4 -> x0, matrix products: 5.56 us -> none  [advance(): return jax.scipy.linalg.solve_triangular(lower, image, lower=True)]
  transfers between devices with their start and end apart: 5 -> 42, of which waited for: 5 -> 38; matrix products, arithmetic and copies ran while one was open for 0% -> 0% of each run, Pallas kernels for 0% -> 17%
where the time goes in v2:
time: 142 us
  starting transfers between devices  53.9 us (38%)
  waiting for transfers between devices  50.3 us (35%)
  Pallas kernels  36 us (25%)
    ppermute x42, starting transfers between devices, swap(): return lax.ppermute(value, axis, [(i, i ^ distance) for i in range(size)])  53.9 us
    ppermute x42, waiting for transfers between devices, swap(): return lax.ppermute(value, axis, [(i, i ^ distance) for i in range(size)])  50.3 us
    pallas_call x44, Pallas kernels, run(): pl.pallas_call(kernel, out_shape=[jax.ShapeDtypeStruct(shape, dtype) for...  36 us
  transfers between devices with their start and end apart: 42, of which 38 were waited for; matrix products, arithmetic and copies ran while one was open for 0% of the time, Pallas kernels for 17%

profile of v2, /device:TPU:0, one launch (start us, length us, event | category | flops | bytes accessed | tf_op | source)
XLA Modules:
  0.0 142.0 jit_solution(1459720737048553148)
XLA Ops:
  1.6 3.9 %first_projection.1 = (f32[32,1536]{1,0:T(8,128)S(1)}, bf16[1536,2048]{1,0:T(8,128)(2,1)S(1)}) custom-call(f32[32,2048]{1,0:T(8,128)S(1)} %copy-done, bf16[1536,2048]{1,0:T(8,128)(2,1)} %rows_hbm.1), custom_call_target="tpu_custom_call" | custom-call | tf_op jit(solution)/shard_map/first_projection/pallas_call | solution.py:26
  7.2 2.9 %collective-permute-start.1 = (bf16[32,1664]{1,0:T(8,128)(2,1)S(1)}, bf16[32,1664]{1,0:T(8,128)(2,1)S(1)}, u32[]{:S(2)}, u32[]{:S(2)}) collective-permute-start(bf16[32,1664]{1,0:T(8,128)(2,1)S(1)} %first_part.1.own_ref), channel_id=1, source_target_pairs={{0,2},{1,3},{2,0},{3,1},{4,6},{5,7},{6,4},{7,5},{8,10},{9,11},{10,... | collective-permute-start | bytes 319496 | tf_op jit(solution)/shard_map/ppermute | solution.py:253
  10.1 3.3 %collective-permute-done.1.got_ref = bf16[32,1664]{1,0:T(8,128)(2,1)S(1)} collective-permute-done((bf16[32,1664]{1,0:T(8,128)(2,1)S(1)}, bf16[32,1664]{1,0:T(8,128)(2,1)S(1)}, u32[]{:S(2)}, u32[]{:S(2)}) %collective-permute-start.1) | collective-permute-done | bytes 106528 | tf_op jit(solution)/shard_map/ppermute | solution.py:253
  14.4 1.8 %collective-permute-start.2 = (f32[40,512]{1,0:T(8,128)S(1)}, f32[40,512]{1,0:T(8,128)S(1)}, u32[]{:S(2)}, u32[]{:S(2)}) collective-permute-start(f32[40,512]{1,0:T(8,128)S(1)} %get-tuple-element.60), channel_id=1, source_target_pairs={{0,4},{4,0},{8,12},{12,8},{16,20},{20,16},{24,28},{28,24},{1,5},{5... | collective-permute-start | bytes 245768 | tf_op jit(solution)/shard_map/ppermute | solution.py:253
  18.9 1.9 %collective-permute-done.3.refs_2_ = f32[40,512]{1,0:T(8,128)S(1)} collective-permute-done((f32[40,512]{1,0:T(8,128)S(1)}, f32[40,512]{1,0:T(8,128)S(1)}, u32[]{:S(2)}, u32[]{:S(2)}) %collective-permute-start.3) | collective-permute-done | bytes 81952 | tf_op jit(solution)/shard_map/ppermute | solution.py:253
  20.8 2.3 %collective-permute-done.4.refs_3_ = f32[40,512]{1,0:T(8,128)S(1)} collective-permute-done((f32[40,512]{1,0:T(8,128)S(1)}, f32[40,512]{1,0:T(8,128)S(1)}, u32[]{:S(2)}, u32[]{:S(2)}) %collective-permute-start.4) | collective-permute-done | bytes 81952 | tf_op jit(solution)/shard_map/ppermute | solution.py:253
  23.2 2.8 %collective-permute-start.5 = (f32[40,512]{1,0:T(8,128)S(1)}, f32[40,512]{1,0:T(8,128)S(1)}, u32[]{:S(2)}, u32[]{:S(2)}) collective-permute-start(f32[40,512]{1,0:T(8,128)S(1)} %add.4.own_ref), channel_id=1, source_target_pairs={{0,16},{4,20},{8,24},{12,28},{16,0},{20,4},{24,8},{28,12},{1,17},{... | collective-permute-start | bytes 245768 | tf_op jit(solution)/shard_map/ppermute | solution.py:253
  26.0 3.4 %collective-permute-done.5.got_ref = f32[40,512]{1,0:T(8,128)S(1)} collective-permute-done((f32[40,512]{1,0:T(8,128)S(1)}, f32[40,512]{1,0:T(8,128)S(1)}, u32[]{:S(2)}, u32[]{:S(2)}) %collective-permute-start.5) | collective-permute-done | bytes 81952 | tf_op jit(solution)/shard_map/ppermute | solution.py:253
  30.2 2.7 %collective-permute-start.6 = (f32[40,512]{1,0:T(8,128)S(1)}, f32[40,512]{1,0:T(8,128)S(1)}, u32[]{:S(2)}, u32[]{:S(2)}) collective-permute-start(f32[40,512]{1,0:T(8,128)S(1)} %total.4.refs_0_.mean_ref.refs_2_), channel_id=1, source_target_pairs={{0,12},{4,8},{8,4},{12,0},{16,28},{20,24},{24,20},{28,16},{1,13},{... | collective-permute-start | bytes 245768 | tf_op jit(solution)/shard_map/ppermute | solution.py:253
  40.5 1.7 %collective-permute-done.11.got_ref = f32[32,128]{1,0:T(8,128)S(1)} collective-permute-done((f32[32,128]{1,0:T(8,128)S(1)}, f32[32,128]{1,0:T(8,128)S(1)}, u32[]{:S(2)}, u32[]{:S(2)}) %collective-permute-start.11) | collective-permute-done | bytes 16416 | tf_op jit(solution)/shard_map/ppermute | solution.py:253
  42.3 3.5 %inverse_factor.4.lower_ref = f32[32,32]{1,0:T(8,128)S(1)} custom-call(f32[32,128]{1,0:T(8,128)S(1)} %get-tuple-element.70.own_ref, f32[32,128]{1,0:T(8,128)S(1)} %collective-permute-done.11.got_ref), custom_call_target="tpu_custom_call" | custom-call | flops 17179869184 | tf_op jit(solution)/shard_map/inverse_factor/pallas_call | solution.py:26
  48.4 2.0 %collective-permute-start.13 = (f32[32,512]{1,0:T(8,128)S(1)}, f32[32,512]{1,0:T(8,128)S(1)}, u32[]{:S(2)}, u32[]{:S(2)}) collective-permute-start(f32[32,512]{1,0:T(8,128)S(1)} %get-tuple-element.74), channel_id=1, source_target_pairs={{0,8},{4,12},{8,0},{12,4},{16,24},{20,28},{24,16},{28,20},{1,9},{5... | collective-permute-start | bytes 196616 | tf_op jit(solution)/shard_map/ppermute | solution.py:253
  52.9 2.7 %collective-permute-done.14.refs_3_ = f32[32,512]{1,0:T(8,128)S(1)} collective-permute-done((f32[32,512]{1,0:T(8,128)S(1)}, f32[32,512]{1,0:T(8,128)S(1)}, u32[]{:S(2)}, u32[]{:S(2)}) %collective-permute-start.14) | collective-permute-done | bytes 65568 | tf_op jit(solution)/shard_map/ppermute | solution.py:253
  55.6 3.5 %collective-permute-start.15 = (f32[32,512]{1,0:T(8,128)S(1)}, f32[32,512]{1,0:T(8,128)S(1)}, u32[]{:S(2)}, u32[]{:S(2)}) collective-permute-start(f32[32,512]{1,0:T(8,128)S(1)} %add.5.refs_0_), channel_id=1, source_target_pairs={{0,16},{4,20},{8,24},{12,28},{16,0},{20,4},{24,8},{28,12},{1,17},{... | collective-permute-start | bytes 196616 | tf_op jit(solution)/shard_map/ppermute | solution.py:253
  59.1 2.4 %collective-permute-done.15.refs_1_ = f32[32,512]{1,0:T(8,128)S(1)} collective-permute-done((f32[32,512]{1,0:T(8,128)S(1)}, f32[32,512]{1,0:T(8,128)S(1)}, u32[]{:S(2)}, u32[]{:S(2)}) %collective-permute-start.15) | collective-permute-done | bytes 65568 | tf_op jit(solution)/shard_map/ppermute | solution.py:253
  62.5 2.6 %collective-permute-start.16 = (f32[32,512]{1,0:T(8,128)S(1)}, f32[32,512]{1,0:T(8,128)S(1)}, u32[]{:S(2)}, u32[]{:S(2)}) collective-permute-start(f32[32,512]{1,0:T(8,128)S(1)} %total.5.refs_0_), channel_id=1, source_target_pairs={{0,12},{4,8},{8,4},{12,0},{16,28},{20,24},{24,20},{28,16},{1,13},{... | collective-permute-start | bytes 196616 | tf_op jit(solution)/shard_map/ppermute | solution.py:253
  72.3 1.8 %collective-permute-done.21.got_ref = f32[32,128]{1,0:T(8,128)S(1)} collective-permute-done((f32[32,128]{1,0:T(8,128)S(1)}, f32[32,128]{1,0:T(8,128)S(1)}, u32[]{:S(2)}, u32[]{:S(2)}) %collective-permute-start.21) | collective-permute-done | bytes 16416 | tf_op jit(solution)/shard_map/ppermute | solution.py:253
  74.1 3.5 %inverse_factor.5.lower_ref = f32[32,32]{1,0:T(8,128)S(1)} custom-call(f32[32,128]{1,0:T(8,128)S(1)} %get-tuple-element.83.own_ref, f32[32,128]{1,0:T(8,128)S(1)} %collective-permute-done.21.got_ref), custom_call_target="tpu_custom_call" | custom-call | flops 17179869184 | tf_op jit(solution)/shard_map/inverse_factor/pallas_call | solution.py:26
  79.7 1.9 %collective-permute-start.23 = (f32[32,512]{1,0:T(8,128)S(1)}, f32[32,512]{1,0:T(8,128)S(1)}, u32[]{:S(2)}, u32[]{:S(2)}) collective-permute-start(f32[32,512]{1,0:T(8,128)S(1)} %get-tuple-element.87), channel_id=1, source_target_pairs={{0,8},{4,12},{8,0},{12,4},{16,24},{20,28},{24,16},{28,20},{1,9},{5... | collective-permute-start | bytes 196616 | tf_op jit(solution)/shard_map/ppermute | solution.py:253
  84.5 2.3 %collective-permute-done.24.refs_3_ = f32[32,512]{1,0:T(8,128)S(1)} collective-permute-done((f32[32,512]{1,0:T(8,128)S(1)}, f32[32,512]{1,0:T(8,128)S(1)}, u32[]{:S(2)}, u32[]{:S(2)}) %collective-permute-start.24) | collective-permute-done | bytes 65568 | tf_op jit(solution)/shard_map/ppermute | solution.py:253
  86.8 3.4 %collective-permute-start.25 = (f32[32,512]{1,0:T(8,128)S(1)}, f32[32,512]{1,0:T(8,128)S(1)}, u32[]{:S(2)}, u32[]{:S(2)}) collective-permute-start(f32[32,512]{1,0:T(8,128)S(1)} %add.6.refs_0_), channel_id=1, source_target_pairs={{0,16},{4,20},{8,24},{12,28},{16,0},{20,4},{24,8},{28,12},{1,17},{... | collective-permute-start | bytes 196616 | tf_op jit(solution)/shard_map/ppermute | solution.py:253
  90.2 2.2 %collective-permute-done.25.refs_1_ = f32[32,512]{1,0:T(8,128)S(1)} collective-permute-done((f32[32,512]{1,0:T(8,128)S(1)}, f32[32,512]{1,0:T(8,128)S(1)}, u32[]{:S(2)}, u32[]{:S(2)}) %collective-permute-start.25) | collective-permute-done | bytes 65568 | tf_op jit(solution)/shard_map/ppermute | solution.py:253
  93.9 2.1 %collective-permute-start.26 = (f32[32,512]{1,0:T(8,128)S(1)}, f32[32,512]{1,0:T(8,128)S(1)}, u32[]{:S(2)}, u32[]{:S(2)}) collective-permute-start(f32[32,512]{1,0:T(8,128)S(1)} %total.6.refs_0_), channel_id=1, source_target_pairs={{0,12},{4,8},{8,4},{12,0},{16,28},{20,24},{24,20},{28,16},{1,13},{... | collective-permute-start | bytes 196616 | tf_op jit(solution)/shard_map/ppermute | solution.py:253
  103.4 1.7 %collective-permute-done.31.got_ref = f32[32,128]{1,0:T(8,128)S(1)} collective-permute-done((f32[32,128]{1,0:T(8,128)S(1)}, f32[32,128]{1,0:T(8,128)S(1)}, u32[]{:S(2)}, u32[]{:S(2)}) %collective-permute-start.31) | collective-permute-done | bytes 16416 | tf_op jit(solution)/shard_map/ppermute | solution.py:253
  105.1 3.5 %inverse_factor.6.lower_ref = f32[32,32]{1,0:T(8,128)S(1)} custom-call(f32[32,128]{1,0:T(8,128)S(1)} %get-tuple-element.96.own_ref, f32[32,128]{1,0:T(8,128)S(1)} %collective-permute-done.31.got_ref), custom_call_target="tpu_custom_call" | custom-call | flops 17179869184 | tf_op jit(solution)/shard_map/inverse_factor/pallas_call | solution.py:26
  111.5 2.0 %collective-permute-start.33 = (f32[32,512]{1,0:T(8,128)S(1)}, f32[32,512]{1,0:T(8,128)S(1)}, u32[]{:S(2)}, u32[]{:S(2)}) collective-permute-start(f32[32,512]{1,0:T(8,128)S(1)} %get-tuple-element.100), channel_id=1, source_target_pairs={{0,8},{4,12},{8,0},{12,4},{16,24},{20,28},{24,16},{28,20},{1,9},{5... | collective-permute-start | bytes 196616 | tf_op jit(solution)/shard_map/ppermute | solution.py:253
  116.3 2.4 %collective-permute-done.34.refs_3_ = f32[32,512]{1,0:T(8,128)S(1)} collective-permute-done((f32[32,512]{1,0:T(8,128)S(1)}, f32[32,512]{1,0:T(8,128)S(1)}, u32[]{:S(2)}, u32[]{:S(2)}) %collective-permute-start.34) | collective-permute-done | bytes 65568 | tf_op jit(solution)/shard_map/ppermute | solution.py:253
  118.7 3.8 %collective-permute-start.35 = (f32[32,512]{1,0:T(8,128)S(1)}, f32[32,512]{1,0:T(8,128)S(1)}, u32[]{:S(2)}, u32[]{:S(2)}) collective-permute-start(f32[32,512]{1,0:T(8,128)S(1)} %add.7.refs_0_), channel_id=1, source_target_pairs={{0,16},{4,20},{8,24},{12,28},{16,0},{20,4},{24,8},{28,12},{1,17},{... | collective-permute-start | bytes 196616 | tf_op jit(solution)/shard_map/ppermute | solution.py:253
  122.5 2.3 %collective-permute-done.35.refs_1_ = f32[32,512]{1,0:T(8,128)S(1)} collective-permute-done((f32[32,512]{1,0:T(8,128)S(1)}, f32[32,512]{1,0:T(8,128)S(1)}, u32[]{:S(2)}, u32[]{:S(2)}) %collective-permute-start.35) | collective-permute-done | bytes 65568 | tf_op jit(solution)/shard_map/ppermute | solution.py:253
  125.7 2.7 %collective-permute-start.36 = (f32[32,512]{1,0:T(8,128)S(1)}, f32[32,512]{1,0:T(8,128)S(1)}, u32[]{:S(2)}, u32[]{:S(2)}) collective-permute-start(f32[32,512]{1,0:T(8,128)S(1)} %total.7.refs_0_.c0), channel_id=1, source_target_pairs={{0,12},{4,8},{8,4},{12,0},{16,28},{20,24},{24,20},{28,16},{1,13},{... | collective-permute-start | bytes 196616 | tf_op jit(solution)/shard_map/ppermute | solution.py:253
  135.7 1.7 %collective-permute-done.41.got_ref = f32[32,128]{1,0:T(8,128)S(1)} collective-permute-done((f32[32,128]{1,0:T(8,128)S(1)}, f32[32,128]{1,0:T(8,128)S(1)}, u32[]{:S(2)}, u32[]{:S(2)}) %collective-permute-start.41) | collective-permute-done | bytes 16416 | tf_op jit(solution)/shard_map/ppermute | solution.py:253
  137.4 3.5 %inverse_factor.7.lower_ref = f32[32,32]{1,0:T(8,128)S(1)} custom-call(f32[32,128]{1,0:T(8,128)S(1)} %get-tuple-element.109.own_ref, f32[32,128]{1,0:T(8,128)S(1)} %collective-permute-done.41.got_ref), custom_call_target="tpu_custom_call" | custom-call | flops 17179869184 | tf_op jit(solution)/shard_map/inverse_factor/pallas_call | solution.py:26
  (98 shorter events, 56.9 us)
Async XLA Ops:
  7.2 6.2 %collective-permute-start.1 = (bf16[32,1664]{1,0:T(8,128)(2,1)S(1)}, bf16[32,1664]{1,0:T(8,128)(2,1)S(1)}, u32[]{:S(2)}, u32[]{:S(2)}) collective-permute-start(bf16[32,1664]{1,0:T(8,128)(2,1)S(1)} %first_part.1.own_ref), channel_id=1, source_target_pairs={{0,2},{1,3},{2,0},{3,1},{4,6},{5,7},{6,4},{7,5},{8,10},{9,11},{10,... | collective-permute-start | bytes 319496 | tf_op jit(solution)/shard_map/ppermute | solution.py:253
  14.4 4.5 %collective-permute-start.2 = (f32[40,512]{1,0:T(8,128)S(1)}, f32[40,512]{1,0:T(8,128)S(1)}, u32[]{:S(2)}, u32[]{:S(2)}) collective-permute-start(f32[40,512]{1,0:T(8,128)S(1)} %get-tuple-element.60), channel_id=1, source_target_pairs={{0,4},{4,0},{8,12},{12,8},{16,20},{20,16},{24,28},{28,24},{1,5},{5... | collective-permute-start | bytes 245768 | tf_op jit(solution)/shard_map/ppermute | solution.py:253
  16.2 4.6 %collective-permute-start.3 = (f32[40,512]{1,0:T(8,128)S(1)}, f32[40,512]{1,0:T(8,128)S(1)}, u32[]{:S(2)}, u32[]{:S(2)}) collective-permute-start(f32[40,512]{1,0:T(8,128)S(1)} %get-tuple-element.61), channel_id=1, source_target_pairs={{0,8},{4,12},{8,0},{12,4},{16,24},{20,28},{24,16},{28,20},{1,9},{5... | collective-permute-start | bytes 245768 | tf_op jit(solution)/shard_map/ppermute | solution.py:253
  17.8 5.3 %collective-permute-start.4 = (f32[40,512]{1,0:T(8,128)S(1)}, f32[40,512]{1,0:T(8,128)S(1)}, u32[]{:S(2)}, u32[]{:S(2)}) collective-permute-start(f32[40,512]{1,0:T(8,128)S(1)} %get-tuple-element.62), channel_id=1, source_target_pairs={{0,12},{4,8},{8,4},{12,0},{16,28},{20,24},{24,20},{28,16},{1,13},{... | collective-permute-start | bytes 245768 | tf_op jit(solution)/shard_map/ppermute | solution.py:253
  23.2 6.2 %collective-permute-start.5 = (f32[40,512]{1,0:T(8,128)S(1)}, f32[40,512]{1,0:T(8,128)S(1)}, u32[]{:S(2)}, u32[]{:S(2)}) collective-permute-start(f32[40,512]{1,0:T(8,128)S(1)} %add.4.own_ref), channel_id=1, source_target_pairs={{0,16},{4,20},{8,24},{12,28},{16,0},{20,4},{24,8},{28,12},{1,17},{... | collective-permute-start | bytes 245768 | tf_op jit(solution)/shard_map/ppermute | solution.py:253
  29.4 4.4 %collective-permute-start.8 = (f32[40,512]{1,0:T(8,128)S(1)}, f32[40,512]{1,0:T(8,128)S(1)}, u32[]{:S(2)}, u32[]{:S(2)}) collective-permute-start(f32[40,512]{1,0:T(8,128)S(1)} %total.4.refs_0_.mean_ref.refs_2_), channel_id=1, source_target_pairs={{0,4},{4,0},{8,12},{12,8},{16,20},{20,16},{24,28},{28,24},{1,5},{5... | collective-permute-start | bytes 245768 | tf_op jit(solution)/shard_map/ppermute | solution.py:253
  30.0 4.5 %collective-permute-start.7 = (f32[40,512]{1,0:T(8,128)S(1)}, f32[40,512]{1,0:T(8,128)S(1)}, u32[]{:S(2)}, u32[]{:S(2)}) collective-permute-start(f32[40,512]{1,0:T(8,128)S(1)} %total.4.refs_0_.mean_ref.refs_2_), channel_id=1, source_target_pairs={{0,8},{4,12},{8,0},{12,4},{16,24},{20,28},{24,16},{28,20},{1,9},{5... | collective-permute-start | bytes 245768 | tf_op jit(solution)/shard_map/ppermute | solution.py:253
  30.2 6.0 %collective-permute-start.6 = (f32[40,512]{1,0:T(8,128)S(1)}, f32[40,512]{1,0:T(8,128)S(1)}, u32[]{:S(2)}, u32[]{:S(2)}) collective-permute-start(f32[40,512]{1,0:T(8,128)S(1)} %total.4.refs_0_.mean_ref.refs_2_), channel_id=1, source_target_pairs={{0,12},{4,8},{8,4},{12,0},{16,28},{20,24},{24,20},{28,16},{1,13},{... | collective-permute-start | bytes 245768 | tf_op jit(solution)/shard_map/ppermute | solution.py:253
  40.0 6.6 %collective-permute-start.10 = (f32[32,1536]{1,0:T(8,128)S(1)}, f32[32,1536]{1,0:T(8,128)S(1)}, u32[]{:S(2)}, u32[]{:S(2)}) collective-permute-start(f32[32,1536]{1,0:T(8,128)S(1)} %get-tuple-element.69.own_ref), channel_id=1, source_target_pairs={{0,2},{1,3},{2,0},{3,1},{4,6},{5,7},{6,4},{7,5},{8,10},{9,11},{10,... | collective-permute-start | bytes 589832 | tf_op jit(solution)/shard_map/ppermute | solution.py:253
  47.8 4.3 %collective-permute-start.12 = (f32[32,512]{1,0:T(8,128)S(1)}, f32[32,512]{1,0:T(8,128)S(1)}, u32[]{:S(2)}, u32[]{:S(2)}) collective-permute-start(f32[32,512]{1,0:T(8,128)S(1)} %get-tuple-element.73), channel_id=1, source_target_pairs={{0,4},{4,0},{8,12},{12,8},{16,20},{20,16},{24,28},{28,24},{1,5},{5... | collective-permute-start | bytes 196616 | tf_op jit(solution)/shard_map/ppermute | solution.py:253
  48.4 4.4 %collective-permute-start.13 = (f32[32,512]{1,0:T(8,128)S(1)}, f32[32,512]{1,0:T(8,128)S(1)}, u32[]{:S(2)}, u32[]{:S(2)}) collective-permute-start(f32[32,512]{1,0:T(8,128)S(1)} %get-tuple-element.74), channel_id=1, source_target_pairs={{0,8},{4,12},{8,0},{12,4},{16,24},{20,28},{24,16},{28,20},{1,9},{5... | collective-permute-start | bytes 196616 | tf_op jit(solution)/shard_map/ppermute | solution.py:253
  50.4 5.2 %collective-permute-start.14 = (f32[32,512]{1,0:T(8,128)S(1)}, f32[32,512]{1,0:T(8,128)S(1)}, u32[]{:S(2)}, u32[]{:S(2)}) collective-permute-start(f32[32,512]{1,0:T(8,128)S(1)} %get-tuple-element.75), channel_id=1, source_target_pairs={{0,12},{4,8},{8,4},{12,0},{16,28},{20,24},{24,20},{28,16},{1,13},{... | collective-permute-start | bytes 196616 | tf_op jit(solution)/shard_map/ppermute | solution.py:253
  55.6 5.8 %collective-permute-start.15 = (f32[32,512]{1,0:T(8,128)S(1)}, f32[32,512]{1,0:T(8,128)S(1)}, u32[]{:S(2)}, u32[]{:S(2)}) collective-permute-start(f32[32,512]{1,0:T(8,128)S(1)} %add.5.refs_0_), channel_id=1, source_target_pairs={{0,16},{4,20},{8,24},{12,28},{16,0},{20,4},{24,8},{28,12},{1,17},{... | collective-permute-start | bytes 196616 | tf_op jit(solution)/shard_map/ppermute | solution.py:253
  61.5 4.3 %collective-permute-start.18 = (f32[32,512]{1,0:T(8,128)S(1)}, f32[32,512]{1,0:T(8,128)S(1)}, u32[]{:S(2)}, u32[]{:S(2)}) collective-permute-start(f32[32,512]{1,0:T(8,128)S(1)} %total.5.refs_0_), channel_id=1, source_target_pairs={{0,4},{4,0},{8,12},{12,8},{16,20},{20,16},{24,28},{28,24},{1,5},{5... | collective-permute-start | bytes 196616 | tf_op jit(solution)/shard_map/ppermute | solution.py:253
  62.2 4.3 %collective-permute-start.17 = (f32[32,512]{1,0:T(8,128)S(1)}, f32[32,512]{1,0:T(8,128)S(1)}, u32[]{:S(2)}, u32[]{:S(2)}) collective-permute-start(f32[32,512]{1,0:T(8,128)S(1)} %total.5.refs_0_), channel_id=1, source_target_pairs={{0,8},{4,12},{8,0},{12,4},{16,24},{20,28},{24,16},{28,20},{1,9},{5... | collective-permute-start | bytes 196616 | tf_op jit(solution)/shard_map/ppermute | solution.py:253
  62.5 5.5 %collective-permute-start.16 = (f32[32,512]{1,0:T(8,128)S(1)}, f32[32,512]{1,0:T(8,128)S(1)}, u32[]{:S(2)}, u32[]{:S(2)}) collective-permute-start(f32[32,512]{1,0:T(8,128)S(1)} %total.5.refs_0_), channel_id=1, source_target_pairs={{0,12},{4,8},{8,4},{12,0},{16,28},{20,24},{24,20},{28,16},{1,13},{... | collective-permute-start | bytes 196616 | tf_op jit(solution)/shard_map/ppermute | solution.py:253
  70.8 6.9 %collective-permute-start.20 = (f32[32,1536]{1,0:T(8,128)S(1)}, f32[32,1536]{1,0:T(8,128)S(1)}, u32[]{:S(2)}, u32[]{:S(2)}) collective-permute-start(f32[32,1536]{1,0:T(8,128)S(1)} %get-tuple-element.82.own_ref), channel_id=1, source_target_pairs={{0,2},{1,3},{2,0},{3,1},{4,6},{5,7},{6,4},{7,5},{8,10},{9,11},{10,... | collective-permute-start | bytes 589832 | tf_op jit(solution)/shard_map/ppermute | solution.py:253
  78.8 4.3 %collective-permute-start.22 = (f32[32,512]{1,0:T(8,128)S(1)}, f32[32,512]{1,0:T(8,128)S(1)}, u32[]{:S(2)}, u32[]{:S(2)}) collective-permute-start(f32[32,512]{1,0:T(8,128)S(1)} %get-tuple-element.86), channel_id=1, source_target_pairs={{0,4},{4,0},{8,12},{12,8},{16,20},{20,16},{24,28},{28,24},{1,5},{5... | collective-permute-start | bytes 196616 | tf_op jit(solution)/shard_map/ppermute | solution.py:253
  79.7 4.8 %collective-permute-start.23 = (f32[32,512]{1,0:T(8,128)S(1)}, f32[32,512]{1,0:T(8,128)S(1)}, u32[]{:S(2)}, u32[]{:S(2)}) collective-permute-start(f32[32,512]{1,0:T(8,128)S(1)} %get-tuple-element.87), channel_id=1, source_target_pairs={{0,8},{4,12},{8,0},{12,4},{16,24},{20,28},{24,16},{28,20},{1,9},{5... | collective-permute-start | bytes 196616 | tf_op jit(solution)/shard_map/ppermute | solution.py:253
  81.6 5.2 %collective-permute-start.24 = (f32[32,512]{1,0:T(8,128)S(1)}, f32[32,512]{1,0:T(8,128)S(1)}, u32[]{:S(2)}, u32[]{:S(2)}) collective-permute-start(f32[32,512]{1,0:T(8,128)S(1)} %get-tuple-element.88), channel_id=1, source_target_pairs={{0,12},{4,8},{8,4},{12,0},{16,28},{20,24},{24,20},{28,16},{1,13},{... | collective-permute-start | bytes 196616 | tf_op jit(solution)/shard_map/ppermute | solution.py:253
  86.8 5.6 %collective-permute-start.25 = (f32[32,512]{1,0:T(8,128)S(1)}, f32[32,512]{1,0:T(8,128)S(1)}, u32[]{:S(2)}, u32[]{:S(2)}) collective-permute-start(f32[32,512]{1,0:T(8,128)S(1)} %add.6.refs_0_), channel_id=1, source_target_pairs={{0,16},{4,20},{8,24},{12,28},{16,0},{20,4},{24,8},{28,12},{1,17},{... | collective-permute-start | bytes 196616 | tf_op jit(solution)/shard_map/ppermute | solution.py:253
  92.5 4.3 %collective-permute-start.28 = (f32[32,512]{1,0:T(8,128)S(1)}, f32[32,512]{1,0:T(8,128)S(1)}, u32[]{:S(2)}, u32[]{:S(2)}) collective-permute-start(f32[32,512]{1,0:T(8,128)S(1)} %total.6.refs_0_), channel_id=1, source_target_pairs={{0,4},{4,0},{8,12},{12,8},{16,20},{20,16},{24,28},{28,24},{1,5},{5... | collective-permute-start | bytes 196616 | tf_op jit(solution)/shard_map/ppermute | solution.py:253
  93.9 5.2 %collective-permute-start.26 = (f32[32,512]{1,0:T(8,128)S(1)}, f32[32,512]{1,0:T(8,128)S(1)}, u32[]{:S(2)}, u32[]{:S(2)}) collective-permute-start(f32[32,512]{1,0:T(8,128)S(1)} %total.6.refs_0_), channel_id=1, source_target_pairs={{0,12},{4,8},{8,4},{12,0},{16,28},{20,24},{24,20},{28,16},{1,13},{... | collective-permute-start | bytes 196616 | tf_op jit(solution)/shard_map/ppermute | solution.py:253
  103.0 6.7 %collective-permute-start.30 = (f32[32,1536]{1,0:T(8,128)S(1)}, f32[32,1536]{1,0:T(8,128)S(1)}, u32[]{:S(2)}, u32[]{:S(2)}) collective-permute-start(f32[32,1536]{1,0:T(8,128)S(1)} %get-tuple-element.95.own_ref), channel_id=1, source_target_pairs={{0,2},{1,3},{2,0},{3,1},{4,6},{5,7},{6,4},{7,5},{8,10},{9,11},{10,... | collective-permute-start | bytes 589832 | tf_op jit(solution)/shard_map/ppermute | solution.py:253
  110.7 4.3 %collective-permute-start.32 = (f32[32,512]{1,0:T(8,128)S(1)}, f32[32,512]{1,0:T(8,128)S(1)}, u32[]{:S(2)}, u32[]{:S(2)}) collective-permute-start(f32[32,512]{1,0:T(8,128)S(1)} %get-tuple-element.99), channel_id=1, source_target_pairs={{0,4},{4,0},{8,12},{12,8},{16,20},{20,16},{24,28},{28,24},{1,5},{5... | collective-permute-start | bytes 196616 | tf_op jit(solution)/shard_map/ppermute | solution.py:253
  111.5 4.8 %collective-permute-start.33 = (f32[32,512]{1,0:T(8,128)S(1)}, f32[32,512]{1,0:T(8,128)S(1)}, u32[]{:S(2)}, u32[]{:S(2)}) collective-permute-start(f32[32,512]{1,0:T(8,128)S(1)} %get-tuple-element.100), channel_id=1, source_target_pairs={{0,8},{4,12},{8,0},{12,4},{16,24},{20,28},{24,16},{28,20},{1,9},{5... | collective-permute-start | bytes 196616 | tf_op jit(solution)/shard_map/ppermute | solution.py:253
  113.6 5.2 %collective-permute-start.34 = (f32[32,512]{1,0:T(8,128)S(1)}, f32[32,512]{1,0:T(8,128)S(1)}, u32[]{:S(2)}, u32[]{:S(2)}) collective-permute-start(f32[32,512]{1,0:T(8,128)S(1)} %get-tuple-element.101), channel_id=1, source_target_pairs={{0,12},{4,8},{8,4},{12,0},{16,28},{20,24},{24,20},{28,16},{1,13},{... | collective-permute-start | bytes 196616 | tf_op jit(solution)/shard_map/ppermute | solution.py:253
  118.7 6.0 %collective-permute-start.35 = (f32[32,512]{1,0:T(8,128)S(1)}, f32[32,512]{1,0:T(8,128)S(1)}, u32[]{:S(2)}, u32[]{:S(2)}) collective-permute-start(f32[32,512]{1,0:T(8,128)S(1)} %add.7.refs_0_), channel_id=1, source_target_pairs={{0,16},{4,20},{8,24},{12,28},{16,0},{20,4},{24,8},{28,12},{1,17},{... | collective-permute-start | bytes 196616 | tf_op jit(solution)/shard_map/ppermute | solution.py:253
  124.8 4.3 %collective-permute-start.38 = (f32[32,512]{1,0:T(8,128)S(1)}, f32[32,512]{1,0:T(8,128)S(1)}, u32[]{:S(2)}, u32[]{:S(2)}) collective-permute-start(f32[32,512]{1,0:T(8,128)S(1)} %total.7.refs_0_.c0), channel_id=1, source_target_pairs={{0,4},{4,0},{8,12},{12,8},{16,20},{20,16},{24,28},{28,24},{1,5},{5... | collective-permute-start | bytes 196616 | tf_op jit(solution)/shard_map/ppermute | solution.py:253
  125.5 4.3 %collective-permute-start.37 = (f32[32,512]{1,0:T(8,128)S(1)}, f32[32,512]{1,0:T(8,128)S(1)}, u32[]{:S(2)}, u32[]{:S(2)}) collective-permute-start(f32[32,512]{1,0:T(8,128)S(1)} %total.7.refs_0_.c0), channel_id=1, source_target_pairs={{0,8},{4,12},{8,0},{12,4},{16,24},{20,28},{24,16},{28,20},{1,9},{5... | collective-permute-start | bytes 196616 | tf_op jit(solution)/shard_map/ppermute | solution.py:253
  125.7 5.6 %collective-permute-start.36 = (f32[32,512]{1,0:T(8,128)S(1)}, f32[32,512]{1,0:T(8,128)S(1)}, u32[]{:S(2)}, u32[]{:S(2)}) collective-permute-start(f32[32,512]{1,0:T(8,128)S(1)} %total.7.refs_0_.c0), channel_id=1, source_target_pairs={{0,12},{4,8},{8,4},{12,0},{16,28},{20,24},{24,20},{28,16},{1,13},{... | collective-permute-start | bytes 196616 | tf_op jit(solution)/shard_map/ppermute | solution.py:253
  134.2 6.7 %collective-permute-start.40 = (bf16[32,1536]{1,0:T(8,128)(2,1)S(1)}, bf16[32,1536]{1,0:T(8,128)(2,1)S(1)}, u32[]{:S(2)}, u32[]{:S(2)}) collective-permute-start(bf16[32,1536]{1,0:T(8,128)(2,1)S(1)} %get-tuple-element.108.own_ref), channel_id=1, source_target_pairs={{0,2},{1,3},{2,0},{3,1},{4,6},{5,7},{6,4},{7,5},{8,10},{9,11},{10,... | collective-permute-start | bytes 294920 | tf_op jit(solution)/shard_map/ppermute | solution.py:253
  (11 other events, 28.3 us)

commit v3 on v2

v3 whole, which is shorter than its diff:
```python
import functools

import jax
import jax.numpy as jnp
from jax import lax
from jax.experimental import pallas as pl
from jax.experimental.pallas import tpu as pltpu
from jax.sharding import PartitionSpec as P

ITERS = 4
PEERS = 4
LANES = 128
EXTRA = 8
ORDER = (0, 3, 1, 2)
TERMS = 3
LONG = pl.CostEstimate(flops=2**34, bytes_accessed=0, transcendentals=0)
SHORT = pl.CostEstimate(flops=2**29, bytes_accessed=0, transcendentals=0)
HIGHEST = lax.Precision.HIGHEST
VMEM = pl.BlockSpec(memory_space=pltpu.VMEM)
HBM = pl.BlockSpec(memory_space=pltpu.HBM)
F32 = jnp.float32
BF16 = jnp.bfloat16


def call(kernel, outputs, name, scratch=(), in_specs=None, mebibytes=20, cost=None):
    def run(*args):
        specs = in_specs or [VMEM] * len(args)
        return pl.pallas_call(
            kernel,
            out_shape=[jax.ShapeDtypeStruct(shape, dtype) for shape, dtype in outputs],
            in_specs=specs,
            out_specs=[VMEM] * len(outputs),
            scratch_shapes=scratch,
            compiler_params=pltpu.CompilerParams(vmem_limit_bytes=mebibytes * 2**20),
            cost_estimate=cost,
            name=name,
        )(*args)

    return run


def split(value, terms=2):
    parts = []
    for _ in range(terms):
        parts.append(value.astype(BF16))
        value = value - parts[-1].astype(F32)
    return jnp.concatenate(parts, axis=0)


def join(value, terms=2):
    height = value.shape[0] // terms
    result = value[-height:]
    for term in range(terms - 2, -1, -1):
        result = value[term * height : (term + 1) * height] + result
    return result


def total(*refs):
    terms = [ref[...].astype(F32) for ref in refs]
    while len(terms) > 1:
        terms = [sum(terms[i + 1 : i + 2], terms[i]) for i in range(0, len(terms), 2)]
    return terms[0]


def contract_last(left, right, precision=None):
    return lax.dot_general(
        left, right, (((1,), (1,)), ((), ())), preferred_element_type=F32, precision=precision
    )


def position():
    return lax.rem(lax.axis_index("tok"), PEERS)


def diagonal(n):
    return lax.broadcasted_iota(jnp.int32, (n, n), 0) == lax.broadcasted_iota(jnp.int32, (n, n), 1)


def first_projection_kernel(blocks, basis_hbm, rows_hbm, out_ref, rows_ref, basis_ref, sems):
    tokens = rows_ref.shape[0]
    height = tokens // blocks
    fetch_basis = pltpu.make_async_copy(basis_hbm, basis_ref, sems.at[blocks])
    fetch_basis.start()
    fetches = []
    for i in range(blocks):
        place = pl.ds(i * height, height)
        fetches.append(
            pltpu.make_async_copy(rows_hbm.at[place, :], rows_ref.at[place, :], sems.at[i])
        )
        fetches[-1].start()
    fetch_basis.wait()
    vectors = split(basis_ref[...])
    for i in range(blocks):
        fetches[i].wait()
        place = pl.ds(i * height, height)
        out_ref[:, place] = join(contract_last(vectors, rows_ref[place, :]))


def core():
    return lax.rem(lax.axis_index("feat"), 2)


def chunk_gram(chunk_ref, n):
    chunk = chunk_ref[:n, :]
    return contract_last(chunk, chunk, HIGHEST)


def projection_kernel(part, first, chunk_ref, rows_ref, *refs):
    mean_ref, refs = (chunk_ref, refs) if first else (refs[0], refs[1:])
    n, width = mean_ref.shape[0] - EXTRA, chunk_ref.shape[1]
    place = pl.ds(pl.multiple_of((position() ^ part) * width, width), width)
    chunk = chunk_ref[:n, :]
    shift = jnp.sum(chunk * mean_ref[n : n + 1, :], axis=1, keepdims=True)
    projected = join(contract_last(split(chunk), rows_ref[:, place])) - shift
    if part != ORDER[0]:
        projected = refs[0][...] + projected
    if part != ORDER[-1]:
        refs[-2][...] = projected
        refs[-1][...] = chunk_gram(chunk_ref, n)
        return
    kept_ref, sent_ref, projected_ref = refs[-3:]
    half = kept_ref.shape[1]
    projected_ref[...] = projected
    kept_ref[...] = projected_ref[:, pl.ds(pl.multiple_of(core() * half, half), half)]
    sent_ref[...] = projected_ref[:, pl.ds(pl.multiple_of((1 - core()) * half, half), half)]


def gram_kernel(chunk_ref, *refs):
    *refs, out_ref = refs
    n = out_ref.shape[0]
    parts = {part: ref[...] for part, ref in zip(ORDER, refs)}
    parts[ORDER[-1]] = chunk_gram(chunk_ref, n)
    out_ref[...] = jnp.zeros(out_ref.shape, F32)
    out_ref[:, :n] = (parts[0] + parts[1]) + (parts[2] + parts[3])


def inverse_factor_kernel(own_ref, got_ref, out_ref):
    n = own_ref.shape[0]
    gram = (own_ref[...] + got_ref[...])[:, :n]
    work = jnp.concatenate([gram, diagonal(n).astype(F32)], axis=1)
    index = lax.broadcasted_iota(jnp.int32, (n, 1), 0)
    scale = jnp.zeros((n, 1), F32)
    for k in range(n):
        pivot = work[k : k + 1, k : k + 1]
        factor = jnp.where(index > k, work[:, k : k + 1] / pivot, 0.0)
        scale = jnp.where(index == k, lax.rsqrt(pivot), scale)
        work = work - factor * work[k : k + 1, :]
    out_ref[...] = work[:, n:] * scale


def first_term(weights, rows, counts, centre, out_ref):
    n, width = counts.shape[0], out_ref.shape[1]
    term = jnp.dot(weights, rows, preferred_element_type=F32)
    sums = term[2 * n : 2 * n + 1]
    out_ref[:n, :] = join(term[: 2 * n]) + centre * sums
    out_ref[n:, :] = jnp.zeros((EXTRA, width), F32)
    out_ref[n : n + 1, :] = sums
    counts = jnp.where(diagonal(n), counts, 0.0)
    out_ref[n + 1 : n + 2, :n] = jnp.sum(counts, axis=0, keepdims=True)


def first_image_kernel(own_ref, got_ref, rows_ref, *outs):
    *outs, weights_ref, side_ref = outs
    tokens, n, width = rows_ref.shape[0], own_ref.shape[0], outs[0].shape[1]
    projected = total(own_ref, got_ref)[:, :tokens]
    centre = [jnp.sum(ref[:, tokens:].astype(F32), axis=1, keepdims=True) for ref in (own_ref, got_ref)]
    centre = centre[0] + centre[1]
    weights = split(projected)
    counts = join(jnp.sum(weights.astype(F32), axis=1, keepdims=True)) + centre * tokens
    weights = jnp.concatenate([weights, jnp.ones((2 * EXTRA, tokens), BF16)], axis=0)
    for part, out in zip(ORDER[1:], outs):
        place = pl.ds(pl.multiple_of((position() ^ part) * width, width), width)
        first_term(weights, rows_ref[:, place], counts, centre, out)
    weights_ref[...] = weights
    side_ref[...] = jnp.broadcast_to(counts, side_ref.shape)
    side_ref[:, 1:2] = centre


def first_own_image_kernel(weights_ref, side_ref, rows_ref, out_ref):
    width = out_ref.shape[1]
    place = pl.ds(pl.multiple_of(position() * width, width), width)
    first_term(weights_ref[...], rows_ref[:, place], side_ref[:, :1], side_ref[:, 1:2], out_ref)


def first_total_kernel(rows_in_all, own_ref, got_ref, out_ref):
    n = own_ref.shape[0] - EXTRA
    value = own_ref[...] + got_ref[...]
    mean = value[n : n + 1] / rows_in_all
    counts = jnp.where(diagonal(n), value[n + 1 : n + 2, :n], 0.0)
    counts = jnp.sum(counts, axis=1, keepdims=True)
    out_ref[:n, :] = value[:n] - counts * mean
    out_ref[n:, :] = jnp.broadcast_to(mean, (EXTRA, mean.shape[1]))


def gather_halves(own_ref, other_ref, projected_ref):
    half = own_ref.shape[1]
    for place, ref in ((core(), own_ref), (1 - core(), other_ref)):
        projected_ref[:, pl.ds(pl.multiple_of(place * half, half), half)] = ref[...]
    return projected_ref[...]


def image_kernel(own_ref, other_ref, rows_ref, *refs):
    means, outs = refs[: PEERS - 1], refs[PEERS - 1 : -3]
    weights_ref, side_ref, projected_ref = refs[-3:]
    n, width = own_ref.shape[0], outs[0].shape[1]
    weights = split(gather_halves(own_ref, other_ref, projected_ref), TERMS)
    counts = join(jnp.sum(weights.astype(F32), axis=1, keepdims=True), TERMS)
    for part, mean, out in zip(ORDER[1:], means, outs):
        place = pl.ds(pl.multiple_of((position() ^ part) * width, width), width)
        term = join(jnp.dot(weights, rows_ref[:, place], preferred_element_type=F32), TERMS)
        out[...] = term - counts * mean[n : n + 1, :]
    weights_ref[...] = weights
    side_ref[...] = jnp.broadcast_to(counts, side_ref.shape)


def own_image_kernel(weights_ref, side_ref, rows_ref, mean_ref, out_ref):
    n, width = out_ref.shape
    place = pl.ds(pl.multiple_of(position() * width, width), width)
    term = join(jnp.dot(weights_ref[...], rows_ref[:, place], preferred_element_type=F32), TERMS)
    out_ref[...] = term - side_ref[:, :1] * mean_ref[n : n + 1, :]


def assemble_kernel(*refs):
    *chunks, out_ref = refs
    n, width = out_ref.shape[0], chunks[0].shape[1]
    for part, chunk in zip(ORDER, chunks):
        place = pl.ds(pl.multiple_of((position() ^ part) * width, width), width)
        out_ref[:, place] = chunk[:n, :]


def last_kernel(own_ref, other_ref, lower_ref, image_ref, scores_ref, basis_ref, projected_ref):
    n, lower = own_ref.shape[0], lower_ref[...]
    basis_ref[...] = jnp.dot(lower, image_ref[...], preferred_element_type=F32, precision=HIGHEST)
    projected = gather_halves(own_ref, other_ref, projected_ref)
    projected = jnp.dot(lower, projected, preferred_element_type=F32, precision=HIGHEST)
    scores_ref[...] = jnp.sum(projected * projected, axis=0) / n


def normalised_total_kernel(own_ref, got_ref, lower_ref, out_ref):
    value = own_ref[...] + got_ref[...]
    out_ref[...] = jnp.dot(lower_ref[...], value, preferred_element_type=F32, precision=HIGHEST)


def add_kernel(*refs):
    refs[-1][...] = total(*refs[:-1]).astype(refs[-1].dtype)


def add(*terms, dtype=F32):
    return call(add_kernel, [(terms[0].shape, dtype)], "add")(*terms)[0]


def first_part_kernel(*refs):
    *terms, out_ref = refs
    tokens = out_ref.shape[1] - LANES
    value = total(*terms)
    centre = jnp.sum(value, axis=1, keepdims=True) / tokens
    out_ref[:, :tokens] = (value - centre).astype(BF16)
    out_ref[:, tokens:] = jnp.zeros((value.shape[0], LANES), BF16)
    for lane in range(3):
        term = centre.astype(BF16)
        out_ref[:, tokens + lane : tokens + lane + 1] = term
        centre = centre - term.astype(F32)


def swap(value, axis, distance):
    size = lax.axis_size(axis)
    return lax.ppermute(value, axis, [(i, i ^ distance) for i in range(size)])


def distances(axis, start):
    step, size = start, lax.axis_size(axis)
    while step < size:
        yield step
        step *= 2


def sum_but_last(value, axis):
    terms = [value]
    for step in list(distances(axis, 1))[:-1]:
        terms = [add(*terms)] if len(terms) > 1 else terms
        terms.append(swap(terms[0], axis, step))
    return terms


def share(value, axis):
    return [value] + [swap(value, axis, part) for part in ORDER[1:]]


def on_device(activations, start_basis):
    tokens, features = activations.shape
    n = start_basis.shape[0]
    width = features // PEERS
    rows_in_all = tokens * lax.axis_size("tok")
    last_feat = lax.axis_size("feat") // 2

    blocks = 3
    partial, rows = call(
        functools.partial(first_projection_kernel, blocks),
        [((n, tokens), F32), (activations.shape, BF16)],
        "first_projection",
        scratch=[pltpu.VMEM((n, features), F32), pltpu.SemaphoreType.DMA((blocks + 1,))],
        in_specs=[HBM, HBM],
        mebibytes=46,
    )(start_basis, activations)
    terms = sum_but_last(partial, "feat")
    own = call(first_part_kernel, [((n, tokens + LANES), BF16)], "first_part")(*terms)[0]
    got = swap(own, "feat", last_feat)
    side = ((n, LANES), F32)
    half = ((n, tokens // 2), F32)
    whole = ((n, tokens), F32)
    for step in range(ITERS):
        first = step == 0
        chunk = ((n + EXTRA if first else n, width), F32)
        weights = ((2 * n + 2 * EXTRA if first else TERMS * n, tokens), BF16)
        outputs = [chunk] * (PEERS - 1) + [weights, side]
        if first:
            *terms, weights, sums = call(first_image_kernel, outputs, "first_image")(own, got, rows)
            kernel, kept_means = first_own_image_kernel, []
        else:
            kernel, kept_means = own_image_kernel, means[:1]
            scratch = [pltpu.VMEM(*whole)]
            *terms, weights, sums = call(image_kernel, outputs, "image", scratch)(
                own, other, rows, *means[1:]
            )
        received = [swap(term, "tok", part) for part, term in zip(ORDER[1:], terms)]
        kept = call(kernel, [chunk], "own_image", cost=SHORT)(weights, sums, rows, *kept_means)
        image = add(*kept, *received)
        *steps, last_step = distances("tok", PEERS)
        for distance in steps:
            image = add(image, swap(image, "tok", distance))
        kernel = functools.partial(first_total_kernel, rows_in_all) if first else normalised_total_kernel
        lower = [] if first else [lower]
        image = call(kernel, [chunk], "total")(image, swap(image, "tok", last_step), *lower)[0]
        images = share(image, "tok")
        if first:
            means = images
        before, grams = [], []
        for place, part in enumerate(ORDER):
            kernel = functools.partial(projection_kernel, part, first)
            operands = [images[place], rows, *([] if first else [means[place]]), *before]
            if part != ORDER[-1]:
                outputs = [whole, ((n, n), F32)]
                *before, gram = call(kernel, outputs, "projection", cost=SHORT)(*operands)
                grams.append(gram)
        gram = call(gram_kernel, [side], "gram")(images[-1], *grams)[0]
        outputs, scratch = [half, half], [pltpu.VMEM(*whole)]
        own, sent = call(kernel, outputs, "last_projection", scratch, cost=SHORT)(*operands)
        for distance in distances("feat", 1):
            got = swap(sent if distance == 1 else own, "feat", distance)
            narrow = step == ITERS - 1 and distance != last_feat
            own = add(own, got, dtype=BF16 if narrow else F32)
            grams = (gram, swap(gram, "feat", distance))
            gram = add(*grams) if distance != last_feat else None
        other = swap(own, "feat", 1)
        lower = call(inverse_factor_kernel, [((n, n), F32)], "inverse_factor", cost=LONG)(*grams)[0]
    image = call(assemble_kernel, [((n, features), F32)], "assemble")(*images)[0]
    outputs, scratch = [((tokens,), F32), ((n, features), F32)], [pltpu.VMEM(*whole)]
    return tuple(call(last_kernel, outputs, "last", scratch)(own, other, lower, image))


def solution(mesh):
    in_specs = (P("tok", "feat"), P(None, "feat"))
    out_specs = (P("tok"), P(None, "feat"))
    return jax.shard_map(
        on_device, mesh=mesh, in_specs=in_specs, out_specs=out_specs, check_vma=False
    )
```

time: 142 us -> 135 us (0.951)
  waiting for transfers between devices: 50.3 us -> 44.2 us
  Pallas kernels: 36 us -> 34 us
    ppermute x42 -> x50, waiting for transfers between devices: 50.3 us -> 44.2 us  [swap(): return lax.ppermute(value, axis, [(i, i ^ distance) for i in range(size)])]
    pallas_call x44 -> x56, Pallas kernels: 36 us -> 34 us  [run(): pl.pallas_call(kernel, out_shape=[jax.ShapeDtypeStruct(shape, dtype) for...]
    ppermute x42 -> x50, starting transfers between devices: 53.9 us -> 55.1 us  [swap(): return lax.ppermute(value, axis, [(i, i ^ distance) for i in range(size)])]
  transfers between devices with their start and end apart: 42 -> 50, of which waited for: 38 -> 32; matrix products, arithmetic and copies ran while one was open for 0% -> 0% of each run, Pallas kernels for 17% -> 18%
where the time goes in v3:
time: 135 us
  starting transfers between devices  55.1 us (41%)
  waiting for transfers between devices  44.2 us (33%)
  Pallas kernels  34 us (25%)
    ppermute x50, starting transfers between devices, swap(): return lax.ppermute(value, axis, [(i, i ^ distance) for i in range(size)])  55.1 us
    ppermute x50, waiting for transfers between devices, swap(): return lax.ppermute(value, axis, [(i, i ^ distance) for i in range(size)])  44.2 us
    pallas_call x56, Pallas kernels, run(): pl.pallas_call(kernel, out_shape=[jax.ShapeDtypeStruct(shape, dtype) for...  34 us
  transfers between devices with their start and end apart: 50, of which 32 were waited for; matrix products, arithmetic and copies ran while one was open for 0% of the time, Pallas kernels for 18%

profile of v3, /device:TPU:0, one launch (start us, length us, event | category | flops | bytes accessed | tf_op | source)
XLA Modules:
  0.0 135.2 jit_solution(10956773199570780583)
XLA Ops:
  1.6 3.9 %first_projection.1 = (f32[32,1536]{1,0:T(8,128)S(1)}, bf16[1536,2048]{1,0:T(8,128)(2,1)S(1)}) custom-call(f32[32,2048]{1,0:T(8,128)S(1)} %copy-done, bf16[1536,2048]{1,0:T(8,128)(2,1)} %rows_hbm.1), custom_call_target="tpu_custom_call" | custom-call | tf_op jit(solution)/shard_map/first_projection/pallas_call | solution.py:28
  7.2 2.9 %collective-permute-start.1 = (bf16[32,1664]{1,0:T(8,128)(2,1)S(1)}, bf16[32,1664]{1,0:T(8,128)(2,1)S(1)}, u32[]{:S(2)}, u32[]{:S(2)}) collective-permute-start(bf16[32,1664]{1,0:T(8,128)(2,1)S(1)} %first_part.1.own_ref), channel_id=1, source_target_pairs={{0,2},{1,3},{2,0},{3,1},{4,6},{5,7},{6,4},{7,5},{8,10},{9,11},{10,... | collective-permute-start | bytes 319496 | tf_op jit(solution)/shard_map/ppermute | solution.py:267
  10.1 3.3 %collective-permute-done.1.got_ref = bf16[32,1664]{1,0:T(8,128)(2,1)S(1)} collective-permute-done((bf16[32,1664]{1,0:T(8,128)(2,1)S(1)}, bf16[32,1664]{1,0:T(8,128)(2,1)S(1)}, u32[]{:S(2)}, u32[]{:S(2)}) %collective-permute-start.1) | collective-permute-done | bytes 106528 | tf_op jit(solution)/shard_map/ppermute | solution.py:267
  14.4 2.9 %collective-permute-start.2 = (f32[40,512]{1,0:T(8,128)S(1)}, f32[40,512]{1,0:T(8,128)S(1)}, u32[]{:S(2)}, u32[]{:S(2)}) collective-permute-start(f32[40,512]{1,0:T(8,128)S(1)} %get-tuple-element.60), channel_id=1, source_target_pairs={{0,12},{4,8},{8,4},{12,0},{16,28},{20,24},{24,20},{28,16},{1,13},{... | collective-permute-start | bytes 245768 | tf_op jit(solution)/shard_map/ppermute | solution.py:267
  18.3 1.6 %collective-permute-done.2.refs_1_ = f32[40,512]{1,0:T(8,128)S(1)} collective-permute-done((f32[40,512]{1,0:T(8,128)S(1)}, f32[40,512]{1,0:T(8,128)S(1)}, u32[]{:S(2)}, u32[]{:S(2)}) %collective-permute-start.2) | collective-permute-done | bytes 81952 | tf_op jit(solution)/shard_map/ppermute | solution.py:267
  19.9 1.8 %collective-permute-done.3.refs_2_ = f32[40,512]{1,0:T(8,128)S(1)} collective-permute-done((f32[40,512]{1,0:T(8,128)S(1)}, f32[40,512]{1,0:T(8,128)S(1)}, u32[]{:S(2)}, u32[]{:S(2)}) %collective-permute-start.3) | collective-permute-done | bytes 81952 | tf_op jit(solution)/shard_map/ppermute | solution.py:267
  22.2 2.8 %collective-permute-start.5 = (f32[40,512]{1,0:T(8,128)S(1)}, f32[40,512]{1,0:T(8,128)S(1)}, u32[]{:S(2)}, u32[]{:S(2)}) collective-permute-start(f32[40,512]{1,0:T(8,128)S(1)} %add.16.own_ref), channel_id=1, source_target_pairs={{0,16},{4,20},{8,24},{12,28},{16,0},{20,4},{24,8},{28,12},{1,17},{... | collective-permute-start | bytes 245768 | tf_op jit(solution)/shard_map/ppermute | solution.py:267
  25.0 3.4 %collective-permute-done.5.got_ref = f32[40,512]{1,0:T(8,128)S(1)} collective-permute-done((f32[40,512]{1,0:T(8,128)S(1)}, f32[40,512]{1,0:T(8,128)S(1)}, u32[]{:S(2)}, u32[]{:S(2)}) %collective-permute-start.5) | collective-permute-done | bytes 81952 | tf_op jit(solution)/shard_map/ppermute | solution.py:267
  30.1 2.0 %collective-permute-start.6 = (f32[40,512]{1,0:T(8,128)S(1)}, f32[40,512]{1,0:T(8,128)S(1)}, u32[]{:S(2)}, u32[]{:S(2)}) collective-permute-start(f32[40,512]{1,0:T(8,128)S(1)} %total.4.chunk_ref.mean_ref.refs_0_), channel_id=1, source_target_pairs={{0,8},{4,12},{8,0},{12,4},{16,24},{20,28},{24,16},{28,20},{1,9},{5... | collective-permute-start | bytes 245768 | tf_op jit(solution)/shard_map/ppermute | solution.py:267
  37.4 1.6 %collective-permute-start.10 = (f32[32,768]{1,0:T(8,128)S(1)}, f32[32,768]{1,0:T(8,128)S(1)}, u32[]{:S(2)}, u32[]{:S(2)}) collective-permute-start(f32[32,768]{1,0:T(8,128)S(1)} %add.17.refs_0_), channel_id=1, source_target_pairs={{0,2},{1,3},{2,0},{3,1},{4,6},{5,7},{6,4},{7,5},{8,10},{9,11},{10,... | collective-permute-start | bytes 294920 | tf_op jit(solution)/shard_map/ppermute | solution.py:267
  39.0 3.4 %collective-permute-done.10.refs_1_ = f32[32,768]{1,0:T(8,128)S(1)} collective-permute-done((f32[32,768]{1,0:T(8,128)S(1)}, f32[32,768]{1,0:T(8,128)S(1)}, u32[]{:S(2)}, u32[]{:S(2)}) %collective-permute-start.10) | collective-permute-done | bytes 98336 | tf_op jit(solution)/shard_map/ppermute | solution.py:267
  44.6 2.0 %collective-permute-start.12 = (f32[32,512]{1,0:T(8,128)S(1)}, f32[32,512]{1,0:T(8,128)S(1)}, u32[]{:S(2)}, u32[]{:S(2)}) collective-permute-start(f32[32,512]{1,0:T(8,128)S(1)} %get-tuple-element.70), channel_id=1, source_target_pairs={{0,12},{4,8},{8,4},{12,0},{16,28},{20,24},{24,20},{28,16},{1,13},{... | collective-permute-start | bytes 196616 | tf_op jit(solution)/shard_map/ppermute | solution.py:267
  48.1 1.5 %collective-permute-start.17 = (f32[32,128]{1,0:T(8,128)S(1)}, f32[32,128]{1,0:T(8,128)S(1)}, u32[]{:S(2)}, u32[]{:S(2)}) collective-permute-start(f32[32,128]{1,0:T(8,128)S(1)} %add.20.own_ref), channel_id=1, source_target_pairs={{0,2},{1,3},{2,0},{3,1},{4,6},{5,7},{6,4},{7,5},{8,10},{9,11},{10,... | collective-permute-start | bytes 49160 | tf_op jit(solution)/shard_map/ppermute | solution.py:267
  51.6 2.5 %collective-permute-start.15 = (f32[32,512]{1,0:T(8,128)S(1)}, f32[32,512]{1,0:T(8,128)S(1)}, u32[]{:S(2)}, u32[]{:S(2)}) collective-permute-start(f32[32,512]{1,0:T(8,128)S(1)} %add.19.own_ref), channel_id=1, source_target_pairs={{0,16},{4,20},{8,24},{12,28},{16,0},{20,4},{24,8},{28,12},{1,17},{... | collective-permute-start | bytes 196616 | tf_op jit(solution)/shard_map/ppermute | solution.py:267
  54.1 2.9 %inverse_factor.4.lower_ref = f32[32,32]{1,0:T(8,128)S(1)} custom-call(f32[32,128]{1,0:T(8,128)S(1)} %add.20.own_ref, f32[32,128]{1,0:T(8,128)S(1)} %collective-permute-done.17.got_ref), custom_call_target="tpu_custom_call" | custom-call | flops 17179869184 | tf_op jit(solution)/shard_map/inverse_factor/pallas_call | solution.py:28
  59.4 1.8 %collective-permute-start.18 = (f32[32,512]{1,0:T(8,128)S(1)}, f32[32,512]{1,0:T(8,128)S(1)}, u32[]{:S(2)}, u32[]{:S(2)}) collective-permute-start(f32[32,512]{1,0:T(8,128)S(1)} %total.5.chunk_ref), channel_id=1, source_target_pairs={{0,8},{4,12},{8,0},{12,4},{16,24},{20,28},{24,16},{28,20},{1,9},{5... | collective-permute-start | bytes 196616 | tf_op jit(solution)/shard_map/ppermute | solution.py:267
  66.3 1.6 %collective-permute-start.22 = (f32[32,768]{1,0:T(8,128)S(1)}, f32[32,768]{1,0:T(8,128)S(1)}, u32[]{:S(2)}, u32[]{:S(2)}) collective-permute-start(f32[32,768]{1,0:T(8,128)S(1)} %add.21.refs_0_), channel_id=1, source_target_pairs={{0,2},{1,3},{2,0},{3,1},{4,6},{5,7},{6,4},{7,5},{8,10},{9,11},{10,... | collective-permute-start | bytes 294920 | tf_op jit(solution)/shard_map/ppermute | solution.py:267
  67.9 3.4 %collective-permute-done.22.refs_1_ = f32[32,768]{1,0:T(8,128)S(1)} collective-permute-done((f32[32,768]{1,0:T(8,128)S(1)}, f32[32,768]{1,0:T(8,128)S(1)}, u32[]{:S(2)}, u32[]{:S(2)}) %collective-permute-start.22) | collective-permute-done | bytes 98336 | tf_op jit(solution)/shard_map/ppermute | solution.py:267
  73.5 1.9 %collective-permute-start.24 = (f32[32,512]{1,0:T(8,128)S(1)}, f32[32,512]{1,0:T(8,128)S(1)}, u32[]{:S(2)}, u32[]{:S(2)}) collective-permute-start(f32[32,512]{1,0:T(8,128)S(1)} %get-tuple-element.83), channel_id=1, source_target_pairs={{0,12},{4,8},{8,4},{12,0},{16,28},{20,24},{24,20},{28,16},{1,13},{... | collective-permute-start | bytes 196616 | tf_op jit(solution)/shard_map/ppermute | solution.py:267
  77.0 1.6 %collective-permute-start.29 = (f32[32,128]{1,0:T(8,128)S(1)}, f32[32,128]{1,0:T(8,128)S(1)}, u32[]{:S(2)}, u32[]{:S(2)}) collective-permute-start(f32[32,128]{1,0:T(8,128)S(1)} %add.24.own_ref), channel_id=1, source_target_pairs={{0,2},{1,3},{2,0},{3,1},{4,6},{5,7},{6,4},{7,5},{8,10},{9,11},{10,... | collective-permute-start | bytes 49160 | tf_op jit(solution)/shard_map/ppermute | solution.py:267
  80.4 2.2 %collective-permute-start.27 = (f32[32,512]{1,0:T(8,128)S(1)}, f32[32,512]{1,0:T(8,128)S(1)}, u32[]{:S(2)}, u32[]{:S(2)}) collective-permute-start(f32[32,512]{1,0:T(8,128)S(1)} %add.23.own_ref), channel_id=1, source_target_pairs={{0,16},{4,20},{8,24},{12,28},{16,0},{20,4},{24,8},{28,12},{1,17},{... | collective-permute-start | bytes 196616 | tf_op jit(solution)/shard_map/ppermute | solution.py:267
  82.7 2.9 %inverse_factor.5.lower_ref = f32[32,32]{1,0:T(8,128)S(1)} custom-call(f32[32,128]{1,0:T(8,128)S(1)} %add.24.own_ref, f32[32,128]{1,0:T(8,128)S(1)} %collective-permute-done.29.got_ref), custom_call_target="tpu_custom_call" | custom-call | flops 17179869184 | tf_op jit(solution)/shard_map/inverse_factor/pallas_call | solution.py:28
  88.4 1.6 %collective-permute-start.30 = (f32[32,512]{1,0:T(8,128)S(1)}, f32[32,512]{1,0:T(8,128)S(1)}, u32[]{:S(2)}, u32[]{:S(2)}) collective-permute-start(f32[32,512]{1,0:T(8,128)S(1)} %total.6.chunk_ref), channel_id=1, source_target_pairs={{0,8},{4,12},{8,0},{12,4},{16,24},{20,28},{24,16},{28,20},{1,9},{5... | collective-permute-start | bytes 196616 | tf_op jit(solution)/shard_map/ppermute | solution.py:267
  95.6 1.6 %collective-permute-start.34 = (f32[32,768]{1,0:T(8,128)S(1)}, f32[32,768]{1,0:T(8,128)S(1)}, u32[]{:S(2)}, u32[]{:S(2)}) collective-permute-start(f32[32,768]{1,0:T(8,128)S(1)} %add.25.refs_0_), channel_id=1, source_target_pairs={{0,2},{1,3},{2,0},{3,1},{4,6},{5,7},{6,4},{7,5},{8,10},{9,11},{10,... | collective-permute-start | bytes 294920 | tf_op jit(solution)/shard_map/ppermute | solution.py:267
  97.1 3.4 %collective-permute-done.34.refs_1_ = f32[32,768]{1,0:T(8,128)S(1)} collective-permute-done((f32[32,768]{1,0:T(8,128)S(1)}, f32[32,768]{1,0:T(8,128)S(1)}, u32[]{:S(2)}, u32[]{:S(2)}) %collective-permute-start.34) | collective-permute-done | bytes 98336 | tf_op jit(solution)/shard_map/ppermute | solution.py:267
  106.3 1.5 %collective-permute-start.41 = (f32[32,128]{1,0:T(8,128)S(1)}, f32[32,128]{1,0:T(8,128)S(1)}, u32[]{:S(2)}, u32[]{:S(2)}) collective-permute-start(f32[32,128]{1,0:T(8,128)S(1)} %add.28.own_ref), channel_id=1, source_target_pairs={{0,2},{1,3},{2,0},{3,1},{4,6},{5,7},{6,4},{7,5},{8,10},{9,11},{10,... | collective-permute-start | bytes 49160 | tf_op jit(solution)/shard_map/ppermute | solution.py:267
  109.5 2.2 %collective-permute-start.39 = (f32[32,512]{1,0:T(8,128)S(1)}, f32[32,512]{1,0:T(8,128)S(1)}, u32[]{:S(2)}, u32[]{:S(2)}) collective-permute-start(f32[32,512]{1,0:T(8,128)S(1)} %add.27.own_ref), channel_id=1, source_target_pairs={{0,16},{4,20},{8,24},{12,28},{16,0},{20,4},{24,8},{28,12},{1,17},{... | collective-permute-start | bytes 196616 | tf_op jit(solution)/shard_map/ppermute | solution.py:267
  111.7 2.9 %inverse_factor.6.lower_ref = f32[32,32]{1,0:T(8,128)S(1)} custom-call(f32[32,128]{1,0:T(8,128)S(1)} %add.28.own_ref, f32[32,128]{1,0:T(8,128)S(1)} %collective-permute-done.41.got_ref), custom_call_target="tpu_custom_call" | custom-call | flops 17179869184 | tf_op jit(solution)/shard_map/inverse_factor/pallas_call | solution.py:28
  117.6 1.7 %collective-permute-start.42 = (f32[32,512]{1,0:T(8,128)S(1)}, f32[32,512]{1,0:T(8,128)S(1)}, u32[]{:S(2)}, u32[]{:S(2)}) collective-permute-start(f32[32,512]{1,0:T(8,128)S(1)} %total.7.chunk_ref.refs_0_), channel_id=1, source_target_pairs={{0,8},{4,12},{8,0},{12,4},{16,24},{20,28},{24,16},{28,20},{1,9},{5... | collective-permute-start | bytes 196616 | tf_op jit(solution)/shard_map/ppermute | solution.py:267
  124.5 1.6 %collective-permute-start.46 = (bf16[32,768]{1,0:T(8,128)(2,1)S(1)}, bf16[32,768]{1,0:T(8,128)(2,1)S(1)}, u32[]{:S(2)}, u32[]{:S(2)}) collective-permute-start(bf16[32,768]{1,0:T(8,128)(2,1)S(1)} %add.29.refs_0_), channel_id=1, source_target_pairs={{0,2},{1,3},{2,0},{3,1},{4,6},{5,7},{6,4},{7,5},{8,10},{9,11},{10,... | collective-permute-start | bytes 147464 | tf_op jit(solution)/shard_map/ppermute | solution.py:267
  128.7 2.5 %collective-permute-done.49.got_ref = f32[32,128]{1,0:T(8,128)S(1)} collective-permute-done((f32[32,128]{1,0:T(8,128)S(1)}, f32[32,128]{1,0:T(8,128)S(1)}, u32[]{:S(2)}, u32[]{:S(2)}) %collective-permute-start.49) | collective-permute-done | bytes 16416 | tf_op jit(solution)/shard_map/ppermute | solution.py:267
  131.2 2.9 %inverse_factor.7.lower_ref = f32[32,32]{1,0:T(8,128)S(1)} custom-call(f32[32,128]{1,0:T(8,128)S(1)} %add.31.own_ref, f32[32,128]{1,0:T(8,128)S(1)} %collective-permute-done.49.got_ref), custom_call_target="tpu_custom_call" | custom-call | flops 17179869184 | tf_op jit(solution)/shard_map/inverse_factor/pallas_call | solution.py:28
  (126 shorter events, 58.6 us)
Async XLA Ops:
  7.2 6.2 %collective-permute-start.1 = (bf16[32,1664]{1,0:T(8,128)(2,1)S(1)}, bf16[32,1664]{1,0:T(8,128)(2,1)S(1)}, u32[]{:S(2)}, u32[]{:S(2)}) collective-permute-start(bf16[32,1664]{1,0:T(8,128)(2,1)S(1)} %first_part.1.own_ref), channel_id=1, source_target_pairs={{0,2},{1,3},{2,0},{3,1},{4,6},{5,7},{6,4},{7,5},{8,10},{9,11},{10,... | collective-permute-start | bytes 319496 | tf_op jit(solution)/shard_map/ppermute | solution.py:267
  14.4 5.5 %collective-permute-start.2 = (f32[40,512]{1,0:T(8,128)S(1)}, f32[40,512]{1,0:T(8,128)S(1)}, u32[]{:S(2)}, u32[]{:S(2)}) collective-permute-start(f32[40,512]{1,0:T(8,128)S(1)} %get-tuple-element.60), channel_id=1, source_target_pairs={{0,12},{4,8},{8,4},{12,0},{16,28},{20,24},{24,20},{28,16},{1,13},{... | collective-permute-start | bytes 245768 | tf_op jit(solution)/shard_map/ppermute | solution.py:267
  22.2 6.3 %collective-permute-start.5 = (f32[40,512]{1,0:T(8,128)S(1)}, f32[40,512]{1,0:T(8,128)S(1)}, u32[]{:S(2)}, u32[]{:S(2)}) collective-permute-start(f32[40,512]{1,0:T(8,128)S(1)} %add.16.own_ref), channel_id=1, source_target_pairs={{0,16},{4,20},{8,24},{12,28},{16,0},{20,4},{24,8},{28,12},{1,17},{... | collective-permute-start | bytes 245768 | tf_op jit(solution)/shard_map/ppermute | solution.py:267
  28.6 5.4 %collective-permute-start.8 = (f32[40,512]{1,0:T(8,128)S(1)}, f32[40,512]{1,0:T(8,128)S(1)}, u32[]{:S(2)}, u32[]{:S(2)}) collective-permute-start(f32[40,512]{1,0:T(8,128)S(1)} %total.4.chunk_ref.mean_ref.refs_0_), channel_id=1, source_target_pairs={{0,12},{4,8},{8,4},{12,0},{16,28},{20,24},{24,20},{28,16},{1,13},{... | collective-permute-start | bytes 245768 | tf_op jit(solution)/shard_map/ppermute | solution.py:267
  29.2 5.5 %collective-permute-start.7 = (f32[40,512]{1,0:T(8,128)S(1)}, f32[40,512]{1,0:T(8,128)S(1)}, u32[]{:S(2)}, u32[]{:S(2)}) collective-permute-start(f32[40,512]{1,0:T(8,128)S(1)} %total.4.chunk_ref.mean_ref.refs_0_), channel_id=1, source_target_pairs={{0,4},{4,0},{8,12},{12,8},{16,20},{20,16},{24,28},{28,24},{1,5},{5... | collective-permute-start | bytes 245768 | tf_op jit(solution)/shard_map/ppermute | solution.py:267
  30.1 5.3 %collective-permute-start.6 = (f32[40,512]{1,0:T(8,128)S(1)}, f32[40,512]{1,0:T(8,128)S(1)}, u32[]{:S(2)}, u32[]{:S(2)}) collective-permute-start(f32[40,512]{1,0:T(8,128)S(1)} %total.4.chunk_ref.mean_ref.refs_0_), channel_id=1, source_target_pairs={{0,8},{4,12},{8,0},{12,4},{16,24},{20,28},{24,16},{28,20},{1,9},{5... | collective-permute-start | bytes 245768 | tf_op jit(solution)/shard_map/ppermute | solution.py:267
  37.4 4.9 %collective-permute-start.10 = (f32[32,768]{1,0:T(8,128)S(1)}, f32[32,768]{1,0:T(8,128)S(1)}, u32[]{:S(2)}, u32[]{:S(2)}) collective-permute-start(f32[32,768]{1,0:T(8,128)S(1)} %add.17.refs_0_), channel_id=1, source_target_pairs={{0,2},{1,3},{2,0},{3,1},{4,6},{5,7},{6,4},{7,5},{8,10},{9,11},{10,... | collective-permute-start | bytes 294920 | tf_op jit(solution)/shard_map/ppermute | solution.py:267
  42.6 5.5 %collective-permute-start.16 = (f32[32,128]{1,0:T(8,128)S(1)}, f32[32,128]{1,0:T(8,128)S(1)}, u32[]{:S(2)}, u32[]{:S(2)}) collective-permute-start(f32[32,128]{1,0:T(8,128)S(1)} %gram.4.refs_0_), channel_id=1, source_target_pairs={{0,1},{1,0},{2,3},{3,2},{4,5},{5,4},{6,7},{7,6},{8,9},{9,8},{10,11... | collective-permute-start | bytes 49160 | tf_op jit(solution)/shard_map/ppermute | solution.py:267
  44.6 5.5 %collective-permute-start.12 = (f32[32,512]{1,0:T(8,128)S(1)}, f32[32,512]{1,0:T(8,128)S(1)}, u32[]{:S(2)}, u32[]{:S(2)}) collective-permute-start(f32[32,512]{1,0:T(8,128)S(1)} %get-tuple-element.70), channel_id=1, source_target_pairs={{0,12},{4,8},{8,4},{12,0},{16,28},{20,24},{24,20},{28,16},{1,13},{... | collective-permute-start | bytes 196616 | tf_op jit(solution)/shard_map/ppermute | solution.py:267
  48.1 6.0 %collective-permute-start.17 = (f32[32,128]{1,0:T(8,128)S(1)}, f32[32,128]{1,0:T(8,128)S(1)}, u32[]{:S(2)}, u32[]{:S(2)}) collective-permute-start(f32[32,128]{1,0:T(8,128)S(1)} %add.20.own_ref), channel_id=1, source_target_pairs={{0,2},{1,3},{2,0},{3,1},{4,6},{5,7},{6,4},{7,5},{8,10},{9,11},{10,... | collective-permute-start | bytes 49160 | tf_op jit(solution)/shard_map/ppermute | solution.py:267
  51.6 5.9 %collective-permute-start.15 = (f32[32,512]{1,0:T(8,128)S(1)}, f32[32,512]{1,0:T(8,128)S(1)}, u32[]{:S(2)}, u32[]{:S(2)}) collective-permute-start(f32[32,512]{1,0:T(8,128)S(1)} %add.19.own_ref), channel_id=1, source_target_pairs={{0,16},{4,20},{8,24},{12,28},{16,0},{20,4},{24,8},{28,12},{1,17},{... | collective-permute-start | bytes 196616 | tf_op jit(solution)/shard_map/ppermute | solution.py:267
  57.7 5.2 %collective-permute-start.20 = (f32[32,512]{1,0:T(8,128)S(1)}, f32[32,512]{1,0:T(8,128)S(1)}, u32[]{:S(2)}, u32[]{:S(2)}) collective-permute-start(f32[32,512]{1,0:T(8,128)S(1)} %total.5.chunk_ref), channel_id=1, source_target_pairs={{0,12},{4,8},{8,4},{12,0},{16,28},{20,24},{24,20},{28,16},{1,13},{... | collective-permute-start | bytes 196616 | tf_op jit(solution)/shard_map/ppermute | solution.py:267
  58.9 4.7 %collective-permute-start.19 = (f32[32,512]{1,0:T(8,128)S(1)}, f32[32,512]{1,0:T(8,128)S(1)}, u32[]{:S(2)}, u32[]{:S(2)}) collective-permute-start(f32[32,512]{1,0:T(8,128)S(1)} %total.5.chunk_ref), channel_id=1, source_target_pairs={{0,4},{4,0},{8,12},{12,8},{16,20},{20,16},{24,28},{28,24},{1,5},{5... | collective-permute-start | bytes 196616 | tf_op jit(solution)/shard_map/ppermute | solution.py:267
  59.4 4.9 %collective-permute-start.18 = (f32[32,512]{1,0:T(8,128)S(1)}, f32[32,512]{1,0:T(8,128)S(1)}, u32[]{:S(2)}, u32[]{:S(2)}) collective-permute-start(f32[32,512]{1,0:T(8,128)S(1)} %total.5.chunk_ref), channel_id=1, source_target_pairs={{0,8},{4,12},{8,0},{12,4},{16,24},{20,28},{24,16},{28,20},{1,9},{5... | collective-permute-start | bytes 196616 | tf_op jit(solution)/shard_map/ppermute | solution.py:267
  66.3 4.9 %collective-permute-start.22 = (f32[32,768]{1,0:T(8,128)S(1)}, f32[32,768]{1,0:T(8,128)S(1)}, u32[]{:S(2)}, u32[]{:S(2)}) collective-permute-start(f32[32,768]{1,0:T(8,128)S(1)} %add.21.refs_0_), channel_id=1, source_target_pairs={{0,2},{1,3},{2,0},{3,1},{4,6},{5,7},{6,4},{7,5},{8,10},{9,11},{10,... | collective-permute-start | bytes 294920 | tf_op jit(solution)/shard_map/ppermute | solution.py:267
  71.5 5.5 %collective-permute-start.28 = (f32[32,128]{1,0:T(8,128)S(1)}, f32[32,128]{1,0:T(8,128)S(1)}, u32[]{:S(2)}, u32[]{:S(2)}) collective-permute-start(f32[32,128]{1,0:T(8,128)S(1)} %gram.5.refs_0_), channel_id=1, source_target_pairs={{0,1},{1,0},{2,3},{3,2},{4,5},{5,4},{6,7},{7,6},{8,9},{9,8},{10,11... | collective-permute-start | bytes 49160 | tf_op jit(solution)/shard_map/ppermute | solution.py:267
  73.5 5.5 %collective-permute-start.24 = (f32[32,512]{1,0:T(8,128)S(1)}, f32[32,512]{1,0:T(8,128)S(1)}, u32[]{:S(2)}, u32[]{:S(2)}) collective-permute-start(f32[32,512]{1,0:T(8,128)S(1)} %get-tuple-element.83), channel_id=1, source_target_pairs={{0,12},{4,8},{8,4},{12,0},{16,28},{20,24},{24,20},{28,16},{1,13},{... | collective-permute-start | bytes 196616 | tf_op jit(solution)/shard_map/ppermute | solution.py:267
  77.0 5.6 %collective-permute-start.29 = (f32[32,128]{1,0:T(8,128)S(1)}, f32[32,128]{1,0:T(8,128)S(1)}, u32[]{:S(2)}, u32[]{:S(2)}) collective-permute-start(f32[32,128]{1,0:T(8,128)S(1)} %add.24.own_ref), channel_id=1, source_target_pairs={{0,2},{1,3},{2,0},{3,1},{4,6},{5,7},{6,4},{7,5},{8,10},{9,11},{10,... | collective-permute-start | bytes 49160 | tf_op jit(solution)/shard_map/ppermute | solution.py:267
  80.4 5.9 %collective-permute-start.27 = (f32[32,512]{1,0:T(8,128)S(1)}, f32[32,512]{1,0:T(8,128)S(1)}, u32[]{:S(2)}, u32[]{:S(2)}) collective-permute-start(f32[32,512]{1,0:T(8,128)S(1)} %add.23.own_ref), channel_id=1, source_target_pairs={{0,16},{4,20},{8,24},{12,28},{16,0},{20,4},{24,8},{28,12},{1,17},{... | collective-permute-start | bytes 196616 | tf_op jit(solution)/shard_map/ppermute | solution.py:267
  86.6 5.5 %collective-permute-start.32 = (f32[32,512]{1,0:T(8,128)S(1)}, f32[32,512]{1,0:T(8,128)S(1)}, u32[]{:S(2)}, u32[]{:S(2)}) collective-permute-start(f32[32,512]{1,0:T(8,128)S(1)} %total.6.chunk_ref), channel_id=1, source_target_pairs={{0,12},{4,8},{8,4},{12,0},{16,28},{20,24},{24,20},{28,16},{1,13},{... | collective-permute-start | bytes 196616 | tf_op jit(solution)/shard_map/ppermute | solution.py:267
  87.7 5.0 %collective-permute-start.31 = (f32[32,512]{1,0:T(8,128)S(1)}, f32[32,512]{1,0:T(8,128)S(1)}, u32[]{:S(2)}, u32[]{:S(2)}) collective-permute-start(f32[32,512]{1,0:T(8,128)S(1)} %total.6.chunk_ref), channel_id=1, source_target_pairs={{0,4},{4,0},{8,12},{12,8},{16,20},{20,16},{24,28},{28,24},{1,5},{5... | collective-permute-start | bytes 196616 | tf_op jit(solution)/shard_map/ppermute | solution.py:267
  88.4 5.1 %collective-permute-start.30 = (f32[32,512]{1,0:T(8,128)S(1)}, f32[32,512]{1,0:T(8,128)S(1)}, u32[]{:S(2)}, u32[]{:S(2)}) collective-permute-start(f32[32,512]{1,0:T(8,128)S(1)} %total.6.chunk_ref), channel_id=1, source_target_pairs={{0,8},{4,12},{8,0},{12,4},{16,24},{20,28},{24,16},{28,20},{1,9},{5... | collective-permute-start | bytes 196616 | tf_op jit(solution)/shard_map/ppermute | solution.py:267
  95.6 4.9 %collective-permute-start.34 = (f32[32,768]{1,0:T(8,128)S(1)}, f32[32,768]{1,0:T(8,128)S(1)}, u32[]{:S(2)}, u32[]{:S(2)}) collective-permute-start(f32[32,768]{1,0:T(8,128)S(1)} %add.25.refs_0_), channel_id=1, source_target_pairs={{0,2},{1,3},{2,0},{3,1},{4,6},{5,7},{6,4},{7,5},{8,10},{9,11},{10,... | collective-permute-start | bytes 294920 | tf_op jit(solution)/shard_map/ppermute | solution.py:267
  100.8 5.5 %collective-permute-start.40 = (f32[32,128]{1,0:T(8,128)S(1)}, f32[32,128]{1,0:T(8,128)S(1)}, u32[]{:S(2)}, u32[]{:S(2)}) collective-permute-start(f32[32,128]{1,0:T(8,128)S(1)} %gram.6.refs_0_), channel_id=1, source_target_pairs={{0,1},{1,0},{2,3},{3,2},{4,5},{5,4},{6,7},{7,6},{8,9},{9,8},{10,11... | collective-permute-start | bytes 49160 | tf_op jit(solution)/shard_map/ppermute | solution.py:267
  102.8 5.5 %collective-permute-start.36 = (f32[32,512]{1,0:T(8,128)S(1)}, f32[32,512]{1,0:T(8,128)S(1)}, u32[]{:S(2)}, u32[]{:S(2)}) collective-permute-start(f32[32,512]{1,0:T(8,128)S(1)} %get-tuple-element.96), channel_id=1, source_target_pairs={{0,12},{4,8},{8,4},{12,0},{16,28},{20,24},{24,20},{28,16},{1,13},{... | collective-permute-start | bytes 196616 | tf_op jit(solution)/shard_map/ppermute | solution.py:267
  104.3 4.9 %collective-permute-start.37 = (f32[32,512]{1,0:T(8,128)S(1)}, f32[32,512]{1,0:T(8,128)S(1)}, u32[]{:S(2)}, u32[]{:S(2)}) collective-permute-start(f32[32,512]{1,0:T(8,128)S(1)} %get-tuple-element.97), channel_id=1, source_target_pairs={{0,4},{4,0},{8,12},{12,8},{16,20},{20,16},{24,28},{28,24},{1,5},{5... | collective-permute-start | bytes 196616 | tf_op jit(solution)/shard_map/ppermute | solution.py:267
  106.3 5.4 %collective-permute-start.41 = (f32[32,128]{1,0:T(8,128)S(1)}, f32[32,128]{1,0:T(8,128)S(1)}, u32[]{:S(2)}, u32[]{:S(2)}) collective-permute-start(f32[32,128]{1,0:T(8,128)S(1)} %add.28.own_ref), channel_id=1, source_target_pairs={{0,2},{1,3},{2,0},{3,1},{4,6},{5,7},{6,4},{7,5},{8,10},{9,11},{10,... | collective-permute-start | bytes 49160 | tf_op jit(solution)/shard_map/ppermute | solution.py:267
  109.5 6.1 %collective-permute-start.39 = (f32[32,512]{1,0:T(8,128)S(1)}, f32[32,512]{1,0:T(8,128)S(1)}, u32[]{:S(2)}, u32[]{:S(2)}) collective-permute-start(f32[32,512]{1,0:T(8,128)S(1)} %add.27.own_ref), channel_id=1, source_target_pairs={{0,16},{4,20},{8,24},{12,28},{16,0},{20,4},{24,8},{28,12},{1,17},{... | collective-permute-start | bytes 196616 | tf_op jit(solution)/shard_map/ppermute | solution.py:267
  115.8 5.3 %collective-permute-start.44 = (f32[32,512]{1,0:T(8,128)S(1)}, f32[32,512]{1,0:T(8,128)S(1)}, u32[]{:S(2)}, u32[]{:S(2)}) collective-permute-start(f32[32,512]{1,0:T(8,128)S(1)} %total.7.chunk_ref.refs_0_), channel_id=1, source_target_pairs={{0,12},{4,8},{8,4},{12,0},{16,28},{20,24},{24,20},{28,16},{1,13},{... | collective-permute-start | bytes 196616 | tf_op jit(solution)/shard_map/ppermute | solution.py:267
  116.7 5.1 %collective-permute-start.43 = (f32[32,512]{1,0:T(8,128)S(1)}, f32[32,512]{1,0:T(8,128)S(1)}, u32[]{:S(2)}, u32[]{:S(2)}) collective-permute-start(f32[32,512]{1,0:T(8,128)S(1)} %total.7.chunk_ref.refs_0_), channel_id=1, source_target_pairs={{0,4},{4,0},{8,12},{12,8},{16,20},{20,16},{24,28},{28,24},{1,5},{5... | collective-permute-start | bytes 196616 | tf_op jit(solution)/shard_map/ppermute | solution.py:267
  117.6 4.9 %collective-permute-start.42 = (f32[32,512]{1,0:T(8,128)S(1)}, f32[32,512]{1,0:T(8,128)S(1)}, u32[]{:S(2)}, u32[]{:S(2)}) collective-permute-start(f32[32,512]{1,0:T(8,128)S(1)} %total.7.chunk_ref.refs_0_), channel_id=1, source_target_pairs={{0,8},{4,12},{8,0},{12,4},{16,24},{20,28},{24,16},{28,20},{1,9},{5... | collective-permute-start | bytes 196616 | tf_op jit(solution)/shard_map/ppermute | solution.py:267
  128.6 5.5 %collective-permute-start.47 = (f32[32,768]{1,0:T(8,128)S(1)}, f32[32,768]{1,0:T(8,128)S(1)}, u32[]{:S(2)}, u32[]{:S(2)}) collective-permute-start(f32[32,768]{1,0:T(8,128)S(1)} %add.30.own_ref), channel_id=1, source_target_pairs={{0,1},{1,0},{2,3},{3,2},{4,5},{5,4},{6,7},{7,6},{8,9},{9,8},{10,11... | collective-permute-start | bytes 294920 | tf_op jit(solution)/shard_map/ppermute | solution.py:267
  (19 other events, 52.1 us)

commit v4 on v3

--- a/solution.py
+++ b/solution.py
@@ -22,7 +22,7 @@
 BF16 = jnp.bfloat16
 
 
-def call(kernel, outputs, name, scratch=(), in_specs=None, mebibytes=20, cost=None):
+def call(kernel, outputs, name, scratch=(), in_specs=None, aliases=None, mebibytes=20, cost=None):
     def run(*args):
         specs = in_specs or [VMEM] * len(args)
         return pl.pallas_call(
@@ -33,6 +33,7 @@
             scratch_shapes=scratch,
             compiler_params=pltpu.CompilerParams(vmem_limit_bytes=mebibytes * 2**20),
             cost_estimate=cost,
+            input_output_aliases=aliases or {},
             name=name,
         )(*args)
 
@@ -76,23 +77,35 @@
     return lax.broadcasted_iota(jnp.int32, (n, n), 0) == lax.broadcasted_iota(jnp.int32, (n, n), 1)
 
 
-def first_projection_kernel(blocks, basis_hbm, rows_hbm, out_ref, rows_ref, basis_ref, sems):
-    tokens = rows_ref.shape[0]
-    height = tokens // blocks
-    fetch_basis = pltpu.make_async_copy(basis_hbm, basis_ref, sems.at[blocks])
-    fetch_basis.start()
-    fetches = []
-    for i in range(blocks):
-        place = pl.ds(i * height, height)
-        fetches.append(
-            pltpu.make_async_copy(rows_hbm.at[place, :], rows_ref.at[place, :], sems.at[i])
-        )
-        fetches[-1].start()
-    fetch_basis.wait()
+def row_blocks(first, last, sizes):
+    starts = [first]
+    for size in sizes:
+        starts.append(starts[-1] + size)
+    return [pl.ds(start, size) for start, size in zip(starts, sizes)]
+
+
+def fetch(rows_hbm, rows_ref, places, sems):
+    copies = [
+        pltpu.make_async_copy(rows_hbm.at[place, :], rows_ref.at[place, :], sems.at[i])
+        for i, place in enumerate(places)
+    ]
+    for copy in copies:
+        copy.start()
+    return copies
+
+
+def fetch_kernel(places, rows_hbm, rows_ref, sems):
+    for copy in fetch(rows_hbm, rows_ref, places, sems):
+        copy.wait()
+
+
+def first_projection_kernel(ready, places, basis_ref, rows_hbm, ready_ref, out_ref, rows_ref, sems):
+    copies = fetch(rows_hbm, rows_ref, places, sems)
     vectors = split(basis_ref[...])
-    for i in range(blocks):
-        fetches[i].wait()
-        place = pl.ds(i * height, height)
+    for place in ready:
+        out_ref[:, place] = join(contract_last(vectors, rows_ref[place, :]))
+    for copy, place in zip(copies, places):
+        copy.wait()
         out_ref[:, place] = join(contract_last(vectors, rows_ref[place, :]))
 
 
@@ -100,36 +113,36 @@
     return lax.rem(lax.axis_index("feat"), 2)
 
 
-def chunk_gram(chunk_ref, n):
-    chunk = chunk_ref[:n, :]
-    return contract_last(chunk, chunk, HIGHEST)
-
-
-def projection_kernel(part, first, chunk_ref, rows_ref, *refs):
-    mean_ref, refs = (chunk_ref, refs) if first else (refs[0], refs[1:])
+def aligned(index, size):
+    return pl.ds(pl.multiple_of(index * size, size), size)
+
+
+def chunk_projection(part, chunk_ref, mean_ref, rows_ref, tokens):
     n, width = mean_ref.shape[0] - EXTRA, chunk_ref.shape[1]
-    place = pl.ds(pl.multiple_of((position() ^ part) * width, width), width)
     chunk = chunk_ref[:n, :]
     shift = jnp.sum(chunk * mean_ref[n : n + 1, :], axis=1, keepdims=True)
-    projected = join(contract_last(split(chunk), rows_ref[:, place])) - shift
-    if part != ORDER[0]:
-        projected = refs[0][...] + projected
-    if part != ORDER[-1]:
-        refs[-2][...] = projected
-        refs[-1][...] = chunk_gram(chunk_ref, n)
-        return
-    kept_ref, sent_ref, projected_ref = refs[-3:]
-    half = kept_ref.shape[1]
-    projected_ref[...] = projected
-    kept_ref[...] = projected_ref[:, pl.ds(pl.multiple_of(core() * half, half), half)]
-    sent_ref[...] = projected_ref[:, pl.ds(pl.multiple_of((1 - core()) * half, half), half)]
-
-
-def gram_kernel(chunk_ref, *refs):
+    rows = rows_ref[tokens, aligned(position() ^ part, width)]
+    return join(contract_last(split(chunk), rows)) - shift
+
+
+def own_projection_kernel(chunk_ref, mean_ref, rows_ref, out_ref):
+    out_ref[...] = chunk_projection(0, chunk_ref, mean_ref, rows_ref, slice(None))
+
+
+def rest_projection_kernel(kept, *refs):
+    chunks, means, (rows_ref, own_ref), out_ref = refs[:3], refs[3:6], refs[6:8], refs[-1]
+    place = aligned(core() if kept else 1 - core(), out_ref.shape[1])
+    value = own_ref[:, place]
+    for part, chunk_ref, mean_ref in zip(ORDER[1:], chunks, means):
+        value = value + chunk_projection(part, chunk_ref, mean_ref, rows_ref, place)
+    out_ref[...] = value
+
+
+def gram_kernel(*refs):
     *refs, out_ref = refs
     n = out_ref.shape[0]
-    parts = {part: ref[...] for part, ref in zip(ORDER, refs)}
-    parts[ORDER[-1]] = chunk_gram(chunk_ref, n)
+    chunks = {part: ref[:n, :] for part, ref in zip(ORDER, refs)}
+    parts = [contract_last(chunks[part], chunks[part], HIGHEST) for part in range(PEERS)]
     out_ref[...] = jnp.zeros(out_ref.shape, F32)
     out_ref[:, :n] = (parts[0] + parts[1]) + (parts[2] + parts[3])
 
@@ -169,7 +182,7 @@
     counts = join(jnp.sum(weights.astype(F32), axis=1, keepdims=True)) + centre * tokens
     weights = jnp.concatenate([weights, jnp.ones((2 * EXTRA, tokens), BF16)], axis=0)
     for part, out in zip(ORDER[1:], outs):
-        place = pl.ds(pl.multiple_of((position() ^ part) * width, width), width)
+        place = aligned(position() ^ part, width)
         first_term(weights, rows_ref[:, place], counts, centre, out)
     weights_ref[...] = weights
     side_ref[...] = jnp.broadcast_to(counts, side_ref.shape)
@@ -178,7 +191,7 @@
 
 def first_own_image_kernel(weights_ref, side_ref, rows_ref, out_ref):
     width = out_ref.shape[1]
-    place = pl.ds(pl.multiple_of(position() * width, width), width)
+    place = aligned(position(), width)
     first_term(weights_ref[...], rows_ref[:, place], side_ref[:, :1], side_ref[:, 1:2], out_ref)
 
 
@@ -199,32 +212,56 @@
     return projected_ref[...]
 
 
-def image_kernel(own_ref, other_ref, rows_ref, *refs):
-    means, outs = refs[: PEERS - 1], refs[PEERS - 1 : -3]
-    weights_ref, side_ref, projected_ref = refs[-3:]
-    n, width = own_ref.shape[0], outs[0].shape[1]
-    weights = split(gather_halves(own_ref, other_ref, projected_ref), TERMS)
-    counts = join(jnp.sum(weights.astype(F32), axis=1, keepdims=True), TERMS)
-    for part, mean, out in zip(ORDER[1:], means, outs):
-        place = pl.ds(pl.multiple_of((position() ^ part) * width, width), width)
-        term = join(jnp.dot(weights, rows_ref[:, place], preferred_element_type=F32), TERMS)
-        out[...] = term - counts * mean[n : n + 1, :]
+def weights_of(projected_ref):
+    weights = split(projected_ref[...], TERMS)
+    return weights, join(jnp.sum(weights.astype(F32), axis=1, keepdims=True), TERMS)
+
+
+def image_term(weights, counts, rows, mean_ref):
+    n = counts.shape[0]
+    term = join(jnp.dot(weights, rows, preferred_element_type=F32), TERMS)
+    return term - counts * mean_ref[n : n + 1, :]
+
+
+def half_image_kernel(own_ref, rows_ref, *refs):
+    means, outs = refs[:PEERS], refs[PEERS:]
+    tokens = aligned(core(), own_ref.shape[1])
+    weights, counts = weights_of(own_ref)
+    for part, mean_ref, out_ref in zip(ORDER, means, outs):
+        rows = rows_ref[tokens, aligned(position() ^ part, out_ref.shape[1])]
+        out_ref[...] = image_term(weights, counts, rows, mean_ref)
+
+
+def image_kernel(other_ref, rows_ref, *refs):
+    means, halves, outs = refs[: PEERS - 1], refs[PEERS - 1 : 2 * PEERS - 2], refs[2 * PEERS - 2 :]
+    *outs, weights_ref, side_ref = outs
+    tokens = aligned(1 - core(), other_ref.shape[1])
+    weights, counts = weights_of(other_ref)
+    for part, mean_ref, half_ref, out_ref in zip(ORDER[1:], means, halves, outs):
+        rows = rows_ref[tokens, aligned(position() ^ part, out_ref.shape[1])]
+        out_ref[...] = half_ref[...] + image_term(weights, counts, rows, mean_ref)
     weights_ref[...] = weights
     side_ref[...] = jnp.broadcast_to(counts, side_ref.shape)
 
 
-def own_image_kernel(weights_ref, side_ref, rows_ref, mean_ref, out_ref):
-    n, width = out_ref.shape
-    place = pl.ds(pl.multiple_of(position() * width, width), width)
-    term = join(jnp.dot(weights_ref[...], rows_ref[:, place], preferred_element_type=F32), TERMS)
-    out_ref[...] = term - side_ref[:, :1] * mean_ref[n : n + 1, :]
+def own_image_kernel(weights_ref, side_ref, rows_ref, mean_ref, half_ref, out_ref):
+    tokens = aligned(1 - core(), weights_ref.shape[1])
+    rows = rows_ref[tokens, aligned(position(), out_ref.shape[1])]
+    out_ref[...] = half_ref[...] + image_term(weights_ref[...], side_ref[:, :1], rows, mean_ref)
+
+
+def gather_halves(own_ref, other_ref, projected_ref):
+    half = own_ref.shape[1]
+    projected_ref[:, aligned(core(), half)] = own_ref[...]
+    projected_ref[:, aligned(1 - core(), half)] = other_ref[...]
+    return projected_ref[...]
 
 
 def assemble_kernel(*refs):
     *chunks, out_ref = refs
     n, width = out_ref.shape[0], chunks[0].shape[1]
     for part, chunk in zip(ORDER, chunks):
-        place = pl.ds(pl.multiple_of((position() ^ part) * width, width), width)
+        place = aligned(position() ^ part, width)
         out_ref[:, place] = chunk[:n, :]
 
 
@@ -239,6 +276,10 @@
 def normalised_total_kernel(own_ref, got_ref, lower_ref, out_ref):
     value = own_ref[...] + got_ref[...]
     out_ref[...] = jnp.dot(lower_ref[...], value, preferred_element_type=F32, precision=HIGHEST)
+
+
+def ordered_add_kernel(own_ref, got_ref, before_ref, out_ref):
+    out_ref[...] = total(own_ref, got_ref).astype(out_ref.dtype)
 
 
 def add_kernel(*refs):
@@ -293,15 +334,25 @@
     rows_in_all = tokens * lax.axis_size("tok")
     last_feat = lax.axis_size("feat") // 2
 
-    blocks = 3
+    ready = row_blocks(0, tokens, [tokens // 2])
+    places = row_blocks(tokens // 2, tokens, [tokens // 3, tokens // 6])
+    rows = call(
+        functools.partial(fetch_kernel, ready),
+        [(activations.shape, BF16)],
+        "fetch",
+        scratch=[pltpu.SemaphoreType.DMA((len(ready),))],
+        in_specs=[HBM],
+        mebibytes=46,
+    )(activations)[0]
     partial, rows = call(
-        functools.partial(first_projection_kernel, blocks),
+        functools.partial(first_projection_kernel, ready, places),
         [((n, tokens), F32), (activations.shape, BF16)],
         "first_projection",
-        scratch=[pltpu.VMEM((n, features), F32), pltpu.SemaphoreType.DMA((blocks + 1,))],
-        in_specs=[HBM, HBM],
+        scratch=[pltpu.SemaphoreType.DMA((len(places),))],
+        in_specs=[VMEM, HBM, VMEM],
+        aliases={2: 1},
         mebibytes=46,
-    )(start_basis, activations)
+    )(start_basis, activations, rows)
     terms = sum_but_last(partial, "feat")
     own = call(first_part_kernel, [((n, tokens + LANES), BF16)], "first_part")(*terms)[0]
     got = swap(own, "feat", last_feat)
@@ -311,19 +362,21 @@
     for step in range(ITERS):
         first = step == 0
         chunk = ((n + EXTRA if first else n, width), F32)
-        weights = ((2 * n + 2 * EXTRA if first else TERMS * n, tokens), BF16)
-        outputs = [chunk] * (PEERS - 1) + [weights, side]
         if first:
+            weights = ((2 * n + 2 * EXTRA, tokens), BF16)
+            outputs = [chunk] * (PEERS - 1) + [weights, side]
             *terms, weights, sums = call(first_image_kernel, outputs, "first_image")(own, got, rows)
-            kernel, kept_means = first_own_image_kernel, []
+            kernel, kept = first_own_image_kernel, []
         else:
-            kernel, kept_means = own_image_kernel, means[:1]
-            scratch = [pltpu.VMEM(*whole)]
-            *terms, weights, sums = call(image_kernel, outputs, "image", scratch)(
-                own, other, rows, *means[1:]
+            weights = ((TERMS * n, tokens // 2), BF16)
+            halves = call(half_image_kernel, [chunk] * PEERS, "half_image", cost=SHORT)(own, rows, *means)
+            outputs = [chunk] * (PEERS - 1) + [weights, side]
+            *terms, weights, sums = call(image_kernel, outputs, "image")(
+                other, rows, *means[1:], *halves[1:]
             )
+            kernel, kept = own_image_kernel, [means[0], halves[0]]
         received = [swap(term, "tok", part) for part, term in zip(ORDER[1:], terms)]
-        kept = call(kernel, [chunk], "own_image", cost=SHORT)(weights, sums, rows, *kept_means)
+        kept = call(kernel, [chunk], "own_image", cost=SHORT)(weights, sums, rows, *kept)
         image = add(*kept, *received)
         *steps, last_step = distances("tok", PEERS)
         for distance in steps:
@@ -334,23 +387,26 @@
         images = share(image, "tok")
         if first:
             means = images
-        before, grams = [], []
-        for place, part in enumerate(ORDER):
-            kernel = functools.partial(projection_kernel, part, first)
-            operands = [images[place], rows, *([] if first else [means[place]]), *before]
-            if part != ORDER[-1]:
-                outputs = [whole, ((n, n), F32)]
-                *before, gram = call(kernel, outputs, "projection", cost=SHORT)(*operands)
-                grams.append(gram)
-        gram = call(gram_kernel, [side], "gram")(images[-1], *grams)[0]
-        outputs, scratch = [half, half], [pltpu.VMEM(*whole)]
-        own, sent = call(kernel, outputs, "last_projection", scratch, cost=SHORT)(*operands)
+        last = step == ITERS - 1
+        projected = call(own_projection_kernel, [whole], "own_projection", cost=SHORT)(
+            images[0], means[0], rows
+        )[0]
+        gram = call(gram_kernel, [side], "gram")(*images)[0]
+        operands = [*images[1:], *means[1:], rows, projected]
+        kernel = functools.partial(rest_projection_kernel, False)
+        sent = call(kernel, [half], "sent_projection")(*operands, *([gram] if last else []))[0]
+        kernel = functools.partial(rest_projection_kernel, True)
+        own = call(kernel, [half], "kept_projection", cost=SHORT)(*operands)[0]
         for distance in distances("feat", 1):
-            got = swap(sent if distance == 1 else own, "feat", distance)
-            narrow = step == ITERS - 1 and distance != last_feat
-            own = add(own, got, dtype=BF16 if narrow else F32)
             grams = (gram, swap(gram, "feat", distance))
             gram = add(*grams) if distance != last_feat else None
+            got = swap(sent if distance == 1 else own, "feat", distance)
+            if last and distance == 1:
+                own = call(ordered_add_kernel, [(half[0], BF16)], "add")(own, got, gram)[0]
+            elif distance == last_feat:
+                own = call(ordered_add_kernel, [half], "add")(own, got, grams[0])[0]
+            else:
+                own = add(own, got)
         other = swap(own, "feat", 1)
         lower = call(inverse_factor_kernel, [((n, n), F32)], "inverse_factor", cost=LONG)(*grams)[0]
     image = call(assemble_kernel, [((n, features), F32)], "assemble")(*images)[0]

time: 135 us -> 135 us (level)
  starting transfers between devices: 55.1 us -> 53.7 us
    ppermute x50, starting transfers between devices: 55.1 us -> 53.7 us  [swap(): return lax.ppermute(value, axis, [(i, i ^ distance) for i in range(size)])]
  transfers between devices with their start and end apart: 50 -> 50, of which waited for: 32 -> 40; matrix products, arithmetic and copies ran while one was open for 0% -> 0% of each run, Pallas kernels for 18% -> 16%
where the time goes in v4:
time: 135 us; the launch traced here: 134 us
  starting transfers between devices  53.7 us (40%)
  waiting for transfers between devices  45 us (33%)
  Pallas kernels  34.8 us (26%)
    ppermute x50, starting transfers between devices, swap(): return lax.ppermute(value, axis, [(i, i ^ distance) for i in range(size)])  53.7 us
    ppermute x50, waiting for transfers between devices, swap(): return lax.ppermute(value, axis, [(i, i ^ distance) for i in range(size)])  45 us
    pallas_call x56, Pallas kernels, run(): pl.pallas_call(kernel, out_shape=[jax.ShapeDtypeStruct(shape, dtype) for...  34.8 us
  transfers between devices with their start and end apart: 50, of which 40 were waited for; matrix products, arithmetic and copies ran while one was open for 0% of the time, Pallas kernels for 16%

profile of v4, /device:TPU:0, one launch (start us, length us, event | category | flops | bytes accessed | tf_op | source)
XLA Modules:
  0.0 134.5 jit_solution(15188000774118568780)
XLA Ops:
  0.6 1.9 %fetch.1.ready_ref = bf16[1536,2048]{1,0:T(8,128)(2,1)S(1)} custom-call(bf16[1536,2048]{1,0:T(8,128)(2,1)} %rows_hbm.3), custom_call_target="tpu_custom_call" | custom-call | tf_op jit(solution)/shard_map/fetch/pallas_call | solution.py:28
  2.6 3.1 %first_projection.1 = (f32[32,1536]{1,0:T(8,128)S(1)}, bf16[1536,2048]{1,0:T(8,128)(2,1)S(1)}) custom-call(f32[32,2048]{1,0:T(8,128)S(1)} %copy-done, bf16[1536,2048]{1,0:T(8,128)(2,1)} %rows_hbm.3, bf16[1536,2048]{1,0:T(8,128)(2,1)S(1)} %fetch.1.ready_ref), custom_call_target="tpu_custom_call", output_to_operand_aliasing={{1}: (2, {})} | custom-call | tf_op jit(solution)/shard_map/first_projection/pallas_call | solution.py:28
  7.4 2.9 %collective-permute-start.1 = (bf16[32,1664]{1,0:T(8,128)(2,1)S(1)}, bf16[32,1664]{1,0:T(8,128)(2,1)S(1)}, u32[]{:S(2)}, u32[]{:S(2)}) collective-permute-start(bf16[32,1664]{1,0:T(8,128)(2,1)S(1)} %first_part.1.own_ref), channel_id=1, source_target_pairs={{0,2},{1,3},{2,0},{3,1},{4,6},{5,7},{6,4},{7,5},{8,10},{9,11},{10,... | collective-permute-start | bytes 319496 | tf_op jit(solution)/shard_map/ppermute | solution.py:308
  10.3 3.3 %collective-permute-done.1.got_ref = bf16[32,1664]{1,0:T(8,128)(2,1)S(1)} collective-permute-done((bf16[32,1664]{1,0:T(8,128)(2,1)S(1)}, bf16[32,1664]{1,0:T(8,128)(2,1)S(1)}, u32[]{:S(2)}, u32[]{:S(2)}) %collective-permute-start.1) | collective-permute-done | bytes 106528 | tf_op jit(solution)/shard_map/ppermute | solution.py:308
  14.5 2.9 %collective-permute-start.2 = (f32[40,512]{1,0:T(8,128)S(1)}, f32[40,512]{1,0:T(8,128)S(1)}, u32[]{:S(2)}, u32[]{:S(2)}) collective-permute-start(f32[40,512]{1,0:T(8,128)S(1)} %get-tuple-element.40), channel_id=1, source_target_pairs={{0,12},{4,8},{8,4},{12,0},{16,28},{20,24},{24,20},{28,16},{1,13},{... | collective-permute-start | bytes 245768 | tf_op jit(solution)/shard_map/ppermute | solution.py:308
  18.5 1.6 %collective-permute-done.2.refs_1_ = f32[40,512]{1,0:T(8,128)S(1)} collective-permute-done((f32[40,512]{1,0:T(8,128)S(1)}, f32[40,512]{1,0:T(8,128)S(1)}, u32[]{:S(2)}, u32[]{:S(2)}) %collective-permute-start.2) | collective-permute-done | bytes 81952 | tf_op jit(solution)/shard_map/ppermute | solution.py:308
  20.1 1.8 %collective-permute-done.3.refs_2_ = f32[40,512]{1,0:T(8,128)S(1)} collective-permute-done((f32[40,512]{1,0:T(8,128)S(1)}, f32[40,512]{1,0:T(8,128)S(1)}, u32[]{:S(2)}, u32[]{:S(2)}) %collective-permute-start.3) | collective-permute-done | bytes 81952 | tf_op jit(solution)/shard_map/ppermute | solution.py:308
  22.4 2.8 %collective-permute-start.5 = (f32[40,512]{1,0:T(8,128)S(1)}, f32[40,512]{1,0:T(8,128)S(1)}, u32[]{:S(2)}, u32[]{:S(2)}) collective-permute-start(f32[40,512]{1,0:T(8,128)S(1)} %add.16.own_ref), channel_id=1, source_target_pairs={{0,16},{4,20},{8,24},{12,28},{16,0},{20,4},{24,8},{28,12},{1,17},{... | collective-permute-start | bytes 245768 | tf_op jit(solution)/shard_map/ppermute | solution.py:308
  25.2 3.5 %collective-permute-done.5.got_ref = f32[40,512]{1,0:T(8,128)S(1)} collective-permute-done((f32[40,512]{1,0:T(8,128)S(1)}, f32[40,512]{1,0:T(8,128)S(1)}, u32[]{:S(2)}, u32[]{:S(2)}) %collective-permute-start.5) | collective-permute-done | bytes 81952 | tf_op jit(solution)/shard_map/ppermute | solution.py:308
  30.3 2.0 %collective-permute-start.6 = (f32[40,512]{1,0:T(8,128)S(1)}, f32[40,512]{1,0:T(8,128)S(1)}, u32[]{:S(2)}, u32[]{:S(2)}) collective-permute-start(f32[40,512]{1,0:T(8,128)S(1)} %total.4.chunk_ref.mean_ref.refs_0_), channel_id=1, source_target_pairs={{0,12},{4,8},{8,4},{12,0},{16,28},{20,24},{24,20},{28,16},{1,13},{... | collective-permute-start | bytes 245768 | tf_op jit(solution)/shard_map/ppermute | solution.py:308
  33.3 2.3 %collective-permute-done.6.refs_0_.refs_3_.refs_1_ = f32[40,512]{1,0:T(8,128)S(1)} collective-permute-done((f32[40,512]{1,0:T(8,128)S(1)}, f32[40,512]{1,0:T(8,128)S(1)}, u32[]{:S(2)}, u32[]{:S(2)}) %collective-permute-start.6) | collective-permute-done | bytes 81952 | tf_op jit(solution)/shard_map/ppermute | solution.py:308
  37.8 1.6 %collective-permute-start.10 = (f32[32,768]{1,0:T(8,128)S(1)}, f32[32,768]{1,0:T(8,128)S(1)}, u32[]{:S(2)}, u32[]{:S(2)}) collective-permute-start(f32[32,768]{1,0:T(8,128)S(1)} %add.17.own_ref), channel_id=1, source_target_pairs={{0,2},{1,3},{2,0},{3,1},{4,6},{5,7},{6,4},{7,5},{8,10},{9,11},{10,... | collective-permute-start | bytes 294920 | tf_op jit(solution)/shard_map/ppermute | solution.py:308
  40.9 1.8 %collective-permute-done.10.got_ref = f32[32,768]{1,0:T(8,128)S(1)} collective-permute-done((f32[32,768]{1,0:T(8,128)S(1)}, f32[32,768]{1,0:T(8,128)S(1)}, u32[]{:S(2)}, u32[]{:S(2)}) %collective-permute-start.10) | collective-permute-done | bytes 98336 | tf_op jit(solution)/shard_map/ppermute | solution.py:308
  44.7 2.0 %collective-permute-start.13 = (f32[32,512]{1,0:T(8,128)S(1)}, f32[32,512]{1,0:T(8,128)S(1)}, u32[]{:S(2)}, u32[]{:S(2)}) collective-permute-start(f32[32,512]{1,0:T(8,128)S(1)} %get-tuple-element.49), channel_id=1, source_target_pairs={{0,12},{4,8},{8,4},{12,0},{16,28},{20,24},{24,20},{28,16},{1,13},{... | collective-permute-start | bytes 196616 | tf_op jit(solution)/shard_map/ppermute | solution.py:308
  52.4 2.8 %collective-permute-start.16 = (f32[32,512]{1,0:T(8,128)S(1)}, f32[32,512]{1,0:T(8,128)S(1)}, u32[]{:S(2)}, u32[]{:S(2)}) collective-permute-start(f32[32,512]{1,0:T(8,128)S(1)} %add.20.own_ref), channel_id=1, source_target_pairs={{0,16},{4,20},{8,24},{12,28},{16,0},{20,4},{24,8},{28,12},{1,17},{... | collective-permute-start | bytes 196616 | tf_op jit(solution)/shard_map/ppermute | solution.py:308
  55.2 2.9 %inverse_factor.4.lower_ref = f32[32,32]{1,0:T(8,128)S(1)} custom-call(f32[32,128]{1,0:T(8,128)S(1)} %add.18.before_ref.own_ref, f32[32,128]{1,0:T(8,128)S(1)} %collective-permute-done.17.got_ref), custom_call_target="tpu_custom_call" | custom-call | flops 17179869184 | tf_op jit(solution)/shard_map/inverse_factor/pallas_call | solution.py:28
  59.6 2.2 %collective-permute-start.18 = (f32[32,512]{1,0:T(8,128)S(1)}, f32[32,512]{1,0:T(8,128)S(1)}, u32[]{:S(2)}, u32[]{:S(2)}) collective-permute-start(f32[32,512]{1,0:T(8,128)S(1)} %total.5.chunk_ref.refs_0_), channel_id=1, source_target_pairs={{0,12},{4,8},{8,4},{12,0},{16,28},{20,24},{24,20},{28,16},{1,13},{... | collective-permute-start | bytes 196616 | tf_op jit(solution)/shard_map/ppermute | solution.py:308
  63.2 1.6 %collective-permute-done.18.refs_0_.refs_1_ = f32[32,512]{1,0:T(8,128)S(1)} collective-permute-done((f32[32,512]{1,0:T(8,128)S(1)}, f32[32,512]{1,0:T(8,128)S(1)}, u32[]{:S(2)}, u32[]{:S(2)}) %collective-permute-start.18) | collective-permute-done | bytes 65568 | tf_op jit(solution)/shard_map/ppermute | solution.py:308
  70.1 1.8 %collective-permute-done.22.got_ref = f32[32,768]{1,0:T(8,128)S(1)} collective-permute-done((f32[32,768]{1,0:T(8,128)S(1)}, f32[32,768]{1,0:T(8,128)S(1)}, u32[]{:S(2)}, u32[]{:S(2)}) %collective-permute-start.22) | collective-permute-done | bytes 98336 | tf_op jit(solution)/shard_map/ppermute | solution.py:308
  73.8 2.3 %collective-permute-start.25 = (f32[32,512]{1,0:T(8,128)S(1)}, f32[32,512]{1,0:T(8,128)S(1)}, u32[]{:S(2)}, u32[]{:S(2)}) collective-permute-start(f32[32,512]{1,0:T(8,128)S(1)} %get-tuple-element.58), channel_id=1, source_target_pairs={{0,12},{4,8},{8,4},{12,0},{16,28},{20,24},{24,20},{28,16},{1,13},{... | collective-permute-start | bytes 196616 | tf_op jit(solution)/shard_map/ppermute | solution.py:308
  81.2 2.1 %collective-permute-start.28 = (f32[32,512]{1,0:T(8,128)S(1)}, f32[32,512]{1,0:T(8,128)S(1)}, u32[]{:S(2)}, u32[]{:S(2)}) collective-permute-start(f32[32,512]{1,0:T(8,128)S(1)} %add.24.own_ref), channel_id=1, source_target_pairs={{0,16},{4,20},{8,24},{12,28},{16,0},{20,4},{24,8},{28,12},{1,17},{... | collective-permute-start | bytes 196616 | tf_op jit(solution)/shard_map/ppermute | solution.py:308
  83.3 2.9 %inverse_factor.5.lower_ref = f32[32,32]{1,0:T(8,128)S(1)} custom-call(f32[32,128]{1,0:T(8,128)S(1)} %add.22.before_ref.own_ref, f32[32,128]{1,0:T(8,128)S(1)} %collective-permute-done.29.got_ref), custom_call_target="tpu_custom_call" | custom-call | flops 17179869184 | tf_op jit(solution)/shard_map/inverse_factor/pallas_call | solution.py:28
  88.3 2.4 %collective-permute-start.30 = (f32[32,512]{1,0:T(8,128)S(1)}, f32[32,512]{1,0:T(8,128)S(1)}, u32[]{:S(2)}, u32[]{:S(2)}) collective-permute-start(f32[32,512]{1,0:T(8,128)S(1)} %total.6.chunk_ref.refs_0_), channel_id=1, source_target_pairs={{0,12},{4,8},{8,4},{12,0},{16,28},{20,24},{24,20},{28,16},{1,13},{... | collective-permute-start | bytes 196616 | tf_op jit(solution)/shard_map/ppermute | solution.py:308
  91.6 1.9 %collective-permute-done.30.refs_0_.refs_1_ = f32[32,512]{1,0:T(8,128)S(1)} collective-permute-done((f32[32,512]{1,0:T(8,128)S(1)}, f32[32,512]{1,0:T(8,128)S(1)}, u32[]{:S(2)}, u32[]{:S(2)}) %collective-permute-start.30) | collective-permute-done | bytes 65568 | tf_op jit(solution)/shard_map/ppermute | solution.py:308
  98.8 1.9 %collective-permute-done.34.got_ref = f32[32,768]{1,0:T(8,128)S(1)} collective-permute-done((f32[32,768]{1,0:T(8,128)S(1)}, f32[32,768]{1,0:T(8,128)S(1)}, u32[]{:S(2)}, u32[]{:S(2)}) %collective-permute-start.34) | collective-permute-done | bytes 98336 | tf_op jit(solution)/shard_map/ppermute | solution.py:308
  102.6 2.5 %collective-permute-start.37 = (f32[32,512]{1,0:T(8,128)S(1)}, f32[32,512]{1,0:T(8,128)S(1)}, u32[]{:S(2)}, u32[]{:S(2)}) collective-permute-start(f32[32,512]{1,0:T(8,128)S(1)} %get-tuple-element.67), channel_id=1, source_target_pairs={{0,12},{4,8},{8,4},{12,0},{16,28},{20,24},{24,20},{28,16},{1,13},{... | collective-permute-start | bytes 196616 | tf_op jit(solution)/shard_map/ppermute | solution.py:308
  110.4 1.9 %collective-permute-start.40 = (f32[32,512]{1,0:T(8,128)S(1)}, f32[32,512]{1,0:T(8,128)S(1)}, u32[]{:S(2)}, u32[]{:S(2)}) collective-permute-start(f32[32,512]{1,0:T(8,128)S(1)} %add.28.own_ref), channel_id=1, source_target_pairs={{0,16},{4,20},{8,24},{12,28},{16,0},{20,4},{24,8},{28,12},{1,17},{... | collective-permute-start | bytes 196616 | tf_op jit(solution)/shard_map/ppermute | solution.py:308
  112.3 2.9 %inverse_factor.6.lower_ref = f32[32,32]{1,0:T(8,128)S(1)} custom-call(f32[32,128]{1,0:T(8,128)S(1)} %add.26.before_ref.own_ref, f32[32,128]{1,0:T(8,128)S(1)} %collective-permute-done.41.got_ref), custom_call_target="tpu_custom_call" | custom-call | flops 17179869184 | tf_op jit(solution)/shard_map/inverse_factor/pallas_call | solution.py:28
  117.4 2.4 %collective-permute-start.42 = (f32[32,512]{1,0:T(8,128)S(1)}, f32[32,512]{1,0:T(8,128)S(1)}, u32[]{:S(2)}, u32[]{:S(2)}) collective-permute-start(f32[32,512]{1,0:T(8,128)S(1)} %total.7.chunk_ref.refs_0_), channel_id=1, source_target_pairs={{0,12},{4,8},{8,4},{12,0},{16,28},{20,24},{24,20},{28,16},{1,13},{... | collective-permute-start | bytes 196616 | tf_op jit(solution)/shard_map/ppermute | solution.py:308
  120.7 1.8 %collective-permute-done.42.refs_0_.refs_1_ = f32[32,512]{1,0:T(8,128)S(1)} collective-permute-done((f32[32,512]{1,0:T(8,128)S(1)}, f32[32,512]{1,0:T(8,128)S(1)}, u32[]{:S(2)}, u32[]{:S(2)}) %collective-permute-start.42) | collective-permute-done | bytes 65568 | tf_op jit(solution)/shard_map/ppermute | solution.py:308
  127.3 2.0 %collective-permute-done.47.got_ref = bf16[32,768]{1,0:T(8,128)(2,1)S(1)} collective-permute-done((bf16[32,768]{1,0:T(8,128)(2,1)S(1)}, bf16[32,768]{1,0:T(8,128)(2,1)S(1)}, u32[]{:S(2)}, u32[]{:S(2)}) %collective-permute-start.47) | collective-permute-done | bytes 49184 | tf_op jit(solution)/shard_map/ppermute | solution.py:308
  130.5 2.9 %inverse_factor.7.lower_ref = f32[32,32]{1,0:T(8,128)S(1)} custom-call(f32[32,128]{1,0:T(8,128)S(1)} %add.29.before_ref.own_ref, f32[32,128]{1,0:T(8,128)S(1)} %collective-permute-done.49.got_ref), custom_call_target="tpu_custom_call" | custom-call | flops 17179869184 | tf_op jit(solution)/shard_map/inverse_factor/pallas_call | solution.py:28
  (126 shorter events, 58.9 us)
Async XLA Ops:
  7.4 6.2 %collective-permute-start.1 = (bf16[32,1664]{1,0:T(8,128)(2,1)S(1)}, bf16[32,1664]{1,0:T(8,128)(2,1)S(1)}, u32[]{:S(2)}, u32[]{:S(2)}) collective-permute-start(bf16[32,1664]{1,0:T(8,128)(2,1)S(1)} %first_part.1.own_ref), channel_id=1, source_target_pairs={{0,2},{1,3},{2,0},{3,1},{4,6},{5,7},{6,4},{7,5},{8,10},{9,11},{10,... | collective-permute-start | bytes 319496 | tf_op jit(solution)/shard_map/ppermute | solution.py:308
  14.5 5.5 %collective-permute-start.2 = (f32[40,512]{1,0:T(8,128)S(1)}, f32[40,512]{1,0:T(8,128)S(1)}, u32[]{:S(2)}, u32[]{:S(2)}) collective-permute-start(f32[40,512]{1,0:T(8,128)S(1)} %get-tuple-element.40), channel_id=1, source_target_pairs={{0,12},{4,8},{8,4},{12,0},{16,28},{20,24},{24,20},{28,16},{1,13},{... | collective-permute-start | bytes 245768 | tf_op jit(solution)/shard_map/ppermute | solution.py:308
  17.4 4.4 %collective-permute-start.3 = (f32[40,512]{1,0:T(8,128)S(1)}, f32[40,512]{1,0:T(8,128)S(1)}, u32[]{:S(2)}, u32[]{:S(2)}) collective-permute-start(f32[40,512]{1,0:T(8,128)S(1)} %get-tuple-element.41), channel_id=1, source_target_pairs={{0,4},{4,0},{8,12},{12,8},{16,20},{20,16},{24,28},{28,24},{1,5},{5... | collective-permute-start | bytes 245768 | tf_op jit(solution)/shard_map/ppermute | solution.py:308
  17.9 4.4 %collective-permute-start.4 = (f32[40,512]{1,0:T(8,128)S(1)}, f32[40,512]{1,0:T(8,128)S(1)}, u32[]{:S(2)}, u32[]{:S(2)}) collective-permute-start(f32[40,512]{1,0:T(8,128)S(1)} %get-tuple-element.42), channel_id=1, source_target_pairs={{0,8},{4,12},{8,0},{12,4},{16,24},{20,28},{24,16},{28,20},{1,9},{5... | collective-permute-start | bytes 245768 | tf_op jit(solution)/shard_map/ppermute | solution.py:308
  22.4 6.3 %collective-permute-start.5 = (f32[40,512]{1,0:T(8,128)S(1)}, f32[40,512]{1,0:T(8,128)S(1)}, u32[]{:S(2)}, u32[]{:S(2)}) collective-permute-start(f32[40,512]{1,0:T(8,128)S(1)} %add.16.own_ref), channel_id=1, source_target_pairs={{0,16},{4,20},{8,24},{12,28},{16,0},{20,4},{24,8},{28,12},{1,17},{... | collective-permute-start | bytes 245768 | tf_op jit(solution)/shard_map/ppermute | solution.py:308
  28.7 4.4 %collective-permute-start.8 = (f32[40,512]{1,0:T(8,128)S(1)}, f32[40,512]{1,0:T(8,128)S(1)}, u32[]{:S(2)}, u32[]{:S(2)}) collective-permute-start(f32[40,512]{1,0:T(8,128)S(1)} %total.4.chunk_ref.mean_ref.refs_0_), channel_id=1, source_target_pairs={{0,8},{4,12},{8,0},{12,4},{16,24},{20,28},{24,16},{28,20},{1,9},{5... | collective-permute-start | bytes 245768 | tf_op jit(solution)/shard_map/ppermute | solution.py:308
  28.8 4.5 %collective-permute-start.7 = (f32[40,512]{1,0:T(8,128)S(1)}, f32[40,512]{1,0:T(8,128)S(1)}, u32[]{:S(2)}, u32[]{:S(2)}) collective-permute-start(f32[40,512]{1,0:T(8,128)S(1)} %total.4.chunk_ref.mean_ref.refs_0_), channel_id=1, source_target_pairs={{0,4},{4,0},{8,12},{12,8},{16,20},{20,16},{24,28},{28,24},{1,5},{5... | collective-permute-start | bytes 245768 | tf_op jit(solution)/shard_map/ppermute | solution.py:308
  30.3 5.3 %collective-permute-start.6 = (f32[40,512]{1,0:T(8,128)S(1)}, f32[40,512]{1,0:T(8,128)S(1)}, u32[]{:S(2)}, u32[]{:S(2)}) collective-permute-start(f32[40,512]{1,0:T(8,128)S(1)} %total.4.chunk_ref.mean_ref.refs_0_), channel_id=1, source_target_pairs={{0,12},{4,8},{8,4},{12,0},{16,28},{20,24},{24,20},{28,16},{1,13},{... | collective-permute-start | bytes 245768 | tf_op jit(solution)/shard_map/ppermute | solution.py:308
  37.8 4.9 %collective-permute-start.10 = (f32[32,768]{1,0:T(8,128)S(1)}, f32[32,768]{1,0:T(8,128)S(1)}, u32[]{:S(2)}, u32[]{:S(2)}) collective-permute-start(f32[32,768]{1,0:T(8,128)S(1)} %add.17.own_ref), channel_id=1, source_target_pairs={{0,2},{1,3},{2,0},{3,1},{4,6},{5,7},{6,4},{7,5},{8,10},{9,11},{10,... | collective-permute-start | bytes 294920 | tf_op jit(solution)/shard_map/ppermute | solution.py:308
  44.7 5.3 %collective-permute-start.13 = (f32[32,512]{1,0:T(8,128)S(1)}, f32[32,512]{1,0:T(8,128)S(1)}, u32[]{:S(2)}, u32[]{:S(2)}) collective-permute-start(f32[32,512]{1,0:T(8,128)S(1)} %get-tuple-element.49), channel_id=1, source_target_pairs={{0,12},{4,8},{8,4},{12,0},{16,28},{20,24},{24,20},{28,16},{1,13},{... | collective-permute-start | bytes 196616 | tf_op jit(solution)/shard_map/ppermute | solution.py:308
  46.7 4.6 %collective-permute-start.14 = (f32[32,512]{1,0:T(8,128)S(1)}, f32[32,512]{1,0:T(8,128)S(1)}, u32[]{:S(2)}, u32[]{:S(2)}) collective-permute-start(f32[32,512]{1,0:T(8,128)S(1)} %get-tuple-element.50), channel_id=1, source_target_pairs={{0,4},{4,0},{8,12},{12,8},{16,20},{20,16},{24,28},{28,24},{1,5},{5... | collective-permute-start | bytes 196616 | tf_op jit(solution)/shard_map/ppermute | solution.py:308
  48.2 7.0 %collective-permute-start.17 = (f32[32,128]{1,0:T(8,128)S(1)}, f32[32,128]{1,0:T(8,128)S(1)}, u32[]{:S(2)}, u32[]{:S(2)}) collective-permute-start(f32[32,128]{1,0:T(8,128)S(1)} %add.18.before_ref.own_ref), channel_id=1, source_target_pairs={{0,2},{1,3},{2,0},{3,1},{4,6},{5,7},{6,4},{7,5},{8,10},{9,11},{10,... | collective-permute-start | bytes 49160 | tf_op jit(solution)/shard_map/ppermute | solution.py:308
  52.4 5.7 %collective-permute-start.16 = (f32[32,512]{1,0:T(8,128)S(1)}, f32[32,512]{1,0:T(8,128)S(1)}, u32[]{:S(2)}, u32[]{:S(2)}) collective-permute-start(f32[32,512]{1,0:T(8,128)S(1)} %add.20.own_ref), channel_id=1, source_target_pairs={{0,16},{4,20},{8,24},{12,28},{16,0},{20,4},{24,8},{28,12},{1,17},{... | collective-permute-start | bytes 196616 | tf_op jit(solution)/shard_map/ppermute | solution.py:308
  58.3 4.3 %collective-permute-start.20 = (f32[32,512]{1,0:T(8,128)S(1)}, f32[32,512]{1,0:T(8,128)S(1)}, u32[]{:S(2)}, u32[]{:S(2)}) collective-permute-start(f32[32,512]{1,0:T(8,128)S(1)} %total.5.chunk_ref.refs_0_), channel_id=1, source_target_pairs={{0,8},{4,12},{8,0},{12,4},{16,24},{20,28},{24,16},{28,20},{1,9},{5... | collective-permute-start | bytes 196616 | tf_op jit(solution)/shard_map/ppermute | solution.py:308
  58.4 4.8 %collective-permute-start.19 = (f32[32,512]{1,0:T(8,128)S(1)}, f32[32,512]{1,0:T(8,128)S(1)}, u32[]{:S(2)}, u32[]{:S(2)}) collective-permute-start(f32[32,512]{1,0:T(8,128)S(1)} %total.5.chunk_ref.refs_0_), channel_id=1, source_target_pairs={{0,4},{4,0},{8,12},{12,8},{16,20},{20,16},{24,28},{28,24},{1,5},{5... | collective-permute-start | bytes 196616 | tf_op jit(solution)/shard_map/ppermute | solution.py:308
  59.6 5.2 %collective-permute-start.18 = (f32[32,512]{1,0:T(8,128)S(1)}, f32[32,512]{1,0:T(8,128)S(1)}, u32[]{:S(2)}, u32[]{:S(2)}) collective-permute-start(f32[32,512]{1,0:T(8,128)S(1)} %total.5.chunk_ref.refs_0_), channel_id=1, source_target_pairs={{0,12},{4,8},{8,4},{12,0},{16,28},{20,24},{24,20},{28,16},{1,13},{... | collective-permute-start | bytes 196616 | tf_op jit(solution)/shard_map/ppermute | solution.py:308
  67.0 4.9 %collective-permute-start.22 = (f32[32,768]{1,0:T(8,128)S(1)}, f32[32,768]{1,0:T(8,128)S(1)}, u32[]{:S(2)}, u32[]{:S(2)}) collective-permute-start(f32[32,768]{1,0:T(8,128)S(1)} %add.21.own_ref), channel_id=1, source_target_pairs={{0,2},{1,3},{2,0},{3,1},{4,6},{5,7},{6,4},{7,5},{8,10},{9,11},{10,... | collective-permute-start | bytes 294920 | tf_op jit(solution)/shard_map/ppermute | solution.py:308
  73.8 5.3 %collective-permute-start.25 = (f32[32,512]{1,0:T(8,128)S(1)}, f32[32,512]{1,0:T(8,128)S(1)}, u32[]{:S(2)}, u32[]{:S(2)}) collective-permute-start(f32[32,512]{1,0:T(8,128)S(1)} %get-tuple-element.58), channel_id=1, source_target_pairs={{0,12},{4,8},{8,4},{12,0},{16,28},{20,24},{24,20},{28,16},{1,13},{... | collective-permute-start | bytes 196616 | tf_op jit(solution)/shard_map/ppermute | solution.py:308
  76.1 4.4 %collective-permute-start.26 = (f32[32,512]{1,0:T(8,128)S(1)}, f32[32,512]{1,0:T(8,128)S(1)}, u32[]{:S(2)}, u32[]{:S(2)}) collective-permute-start(f32[32,512]{1,0:T(8,128)S(1)} %get-tuple-element.59), channel_id=1, source_target_pairs={{0,4},{4,0},{8,12},{12,8},{16,20},{20,16},{24,28},{28,24},{1,5},{5... | collective-permute-start | bytes 196616 | tf_op jit(solution)/shard_map/ppermute | solution.py:308
  77.4 5.9 %collective-permute-start.29 = (f32[32,128]{1,0:T(8,128)S(1)}, f32[32,128]{1,0:T(8,128)S(1)}, u32[]{:S(2)}, u32[]{:S(2)}) collective-permute-start(f32[32,128]{1,0:T(8,128)S(1)} %add.22.before_ref.own_ref), channel_id=1, source_target_pairs={{0,2},{1,3},{2,0},{3,1},{4,6},{5,7},{6,4},{7,5},{8,10},{9,11},{10,... | collective-permute-start | bytes 49160 | tf_op jit(solution)/shard_map/ppermute | solution.py:308
  81.2 5.9 %collective-permute-start.28 = (f32[32,512]{1,0:T(8,128)S(1)}, f32[32,512]{1,0:T(8,128)S(1)}, u32[]{:S(2)}, u32[]{:S(2)}) collective-permute-start(f32[32,512]{1,0:T(8,128)S(1)} %add.24.own_ref), channel_id=1, source_target_pairs={{0,16},{4,20},{8,24},{12,28},{16,0},{20,4},{24,8},{28,12},{1,17},{... | collective-permute-start | bytes 196616 | tf_op jit(solution)/shard_map/ppermute | solution.py:308
  87.2 4.3 %collective-permute-start.32 = (f32[32,512]{1,0:T(8,128)S(1)}, f32[32,512]{1,0:T(8,128)S(1)}, u32[]{:S(2)}, u32[]{:S(2)}) collective-permute-start(f32[32,512]{1,0:T(8,128)S(1)} %total.6.chunk_ref.refs_0_), channel_id=1, source_target_pairs={{0,8},{4,12},{8,0},{12,4},{16,24},{20,28},{24,16},{28,20},{1,9},{5... | collective-permute-start | bytes 196616 | tf_op jit(solution)/shard_map/ppermute | solution.py:308
  87.3 4.3 %collective-permute-start.31 = (f32[32,512]{1,0:T(8,128)S(1)}, f32[32,512]{1,0:T(8,128)S(1)}, u32[]{:S(2)}, u32[]{:S(2)}) collective-permute-start(f32[32,512]{1,0:T(8,128)S(1)} %total.6.chunk_ref.refs_0_), channel_id=1, source_target_pairs={{0,4},{4,0},{8,12},{12,8},{16,20},{20,16},{24,28},{28,24},{1,5},{5... | collective-permute-start | bytes 196616 | tf_op jit(solution)/shard_map/ppermute | solution.py:308
  88.3 5.2 %collective-permute-start.30 = (f32[32,512]{1,0:T(8,128)S(1)}, f32[32,512]{1,0:T(8,128)S(1)}, u32[]{:S(2)}, u32[]{:S(2)}) collective-permute-start(f32[32,512]{1,0:T(8,128)S(1)} %total.6.chunk_ref.refs_0_), channel_id=1, source_target_pairs={{0,12},{4,8},{8,4},{12,0},{16,28},{20,24},{24,20},{28,16},{1,13},{... | collective-permute-start | bytes 196616 | tf_op jit(solution)/shard_map/ppermute | solution.py:308
  95.7 5.0 %collective-permute-start.34 = (f32[32,768]{1,0:T(8,128)S(1)}, f32[32,768]{1,0:T(8,128)S(1)}, u32[]{:S(2)}, u32[]{:S(2)}) collective-permute-start(f32[32,768]{1,0:T(8,128)S(1)} %add.25.own_ref), channel_id=1, source_target_pairs={{0,2},{1,3},{2,0},{3,1},{4,6},{5,7},{6,4},{7,5},{8,10},{9,11},{10,... | collective-permute-start | bytes 294920 | tf_op jit(solution)/shard_map/ppermute | solution.py:308
  102.6 5.3 %collective-permute-start.37 = (f32[32,512]{1,0:T(8,128)S(1)}, f32[32,512]{1,0:T(8,128)S(1)}, u32[]{:S(2)}, u32[]{:S(2)}) collective-permute-start(f32[32,512]{1,0:T(8,128)S(1)} %get-tuple-element.67), channel_id=1, source_target_pairs={{0,12},{4,8},{8,4},{12,0},{16,28},{20,24},{24,20},{28,16},{1,13},{... | collective-permute-start | bytes 196616 | tf_op jit(solution)/shard_map/ppermute | solution.py:308
  106.1 4.3 %collective-permute-start.39 = (f32[32,512]{1,0:T(8,128)S(1)}, f32[32,512]{1,0:T(8,128)S(1)}, u32[]{:S(2)}, u32[]{:S(2)}) collective-permute-start(f32[32,512]{1,0:T(8,128)S(1)} %get-tuple-element.69), channel_id=1, source_target_pairs={{0,8},{4,12},{8,0},{12,4},{16,24},{20,28},{24,16},{28,20},{1,9},{5... | collective-permute-start | bytes 196616 | tf_op jit(solution)/shard_map/ppermute | solution.py:308
  106.2 6.1 %collective-permute-start.41 = (f32[32,128]{1,0:T(8,128)S(1)}, f32[32,128]{1,0:T(8,128)S(1)}, u32[]{:S(2)}, u32[]{:S(2)}) collective-permute-start(f32[32,128]{1,0:T(8,128)S(1)} %add.26.before_ref.own_ref), channel_id=1, source_target_pairs={{0,2},{1,3},{2,0},{3,1},{4,6},{5,7},{6,4},{7,5},{8,10},{9,11},{10,... | collective-permute-start | bytes 49160 | tf_op jit(solution)/shard_map/ppermute | solution.py:308
  110.4 5.7 %collective-permute-start.40 = (f32[32,512]{1,0:T(8,128)S(1)}, f32[32,512]{1,0:T(8,128)S(1)}, u32[]{:S(2)}, u32[]{:S(2)}) collective-permute-start(f32[32,512]{1,0:T(8,128)S(1)} %add.28.own_ref), channel_id=1, source_target_pairs={{0,16},{4,20},{8,24},{12,28},{16,0},{20,4},{24,8},{28,12},{1,17},{... | collective-permute-start | bytes 196616 | tf_op jit(solution)/shard_map/ppermute | solution.py:308
  116.2 4.3 %collective-permute-start.44 = (f32[32,512]{1,0:T(8,128)S(1)}, f32[32,512]{1,0:T(8,128)S(1)}, u32[]{:S(2)}, u32[]{:S(2)}) collective-permute-start(f32[32,512]{1,0:T(8,128)S(1)} %total.7.chunk_ref.refs_0_), channel_id=1, source_target_pairs={{0,8},{4,12},{8,0},{12,4},{16,24},{20,28},{24,16},{28,20},{1,9},{5... | collective-permute-start | bytes 196616 | tf_op jit(solution)/shard_map/ppermute | solution.py:308
  116.3 4.4 %collective-permute-start.43 = (f32[32,512]{1,0:T(8,128)S(1)}, f32[32,512]{1,0:T(8,128)S(1)}, u32[]{:S(2)}, u32[]{:S(2)}) collective-permute-start(f32[32,512]{1,0:T(8,128)S(1)} %total.7.chunk_ref.refs_0_), channel_id=1, source_target_pairs={{0,4},{4,0},{8,12},{12,8},{16,20},{20,16},{24,28},{28,24},{1,5},{5... | collective-permute-start | bytes 196616 | tf_op jit(solution)/shard_map/ppermute | solution.py:308
  117.4 5.2 %collective-permute-start.42 = (f32[32,512]{1,0:T(8,128)S(1)}, f32[32,512]{1,0:T(8,128)S(1)}, u32[]{:S(2)}, u32[]{:S(2)}) collective-permute-start(f32[32,512]{1,0:T(8,128)S(1)} %total.7.chunk_ref.refs_0_), channel_id=1, source_target_pairs={{0,12},{4,8},{8,4},{12,0},{16,28},{20,24},{24,20},{28,16},{1,13},{... | collective-permute-start | bytes 196616 | tf_op jit(solution)/shard_map/ppermute | solution.py:308
  (19 other events, 42.9 us)

commit v5 on v4

--- a/solution.py
+++ b/solution.py
@@ -117,24 +117,33 @@
     return pl.ds(pl.multiple_of(index * size, size), size)
 
 
-def chunk_projection(part, chunk_ref, mean_ref, rows_ref, tokens):
+def split_kernel(chunk_ref, out_ref):
+    out_ref[...] = split(chunk_ref[: out_ref.shape[0] // 2, :])
+
+
+def chunk_projection(part, terms, chunk_ref, mean_ref, rows_ref, tokens):
     n, width = mean_ref.shape[0] - EXTRA, chunk_ref.shape[1]
-    chunk = chunk_ref[:n, :]
-    shift = jnp.sum(chunk * mean_ref[n : n + 1, :], axis=1, keepdims=True)
+    shift = jnp.sum(chunk_ref[:n, :] * mean_ref[n : n + 1, :], axis=1, keepdims=True)
     rows = rows_ref[tokens, aligned(position() ^ part, width)]
-    return join(contract_last(split(chunk), rows)) - shift
+    return join(contract_last(terms, rows)) - shift
 
 
 def own_projection_kernel(chunk_ref, mean_ref, rows_ref, out_ref):
-    out_ref[...] = chunk_projection(0, chunk_ref, mean_ref, rows_ref, slice(None))
-
-
-def rest_projection_kernel(kept, *refs):
-    chunks, means, (rows_ref, own_ref), out_ref = refs[:3], refs[3:6], refs[6:8], refs[-1]
-    place = aligned(core() if kept else 1 - core(), out_ref.shape[1])
+    terms = split(chunk_ref[: out_ref.shape[0], :])
+    out_ref[...] = chunk_projection(0, terms, chunk_ref, mean_ref, rows_ref, slice(None))
+
+
+def rest_projection_kernel(half, chunk3, chunk1, chunk2, mean3, mean1, mean2, terms_ref, rows_ref, own_ref, *refs):
+    out_ref = refs[-1]
+    n, tokens = out_ref.shape
+    place = slice(None) if half is None else aligned(core() if half == "kept" else 1 - core(), tokens)
     value = own_ref[:, place]
-    for part, chunk_ref, mean_ref in zip(ORDER[1:], chunks, means):
-        value = value + chunk_projection(part, chunk_ref, mean_ref, rows_ref, place)
+    for part, terms, chunk_ref, mean_ref in (
+        (3, terms_ref[...], chunk3, mean3),
+        (1, split(chunk1[:n, :]), chunk1, mean1),
+        (2, split(chunk2[:n, :]), chunk2, mean2),
+    ):
+        value = value + chunk_projection(part, terms, chunk_ref, mean_ref, rows_ref, place)
     out_ref[...] = value
 
 
@@ -205,13 +214,6 @@
     out_ref[n:, :] = jnp.broadcast_to(mean, (EXTRA, mean.shape[1]))
 
 
-def gather_halves(own_ref, other_ref, projected_ref):
-    half = own_ref.shape[1]
-    for place, ref in ((core(), own_ref), (1 - core(), other_ref)):
-        projected_ref[:, pl.ds(pl.multiple_of(place * half, half), half)] = ref[...]
-    return projected_ref[...]
-
-
 def weights_of(projected_ref):
     weights = split(projected_ref[...], TERMS)
     return weights, join(jnp.sum(weights.astype(F32), axis=1, keepdims=True), TERMS)
@@ -250,13 +252,6 @@
     out_ref[...] = half_ref[...] + image_term(weights_ref[...], side_ref[:, :1], rows, mean_ref)
 
 
-def gather_halves(own_ref, other_ref, projected_ref):
-    half = own_ref.shape[1]
-    projected_ref[:, aligned(core(), half)] = own_ref[...]
-    projected_ref[:, aligned(1 - core(), half)] = other_ref[...]
-    return projected_ref[...]
-
-
 def assemble_kernel(*refs):
     *chunks, out_ref = refs
     n, width = out_ref.shape[0], chunks[0].shape[1]
@@ -265,10 +260,10 @@
         out_ref[:, place] = chunk[:n, :]
 
 
-def last_kernel(own_ref, other_ref, lower_ref, image_ref, scores_ref, basis_ref, projected_ref):
-    n, lower = own_ref.shape[0], lower_ref[...]
+def last_kernel(own_ref, got_ref, lower_ref, image_ref, scores_ref, basis_ref):
+    n, lower = lower_ref.shape[0], lower_ref[...]
     basis_ref[...] = jnp.dot(lower, image_ref[...], preferred_element_type=F32, precision=HIGHEST)
-    projected = gather_halves(own_ref, other_ref, projected_ref)
+    projected = total(own_ref, got_ref)
     projected = jnp.dot(lower, projected, preferred_element_type=F32, precision=HIGHEST)
     scores_ref[...] = jnp.sum(projected * projected, axis=0) / n
 
@@ -391,27 +386,36 @@
         projected = call(own_projection_kernel, [whole], "own_projection", cost=SHORT)(
             images[0], means[0], rows
         )[0]
+        terms = call(split_kernel, [((2 * n, width), BF16)], "split", cost=SHORT)(images[1])[0]
         gram = call(gram_kernel, [side], "gram")(*images)[0]
-        operands = [*images[1:], *means[1:], rows, projected]
-        kernel = functools.partial(rest_projection_kernel, False)
-        sent = call(kernel, [half], "sent_projection")(*operands, *([gram] if last else []))[0]
-        kernel = functools.partial(rest_projection_kernel, True)
-        own = call(kernel, [half], "kept_projection", cost=SHORT)(*operands)[0]
+        operands = [*images[1:], *means[1:], terms, rows, projected]
+        if last:
+            kernel = functools.partial(rest_projection_kernel, None)
+            own = call(kernel, [whole], "projection")(*operands, gram)[0]
+        else:
+            kernel = functools.partial(rest_projection_kernel, "sent")
+            sent = call(kernel, [half], "sent_projection")(*operands)[0]
+            kernel = functools.partial(rest_projection_kernel, "kept")
+            own = call(kernel, [half], "kept_projection", cost=SHORT)(*operands)[0]
         for distance in distances("feat", 1):
+            got = swap(own if last or distance > 1 else sent, "feat", distance)
             grams = (gram, swap(gram, "feat", distance))
             gram = add(*grams) if distance != last_feat else None
-            got = swap(sent if distance == 1 else own, "feat", distance)
-            if last and distance == 1:
-                own = call(ordered_add_kernel, [(half[0], BF16)], "add")(own, got, gram)[0]
+            if last:
+                narrow = ((n, tokens), BF16 if distance == last_feat // 2 else F32)
+                if distance != last_feat:
+                    own = call(ordered_add_kernel, [narrow], "add")(own, got, gram)[0]
+                else:
+                    other = got
             elif distance == last_feat:
                 own = call(ordered_add_kernel, [half], "add")(own, got, grams[0])[0]
+                other = swap(own, "feat", 1)
             else:
                 own = add(own, got)
-        other = swap(own, "feat", 1)
         lower = call(inverse_factor_kernel, [((n, n), F32)], "inverse_factor", cost=LONG)(*grams)[0]
     image = call(assemble_kernel, [((n, features), F32)], "assemble")(*images)[0]
-    outputs, scratch = [((tokens,), F32), ((n, features), F32)], [pltpu.VMEM(*whole)]
-    return tuple(call(last_kernel, outputs, "last", scratch)(own, other, lower, image))
+    outputs = [((tokens,), F32), ((n, features), F32)]
+    return tuple(call(last_kernel, outputs, "last")(own, other, lower, image))
 
 
 def solution(mesh):

time: 135 us -> 131 us (0.970)
  waiting for transfers between devices: 45 us -> 41.1 us
    ppermute x50 -> x49, waiting for transfers between devices: 45 us -> 41.1 us  [swap(): return lax.ppermute(value, axis, [(i, i ^ distance) for i in range(size)])]
    ppermute x50 -> x49, starting transfers between devices: 53.7 us -> 54.6 us  [swap(): return lax.ppermute(value, axis, [(i, i ^ distance) for i in range(size)])]
    pallas_call x56 -> x58, Pallas kernels: 34.8 us -> 34.7 us  [run(): pl.pallas_call(kernel, out_shape=[jax.ShapeDtypeStruct(shape, dtype) for...]
  transfers between devices with their start and end apart: 50 -> 49, of which waited for: 40 -> 37; matrix products, arithmetic and copies ran while one was open for 0% -> 0% of each run, Pallas kernels for 16% -> 16%
where the time goes in v5:
time: 131 us
  starting transfers between devices  54.6 us (42%)
  waiting for transfers between devices  41.1 us (31%)
  Pallas kernels  34.7 us (26%)
    ppermute x49, starting transfers between devices, swap(): return lax.ppermute(value, axis, [(i, i ^ distance) for i in range(size)])  54.6 us
    ppermute x49, waiting for transfers between devices, swap(): return lax.ppermute(value, axis, [(i, i ^ distance) for i in range(size)])  41.1 us
    pallas_call x58, Pallas kernels, run(): pl.pallas_call(kernel, out_shape=[jax.ShapeDtypeStruct(shape, dtype) for...  34.7 us
  transfers between devices with their start and end apart: 49, of which 37 were waited for; matrix products, arithmetic and copies ran while one was open for 0% of the time, Pallas kernels for 16%

profile of v5, /device:TPU:0, one launch (start us, length us, event | category | flops | bytes accessed | tf_op | source)
XLA Modules:
  0.0 131.3 jit_solution(6371306912848215885)
XLA Ops:
  0.6 1.9 %fetch.1.ready_ref = bf16[1536,2048]{1,0:T(8,128)(2,1)S(1)} custom-call(bf16[1536,2048]{1,0:T(8,128)(2,1)} %rows_hbm.3), custom_call_target="tpu_custom_call" | custom-call | tf_op jit(solution)/shard_map/fetch/pallas_call | solution.py:28
  2.6 3.1 %first_projection.1 = (f32[32,1536]{1,0:T(8,128)S(1)}, bf16[1536,2048]{1,0:T(8,128)(2,1)S(1)}) custom-call(f32[32,2048]{1,0:T(8,128)S(1)} %copy-done, bf16[1536,2048]{1,0:T(8,128)(2,1)} %rows_hbm.3, bf16[1536,2048]{1,0:T(8,128)(2,1)S(1)} %fetch.1.ready_ref), custom_call_target="tpu_custom_call", output_to_operand_aliasing={{1}: (2, {})} | custom-call | tf_op jit(solution)/shard_map/first_projection/pallas_call | solution.py:28
  7.4 2.9 %collective-permute-start.1 = (bf16[32,1664]{1,0:T(8,128)(2,1)S(1)}, bf16[32,1664]{1,0:T(8,128)(2,1)S(1)}, u32[]{:S(2)}, u32[]{:S(2)}) collective-permute-start(bf16[32,1664]{1,0:T(8,128)(2,1)S(1)} %first_part.1.own_ref), channel_id=1, source_target_pairs={{0,2},{1,3},{2,0},{3,1},{4,6},{5,7},{6,4},{7,5},{8,10},{9,11},{10,... | collective-permute-start | bytes 319496 | tf_op jit(solution)/shard_map/ppermute | solution.py:303
  10.3 3.3 %collective-permute-done.1.got_ref = bf16[32,1664]{1,0:T(8,128)(2,1)S(1)} collective-permute-done((bf16[32,1664]{1,0:T(8,128)(2,1)S(1)}, bf16[32,1664]{1,0:T(8,128)(2,1)S(1)}, u32[]{:S(2)}, u32[]{:S(2)}) %collective-permute-start.1) | collective-permute-done | bytes 106528 | tf_op jit(solution)/shard_map/ppermute | solution.py:303
  14.5 2.9 %collective-permute-start.2 = (f32[40,512]{1,0:T(8,128)S(1)}, f32[40,512]{1,0:T(8,128)S(1)}, u32[]{:S(2)}, u32[]{:S(2)}) collective-permute-start(f32[40,512]{1,0:T(8,128)S(1)} %get-tuple-element.40), channel_id=1, source_target_pairs={{0,12},{4,8},{8,4},{12,0},{16,28},{20,24},{24,20},{28,16},{1,13},{... | collective-permute-start | bytes 245768 | tf_op jit(solution)/shard_map/ppermute | solution.py:303
  18.5 1.6 %collective-permute-done.2.refs_1_ = f32[40,512]{1,0:T(8,128)S(1)} collective-permute-done((f32[40,512]{1,0:T(8,128)S(1)}, f32[40,512]{1,0:T(8,128)S(1)}, u32[]{:S(2)}, u32[]{:S(2)}) %collective-permute-start.2) | collective-permute-done | bytes 81952 | tf_op jit(solution)/shard_map/ppermute | solution.py:303
  20.1 1.8 %collective-permute-done.3.refs_2_ = f32[40,512]{1,0:T(8,128)S(1)} collective-permute-done((f32[40,512]{1,0:T(8,128)S(1)}, f32[40,512]{1,0:T(8,128)S(1)}, u32[]{:S(2)}, u32[]{:S(2)}) %collective-permute-start.3) | collective-permute-done | bytes 81952 | tf_op jit(solution)/shard_map/ppermute | solution.py:303
  22.4 2.8 %collective-permute-start.5 = (f32[40,512]{1,0:T(8,128)S(1)}, f32[40,512]{1,0:T(8,128)S(1)}, u32[]{:S(2)}, u32[]{:S(2)}) collective-permute-start(f32[40,512]{1,0:T(8,128)S(1)} %add.15.own_ref), channel_id=1, source_target_pairs={{0,16},{4,20},{8,24},{12,28},{16,0},{20,4},{24,8},{28,12},{1,17},{... | collective-permute-start | bytes 245768 | tf_op jit(solution)/shard_map/ppermute | solution.py:303
  25.2 3.5 %collective-permute-done.5.got_ref = f32[40,512]{1,0:T(8,128)S(1)} collective-permute-done((f32[40,512]{1,0:T(8,128)S(1)}, f32[40,512]{1,0:T(8,128)S(1)}, u32[]{:S(2)}, u32[]{:S(2)}) %collective-permute-start.5) | collective-permute-done | bytes 81952 | tf_op jit(solution)/shard_map/ppermute | solution.py:303
  29.3 2.3 %collective-permute-start.8 = (f32[40,512]{1,0:T(8,128)S(1)}, f32[40,512]{1,0:T(8,128)S(1)}, u32[]{:S(2)}, u32[]{:S(2)}) collective-permute-start(f32[40,512]{1,0:T(8,128)S(1)} %total.4.chunk_ref.mean_ref.refs_0_), channel_id=1, source_target_pairs={{0,8},{4,12},{8,0},{12,4},{16,24},{20,28},{24,16},{28,20},{1,9},{5... | collective-permute-start | bytes 245768 | tf_op jit(solution)/shard_map/ppermute | solution.py:303
  38.2 1.6 %collective-permute-start.10 = (f32[32,768]{1,0:T(8,128)S(1)}, f32[32,768]{1,0:T(8,128)S(1)}, u32[]{:S(2)}, u32[]{:S(2)}) collective-permute-start(f32[32,768]{1,0:T(8,128)S(1)} %add.16.own_ref), channel_id=1, source_target_pairs={{0,2},{1,3},{2,0},{3,1},{4,6},{5,7},{6,4},{7,5},{8,10},{9,11},{10,... | collective-permute-start | bytes 294920 | tf_op jit(solution)/shard_map/ppermute | solution.py:303
  41.4 1.8 %collective-permute-done.10.got_ref = f32[32,768]{1,0:T(8,128)S(1)} collective-permute-done((f32[32,768]{1,0:T(8,128)S(1)}, f32[32,768]{1,0:T(8,128)S(1)}, u32[]{:S(2)}, u32[]{:S(2)}) %collective-permute-start.10) | collective-permute-done | bytes 98336 | tf_op jit(solution)/shard_map/ppermute | solution.py:303
  46.6 2.0 %collective-permute-start.15 = (f32[32,512]{1,0:T(8,128)S(1)}, f32[32,512]{1,0:T(8,128)S(1)}, u32[]{:S(2)}, u32[]{:S(2)}) collective-permute-start(f32[32,512]{1,0:T(8,128)S(1)} %get-tuple-element.51), channel_id=1, source_target_pairs={{0,8},{4,12},{8,0},{12,4},{16,24},{20,28},{24,16},{28,20},{1,9},{5... | collective-permute-start | bytes 196616 | tf_op jit(solution)/shard_map/ppermute | solution.py:303
  48.6 1.5 %collective-permute-start.17 = (f32[32,128]{1,0:T(8,128)S(1)}, f32[32,128]{1,0:T(8,128)S(1)}, u32[]{:S(2)}, u32[]{:S(2)}) collective-permute-start(f32[32,128]{1,0:T(8,128)S(1)} %add.17.before_ref.own_ref), channel_id=1, source_target_pairs={{0,2},{1,3},{2,0},{3,1},{4,6},{5,7},{6,4},{7,5},{8,10},{9,11},{10,... | collective-permute-start | bytes 49160 | tf_op jit(solution)/shard_map/ppermute | solution.py:303
  50.9 2.5 %collective-permute-start.16 = (f32[32,512]{1,0:T(8,128)S(1)}, f32[32,512]{1,0:T(8,128)S(1)}, u32[]{:S(2)}, u32[]{:S(2)}) collective-permute-start(f32[32,512]{1,0:T(8,128)S(1)} %add.19.own_ref), channel_id=1, source_target_pairs={{0,16},{4,20},{8,24},{12,28},{16,0},{20,4},{24,8},{28,12},{1,17},{... | collective-permute-start | bytes 196616 | tf_op jit(solution)/shard_map/ppermute | solution.py:303
  53.5 2.9 %inverse_factor.4.lower_ref = f32[32,32]{1,0:T(8,128)S(1)} custom-call(f32[32,128]{1,0:T(8,128)S(1)} %add.17.before_ref.own_ref, f32[32,128]{1,0:T(8,128)S(1)} %collective-permute-done.17.got_ref), custom_call_target="tpu_custom_call" | custom-call | flops 17179869184 | tf_op jit(solution)/shard_map/inverse_factor/pallas_call | solution.py:28
  56.5 1.9 %collective-permute-start.18 = (f32[32,512]{1,0:T(8,128)S(1)}, f32[32,512]{1,0:T(8,128)S(1)}, u32[]{:S(2)}, u32[]{:S(2)}) collective-permute-start(f32[32,512]{1,0:T(8,128)S(1)} %total.5.chunk_ref.refs_0_), channel_id=1, source_target_pairs={{0,12},{4,8},{8,4},{12,0},{16,28},{20,24},{24,20},{28,16},{1,13},{... | collective-permute-start | bytes 196616 | tf_op jit(solution)/shard_map/ppermute | solution.py:303
  65.7 1.6 %collective-permute-start.22 = (f32[32,768]{1,0:T(8,128)S(1)}, f32[32,768]{1,0:T(8,128)S(1)}, u32[]{:S(2)}, u32[]{:S(2)}) collective-permute-start(f32[32,768]{1,0:T(8,128)S(1)} %add.20.own_ref), channel_id=1, source_target_pairs={{0,2},{1,3},{2,0},{3,1},{4,6},{5,7},{6,4},{7,5},{8,10},{9,11},{10,... | collective-permute-start | bytes 294920 | tf_op jit(solution)/shard_map/ppermute | solution.py:303
  68.9 1.8 %collective-permute-done.22.got_ref = f32[32,768]{1,0:T(8,128)S(1)} collective-permute-done((f32[32,768]{1,0:T(8,128)S(1)}, f32[32,768]{1,0:T(8,128)S(1)}, u32[]{:S(2)}, u32[]{:S(2)}) %collective-permute-start.22) | collective-permute-done | bytes 98336 | tf_op jit(solution)/shard_map/ppermute | solution.py:303
  72.6 2.3 %collective-permute-start.25 = (f32[32,512]{1,0:T(8,128)S(1)}, f32[32,512]{1,0:T(8,128)S(1)}, u32[]{:S(2)}, u32[]{:S(2)}) collective-permute-start(f32[32,512]{1,0:T(8,128)S(1)} %get-tuple-element.58), channel_id=1, source_target_pairs={{0,12},{4,8},{8,4},{12,0},{16,28},{20,24},{24,20},{28,16},{1,13},{... | collective-permute-start | bytes 196616 | tf_op jit(solution)/shard_map/ppermute | solution.py:303
  79.5 2.9 %collective-permute-start.28 = (f32[32,512]{1,0:T(8,128)S(1)}, f32[32,512]{1,0:T(8,128)S(1)}, u32[]{:S(2)}, u32[]{:S(2)}) collective-permute-start(f32[32,512]{1,0:T(8,128)S(1)} %add.23.own_ref), channel_id=1, source_target_pairs={{0,16},{4,20},{8,24},{12,28},{16,0},{20,4},{24,8},{28,12},{1,17},{... | collective-permute-start | bytes 196616 | tf_op jit(solution)/shard_map/ppermute | solution.py:303
  82.5 2.9 %inverse_factor.5.lower_ref = f32[32,32]{1,0:T(8,128)S(1)} custom-call(f32[32,128]{1,0:T(8,128)S(1)} %add.21.before_ref.own_ref, f32[32,128]{1,0:T(8,128)S(1)} %collective-permute-done.29.got_ref), custom_call_target="tpu_custom_call" | custom-call | flops 17179869184 | tf_op jit(solution)/shard_map/inverse_factor/pallas_call | solution.py:28
  86.4 2.1 %collective-permute-start.32 = (f32[32,512]{1,0:T(8,128)S(1)}, f32[32,512]{1,0:T(8,128)S(1)}, u32[]{:S(2)}, u32[]{:S(2)}) collective-permute-start(f32[32,512]{1,0:T(8,128)S(1)} %total.6.chunk_ref.refs_0_), channel_id=1, source_target_pairs={{0,8},{4,12},{8,0},{12,4},{16,24},{20,28},{24,16},{28,20},{1,9},{5... | collective-permute-start | bytes 196616 | tf_op jit(solution)/shard_map/ppermute | solution.py:303
  94.9 1.6 %collective-permute-start.34 = (f32[32,768]{1,0:T(8,128)S(1)}, f32[32,768]{1,0:T(8,128)S(1)}, u32[]{:S(2)}, u32[]{:S(2)}) collective-permute-start(f32[32,768]{1,0:T(8,128)S(1)} %add.24.own_ref), channel_id=1, source_target_pairs={{0,2},{1,3},{2,0},{3,1},{4,6},{5,7},{6,4},{7,5},{8,10},{9,11},{10,... | collective-permute-start | bytes 294920 | tf_op jit(solution)/shard_map/ppermute | solution.py:303
  98.0 1.9 %collective-permute-done.34.got_ref = f32[32,768]{1,0:T(8,128)S(1)} collective-permute-done((f32[32,768]{1,0:T(8,128)S(1)}, f32[32,768]{1,0:T(8,128)S(1)}, u32[]{:S(2)}, u32[]{:S(2)}) %collective-permute-start.34) | collective-permute-done | bytes 98336 | tf_op jit(solution)/shard_map/ppermute | solution.py:303
  103.4 2.0 %collective-permute-start.39 = (f32[32,512]{1,0:T(8,128)S(1)}, f32[32,512]{1,0:T(8,128)S(1)}, u32[]{:S(2)}, u32[]{:S(2)}) collective-permute-start(f32[32,512]{1,0:T(8,128)S(1)} %get-tuple-element.69), channel_id=1, source_target_pairs={{0,8},{4,12},{8,0},{12,4},{16,24},{20,28},{24,16},{28,20},{1,9},{5... | collective-permute-start | bytes 196616 | tf_op jit(solution)/shard_map/ppermute | solution.py:303
  107.7 2.3 %collective-permute-start.40 = (f32[32,512]{1,0:T(8,128)S(1)}, f32[32,512]{1,0:T(8,128)S(1)}, u32[]{:S(2)}, u32[]{:S(2)}) collective-permute-start(f32[32,512]{1,0:T(8,128)S(1)} %add.27.own_ref), channel_id=1, source_target_pairs={{0,16},{4,20},{8,24},{12,28},{16,0},{20,4},{24,8},{28,12},{1,17},{... | collective-permute-start | bytes 196616 | tf_op jit(solution)/shard_map/ppermute | solution.py:303
  110.0 2.9 %inverse_factor.6.lower_ref = f32[32,32]{1,0:T(8,128)S(1)} custom-call(f32[32,128]{1,0:T(8,128)S(1)} %add.25.before_ref.own_ref, f32[32,128]{1,0:T(8,128)S(1)} %collective-permute-done.41.got_ref), custom_call_target="tpu_custom_call" | custom-call | flops 17179869184 | tf_op jit(solution)/shard_map/inverse_factor/pallas_call | solution.py:28
  113.1 2.1 %collective-permute-start.42 = (f32[32,512]{1,0:T(8,128)S(1)}, f32[32,512]{1,0:T(8,128)S(1)}, u32[]{:S(2)}, u32[]{:S(2)}) collective-permute-start(f32[32,512]{1,0:T(8,128)S(1)} %total.7.chunk_ref.refs_0_), channel_id=1, source_target_pairs={{0,12},{4,8},{8,4},{12,0},{16,28},{20,24},{24,20},{28,16},{1,13},{... | collective-permute-start | bytes 196616 | tf_op jit(solution)/shard_map/ppermute | solution.py:303
  120.4 1.5 %projection.1.own_ref = f32[32,1536]{1,0:T(8,128)S(1)} custom-call(f32[32,512]{1,0:T(8,128)S(1)} %collective-permute-done.42.chunk_ref.refs_1_.chunk3, f32[32,512]{1,0:T(8,128)S(1)} %collective-permute-done.43.refs_2_.chunk1, f32[32,512]{1,0:T(8,128)S(1)} %collective-permute-done.44.refs_3_.chunk2, ...), custom_call_target="tpu_custom_call" | custom-call | tf_op jit(solution)/shard_map/projection/pallas_call | solution.py:28
  125.7 1.6 %collective-permute-done.48.got_ref = f32[32,128]{1,0:T(8,128)S(1)} collective-permute-done((f32[32,128]{1,0:T(8,128)S(1)}, f32[32,128]{1,0:T(8,128)S(1)}, u32[]{:S(2)}, u32[]{:S(2)}) %collective-permute-start.48) | collective-permute-done | bytes 16416 | tf_op jit(solution)/shard_map/ppermute | solution.py:303
  127.3 2.9 %inverse_factor.7.lower_ref = f32[32,32]{1,0:T(8,128)S(1)} custom-call(f32[32,128]{1,0:T(8,128)S(1)} %add.28.before_ref.own_ref, f32[32,128]{1,0:T(8,128)S(1)} %collective-permute-done.48.got_ref), custom_call_target="tpu_custom_call" | custom-call | flops 17179869184 | tf_op jit(solution)/shard_map/inverse_factor/pallas_call | solution.py:28
  (126 shorter events, 58.0 us)
Async XLA Ops:
  7.4 6.2 %collective-permute-start.1 = (bf16[32,1664]{1,0:T(8,128)(2,1)S(1)}, bf16[32,1664]{1,0:T(8,128)(2,1)S(1)}, u32[]{:S(2)}, u32[]{:S(2)}) collective-permute-start(bf16[32,1664]{1,0:T(8,128)(2,1)S(1)} %first_part.1.own_ref), channel_id=1, source_target_pairs={{0,2},{1,3},{2,0},{3,1},{4,6},{5,7},{6,4},{7,5},{8,10},{9,11},{10,... | collective-permute-start | bytes 319496 | tf_op jit(solution)/shard_map/ppermute | solution.py:303
  14.5 5.5 %collective-permute-start.2 = (f32[40,512]{1,0:T(8,128)S(1)}, f32[40,512]{1,0:T(8,128)S(1)}, u32[]{:S(2)}, u32[]{:S(2)}) collective-permute-start(f32[40,512]{1,0:T(8,128)S(1)} %get-tuple-element.40), channel_id=1, source_target_pairs={{0,12},{4,8},{8,4},{12,0},{16,28},{20,24},{24,20},{28,16},{1,13},{... | collective-permute-start | bytes 245768 | tf_op jit(solution)/shard_map/ppermute | solution.py:303
  17.4 4.4 %collective-permute-start.3 = (f32[40,512]{1,0:T(8,128)S(1)}, f32[40,512]{1,0:T(8,128)S(1)}, u32[]{:S(2)}, u32[]{:S(2)}) collective-permute-start(f32[40,512]{1,0:T(8,128)S(1)} %get-tuple-element.41), channel_id=1, source_target_pairs={{0,4},{4,0},{8,12},{12,8},{16,20},{20,16},{24,28},{28,24},{1,5},{5... | collective-permute-start | bytes 245768 | tf_op jit(solution)/shard_map/ppermute | solution.py:303
  17.9 4.4 %collective-permute-start.4 = (f32[40,512]{1,0:T(8,128)S(1)}, f32[40,512]{1,0:T(8,128)S(1)}, u32[]{:S(2)}, u32[]{:S(2)}) collective-permute-start(f32[40,512]{1,0:T(8,128)S(1)} %get-tuple-element.42), channel_id=1, source_target_pairs={{0,8},{4,12},{8,0},{12,4},{16,24},{20,28},{24,16},{28,20},{1,9},{5... | collective-permute-start | bytes 245768 | tf_op jit(solution)/shard_map/ppermute | solution.py:303
  22.4 6.3 %collective-permute-start.5 = (f32[40,512]{1,0:T(8,128)S(1)}, f32[40,512]{1,0:T(8,128)S(1)}, u32[]{:S(2)}, u32[]{:S(2)}) collective-permute-start(f32[40,512]{1,0:T(8,128)S(1)} %add.15.own_ref), channel_id=1, source_target_pairs={{0,16},{4,20},{8,24},{12,28},{16,0},{20,4},{24,8},{28,12},{1,17},{... | collective-permute-start | bytes 245768 | tf_op jit(solution)/shard_map/ppermute | solution.py:303
  28.7 5.3 %collective-permute-start.6 = (f32[40,512]{1,0:T(8,128)S(1)}, f32[40,512]{1,0:T(8,128)S(1)}, u32[]{:S(2)}, u32[]{:S(2)}) collective-permute-start(f32[40,512]{1,0:T(8,128)S(1)} %total.4.chunk_ref.mean_ref.refs_0_), channel_id=1, source_target_pairs={{0,12},{4,8},{8,4},{12,0},{16,28},{20,24},{24,20},{28,16},{1,13},{... | collective-permute-start | bytes 245768 | tf_op jit(solution)/shard_map/ppermute | solution.py:303
  29.3 5.6 %collective-permute-start.8 = (f32[40,512]{1,0:T(8,128)S(1)}, f32[40,512]{1,0:T(8,128)S(1)}, u32[]{:S(2)}, u32[]{:S(2)}) collective-permute-start(f32[40,512]{1,0:T(8,128)S(1)} %total.4.chunk_ref.mean_ref.refs_0_), channel_id=1, source_target_pairs={{0,8},{4,12},{8,0},{12,4},{16,24},{20,28},{24,16},{28,20},{1,9},{5... | collective-permute-start | bytes 245768 | tf_op jit(solution)/shard_map/ppermute | solution.py:303
  31.6 4.4 %collective-permute-start.7 = (f32[40,512]{1,0:T(8,128)S(1)}, f32[40,512]{1,0:T(8,128)S(1)}, u32[]{:S(2)}, u32[]{:S(2)}) collective-permute-start(f32[40,512]{1,0:T(8,128)S(1)} %total.4.chunk_ref.mean_ref.refs_0_), channel_id=1, source_target_pairs={{0,4},{4,0},{8,12},{12,8},{16,20},{20,16},{24,28},{28,24},{1,5},{5... | collective-permute-start | bytes 245768 | tf_op jit(solution)/shard_map/ppermute | solution.py:303
  38.2 4.9 %collective-permute-start.10 = (f32[32,768]{1,0:T(8,128)S(1)}, f32[32,768]{1,0:T(8,128)S(1)}, u32[]{:S(2)}, u32[]{:S(2)}) collective-permute-start(f32[32,768]{1,0:T(8,128)S(1)} %add.16.own_ref), channel_id=1, source_target_pairs={{0,2},{1,3},{2,0},{3,1},{4,6},{5,7},{6,4},{7,5},{8,10},{9,11},{10,... | collective-permute-start | bytes 294920 | tf_op jit(solution)/shard_map/ppermute | solution.py:303
  45.1 5.8 %collective-permute-start.13 = (f32[32,512]{1,0:T(8,128)S(1)}, f32[32,512]{1,0:T(8,128)S(1)}, u32[]{:S(2)}, u32[]{:S(2)}) collective-permute-start(f32[32,512]{1,0:T(8,128)S(1)} %get-tuple-element.49), channel_id=1, source_target_pairs={{0,12},{4,8},{8,4},{12,0},{16,28},{20,24},{24,20},{28,16},{1,13},{... | collective-permute-start | bytes 196616 | tf_op jit(solution)/shard_map/ppermute | solution.py:303
  45.2 5.7 %collective-permute-start.14 = (f32[32,512]{1,0:T(8,128)S(1)}, f32[32,512]{1,0:T(8,128)S(1)}, u32[]{:S(2)}, u32[]{:S(2)}) collective-permute-start(f32[32,512]{1,0:T(8,128)S(1)} %get-tuple-element.50), channel_id=1, source_target_pairs={{0,4},{4,0},{8,12},{12,8},{16,20},{20,16},{24,28},{28,24},{1,5},{5... | collective-permute-start | bytes 196616 | tf_op jit(solution)/shard_map/ppermute | solution.py:303
  46.6 4.3 %collective-permute-start.15 = (f32[32,512]{1,0:T(8,128)S(1)}, f32[32,512]{1,0:T(8,128)S(1)}, u32[]{:S(2)}, u32[]{:S(2)}) collective-permute-start(f32[32,512]{1,0:T(8,128)S(1)} %get-tuple-element.51), channel_id=1, source_target_pairs={{0,8},{4,12},{8,0},{12,4},{16,24},{20,28},{24,16},{28,20},{1,9},{5... | collective-permute-start | bytes 196616 | tf_op jit(solution)/shard_map/ppermute | solution.py:303
  48.6 4.8 %collective-permute-start.17 = (f32[32,128]{1,0:T(8,128)S(1)}, f32[32,128]{1,0:T(8,128)S(1)}, u32[]{:S(2)}, u32[]{:S(2)}) collective-permute-start(f32[32,128]{1,0:T(8,128)S(1)} %add.17.before_ref.own_ref), channel_id=1, source_target_pairs={{0,2},{1,3},{2,0},{3,1},{4,6},{5,7},{6,4},{7,5},{8,10},{9,11},{10,... | collective-permute-start | bytes 49160 | tf_op jit(solution)/shard_map/ppermute | solution.py:303
  50.9 5.4 %collective-permute-start.16 = (f32[32,512]{1,0:T(8,128)S(1)}, f32[32,512]{1,0:T(8,128)S(1)}, u32[]{:S(2)}, u32[]{:S(2)}) collective-permute-start(f32[32,512]{1,0:T(8,128)S(1)} %add.19.own_ref), channel_id=1, source_target_pairs={{0,16},{4,20},{8,24},{12,28},{16,0},{20,4},{24,8},{28,12},{1,17},{... | collective-permute-start | bytes 196616 | tf_op jit(solution)/shard_map/ppermute | solution.py:303
  56.5 5.3 %collective-permute-start.18 = (f32[32,512]{1,0:T(8,128)S(1)}, f32[32,512]{1,0:T(8,128)S(1)}, u32[]{:S(2)}, u32[]{:S(2)}) collective-permute-start(f32[32,512]{1,0:T(8,128)S(1)} %total.5.chunk_ref.refs_0_), channel_id=1, source_target_pairs={{0,12},{4,8},{8,4},{12,0},{16,28},{20,24},{24,20},{28,16},{1,13},{... | collective-permute-start | bytes 196616 | tf_op jit(solution)/shard_map/ppermute | solution.py:303
  59.3 4.3 %collective-permute-start.19 = (f32[32,512]{1,0:T(8,128)S(1)}, f32[32,512]{1,0:T(8,128)S(1)}, u32[]{:S(2)}, u32[]{:S(2)}) collective-permute-start(f32[32,512]{1,0:T(8,128)S(1)} %total.5.chunk_ref.refs_0_), channel_id=1, source_target_pairs={{0,4},{4,0},{8,12},{12,8},{16,20},{20,16},{24,28},{28,24},{1,5},{5... | collective-permute-start | bytes 196616 | tf_op jit(solution)/shard_map/ppermute | solution.py:303
  65.7 4.9 %collective-permute-start.22 = (f32[32,768]{1,0:T(8,128)S(1)}, f32[32,768]{1,0:T(8,128)S(1)}, u32[]{:S(2)}, u32[]{:S(2)}) collective-permute-start(f32[32,768]{1,0:T(8,128)S(1)} %add.20.own_ref), channel_id=1, source_target_pairs={{0,2},{1,3},{2,0},{3,1},{4,6},{5,7},{6,4},{7,5},{8,10},{9,11},{10,... | collective-permute-start | bytes 294920 | tf_op jit(solution)/shard_map/ppermute | solution.py:303
  72.6 5.3 %collective-permute-start.25 = (f32[32,512]{1,0:T(8,128)S(1)}, f32[32,512]{1,0:T(8,128)S(1)}, u32[]{:S(2)}, u32[]{:S(2)}) collective-permute-start(f32[32,512]{1,0:T(8,128)S(1)} %get-tuple-element.58), channel_id=1, source_target_pairs={{0,12},{4,8},{8,4},{12,0},{16,28},{20,24},{24,20},{28,16},{1,13},{... | collective-permute-start | bytes 196616 | tf_op jit(solution)/shard_map/ppermute | solution.py:303
  74.8 4.4 %collective-permute-start.26 = (f32[32,512]{1,0:T(8,128)S(1)}, f32[32,512]{1,0:T(8,128)S(1)}, u32[]{:S(2)}, u32[]{:S(2)}) collective-permute-start(f32[32,512]{1,0:T(8,128)S(1)} %get-tuple-element.59), channel_id=1, source_target_pairs={{0,4},{4,0},{8,12},{12,8},{16,20},{20,16},{24,28},{28,24},{1,5},{5... | collective-permute-start | bytes 196616 | tf_op jit(solution)/shard_map/ppermute | solution.py:303
  76.1 6.3 %collective-permute-start.29 = (f32[32,128]{1,0:T(8,128)S(1)}, f32[32,128]{1,0:T(8,128)S(1)}, u32[]{:S(2)}, u32[]{:S(2)}) collective-permute-start(f32[32,128]{1,0:T(8,128)S(1)} %add.21.before_ref.own_ref), channel_id=1, source_target_pairs={{0,2},{1,3},{2,0},{3,1},{4,6},{5,7},{6,4},{7,5},{8,10},{9,11},{10,... | collective-permute-start | bytes 49160 | tf_op jit(solution)/shard_map/ppermute | solution.py:303
  79.5 5.9 %collective-permute-start.28 = (f32[32,512]{1,0:T(8,128)S(1)}, f32[32,512]{1,0:T(8,128)S(1)}, u32[]{:S(2)}, u32[]{:S(2)}) collective-permute-start(f32[32,512]{1,0:T(8,128)S(1)} %add.23.own_ref), channel_id=1, source_target_pairs={{0,16},{4,20},{8,24},{12,28},{16,0},{20,4},{24,8},{28,12},{1,17},{... | collective-permute-start | bytes 196616 | tf_op jit(solution)/shard_map/ppermute | solution.py:303
  85.6 5.2 %collective-permute-start.30 = (f32[32,512]{1,0:T(8,128)S(1)}, f32[32,512]{1,0:T(8,128)S(1)}, u32[]{:S(2)}, u32[]{:S(2)}) collective-permute-start(f32[32,512]{1,0:T(8,128)S(1)} %total.6.chunk_ref.refs_0_), channel_id=1, source_target_pairs={{0,12},{4,8},{8,4},{12,0},{16,28},{20,24},{24,20},{28,16},{1,13},{... | collective-permute-start | bytes 196616 | tf_op jit(solution)/shard_map/ppermute | solution.py:303
  86.4 5.0 %collective-permute-start.32 = (f32[32,512]{1,0:T(8,128)S(1)}, f32[32,512]{1,0:T(8,128)S(1)}, u32[]{:S(2)}, u32[]{:S(2)}) collective-permute-start(f32[32,512]{1,0:T(8,128)S(1)} %total.6.chunk_ref.refs_0_), channel_id=1, source_target_pairs={{0,8},{4,12},{8,0},{12,4},{16,24},{20,28},{24,16},{28,20},{1,9},{5... | collective-permute-start | bytes 196616 | tf_op jit(solution)/shard_map/ppermute | solution.py:303
  94.9 5.0 %collective-permute-start.34 = (f32[32,768]{1,0:T(8,128)S(1)}, f32[32,768]{1,0:T(8,128)S(1)}, u32[]{:S(2)}, u32[]{:S(2)}) collective-permute-start(f32[32,768]{1,0:T(8,128)S(1)} %add.24.own_ref), channel_id=1, source_target_pairs={{0,2},{1,3},{2,0},{3,1},{4,6},{5,7},{6,4},{7,5},{8,10},{9,11},{10,... | collective-permute-start | bytes 294920 | tf_op jit(solution)/shard_map/ppermute | solution.py:303
  101.8 5.8 %collective-permute-start.37 = (f32[32,512]{1,0:T(8,128)S(1)}, f32[32,512]{1,0:T(8,128)S(1)}, u32[]{:S(2)}, u32[]{:S(2)}) collective-permute-start(f32[32,512]{1,0:T(8,128)S(1)} %get-tuple-element.67), channel_id=1, source_target_pairs={{0,12},{4,8},{8,4},{12,0},{16,28},{20,24},{24,20},{28,16},{1,13},{... | collective-permute-start | bytes 196616 | tf_op jit(solution)/shard_map/ppermute | solution.py:303
  102.4 5.3 %collective-permute-start.38 = (f32[32,512]{1,0:T(8,128)S(1)}, f32[32,512]{1,0:T(8,128)S(1)}, u32[]{:S(2)}, u32[]{:S(2)}) collective-permute-start(f32[32,512]{1,0:T(8,128)S(1)} %get-tuple-element.68), channel_id=1, source_target_pairs={{0,4},{4,0},{8,12},{12,8},{16,20},{20,16},{24,28},{28,24},{1,5},{5... | collective-permute-start | bytes 196616 | tf_op jit(solution)/shard_map/ppermute | solution.py:303
  103.4 4.3 %collective-permute-start.39 = (f32[32,512]{1,0:T(8,128)S(1)}, f32[32,512]{1,0:T(8,128)S(1)}, u32[]{:S(2)}, u32[]{:S(2)}) collective-permute-start(f32[32,512]{1,0:T(8,128)S(1)} %get-tuple-element.69), channel_id=1, source_target_pairs={{0,8},{4,12},{8,0},{12,4},{16,24},{20,28},{24,16},{28,20},{1,9},{5... | collective-permute-start | bytes 196616 | tf_op jit(solution)/shard_map/ppermute | solution.py:303
  105.4 4.6 %collective-permute-start.41 = (f32[32,128]{1,0:T(8,128)S(1)}, f32[32,128]{1,0:T(8,128)S(1)}, u32[]{:S(2)}, u32[]{:S(2)}) collective-permute-start(f32[32,128]{1,0:T(8,128)S(1)} %add.25.before_ref.own_ref), channel_id=1, source_target_pairs={{0,2},{1,3},{2,0},{3,1},{4,6},{5,7},{6,4},{7,5},{8,10},{9,11},{10,... | collective-permute-start | bytes 49160 | tf_op jit(solution)/shard_map/ppermute | solution.py:303
  107.7 5.2 %collective-permute-start.40 = (f32[32,512]{1,0:T(8,128)S(1)}, f32[32,512]{1,0:T(8,128)S(1)}, u32[]{:S(2)}, u32[]{:S(2)}) collective-permute-start(f32[32,512]{1,0:T(8,128)S(1)} %add.27.own_ref), channel_id=1, source_target_pairs={{0,16},{4,20},{8,24},{12,28},{16,0},{20,4},{24,8},{28,12},{1,17},{... | collective-permute-start | bytes 196616 | tf_op jit(solution)/shard_map/ppermute | solution.py:303
  113.1 5.2 %collective-permute-start.42 = (f32[32,512]{1,0:T(8,128)S(1)}, f32[32,512]{1,0:T(8,128)S(1)}, u32[]{:S(2)}, u32[]{:S(2)}) collective-permute-start(f32[32,512]{1,0:T(8,128)S(1)} %total.7.chunk_ref.refs_0_), channel_id=1, source_target_pairs={{0,12},{4,8},{8,4},{12,0},{16,28},{20,24},{24,20},{28,16},{1,13},{... | collective-permute-start | bytes 196616 | tf_op jit(solution)/shard_map/ppermute | solution.py:303
  115.8 4.3 %collective-permute-start.43 = (f32[32,512]{1,0:T(8,128)S(1)}, f32[32,512]{1,0:T(8,128)S(1)}, u32[]{:S(2)}, u32[]{:S(2)}) collective-permute-start(f32[32,512]{1,0:T(8,128)S(1)} %total.7.chunk_ref.refs_0_), channel_id=1, source_target_pairs={{0,4},{4,0},{8,12},{12,8},{16,20},{20,16},{24,28},{28,24},{1,5},{5... | collective-permute-start | bytes 196616 | tf_op jit(solution)/shard_map/ppermute | solution.py:303
  125.1 5.1 %collective-permute-start.47 = (bf16[32,1536]{1,0:T(8,128)(2,1)S(1)}, bf16[32,1536]{1,0:T(8,128)(2,1)S(1)}, u32[]{:S(2)}, u32[]{:S(2)}) collective-permute-start(bf16[32,1536]{1,0:T(8,128)(2,1)S(1)} %add.29.own_ref), channel_id=1, source_target_pairs={{0,2},{1,3},{2,0},{3,1},{4,6},{5,7},{6,4},{7,5},{8,10},{9,11},{10,... | collective-permute-start | bytes 294920 | tf_op jit(solution)/shard_map/ppermute | solution.py:303
  (18 other events, 40.7 us)

commit v6 on v5

v6 whole, which is shorter than its diff:
```python
import functools

import jax
import jax.numpy as jnp
from jax import lax
from jax.experimental import pallas as pl
from jax.experimental.pallas import tpu as pltpu
from jax.sharding import PartitionSpec as P

ITERS = 4
PEERS = 4
LANES = 128
EXTRA = 8
ORDER = (0, 3, 2, 1)
TERMS = 3
LONG = pl.CostEstimate(flops=2**34, bytes_accessed=0, transcendentals=0)
SHORT = pl.CostEstimate(flops=2**29, bytes_accessed=0, transcendentals=0)
HIGHEST = lax.Precision.HIGHEST
VMEM = pl.BlockSpec(memory_space=pltpu.VMEM)
HBM = pl.BlockSpec(memory_space=pltpu.HBM)
F32 = jnp.float32
BF16 = jnp.bfloat16


def call(kernel, outputs, name, scratch=(), in_specs=None, aliases=None, mebibytes=20, cost=None):
    def run(*args):
        specs = in_specs or [VMEM] * len(args)
        return pl.pallas_call(
            kernel,
            out_shape=[jax.ShapeDtypeStruct(shape, dtype) for shape, dtype in outputs],
            in_specs=specs,
            out_specs=[VMEM] * len(outputs),
            scratch_shapes=scratch,
            compiler_params=pltpu.CompilerParams(vmem_limit_bytes=mebibytes * 2**20),
            cost_estimate=cost,
            input_output_aliases=aliases or {},
            name=name,
        )(*args)

    return run


def split(value, terms=2):
    parts = []
    for _ in range(terms):
        parts.append(value.astype(BF16))
        value = value - parts[-1].astype(F32)
    return jnp.concatenate(parts, axis=0)


def join(value, terms=2):
    height = value.shape[0] // terms
    result = value[-height:]
    for term in range(terms - 2, -1, -1):
        result = value[term * height : (term + 1) * height] + result
    return result


def total(*refs):
    terms = [ref[...].astype(F32) for ref in refs]
    while len(terms) > 1:
        terms = [sum(terms[i + 1 : i + 2], terms[i]) for i in range(0, len(terms), 2)]
    return terms[0]


def contract_last(left, right, precision=None):
    return lax.dot_general(
        left, right, (((1,), (1,)), ((), ())), preferred_element_type=F32, precision=precision
    )


def position():
    return lax.rem(lax.axis_index("tok"), PEERS)


def diagonal(n):
    return lax.broadcasted_iota(jnp.int32, (n, n), 0) == lax.broadcasted_iota(jnp.int32, (n, n), 1)


def core():
    return lax.rem(lax.axis_index("feat"), 2)


def aligned(index, size):
    return pl.ds(pl.multiple_of(index * size, size), size)


def fetch_kernel(rows_hbm, rows_ref, sem):
    place = aligned(1 - core(), rows_ref.shape[0] // 2)
    copy = pltpu.make_async_copy(rows_hbm.at[place, :], rows_ref.at[place, :], sem)
    copy.start()
    copy.wait()


def first_sent_kernel(basis_ref, rows_hbm, ready_ref, out_ref, rows_ref, sem):
    half = out_ref.shape[1]
    place = aligned(core(), half)
    copy = pltpu.make_async_copy(rows_hbm.at[place, :], rows_ref.at[place, :], sem)
    copy.start()
    rows = rows_ref[aligned(1 - core(), half), :]
    out_ref[...] = join(contract_last(split(basis_ref[...]), rows))
    copy.wait()


def first_kept_kernel(basis_ref, rows_ref, out_ref):
    rows = rows_ref[aligned(core(), out_ref.shape[1]), :]
    out_ref[...] = join(contract_last(split(basis_ref[...]), rows))


def projection_kernel(part, half, chunk_ref, mean_ref, rows_ref, *refs):
    out_ref = refs[-1]
    n, tokens = out_ref.shape
    place = {"all": 0, "kept": core(), "sent": 1 - core()}[half]
    place = aligned(place, tokens) if half != "all" else slice(None)
    chunk = chunk_ref[:n, :]
    shift = jnp.sum(chunk * mean_ref[n : n + 1, :], axis=1, keepdims=True)
    rows = rows_ref[place, aligned(position() ^ part, chunk.shape[1])]
    value = join(contract_last(split(chunk), rows)) - shift
    out_ref[...] = value if part == ORDER[0] else refs[0][:, place] + value


def gram_kernel(*refs):
    *refs, out_ref = refs
    n = out_ref.shape[0]
    chunks = {part: ref[:n, :] for part, ref in zip(ORDER, refs)}
    parts = [contract_last(chunks[part], chunks[part], HIGHEST) for part in range(PEERS)]
    out_ref[...] = jnp.zeros(out_ref.shape, F32)
    out_ref[:, :n] = (parts[0] + parts[1]) + (parts[2] + parts[3])


def inverse_factor_kernel(own_ref, got_ref, out_ref):
    n = own_ref.shape[0]
    gram = (own_ref[...] + got_ref[...])[:, :n]
    work = jnp.concatenate([gram, diagonal(n).astype(F32)], axis=1)
    index = lax.broadcasted_iota(jnp.int32, (n, 1), 0)
    scale = jnp.zeros((n, 1), F32)
    for k in range(n):
        pivot = work[k : k + 1, k : k + 1]
        factor = jnp.where(index > k, work[:, k : k + 1] / pivot, 0.0)
        scale = jnp.where(index == k, lax.rsqrt(pivot), scale)
        work = work - factor * work[k : k + 1, :]
    out_ref[...] = work[:, n:] * scale


def first_total_kernel(rows_in_all, own_ref, got_ref, out_ref):
    n = own_ref.shape[0] - EXTRA
    value = own_ref[...] + got_ref[...]
    mean = value[n : n + 1] / rows_in_all
    counts = jnp.where(diagonal(n), value[n + 1 : n + 2, :n], 0.0)
    counts = jnp.sum(counts, axis=1, keepdims=True)
    out_ref[:n, :] = value[:n] - counts * mean
    out_ref[n:, :] = jnp.broadcast_to(mean, (EXTRA, mean.shape[1]))


def weights_of(first, projected_ref):
    projected = projected_ref[...]
    centre = jnp.zeros((projected.shape[0], 1), F32)
    if first:
        centre = jnp.sum(projected, axis=1, keepdims=True) / projected.shape[1]
    weights = split(projected - centre if first else projected, TERMS)
    counts = join(jnp.sum(weights.astype(F32), axis=1, keepdims=True), TERMS)
    if first:
        counts = counts + centre * projected.shape[1]
        weights = jnp.concatenate([weights, jnp.ones((2 * EXTRA, projected.shape[1]), BF16)], axis=0)
    return weights, counts, centre


def image_term(first, weights, counts, centre, rows, mean_ref):
    n = counts.shape[0]
    term = jnp.dot(weights, rows, preferred_element_type=F32)
    value = join(term[: TERMS * n], TERMS)
    if not first:
        return value - counts * mean_ref[n : n + 1, :]
    sums = term[TERMS * n : TERMS * n + 1]
    counts = jnp.sum(jnp.where(diagonal(n), counts, 0.0), axis=0, keepdims=True)
    counts = jnp.concatenate([counts, jnp.zeros((1, sums.shape[1] - n), F32)], axis=1)
    below = jnp.zeros((EXTRA - 2, sums.shape[1]), F32)
    return jnp.concatenate([value + centre * sums, sums, counts, below], axis=0)


def half_image_kernel(first, own_ref, rows_ref, *refs):
    means, outs = ([None] * PEERS if first else refs[:PEERS]), refs[-PEERS:]
    tokens = aligned(core(), own_ref.shape[1])
    sides = weights_of(first, own_ref)
    for part, mean_ref, out_ref in zip(ORDER, means, outs):
        rows = rows_ref[tokens, aligned(position() ^ part, out_ref.shape[1])]
        out_ref[...] = image_term(first, *sides, rows, mean_ref)


def image_kernel(first, other_ref, rows_ref, *refs):
    *refs, weights_ref, side_ref = refs
    peers = PEERS - 1
    means, halves, outs = ([None] * peers if first else refs[:peers]), refs[-2 * peers : -peers], refs[-peers:]
    tokens = aligned(1 - core(), other_ref.shape[1])
    weights, counts, centre = weights_of(first, other_ref)
    for part, mean_ref, half_ref, out_ref in zip(ORDER[1:], means, halves, outs):
        rows = rows_ref[tokens, aligned(position() ^ part, out_ref.shape[1])]
        out_ref[...] = half_ref[...] + image_term(first, weights, counts, centre, rows, mean_ref)
    weights_ref[...] = weights
    side_ref[...] = jnp.broadcast_to(counts, side_ref.shape)
    side_ref[:, 1:2] = centre


def own_image_kernel(first, weights_ref, side_ref, rows_ref, half_ref, *refs):
    mean_ref, out_ref = (None if first else refs[0]), refs[-1]
    tokens = aligned(1 - core(), weights_ref.shape[1])
    rows = rows_ref[tokens, aligned(position(), out_ref.shape[1])]
    sides = weights_ref[...], side_ref[:, :1], side_ref[:, 1:2]
    out_ref[...] = half_ref[...] + image_term(first, *sides, rows, mean_ref)


def assemble_kernel(*refs):
    *chunks, out_ref = refs
    n, width = out_ref.shape[0], chunks[0].shape[1]
    for part, chunk in zip(ORDER, chunks):
        place = aligned(position() ^ part, width)
        out_ref[:, place] = chunk[:n, :]


def last_kernel(own_ref, got_ref, lower_ref, image_ref, scores_ref, basis_ref):
    n, lower = lower_ref.shape[0], lower_ref[...]
    basis_ref[...] = jnp.dot(lower, image_ref[...], preferred_element_type=F32, precision=HIGHEST)
    projected = total(own_ref, got_ref)
    projected = jnp.dot(lower, projected, preferred_element_type=F32, precision=HIGHEST)
    scores_ref[...] = jnp.sum(projected * projected, axis=0) / n


def normalised_total_kernel(own_ref, got_ref, lower_ref, out_ref):
    value = own_ref[...] + got_ref[...]
    out_ref[...] = jnp.dot(lower_ref[...], value, preferred_element_type=F32, precision=HIGHEST)


def ordered_add_kernel(own_ref, got_ref, before_ref, out_ref):
    out_ref[...] = total(own_ref, got_ref).astype(out_ref.dtype)


def add_kernel(*refs):
    refs[-1][...] = total(*refs[:-1]).astype(refs[-1].dtype)


def add(*terms, dtype=F32):
    return call(add_kernel, [(terms[0].shape, dtype)], "add")(*terms)[0]


def swap(value, axis, distance):
    size = lax.axis_size(axis)
    return lax.ppermute(value, axis, [(i, i ^ distance) for i in range(size)])


def distances(axis, start):
    step, size = start, lax.axis_size(axis)
    while step < size:
        yield step
        step *= 2


def share(value, axis):
    return [value] + [swap(value, axis, part) for part in ORDER[1:]]


def on_device(activations, start_basis):
    tokens, features = activations.shape
    n = start_basis.shape[0]
    width = features // PEERS
    rows_in_all = tokens * lax.axis_size("tok")
    last_feat = lax.axis_size("feat") // 2
    side = ((n, LANES), F32)
    half = ((n, tokens // 2), F32)
    whole = ((n, tokens), F32)

    fetched, sem = (activations.shape, BF16), [pltpu.SemaphoreType.DMA(())]
    rows = call(fetch_kernel, [fetched], "fetch", sem, in_specs=[HBM], mebibytes=46)(activations)[0]
    sent, rows = call(
        first_sent_kernel,
        [half, fetched],
        "sent_projection",
        sem,
        in_specs=[VMEM, HBM, VMEM],
        aliases={2: 1},
        mebibytes=46,
    )(start_basis, activations, rows)
    own = call(first_kept_kernel, [half], "kept_projection", cost=SHORT)(start_basis, rows)[0]
    for distance in distances("feat", 1):
        own = add(own, swap(sent if distance == 1 else own, "feat", distance))
    other = swap(own, "feat", 1)
    means, lower = [], []
    for step in range(ITERS):
        first, last = step == 0, step == ITERS - 1
        chunk = ((n + EXTRA if first else n, width), F32)
        weights = ((TERMS * n + 2 * EXTRA if first else TERMS * n, tokens // 2), BF16)
        kernel = functools.partial(half_image_kernel, first)
        kept, *halves = call(kernel, [chunk] * PEERS, "half_image", cost=SHORT)(own, rows, *means)
        kernel = functools.partial(image_kernel, first)
        *terms, weights, sums = call(kernel, [chunk] * (PEERS - 1) + [weights, side], "image")(
            other, rows, *means[1:], *halves
        )
        received = [swap(term, "tok", part) for part, term in zip(ORDER[1:], terms)]
        kernel = functools.partial(own_image_kernel, first)
        kept = call(kernel, [chunk], "own_image", cost=SHORT)(weights, sums, rows, kept, *means[:1])
        image = add(*kept, *received)
        *steps, last_step = distances("tok", PEERS)
        for distance in steps:
            image = add(image, swap(image, "tok", distance))
        kernel = functools.partial(first_total_kernel, rows_in_all) if first else normalised_total_kernel
        image = call(kernel, [chunk], "total")(image, swap(image, "tok", last_step), *lower)[0]
        images = share(image, "tok")
        means = means or images
        gram = call(gram_kernel, [side], "gram")(*images)[0]
        grams = (gram, swap(gram, "feat", 1))
        before = []
        for part, image, mean in zip(ORDER, images, means):
            operands = [image, mean, rows, *before]
            if part != ORDER[-1]:
                kernel = functools.partial(projection_kernel, part, "all")
                before = call(kernel, [whole], "projection", cost=SHORT)(*operands)
        if last:
            gram = add(*grams)
            kernel = functools.partial(projection_kernel, part, "all")
            own = call(kernel, [whole], "projection")(*operands, gram)[0]
            for distance in distances("feat", 1):
                terms = (own, swap(own, "feat", distance))
                if distance != last_feat:
                    narrow = ((n, tokens), BF16 if distance == last_feat // 2 else F32)
                    own = call(add_kernel, [narrow], "add")(*terms)[0]
            own, other = terms
            for distance in distances("feat", 2):
                grams = (gram, swap(gram, "feat", distance))
                gram = add(*grams)
        else:
            kernel = functools.partial(projection_kernel, part, "sent")
            sent = call(kernel, [half], "sent_projection")(*operands)[0]
            kernel = functools.partial(projection_kernel, part, "kept")
            own = call(kernel, [half], "kept_projection", cost=SHORT)(*operands)[0]
            for distance in distances("feat", 1):
                got = swap(sent if distance == 1 else own, "feat", distance)
                if distance > 1:
                    gram = add(*grams)
                    grams = (gram, swap(gram, "feat", distance))
                if distance == last_feat:
                    own = call(ordered_add_kernel, [half], "add")(own, got, gram)[0]
                else:
                    own = add(own, got)
            other = swap(own, "feat", 1)
        lower = call(inverse_factor_kernel, [((n, n), F32)], "inverse_factor", cost=LONG)(*grams)
    image = call(assemble_kernel, [((n, features), F32)], "assemble")(*images)[0]
    outputs = [((tokens,), F32), ((n, features), F32)]
    return tuple(call(last_kernel, outputs, "last")(own, other, *lower, image))


def solution(mesh):
    in_specs = (P("tok", "feat"), P(None, "feat"))
    out_specs = (P("tok"), P(None, "feat"))
    return jax.shard_map(
        on_device, mesh=mesh, in_specs=in_specs, out_specs=out_specs, check_vma=False
    )
```

time: 131 us -> 132 us (level)
    ppermute x49 -> x50, waiting for transfers between devices: 41.1 us -> 40 us  [swap(): return lax.ppermute(value, axis, [(i, i ^ distance) for i in range(size)])]
    pallas_call x58 -> x65, Pallas kernels: 34.7 us -> 35.7 us  [run(): pl.pallas_call(kernel, out_shape=[jax.ShapeDtypeStruct(shape, dtype) for...]
    ppermute x49 -> x50, starting transfers between devices: 54.6 us -> 54.8 us  [swap(): return lax.ppermute(value, axis, [(i, i ^ distance) for i in range(size)])]
  transfers between devices with their start and end apart: 49 -> 50, of which waited for: 37 -> 39; matrix products, arithmetic and copies ran while one was open for 0% -> 0% of each run, Pallas kernels for 16% -> 20%
where the time goes in v6:
time: 132 us; the launch traced here: 131 us
  starting transfers between devices  54.8 us (42%)
  waiting for transfers between devices  40 us (30%)
  Pallas kernels  35.7 us (27%)
    ppermute x50, starting transfers between devices, swap(): return lax.ppermute(value, axis, [(i, i ^ distance) for i in range(size)])  54.8 us
    ppermute x50, waiting for transfers between devices, swap(): return lax.ppermute(value, axis, [(i, i ^ distance) for i in range(size)])  40 us
    pallas_call x65, Pallas kernels, run(): pl.pallas_call(kernel, out_shape=[jax.ShapeDtypeStruct(shape, dtype) for...  35.7 us
  transfers between devices with their start and end apart: 50, of which 39 were waited for; matrix products, arithmetic and copies ran while one was open for 0% of the time, Pallas kernels for 20%

profile of v6, /device:TPU:0, one launch (start us, length us, event | category | flops | bytes accessed | tf_op | source)
XLA Modules:
  0.0 131.4 jit_solution(18294426468521812767)
XLA Ops:
  0.6 2.0 %fetch.1.ready_ref = bf16[1536,2048]{1,0:T(8,128)(2,1)S(1)} custom-call(bf16[1536,2048]{1,0:T(8,128)(2,1)} %rows_hbm.3), custom_call_target="tpu_custom_call" | custom-call | tf_op jit(solution)/shard_map/fetch/pallas_call | solution.py:28
  2.6 1.9 %sent_projection.4 = (f32[32,768]{1,0:T(8,128)S(1)}, bf16[1536,2048]{1,0:T(8,128)(2,1)S(1)}) custom-call(f32[32,2048]{1,0:T(8,128)S(1)} %copy-done, bf16[1536,2048]{1,0:T(8,128)(2,1)} %rows_hbm.3, bf16[1536,2048]{1,0:T(8,128)(2,1)S(1)} %fetch.1.ready_ref), custom_call_target="tpu_custom_call", output_to_operand_aliasing={{1}: (2, {})} | custom-call | tf_op jit(solution)/shard_map/sent_projection/pallas_call | solution.py:28
  6.1 2.8 %collective-permute-start.1 = (f32[32,768]{1,0:T(8,128)S(1)}, f32[32,768]{1,0:T(8,128)S(1)}, u32[]{:S(2)}, u32[]{:S(2)}) collective-permute-start(f32[32,768]{1,0:T(8,128)S(1)} %add.17.refs_0_), channel_id=1, source_target_pairs={{0,2},{1,3},{2,0},{3,1},{4,6},{5,7},{6,4},{7,5},{8,10},{9,11},{10,... | collective-permute-start | bytes 294920 | tf_op jit(solution)/shard_map/ppermute | solution.py:247
  8.9 3.3 %collective-permute-done.1.refs_1_ = f32[32,768]{1,0:T(8,128)S(1)} collective-permute-done((f32[32,768]{1,0:T(8,128)S(1)}, f32[32,768]{1,0:T(8,128)S(1)}, u32[]{:S(2)}, u32[]{:S(2)}) %collective-permute-start.1) | collective-permute-done | bytes 98336 | tf_op jit(solution)/shard_map/ppermute | solution.py:247
  14.1 2.8 %collective-permute-start.3 = (f32[40,512]{1,0:T(8,128)S(1)}, f32[40,512]{1,0:T(8,128)S(1)}, u32[]{:S(2)}, u32[]{:S(2)}) collective-permute-start(f32[40,512]{1,0:T(8,128)S(1)} %get-tuple-element.48), channel_id=1, source_target_pairs={{0,12},{4,8},{8,4},{12,0},{16,28},{20,24},{24,20},{28,16},{1,13},{... | collective-permute-start | bytes 245768 | tf_op jit(solution)/shard_map/ppermute | solution.py:247
  18.0 2.2 %collective-permute-done.3.refs_1_ = f32[40,512]{1,0:T(8,128)S(1)} collective-permute-done((f32[40,512]{1,0:T(8,128)S(1)}, f32[40,512]{1,0:T(8,128)S(1)}, u32[]{:S(2)}, u32[]{:S(2)}) %collective-permute-start.3) | collective-permute-done | bytes 81952 | tf_op jit(solution)/shard_map/ppermute | solution.py:247
  20.1 1.5 %collective-permute-done.4.refs_2_ = f32[40,512]{1,0:T(8,128)S(1)} collective-permute-done((f32[40,512]{1,0:T(8,128)S(1)}, f32[40,512]{1,0:T(8,128)S(1)}, u32[]{:S(2)}, u32[]{:S(2)}) %collective-permute-start.4) | collective-permute-done | bytes 81952 | tf_op jit(solution)/shard_map/ppermute | solution.py:247
  21.9 2.7 %collective-permute-start.6 = (f32[40,512]{1,0:T(8,128)S(1)}, f32[40,512]{1,0:T(8,128)S(1)}, u32[]{:S(2)}, u32[]{:S(2)}) collective-permute-start(f32[40,512]{1,0:T(8,128)S(1)} %add.19.own_ref), channel_id=1, source_target_pairs={{0,16},{4,20},{8,24},{12,28},{16,0},{20,4},{24,8},{28,12},{1,17},{... | collective-permute-start | bytes 245768 | tf_op jit(solution)/shard_map/ppermute | solution.py:247
  24.6 2.9 %collective-permute-done.6.got_ref = f32[40,512]{1,0:T(8,128)S(1)} collective-permute-done((f32[40,512]{1,0:T(8,128)S(1)}, f32[40,512]{1,0:T(8,128)S(1)}, u32[]{:S(2)}, u32[]{:S(2)}) %collective-permute-start.6) | collective-permute-done | bytes 81952 | tf_op jit(solution)/shard_map/ppermute | solution.py:247
  27.6 2.6 %collective-permute-start.9 = (f32[40,512]{1,0:T(8,128)S(1)}, f32[40,512]{1,0:T(8,128)S(1)}, u32[]{:S(2)}, u32[]{:S(2)}) collective-permute-start(f32[40,512]{1,0:T(8,128)S(1)} %total.4.chunk_ref.mean_ref.refs_0_), channel_id=1, source_target_pairs={{0,12},{4,8},{8,4},{12,0},{16,28},{20,24},{24,20},{28,16},{1,13},{... | collective-permute-start | bytes 245768 | tf_op jit(solution)/shard_map/ppermute | solution.py:247
  30.1 1.5 %collective-permute-start.8 = (f32[40,512]{1,0:T(8,128)S(1)}, f32[40,512]{1,0:T(8,128)S(1)}, u32[]{:S(2)}, u32[]{:S(2)}) collective-permute-start(f32[40,512]{1,0:T(8,128)S(1)} %total.4.chunk_ref.mean_ref.refs_0_), channel_id=1, source_target_pairs={{0,8},{4,12},{8,0},{12,4},{16,24},{20,28},{24,16},{28,20},{1,9},{5... | collective-permute-start | bytes 245768 | tf_op jit(solution)/shard_map/ppermute | solution.py:247
  37.8 1.4 %collective-permute-start.11 = (f32[32,768]{1,0:T(8,128)S(1)}, f32[32,768]{1,0:T(8,128)S(1)}, u32[]{:S(2)}, u32[]{:S(2)}) collective-permute-start(f32[32,768]{1,0:T(8,128)S(1)} %add.20.own_ref), channel_id=1, source_target_pairs={{0,2},{1,3},{2,0},{3,1},{4,6},{5,7},{6,4},{7,5},{8,10},{9,11},{10,... | collective-permute-start | bytes 294920 | tf_op jit(solution)/shard_map/ppermute | solution.py:247
  40.8 1.9 %collective-permute-done.11.got_ref = f32[32,768]{1,0:T(8,128)S(1)} collective-permute-done((f32[32,768]{1,0:T(8,128)S(1)}, f32[32,768]{1,0:T(8,128)S(1)}, u32[]{:S(2)}, u32[]{:S(2)}) %collective-permute-start.11) | collective-permute-done | bytes 98336 | tf_op jit(solution)/shard_map/ppermute | solution.py:247
  48.2 1.4 %collective-permute-start.18 = (f32[32,128]{1,0:T(8,128)S(1)}, f32[32,128]{1,0:T(8,128)S(1)}, u32[]{:S(2)}, u32[]{:S(2)}) collective-permute-start(f32[32,128]{1,0:T(8,128)S(1)} %add.21.before_ref.own_ref), channel_id=1, source_target_pairs={{0,2},{1,3},{2,0},{3,1},{4,6},{5,7},{6,4},{7,5},{8,10},{9,11},{10,... | collective-permute-start | bytes 49160 | tf_op jit(solution)/shard_map/ppermute | solution.py:247
  51.2 2.6 %collective-permute-start.17 = (f32[32,512]{1,0:T(8,128)S(1)}, f32[32,512]{1,0:T(8,128)S(1)}, u32[]{:S(2)}, u32[]{:S(2)}) collective-permute-start(f32[32,512]{1,0:T(8,128)S(1)} %add.23.own_ref), channel_id=1, source_target_pairs={{0,16},{4,20},{8,24},{12,28},{16,0},{20,4},{24,8},{28,12},{1,17},{... | collective-permute-start | bytes 196616 | tf_op jit(solution)/shard_map/ppermute | solution.py:247
  53.9 2.9 %inverse_factor.4.lower_ref = f32[32,32]{1,0:T(8,128)S(1)} custom-call(f32[32,128]{1,0:T(8,128)S(1)} %add.21.before_ref.own_ref, f32[32,128]{1,0:T(8,128)S(1)} %collective-permute-done.18.got_ref), custom_call_target="tpu_custom_call" | custom-call | flops 17179869184 | tf_op jit(solution)/shard_map/inverse_factor/pallas_call | solution.py:28
  56.9 2.1 %collective-permute-start.21 = (f32[32,512]{1,0:T(8,128)S(1)}, f32[32,512]{1,0:T(8,128)S(1)}, u32[]{:S(2)}, u32[]{:S(2)}) collective-permute-start(f32[32,512]{1,0:T(8,128)S(1)} %total.5.chunk_ref.refs_0_), channel_id=1, source_target_pairs={{0,12},{4,8},{8,4},{12,0},{16,28},{20,24},{24,20},{28,16},{1,13},{... | collective-permute-start | bytes 196616 | tf_op jit(solution)/shard_map/ppermute | solution.py:247
  66.1 1.4 %collective-permute-start.23 = (f32[32,768]{1,0:T(8,128)S(1)}, f32[32,768]{1,0:T(8,128)S(1)}, u32[]{:S(2)}, u32[]{:S(2)}) collective-permute-start(f32[32,768]{1,0:T(8,128)S(1)} %add.24.own_ref), channel_id=1, source_target_pairs={{0,2},{1,3},{2,0},{3,1},{4,6},{5,7},{6,4},{7,5},{8,10},{9,11},{10,... | collective-permute-start | bytes 294920 | tf_op jit(solution)/shard_map/ppermute | solution.py:247
  69.1 1.9 %collective-permute-done.23.got_ref = f32[32,768]{1,0:T(8,128)S(1)} collective-permute-done((f32[32,768]{1,0:T(8,128)S(1)}, f32[32,768]{1,0:T(8,128)S(1)}, u32[]{:S(2)}, u32[]{:S(2)}) %collective-permute-start.23) | collective-permute-done | bytes 98336 | tf_op jit(solution)/shard_map/ppermute | solution.py:247
  72.9 1.6 %collective-permute-start.26 = (f32[32,512]{1,0:T(8,128)S(1)}, f32[32,512]{1,0:T(8,128)S(1)}, u32[]{:S(2)}, u32[]{:S(2)}) collective-permute-start(f32[32,512]{1,0:T(8,128)S(1)} %get-tuple-element.66), channel_id=1, source_target_pairs={{0,12},{4,8},{8,4},{12,0},{16,28},{20,24},{24,20},{28,16},{1,13},{... | collective-permute-start | bytes 196616 | tf_op jit(solution)/shard_map/ppermute | solution.py:247
  76.5 1.4 %collective-permute-start.30 = (f32[32,128]{1,0:T(8,128)S(1)}, f32[32,128]{1,0:T(8,128)S(1)}, u32[]{:S(2)}, u32[]{:S(2)}) collective-permute-start(f32[32,128]{1,0:T(8,128)S(1)} %add.25.before_ref.own_ref), channel_id=1, source_target_pairs={{0,2},{1,3},{2,0},{3,1},{4,6},{5,7},{6,4},{7,5},{8,10},{9,11},{10,... | collective-permute-start | bytes 49160 | tf_op jit(solution)/shard_map/ppermute | solution.py:247
  79.5 2.7 %collective-permute-start.29 = (f32[32,512]{1,0:T(8,128)S(1)}, f32[32,512]{1,0:T(8,128)S(1)}, u32[]{:S(2)}, u32[]{:S(2)}) collective-permute-start(f32[32,512]{1,0:T(8,128)S(1)} %add.27.own_ref), channel_id=1, source_target_pairs={{0,16},{4,20},{8,24},{12,28},{16,0},{20,4},{24,8},{28,12},{1,17},{... | collective-permute-start | bytes 196616 | tf_op jit(solution)/shard_map/ppermute | solution.py:247
  82.2 2.9 %inverse_factor.5.lower_ref = f32[32,32]{1,0:T(8,128)S(1)} custom-call(f32[32,128]{1,0:T(8,128)S(1)} %add.25.before_ref.own_ref, f32[32,128]{1,0:T(8,128)S(1)} %collective-permute-done.30.got_ref), custom_call_target="tpu_custom_call" | custom-call | flops 17179869184 | tf_op jit(solution)/shard_map/inverse_factor/pallas_call | solution.py:28
  85.3 2.0 %collective-permute-start.33 = (f32[32,512]{1,0:T(8,128)S(1)}, f32[32,512]{1,0:T(8,128)S(1)}, u32[]{:S(2)}, u32[]{:S(2)}) collective-permute-start(f32[32,512]{1,0:T(8,128)S(1)} %total.6.chunk_ref.refs_0_), channel_id=1, source_target_pairs={{0,12},{4,8},{8,4},{12,0},{16,28},{20,24},{24,20},{28,16},{1,13},{... | collective-permute-start | bytes 196616 | tf_op jit(solution)/shard_map/ppermute | solution.py:247
  94.3 1.4 %collective-permute-start.35 = (f32[32,768]{1,0:T(8,128)S(1)}, f32[32,768]{1,0:T(8,128)S(1)}, u32[]{:S(2)}, u32[]{:S(2)}) collective-permute-start(f32[32,768]{1,0:T(8,128)S(1)} %add.28.own_ref), channel_id=1, source_target_pairs={{0,2},{1,3},{2,0},{3,1},{4,6},{5,7},{6,4},{7,5},{8,10},{9,11},{10,... | collective-permute-start | bytes 294920 | tf_op jit(solution)/shard_map/ppermute | solution.py:247
  97.3 1.9 %collective-permute-done.35.got_ref = f32[32,768]{1,0:T(8,128)S(1)} collective-permute-done((f32[32,768]{1,0:T(8,128)S(1)}, f32[32,768]{1,0:T(8,128)S(1)}, u32[]{:S(2)}, u32[]{:S(2)}) %collective-permute-start.35) | collective-permute-done | bytes 98336 | tf_op jit(solution)/shard_map/ppermute | solution.py:247
  104.7 1.4 %collective-permute-start.42 = (f32[32,128]{1,0:T(8,128)S(1)}, f32[32,128]{1,0:T(8,128)S(1)}, u32[]{:S(2)}, u32[]{:S(2)}) collective-permute-start(f32[32,128]{1,0:T(8,128)S(1)} %add.29.before_ref.own_ref), channel_id=1, source_target_pairs={{0,2},{1,3},{2,0},{3,1},{4,6},{5,7},{6,4},{7,5},{8,10},{9,11},{10,... | collective-permute-start | bytes 49160 | tf_op jit(solution)/shard_map/ppermute | solution.py:247
  107.8 2.6 %collective-permute-start.41 = (f32[32,512]{1,0:T(8,128)S(1)}, f32[32,512]{1,0:T(8,128)S(1)}, u32[]{:S(2)}, u32[]{:S(2)}) collective-permute-start(f32[32,512]{1,0:T(8,128)S(1)} %add.31.own_ref), channel_id=1, source_target_pairs={{0,16},{4,20},{8,24},{12,28},{16,0},{20,4},{24,8},{28,12},{1,17},{... | collective-permute-start | bytes 196616 | tf_op jit(solution)/shard_map/ppermute | solution.py:247
  110.4 2.9 %inverse_factor.6.lower_ref = f32[32,32]{1,0:T(8,128)S(1)} custom-call(f32[32,128]{1,0:T(8,128)S(1)} %add.29.before_ref.own_ref, f32[32,128]{1,0:T(8,128)S(1)} %collective-permute-done.42.got_ref), custom_call_target="tpu_custom_call" | custom-call | flops 17179869184 | tf_op jit(solution)/shard_map/inverse_factor/pallas_call | solution.py:28
  113.9 1.6 %collective-permute-start.45 = (f32[32,512]{1,0:T(8,128)S(1)}, f32[32,512]{1,0:T(8,128)S(1)}, u32[]{:S(2)}, u32[]{:S(2)}) collective-permute-start(f32[32,512]{1,0:T(8,128)S(1)} %total.7.chunk_ref.refs_0_), channel_id=1, source_target_pairs={{0,12},{4,8},{8,4},{12,0},{16,28},{20,24},{24,20},{28,16},{1,13},{... | collective-permute-start | bytes 196616 | tf_op jit(solution)/shard_map/ppermute | solution.py:247
  123.7 1.4 %collective-permute-start.49 = (f32[32,128]{1,0:T(8,128)S(1)}, f32[32,128]{1,0:T(8,128)S(1)}, u32[]{:S(2)}, u32[]{:S(2)}) collective-permute-start(f32[32,128]{1,0:T(8,128)S(1)} %add.32.refs_1_.own_ref), channel_id=1, source_target_pairs={{0,2},{1,3},{2,0},{3,1},{4,6},{5,7},{6,4},{7,5},{8,10},{9,11},{10,... | collective-permute-start | bytes 49160 | tf_op jit(solution)/shard_map/ppermute | solution.py:247
  127.4 2.9 %inverse_factor.7.lower_ref = f32[32,32]{1,0:T(8,128)S(1)} custom-call(f32[32,128]{1,0:T(8,128)S(1)} %add.32.refs_1_.own_ref, f32[32,128]{1,0:T(8,128)S(1)} %collective-permute-done.49.got_ref), custom_call_target="tpu_custom_call" | custom-call | flops 17179869184 | tf_op jit(solution)/shard_map/inverse_factor/pallas_call | solution.py:28
  (135 shorter events, 62.2 us)
Async XLA Ops:
  6.1 6.0 %collective-permute-start.1 = (f32[32,768]{1,0:T(8,128)S(1)}, f32[32,768]{1,0:T(8,128)S(1)}, u32[]{:S(2)}, u32[]{:S(2)}) collective-permute-start(f32[32,768]{1,0:T(8,128)S(1)} %add.17.refs_0_), channel_id=1, source_target_pairs={{0,2},{1,3},{2,0},{3,1},{4,6},{5,7},{6,4},{7,5},{8,10},{9,11},{10,... | collective-permute-start | bytes 294920 | tf_op jit(solution)/shard_map/ppermute | solution.py:247
  14.1 6.0 %collective-permute-start.3 = (f32[40,512]{1,0:T(8,128)S(1)}, f32[40,512]{1,0:T(8,128)S(1)}, u32[]{:S(2)}, u32[]{:S(2)}) collective-permute-start(f32[40,512]{1,0:T(8,128)S(1)} %get-tuple-element.48), channel_id=1, source_target_pairs={{0,12},{4,8},{8,4},{12,0},{16,28},{20,24},{24,20},{28,16},{1,13},{... | collective-permute-start | bytes 245768 | tf_op jit(solution)/shard_map/ppermute | solution.py:247
  17.0 4.7 %collective-permute-start.4 = (f32[40,512]{1,0:T(8,128)S(1)}, f32[40,512]{1,0:T(8,128)S(1)}, u32[]{:S(2)}, u32[]{:S(2)}) collective-permute-start(f32[40,512]{1,0:T(8,128)S(1)} %get-tuple-element.49), channel_id=1, source_target_pairs={{0,8},{4,12},{8,0},{12,4},{16,24},{20,28},{24,16},{28,20},{1,9},{5... | collective-permute-start | bytes 245768 | tf_op jit(solution)/shard_map/ppermute | solution.py:247
  17.4 4.4 %collective-permute-start.5 = (f32[40,512]{1,0:T(8,128)S(1)}, f32[40,512]{1,0:T(8,128)S(1)}, u32[]{:S(2)}, u32[]{:S(2)}) collective-permute-start(f32[40,512]{1,0:T(8,128)S(1)} %get-tuple-element.50), channel_id=1, source_target_pairs={{0,4},{4,0},{8,12},{12,8},{16,20},{20,16},{24,28},{28,24},{1,5},{5... | collective-permute-start | bytes 245768 | tf_op jit(solution)/shard_map/ppermute | solution.py:247
  21.9 5.6 %collective-permute-start.6 = (f32[40,512]{1,0:T(8,128)S(1)}, f32[40,512]{1,0:T(8,128)S(1)}, u32[]{:S(2)}, u32[]{:S(2)}) collective-permute-start(f32[40,512]{1,0:T(8,128)S(1)} %add.19.own_ref), channel_id=1, source_target_pairs={{0,16},{4,20},{8,24},{12,28},{16,0},{20,4},{24,8},{28,12},{1,17},{... | collective-permute-start | bytes 245768 | tf_op jit(solution)/shard_map/ppermute | solution.py:247
  27.6 5.8 %collective-permute-start.9 = (f32[40,512]{1,0:T(8,128)S(1)}, f32[40,512]{1,0:T(8,128)S(1)}, u32[]{:S(2)}, u32[]{:S(2)}) collective-permute-start(f32[40,512]{1,0:T(8,128)S(1)} %total.4.chunk_ref.mean_ref.refs_0_), channel_id=1, source_target_pairs={{0,12},{4,8},{8,4},{12,0},{16,28},{20,24},{24,20},{28,16},{1,13},{... | collective-permute-start | bytes 245768 | tf_op jit(solution)/shard_map/ppermute | solution.py:247
  30.1 4.8 %collective-permute-start.8 = (f32[40,512]{1,0:T(8,128)S(1)}, f32[40,512]{1,0:T(8,128)S(1)}, u32[]{:S(2)}, u32[]{:S(2)}) collective-permute-start(f32[40,512]{1,0:T(8,128)S(1)} %total.4.chunk_ref.mean_ref.refs_0_), channel_id=1, source_target_pairs={{0,8},{4,12},{8,0},{12,4},{16,24},{20,28},{24,16},{28,20},{1,9},{5... | collective-permute-start | bytes 245768 | tf_op jit(solution)/shard_map/ppermute | solution.py:247
  31.7 4.4 %collective-permute-start.7 = (f32[40,512]{1,0:T(8,128)S(1)}, f32[40,512]{1,0:T(8,128)S(1)}, u32[]{:S(2)}, u32[]{:S(2)}) collective-permute-start(f32[40,512]{1,0:T(8,128)S(1)} %total.4.chunk_ref.mean_ref.refs_0_), channel_id=1, source_target_pairs={{0,4},{4,0},{8,12},{12,8},{16,20},{20,16},{24,28},{28,24},{1,5},{5... | collective-permute-start | bytes 245768 | tf_op jit(solution)/shard_map/ppermute | solution.py:247
  37.8 4.9 %collective-permute-start.11 = (f32[32,768]{1,0:T(8,128)S(1)}, f32[32,768]{1,0:T(8,128)S(1)}, u32[]{:S(2)}, u32[]{:S(2)}) collective-permute-start(f32[32,768]{1,0:T(8,128)S(1)} %add.20.own_ref), channel_id=1, source_target_pairs={{0,2},{1,3},{2,0},{3,1},{4,6},{5,7},{6,4},{7,5},{8,10},{9,11},{10,... | collective-permute-start | bytes 294920 | tf_op jit(solution)/shard_map/ppermute | solution.py:247
  44.7 5.8 %collective-permute-start.14 = (f32[32,512]{1,0:T(8,128)S(1)}, f32[32,512]{1,0:T(8,128)S(1)}, u32[]{:S(2)}, u32[]{:S(2)}) collective-permute-start(f32[32,512]{1,0:T(8,128)S(1)} %get-tuple-element.57), channel_id=1, source_target_pairs={{0,12},{4,8},{8,4},{12,0},{16,28},{20,24},{24,20},{28,16},{1,13},{... | collective-permute-start | bytes 196616 | tf_op jit(solution)/shard_map/ppermute | solution.py:247
  45.9 4.7 %collective-permute-start.15 = (f32[32,512]{1,0:T(8,128)S(1)}, f32[32,512]{1,0:T(8,128)S(1)}, u32[]{:S(2)}, u32[]{:S(2)}) collective-permute-start(f32[32,512]{1,0:T(8,128)S(1)} %get-tuple-element.58), channel_id=1, source_target_pairs={{0,8},{4,12},{8,0},{12,4},{16,24},{20,28},{24,16},{28,20},{1,9},{5... | collective-permute-start | bytes 196616 | tf_op jit(solution)/shard_map/ppermute | solution.py:247
  46.9 4.3 %collective-permute-start.16 = (f32[32,512]{1,0:T(8,128)S(1)}, f32[32,512]{1,0:T(8,128)S(1)}, u32[]{:S(2)}, u32[]{:S(2)}) collective-permute-start(f32[32,512]{1,0:T(8,128)S(1)} %get-tuple-element.59), channel_id=1, source_target_pairs={{0,4},{4,0},{8,12},{12,8},{16,20},{20,16},{24,28},{28,24},{1,5},{5... | collective-permute-start | bytes 196616 | tf_op jit(solution)/shard_map/ppermute | solution.py:247
  48.2 5.6 %collective-permute-start.18 = (f32[32,128]{1,0:T(8,128)S(1)}, f32[32,128]{1,0:T(8,128)S(1)}, u32[]{:S(2)}, u32[]{:S(2)}) collective-permute-start(f32[32,128]{1,0:T(8,128)S(1)} %add.21.before_ref.own_ref), channel_id=1, source_target_pairs={{0,2},{1,3},{2,0},{3,1},{4,6},{5,7},{6,4},{7,5},{8,10},{9,11},{10,... | collective-permute-start | bytes 49160 | tf_op jit(solution)/shard_map/ppermute | solution.py:247
  51.2 5.5 %collective-permute-start.17 = (f32[32,512]{1,0:T(8,128)S(1)}, f32[32,512]{1,0:T(8,128)S(1)}, u32[]{:S(2)}, u32[]{:S(2)}) collective-permute-start(f32[32,512]{1,0:T(8,128)S(1)} %add.23.own_ref), channel_id=1, source_target_pairs={{0,16},{4,20},{8,24},{12,28},{16,0},{20,4},{24,8},{28,12},{1,17},{... | collective-permute-start | bytes 196616 | tf_op jit(solution)/shard_map/ppermute | solution.py:247
  56.9 5.3 %collective-permute-start.21 = (f32[32,512]{1,0:T(8,128)S(1)}, f32[32,512]{1,0:T(8,128)S(1)}, u32[]{:S(2)}, u32[]{:S(2)}) collective-permute-start(f32[32,512]{1,0:T(8,128)S(1)} %total.5.chunk_ref.refs_0_), channel_id=1, source_target_pairs={{0,12},{4,8},{8,4},{12,0},{16,28},{20,24},{24,20},{28,16},{1,13},{... | collective-permute-start | bytes 196616 | tf_op jit(solution)/shard_map/ppermute | solution.py:247
  59.0 4.3 %collective-permute-start.20 = (f32[32,512]{1,0:T(8,128)S(1)}, f32[32,512]{1,0:T(8,128)S(1)}, u32[]{:S(2)}, u32[]{:S(2)}) collective-permute-start(f32[32,512]{1,0:T(8,128)S(1)} %total.5.chunk_ref.refs_0_), channel_id=1, source_target_pairs={{0,8},{4,12},{8,0},{12,4},{16,24},{20,28},{24,16},{28,20},{1,9},{5... | collective-permute-start | bytes 196616 | tf_op jit(solution)/shard_map/ppermute | solution.py:247
  66.1 4.9 %collective-permute-start.23 = (f32[32,768]{1,0:T(8,128)S(1)}, f32[32,768]{1,0:T(8,128)S(1)}, u32[]{:S(2)}, u32[]{:S(2)}) collective-permute-start(f32[32,768]{1,0:T(8,128)S(1)} %add.24.own_ref), channel_id=1, source_target_pairs={{0,2},{1,3},{2,0},{3,1},{4,6},{5,7},{6,4},{7,5},{8,10},{9,11},{10,... | collective-permute-start | bytes 294920 | tf_op jit(solution)/shard_map/ppermute | solution.py:247
  72.9 5.8 %collective-permute-start.26 = (f32[32,512]{1,0:T(8,128)S(1)}, f32[32,512]{1,0:T(8,128)S(1)}, u32[]{:S(2)}, u32[]{:S(2)}) collective-permute-start(f32[32,512]{1,0:T(8,128)S(1)} %get-tuple-element.66), channel_id=1, source_target_pairs={{0,12},{4,8},{8,4},{12,0},{16,28},{20,24},{24,20},{28,16},{1,13},{... | collective-permute-start | bytes 196616 | tf_op jit(solution)/shard_map/ppermute | solution.py:247
  74.5 4.3 %collective-permute-start.27 = (f32[32,512]{1,0:T(8,128)S(1)}, f32[32,512]{1,0:T(8,128)S(1)}, u32[]{:S(2)}, u32[]{:S(2)}) collective-permute-start(f32[32,512]{1,0:T(8,128)S(1)} %get-tuple-element.67), channel_id=1, source_target_pairs={{0,8},{4,12},{8,0},{12,4},{16,24},{20,28},{24,16},{28,20},{1,9},{5... | collective-permute-start | bytes 196616 | tf_op jit(solution)/shard_map/ppermute | solution.py:247
  75.2 4.3 %collective-permute-start.28 = (f32[32,512]{1,0:T(8,128)S(1)}, f32[32,512]{1,0:T(8,128)S(1)}, u32[]{:S(2)}, u32[]{:S(2)}) collective-permute-start(f32[32,512]{1,0:T(8,128)S(1)} %get-tuple-element.68), channel_id=1, source_target_pairs={{0,4},{4,0},{8,12},{12,8},{16,20},{20,16},{24,28},{28,24},{1,5},{5... | collective-permute-start | bytes 196616 | tf_op jit(solution)/shard_map/ppermute | solution.py:247
  76.5 5.7 %collective-permute-start.30 = (f32[32,128]{1,0:T(8,128)S(1)}, f32[32,128]{1,0:T(8,128)S(1)}, u32[]{:S(2)}, u32[]{:S(2)}) collective-permute-start(f32[32,128]{1,0:T(8,128)S(1)} %add.25.before_ref.own_ref), channel_id=1, source_target_pairs={{0,2},{1,3},{2,0},{3,1},{4,6},{5,7},{6,4},{7,5},{8,10},{9,11},{10,... | collective-permute-start | bytes 49160 | tf_op jit(solution)/shard_map/ppermute | solution.py:247
  79.5 5.6 %collective-permute-start.29 = (f32[32,512]{1,0:T(8,128)S(1)}, f32[32,512]{1,0:T(8,128)S(1)}, u32[]{:S(2)}, u32[]{:S(2)}) collective-permute-start(f32[32,512]{1,0:T(8,128)S(1)} %add.27.own_ref), channel_id=1, source_target_pairs={{0,16},{4,20},{8,24},{12,28},{16,0},{20,4},{24,8},{28,12},{1,17},{... | collective-permute-start | bytes 196616 | tf_op jit(solution)/shard_map/ppermute | solution.py:247
  85.3 5.2 %collective-permute-start.33 = (f32[32,512]{1,0:T(8,128)S(1)}, f32[32,512]{1,0:T(8,128)S(1)}, u32[]{:S(2)}, u32[]{:S(2)}) collective-permute-start(f32[32,512]{1,0:T(8,128)S(1)} %total.6.chunk_ref.refs_0_), channel_id=1, source_target_pairs={{0,12},{4,8},{8,4},{12,0},{16,28},{20,24},{24,20},{28,16},{1,13},{... | collective-permute-start | bytes 196616 | tf_op jit(solution)/shard_map/ppermute | solution.py:247
  87.3 4.3 %collective-permute-start.32 = (f32[32,512]{1,0:T(8,128)S(1)}, f32[32,512]{1,0:T(8,128)S(1)}, u32[]{:S(2)}, u32[]{:S(2)}) collective-permute-start(f32[32,512]{1,0:T(8,128)S(1)} %total.6.chunk_ref.refs_0_), channel_id=1, source_target_pairs={{0,8},{4,12},{8,0},{12,4},{16,24},{20,28},{24,16},{28,20},{1,9},{5... | collective-permute-start | bytes 196616 | tf_op jit(solution)/shard_map/ppermute | solution.py:247
  88.4 4.3 %collective-permute-start.31 = (f32[32,512]{1,0:T(8,128)S(1)}, f32[32,512]{1,0:T(8,128)S(1)}, u32[]{:S(2)}, u32[]{:S(2)}) collective-permute-start(f32[32,512]{1,0:T(8,128)S(1)} %total.6.chunk_ref.refs_0_), channel_id=1, source_target_pairs={{0,4},{4,0},{8,12},{12,8},{16,20},{20,16},{24,28},{28,24},{1,5},{5... | collective-permute-start | bytes 196616 | tf_op jit(solution)/shard_map/ppermute | solution.py:247
  94.3 4.9 %collective-permute-start.35 = (f32[32,768]{1,0:T(8,128)S(1)}, f32[32,768]{1,0:T(8,128)S(1)}, u32[]{:S(2)}, u32[]{:S(2)}) collective-permute-start(f32[32,768]{1,0:T(8,128)S(1)} %add.28.own_ref), channel_id=1, source_target_pairs={{0,2},{1,3},{2,0},{3,1},{4,6},{5,7},{6,4},{7,5},{8,10},{9,11},{10,... | collective-permute-start | bytes 294920 | tf_op jit(solution)/shard_map/ppermute | solution.py:247
  101.2 5.9 %collective-permute-start.38 = (f32[32,512]{1,0:T(8,128)S(1)}, f32[32,512]{1,0:T(8,128)S(1)}, u32[]{:S(2)}, u32[]{:S(2)}) collective-permute-start(f32[32,512]{1,0:T(8,128)S(1)} %get-tuple-element.75), channel_id=1, source_target_pairs={{0,12},{4,8},{8,4},{12,0},{16,28},{20,24},{24,20},{28,16},{1,13},{... | collective-permute-start | bytes 196616 | tf_op jit(solution)/shard_map/ppermute | solution.py:247
  102.5 4.6 %collective-permute-start.39 = (f32[32,512]{1,0:T(8,128)S(1)}, f32[32,512]{1,0:T(8,128)S(1)}, u32[]{:S(2)}, u32[]{:S(2)}) collective-permute-start(f32[32,512]{1,0:T(8,128)S(1)} %get-tuple-element.76), channel_id=1, source_target_pairs={{0,8},{4,12},{8,0},{12,4},{16,24},{20,28},{24,16},{28,20},{1,9},{5... | collective-permute-start | bytes 196616 | tf_op jit(solution)/shard_map/ppermute | solution.py:247
  104.7 5.7 %collective-permute-start.42 = (f32[32,128]{1,0:T(8,128)S(1)}, f32[32,128]{1,0:T(8,128)S(1)}, u32[]{:S(2)}, u32[]{:S(2)}) collective-permute-start(f32[32,128]{1,0:T(8,128)S(1)} %add.29.before_ref.own_ref), channel_id=1, source_target_pairs={{0,2},{1,3},{2,0},{3,1},{4,6},{5,7},{6,4},{7,5},{8,10},{9,11},{10,... | collective-permute-start | bytes 49160 | tf_op jit(solution)/shard_map/ppermute | solution.py:247
  107.8 5.9 %collective-permute-start.41 = (f32[32,512]{1,0:T(8,128)S(1)}, f32[32,512]{1,0:T(8,128)S(1)}, u32[]{:S(2)}, u32[]{:S(2)}) collective-permute-start(f32[32,512]{1,0:T(8,128)S(1)} %add.31.own_ref), channel_id=1, source_target_pairs={{0,16},{4,20},{8,24},{12,28},{16,0},{20,4},{24,8},{28,12},{1,17},{... | collective-permute-start | bytes 196616 | tf_op jit(solution)/shard_map/ppermute | solution.py:247
  113.9 5.2 %collective-permute-start.45 = (f32[32,512]{1,0:T(8,128)S(1)}, f32[32,512]{1,0:T(8,128)S(1)}, u32[]{:S(2)}, u32[]{:S(2)}) collective-permute-start(f32[32,512]{1,0:T(8,128)S(1)} %total.7.chunk_ref.refs_0_), channel_id=1, source_target_pairs={{0,12},{4,8},{8,4},{12,0},{16,28},{20,24},{24,20},{28,16},{1,13},{... | collective-permute-start | bytes 196616 | tf_op jit(solution)/shard_map/ppermute | solution.py:247
  125.1 5.2 %collective-permute-start.48 = (bf16[32,1536]{1,0:T(8,128)(2,1)S(1)}, bf16[32,1536]{1,0:T(8,128)(2,1)S(1)}, u32[]{:S(2)}, u32[]{:S(2)}) collective-permute-start(bf16[32,1536]{1,0:T(8,128)(2,1)S(1)} %add.33.own_ref), channel_id=1, source_target_pairs={{0,2},{1,3},{2,0},{3,1},{4,6},{5,7},{6,4},{7,5},{8,10},{9,11},{10,... | collective-permute-start | bytes 294920 | tf_op jit(solution)/shard_map/ppermute | solution.py:247
  (19 other events, 40.8 us)

commit v7 on v6

--- a/solution.py
+++ b/solution.py
@@ -11,7 +11,8 @@
 PEERS = 4
 LANES = 128
 EXTRA = 8
-ORDER = (0, 3, 2, 1)
+SCATTER = (0, 3, 2, 1)
+GATHER = (0, 3, 1, 2)
 TERMS = 3
 LONG = pl.CostEstimate(flops=2**34, bytes_accessed=0, transcendentals=0)
 SHORT = pl.CostEstimate(flops=2**29, bytes_accessed=0, transcendentals=0)
@@ -116,13 +117,13 @@
     shift = jnp.sum(chunk * mean_ref[n : n + 1, :], axis=1, keepdims=True)
     rows = rows_ref[place, aligned(position() ^ part, chunk.shape[1])]
     value = join(contract_last(split(chunk), rows)) - shift
-    out_ref[...] = value if part == ORDER[0] else refs[0][:, place] + value
+    out_ref[...] = value if part == GATHER[0] else refs[0][:, place] + value
 
 
 def gram_kernel(*refs):
     *refs, out_ref = refs
     n = out_ref.shape[0]
-    chunks = {part: ref[:n, :] for part, ref in zip(ORDER, refs)}
+    chunks = {part: ref[:n, :] for part, ref in zip(GATHER, refs)}
     parts = [contract_last(chunks[part], chunks[part], HIGHEST) for part in range(PEERS)]
     out_ref[...] = jnp.zeros(out_ref.shape, F32)
     out_ref[:, :n] = (parts[0] + parts[1]) + (parts[2] + parts[3])
@@ -182,7 +183,7 @@
     means, outs = ([None] * PEERS if first else refs[:PEERS]), refs[-PEERS:]
     tokens = aligned(core(), own_ref.shape[1])
     sides = weights_of(first, own_ref)
-    for part, mean_ref, out_ref in zip(ORDER, means, outs):
+    for part, mean_ref, out_ref in zip(SCATTER, means, outs):
         rows = rows_ref[tokens, aligned(position() ^ part, out_ref.shape[1])]
         out_ref[...] = image_term(first, *sides, rows, mean_ref)
 
@@ -193,7 +194,7 @@
     means, halves, outs = ([None] * peers if first else refs[:peers]), refs[-2 * peers : -peers], refs[-peers:]
     tokens = aligned(1 - core(), other_ref.shape[1])
     weights, counts, centre = weights_of(first, other_ref)
-    for part, mean_ref, half_ref, out_ref in zip(ORDER[1:], means, halves, outs):
+    for part, mean_ref, half_ref, out_ref in zip(SCATTER[1:], means, halves, outs):
         rows = rows_ref[tokens, aligned(position() ^ part, out_ref.shape[1])]
         out_ref[...] = half_ref[...] + image_term(first, weights, counts, centre, rows, mean_ref)
     weights_ref[...] = weights
@@ -212,7 +213,7 @@
 def assemble_kernel(*refs):
     *chunks, out_ref = refs
     n, width = out_ref.shape[0], chunks[0].shape[1]
-    for part, chunk in zip(ORDER, chunks):
+    for part, chunk in zip(GATHER, chunks):
         place = aligned(position() ^ part, width)
         out_ref[:, place] = chunk[:n, :]
 
@@ -255,7 +256,7 @@
 
 
 def share(value, axis):
-    return [value] + [swap(value, axis, part) for part in ORDER[1:]]
+    return [value] + [swap(value, axis, part) for part in GATHER[1:]]
 
 
 def on_device(activations, start_basis):
@@ -283,18 +284,18 @@
     for distance in distances("feat", 1):
         own = add(own, swap(sent if distance == 1 else own, "feat", distance))
     other = swap(own, "feat", 1)
-    means, lower = [], []
+    means, ranked, lower = [], [], []
     for step in range(ITERS):
         first, last = step == 0, step == ITERS - 1
         chunk = ((n + EXTRA if first else n, width), F32)
         weights = ((TERMS * n + 2 * EXTRA if first else TERMS * n, tokens // 2), BF16)
         kernel = functools.partial(half_image_kernel, first)
-        kept, *halves = call(kernel, [chunk] * PEERS, "half_image", cost=SHORT)(own, rows, *means)
+        kept, *halves = call(kernel, [chunk] * PEERS, "half_image", cost=SHORT)(own, rows, *ranked)
         kernel = functools.partial(image_kernel, first)
         *terms, weights, sums = call(kernel, [chunk] * (PEERS - 1) + [weights, side], "image")(
-            other, rows, *means[1:], *halves
+            other, rows, *ranked[1:], *halves
         )
-        received = [swap(term, "tok", part) for part, term in zip(ORDER[1:], terms)]
+        received = [swap(term, "tok", part) for part, term in zip(SCATTER[1:], terms)]
         kernel = functools.partial(own_image_kernel, first)
         kept = call(kernel, [chunk], "own_image", cost=SHORT)(weights, sums, rows, kept, *means[:1])
         image = add(*kept, *received)
@@ -305,12 +306,13 @@
         image = call(kernel, [chunk], "total")(image, swap(image, "tok", last_step), *lower)[0]
         images = share(image, "tok")
         means = means or images
+        ranked = [means[GATHER.index(part)] for part in SCATTER]
         gram = call(gram_kernel, [side], "gram")(*images)[0]
         grams = (gram, swap(gram, "feat", 1))
         before = []
-        for part, image, mean in zip(ORDER, images, means):
+        for part, image, mean in zip(GATHER, images, means):
             operands = [image, mean, rows, *before]
-            if part != ORDER[-1]:
+            if part != GATHER[-1]:
                 kernel = functools.partial(projection_kernel, part, "all")
                 before = call(kernel, [whole], "projection", cost=SHORT)(*operands)
         if last:

time: 132 us -> 131 us (level)
  waiting for transfers between devices: 40 us -> 38.1 us
    ppermute x50, waiting for transfers between devices: 40 us -> 38.1 us  [swap(): return lax.ppermute(value, axis, [(i, i ^ distance) for i in range(size)])]
    ppermute x50, starting transfers between devices: 54.8 us -> 56.1 us  [swap(): return lax.ppermute(value, axis, [(i, i ^ distance) for i in range(size)])]
  transfers between devices with their start and end apart: 50 -> 50, of which waited for: 39 -> 38; matrix products, arithmetic and copies ran while one was open for 0% -> 0% of each run, Pallas kernels for 20% -> 20%
where the time goes in v7:
time: 131 us
  starting transfers between devices  56.1 us (43%)
  waiting for transfers between devices  38.1 us (29%)
  Pallas kernels  35.7 us (27%)
    ppermute x50, starting transfers between devices, swap(): return lax.ppermute(value, axis, [(i, i ^ distance) for i in range(size)])  56.1 us
    ppermute x50, waiting for transfers between devices, swap(): return lax.ppermute(value, axis, [(i, i ^ distance) for i in range(size)])  38.1 us
    pallas_call x65, Pallas kernels, run(): pl.pallas_call(kernel, out_shape=[jax.ShapeDtypeStruct(shape, dtype) for...  35.7 us
  transfers between devices with their start and end apart: 50, of which 38 were waited for; matrix products, arithmetic and copies ran while one was open for 0% of the time, Pallas kernels for 20%

profile of v7, /device:TPU:0, one launch (start us, length us, event | category | flops | bytes accessed | tf_op | source)
XLA Modules:
  0.0 131.0 jit_solution(7762658174391133313)
XLA Ops:
  0.6 2.0 %fetch.1.ready_ref = bf16[1536,2048]{1,0:T(8,128)(2,1)S(1)} custom-call(bf16[1536,2048]{1,0:T(8,128)(2,1)} %rows_hbm.3), custom_call_target="tpu_custom_call" | custom-call | tf_op jit(solution)/shard_map/fetch/pallas_call | solution.py:29
  2.6 1.9 %sent_projection.4 = (f32[32,768]{1,0:T(8,128)S(1)}, bf16[1536,2048]{1,0:T(8,128)(2,1)S(1)}) custom-call(f32[32,2048]{1,0:T(8,128)S(1)} %copy-done, bf16[1536,2048]{1,0:T(8,128)(2,1)} %rows_hbm.3, bf16[1536,2048]{1,0:T(8,128)(2,1)S(1)} %fetch.1.ready_ref), custom_call_target="tpu_custom_call", output_to_operand_aliasing={{1}: (2, {})} | custom-call | tf_op jit(solution)/shard_map/sent_projection/pallas_call | solution.py:29
  6.1 2.8 %collective-permute-start.1 = (f32[32,768]{1,0:T(8,128)S(1)}, f32[32,768]{1,0:T(8,128)S(1)}, u32[]{:S(2)}, u32[]{:S(2)}) collective-permute-start(f32[32,768]{1,0:T(8,128)S(1)} %add.17.refs_0_), channel_id=1, source_target_pairs={{0,2},{1,3},{2,0},{3,1},{4,6},{5,7},{6,4},{7,5},{8,10},{9,11},{10,... | collective-permute-start | bytes 294920 | tf_op jit(solution)/shard_map/ppermute | solution.py:248
  8.9 3.3 %collective-permute-done.1.refs_1_ = f32[32,768]{1,0:T(8,128)S(1)} collective-permute-done((f32[32,768]{1,0:T(8,128)S(1)}, f32[32,768]{1,0:T(8,128)S(1)}, u32[]{:S(2)}, u32[]{:S(2)}) %collective-permute-start.1) | collective-permute-done | bytes 98336 | tf_op jit(solution)/shard_map/ppermute | solution.py:248
  14.1 2.8 %collective-permute-start.3 = (f32[40,512]{1,0:T(8,128)S(1)}, f32[40,512]{1,0:T(8,128)S(1)}, u32[]{:S(2)}, u32[]{:S(2)}) collective-permute-start(f32[40,512]{1,0:T(8,128)S(1)} %get-tuple-element.48), channel_id=1, source_target_pairs={{0,12},{4,8},{8,4},{12,0},{16,28},{20,24},{24,20},{28,16},{1,13},{... | collective-permute-start | bytes 245768 | tf_op jit(solution)/shard_map/ppermute | solution.py:248
  18.0 2.2 %collective-permute-done.3.refs_1_ = f32[40,512]{1,0:T(8,128)S(1)} collective-permute-done((f32[40,512]{1,0:T(8,128)S(1)}, f32[40,512]{1,0:T(8,128)S(1)}, u32[]{:S(2)}, u32[]{:S(2)}) %collective-permute-start.3) | collective-permute-done | bytes 81952 | tf_op jit(solution)/shard_map/ppermute | solution.py:248
  20.1 1.5 %collective-permute-done.4.refs_2_ = f32[40,512]{1,0:T(8,128)S(1)} collective-permute-done((f32[40,512]{1,0:T(8,128)S(1)}, f32[40,512]{1,0:T(8,128)S(1)}, u32[]{:S(2)}, u32[]{:S(2)}) %collective-permute-start.4) | collective-permute-done | bytes 81952 | tf_op jit(solution)/shard_map/ppermute | solution.py:248
  21.9 2.7 %collective-permute-start.6 = (f32[40,512]{1,0:T(8,128)S(1)}, f32[40,512]{1,0:T(8,128)S(1)}, u32[]{:S(2)}, u32[]{:S(2)}) collective-permute-start(f32[40,512]{1,0:T(8,128)S(1)} %add.19.own_ref), channel_id=1, source_target_pairs={{0,16},{4,20},{8,24},{12,28},{16,0},{20,4},{24,8},{28,12},{1,17},{... | collective-permute-start | bytes 245768 | tf_op jit(solution)/shard_map/ppermute | solution.py:248
  24.6 2.9 %collective-permute-done.6.got_ref = f32[40,512]{1,0:T(8,128)S(1)} collective-permute-done((f32[40,512]{1,0:T(8,128)S(1)}, f32[40,512]{1,0:T(8,128)S(1)}, u32[]{:S(2)}, u32[]{:S(2)}) %collective-permute-start.6) | collective-permute-done | bytes 81952 | tf_op jit(solution)/shard_map/ppermute | solution.py:248
  27.6 2.6 %collective-permute-start.9 = (f32[40,512]{1,0:T(8,128)S(1)}, f32[40,512]{1,0:T(8,128)S(1)}, u32[]{:S(2)}, u32[]{:S(2)}) collective-permute-start(f32[40,512]{1,0:T(8,128)S(1)} %total.4.chunk_ref.mean_ref.refs_0_), channel_id=1, source_target_pairs={{0,12},{4,8},{8,4},{12,0},{16,28},{20,24},{24,20},{28,16},{1,13},{... | collective-permute-start | bytes 245768 | tf_op jit(solution)/shard_map/ppermute | solution.py:248
  37.0 1.6 %collective-permute-start.11 = (f32[32,768]{1,0:T(8,128)S(1)}, f32[32,768]{1,0:T(8,128)S(1)}, u32[]{:S(2)}, u32[]{:S(2)}) collective-permute-start(f32[32,768]{1,0:T(8,128)S(1)} %add.20.own_ref), channel_id=1, source_target_pairs={{0,2},{1,3},{2,0},{3,1},{4,6},{5,7},{6,4},{7,5},{8,10},{9,11},{10,... | collective-permute-start | bytes 294920 | tf_op jit(solution)/shard_map/ppermute | solution.py:248
  40.1 1.8 %collective-permute-done.11.got_ref = f32[32,768]{1,0:T(8,128)S(1)} collective-permute-done((f32[32,768]{1,0:T(8,128)S(1)}, f32[32,768]{1,0:T(8,128)S(1)}, u32[]{:S(2)}, u32[]{:S(2)}) %collective-permute-start.11) | collective-permute-done | bytes 98336 | tf_op jit(solution)/shard_map/ppermute | solution.py:248
  43.9 2.3 %collective-permute-start.14 = (f32[32,512]{1,0:T(8,128)S(1)}, f32[32,512]{1,0:T(8,128)S(1)}, u32[]{:S(2)}, u32[]{:S(2)}) collective-permute-start(f32[32,512]{1,0:T(8,128)S(1)} %get-tuple-element.57), channel_id=1, source_target_pairs={{0,12},{4,8},{8,4},{12,0},{16,28},{20,24},{24,20},{28,16},{1,13},{... | collective-permute-start | bytes 196616 | tf_op jit(solution)/shard_map/ppermute | solution.py:248
  47.4 1.5 %collective-permute-start.18 = (f32[32,128]{1,0:T(8,128)S(1)}, f32[32,128]{1,0:T(8,128)S(1)}, u32[]{:S(2)}, u32[]{:S(2)}) collective-permute-start(f32[32,128]{1,0:T(8,128)S(1)} %add.21.before_ref.own_ref), channel_id=1, source_target_pairs={{0,2},{1,3},{2,0},{3,1},{4,6},{5,7},{6,4},{7,5},{8,10},{9,11},{10,... | collective-permute-start | bytes 49160 | tf_op jit(solution)/shard_map/ppermute | solution.py:248
  51.3 3.1 %collective-permute-start.17 = (f32[32,512]{1,0:T(8,128)S(1)}, f32[32,512]{1,0:T(8,128)S(1)}, u32[]{:S(2)}, u32[]{:S(2)}) collective-permute-start(f32[32,512]{1,0:T(8,128)S(1)} %add.23.own_ref), channel_id=1, source_target_pairs={{0,16},{4,20},{8,24},{12,28},{16,0},{20,4},{24,8},{28,12},{1,17},{... | collective-permute-start | bytes 196616 | tf_op jit(solution)/shard_map/ppermute | solution.py:248
  54.4 2.9 %inverse_factor.4.lower_ref = f32[32,32]{1,0:T(8,128)S(1)} custom-call(f32[32,128]{1,0:T(8,128)S(1)} %add.21.before_ref.own_ref, f32[32,128]{1,0:T(8,128)S(1)} %collective-permute-done.18.got_ref), custom_call_target="tpu_custom_call" | custom-call | flops 17179869184 | tf_op jit(solution)/shard_map/inverse_factor/pallas_call | solution.py:29
  57.5 1.4 %collective-permute-start.21 = (f32[32,512]{1,0:T(8,128)S(1)}, f32[32,512]{1,0:T(8,128)S(1)}, u32[]{:S(2)}, u32[]{:S(2)}) collective-permute-start(f32[32,512]{1,0:T(8,128)S(1)} %total.5.chunk_ref.refs_0_), channel_id=1, source_target_pairs={{0,12},{4,8},{8,4},{12,0},{16,28},{20,24},{24,20},{28,16},{1,13},{... | collective-permute-start | bytes 196616 | tf_op jit(solution)/shard_map/ppermute | solution.py:248
  66.2 1.6 %collective-permute-start.23 = (f32[32,768]{1,0:T(8,128)S(1)}, f32[32,768]{1,0:T(8,128)S(1)}, u32[]{:S(2)}, u32[]{:S(2)}) collective-permute-start(f32[32,768]{1,0:T(8,128)S(1)} %add.24.own_ref), channel_id=1, source_target_pairs={{0,2},{1,3},{2,0},{3,1},{4,6},{5,7},{6,4},{7,5},{8,10},{9,11},{10,... | collective-permute-start | bytes 294920 | tf_op jit(solution)/shard_map/ppermute | solution.py:248
  69.3 1.8 %collective-permute-done.23.got_ref = f32[32,768]{1,0:T(8,128)S(1)} collective-permute-done((f32[32,768]{1,0:T(8,128)S(1)}, f32[32,768]{1,0:T(8,128)S(1)}, u32[]{:S(2)}, u32[]{:S(2)}) %collective-permute-start.23) | collective-permute-done | bytes 98336 | tf_op jit(solution)/shard_map/ppermute | solution.py:248
  76.6 1.5 %collective-permute-start.30 = (f32[32,128]{1,0:T(8,128)S(1)}, f32[32,128]{1,0:T(8,128)S(1)}, u32[]{:S(2)}, u32[]{:S(2)}) collective-permute-start(f32[32,128]{1,0:T(8,128)S(1)} %add.25.before_ref.own_ref), channel_id=1, source_target_pairs={{0,2},{1,3},{2,0},{3,1},{4,6},{5,7},{6,4},{7,5},{8,10},{9,11},{10,... | collective-permute-start | bytes 49160 | tf_op jit(solution)/shard_map/ppermute | solution.py:248
  79.6 3.0 %collective-permute-start.29 = (f32[32,512]{1,0:T(8,128)S(1)}, f32[32,512]{1,0:T(8,128)S(1)}, u32[]{:S(2)}, u32[]{:S(2)}) collective-permute-start(f32[32,512]{1,0:T(8,128)S(1)} %add.27.own_ref), channel_id=1, source_target_pairs={{0,16},{4,20},{8,24},{12,28},{16,0},{20,4},{24,8},{28,12},{1,17},{... | collective-permute-start | bytes 196616 | tf_op jit(solution)/shard_map/ppermute | solution.py:248
  82.6 2.9 %inverse_factor.5.lower_ref = f32[32,32]{1,0:T(8,128)S(1)} custom-call(f32[32,128]{1,0:T(8,128)S(1)} %add.25.before_ref.own_ref, f32[32,128]{1,0:T(8,128)S(1)} %collective-permute-done.30.got_ref), custom_call_target="tpu_custom_call" | custom-call | flops 17179869184 | tf_op jit(solution)/shard_map/inverse_factor/pallas_call | solution.py:29
  87.9 1.4 %collective-permute-start.31 = (f32[32,512]{1,0:T(8,128)S(1)}, f32[32,512]{1,0:T(8,128)S(1)}, u32[]{:S(2)}, u32[]{:S(2)}) collective-permute-start(f32[32,512]{1,0:T(8,128)S(1)} %total.6.chunk_ref.refs_0_), channel_id=1, source_target_pairs={{0,8},{4,12},{8,0},{12,4},{16,24},{20,28},{24,16},{28,20},{1,9},{5... | collective-permute-start | bytes 196616 | tf_op jit(solution)/shard_map/ppermute | solution.py:248
  94.2 1.6 %collective-permute-start.35 = (f32[32,768]{1,0:T(8,128)S(1)}, f32[32,768]{1,0:T(8,128)S(1)}, u32[]{:S(2)}, u32[]{:S(2)}) collective-permute-start(f32[32,768]{1,0:T(8,128)S(1)} %add.28.own_ref), channel_id=1, source_target_pairs={{0,2},{1,3},{2,0},{3,1},{4,6},{5,7},{6,4},{7,5},{8,10},{9,11},{10,... | collective-permute-start | bytes 294920 | tf_op jit(solution)/shard_map/ppermute | solution.py:248
  97.3 1.8 %collective-permute-done.35.got_ref = f32[32,768]{1,0:T(8,128)S(1)} collective-permute-done((f32[32,768]{1,0:T(8,128)S(1)}, f32[32,768]{1,0:T(8,128)S(1)}, u32[]{:S(2)}, u32[]{:S(2)}) %collective-permute-start.35) | collective-permute-done | bytes 98336 | tf_op jit(solution)/shard_map/ppermute | solution.py:248
  101.0 1.8 %collective-permute-start.38 = (f32[32,512]{1,0:T(8,128)S(1)}, f32[32,512]{1,0:T(8,128)S(1)}, u32[]{:S(2)}, u32[]{:S(2)}) collective-permute-start(f32[32,512]{1,0:T(8,128)S(1)} %get-tuple-element.75), channel_id=1, source_target_pairs={{0,12},{4,8},{8,4},{12,0},{16,28},{20,24},{24,20},{28,16},{1,13},{... | collective-permute-start | bytes 196616 | tf_op jit(solution)/shard_map/ppermute | solution.py:248
  104.6 1.5 %collective-permute-start.42 = (f32[32,128]{1,0:T(8,128)S(1)}, f32[32,128]{1,0:T(8,128)S(1)}, u32[]{:S(2)}, u32[]{:S(2)}) collective-permute-start(f32[32,128]{1,0:T(8,128)S(1)} %add.29.before_ref.own_ref), channel_id=1, source_target_pairs={{0,2},{1,3},{2,0},{3,1},{4,6},{5,7},{6,4},{7,5},{8,10},{9,11},{10,... | collective-permute-start | bytes 49160 | tf_op jit(solution)/shard_map/ppermute | solution.py:248
  108.0 2.3 %collective-permute-start.41 = (f32[32,512]{1,0:T(8,128)S(1)}, f32[32,512]{1,0:T(8,128)S(1)}, u32[]{:S(2)}, u32[]{:S(2)}) collective-permute-start(f32[32,512]{1,0:T(8,128)S(1)} %add.31.own_ref), channel_id=1, source_target_pairs={{0,16},{4,20},{8,24},{12,28},{16,0},{20,4},{24,8},{28,12},{1,17},{... | collective-permute-start | bytes 196616 | tf_op jit(solution)/shard_map/ppermute | solution.py:248
  110.4 2.9 %inverse_factor.6.lower_ref = f32[32,32]{1,0:T(8,128)S(1)} custom-call(f32[32,128]{1,0:T(8,128)S(1)} %add.29.before_ref.own_ref, f32[32,128]{1,0:T(8,128)S(1)} %collective-permute-done.42.got_ref), custom_call_target="tpu_custom_call" | custom-call | flops 17179869184 | tf_op jit(solution)/shard_map/inverse_factor/pallas_call | solution.py:29
  116.1 1.5 %collective-permute-start.43 = (f32[32,512]{1,0:T(8,128)S(1)}, f32[32,512]{1,0:T(8,128)S(1)}, u32[]{:S(2)}, u32[]{:S(2)}) collective-permute-start(f32[32,512]{1,0:T(8,128)S(1)} %total.7.chunk_ref.refs_0_), channel_id=1, source_target_pairs={{0,8},{4,12},{8,0},{12,4},{16,24},{20,28},{24,16},{28,20},{1,9},{5... | collective-permute-start | bytes 196616 | tf_op jit(solution)/shard_map/ppermute | solution.py:248
  123.2 1.5 %collective-permute-start.49 = (f32[32,128]{1,0:T(8,128)S(1)}, f32[32,128]{1,0:T(8,128)S(1)}, u32[]{:S(2)}, u32[]{:S(2)}) collective-permute-start(f32[32,128]{1,0:T(8,128)S(1)} %add.32.refs_1_.own_ref), channel_id=1, source_target_pairs={{0,2},{1,3},{2,0},{3,1},{4,6},{5,7},{6,4},{7,5},{8,10},{9,11},{10,... | collective-permute-start | bytes 49160 | tf_op jit(solution)/shard_map/ppermute | solution.py:248
  126.9 2.9 %inverse_factor.7.lower_ref = f32[32,32]{1,0:T(8,128)S(1)} custom-call(f32[32,128]{1,0:T(8,128)S(1)} %add.32.refs_1_.own_ref, f32[32,128]{1,0:T(8,128)S(1)} %collective-permute-done.49.got_ref), custom_call_target="tpu_custom_call" | custom-call | flops 17179869184 | tf_op jit(solution)/shard_map/inverse_factor/pallas_call | solution.py:29
  (135 shorter events, 60.9 us)
Async XLA Ops:
  6.1 6.0 %collective-permute-start.1 = (f32[32,768]{1,0:T(8,128)S(1)}, f32[32,768]{1,0:T(8,128)S(1)}, u32[]{:S(2)}, u32[]{:S(2)}) collective-permute-start(f32[32,768]{1,0:T(8,128)S(1)} %add.17.refs_0_), channel_id=1, source_target_pairs={{0,2},{1,3},{2,0},{3,1},{4,6},{5,7},{6,4},{7,5},{8,10},{9,11},{10,... | collective-permute-start | bytes 294920 | tf_op jit(solution)/shard_map/ppermute | solution.py:248
  14.1 6.0 %collective-permute-start.3 = (f32[40,512]{1,0:T(8,128)S(1)}, f32[40,512]{1,0:T(8,128)S(1)}, u32[]{:S(2)}, u32[]{:S(2)}) collective-permute-start(f32[40,512]{1,0:T(8,128)S(1)} %get-tuple-element.48), channel_id=1, source_target_pairs={{0,12},{4,8},{8,4},{12,0},{16,28},{20,24},{24,20},{28,16},{1,13},{... | collective-permute-start | bytes 245768 | tf_op jit(solution)/shard_map/ppermute | solution.py:248
  17.0 4.7 %collective-permute-start.4 = (f32[40,512]{1,0:T(8,128)S(1)}, f32[40,512]{1,0:T(8,128)S(1)}, u32[]{:S(2)}, u32[]{:S(2)}) collective-permute-start(f32[40,512]{1,0:T(8,128)S(1)} %get-tuple-element.49), channel_id=1, source_target_pairs={{0,8},{4,12},{8,0},{12,4},{16,24},{20,28},{24,16},{28,20},{1,9},{5... | collective-permute-start | bytes 245768 | tf_op jit(solution)/shard_map/ppermute | solution.py:248
  17.4 4.4 %collective-permute-start.5 = (f32[40,512]{1,0:T(8,128)S(1)}, f32[40,512]{1,0:T(8,128)S(1)}, u32[]{:S(2)}, u32[]{:S(2)}) collective-permute-start(f32[40,512]{1,0:T(8,128)S(1)} %get-tuple-element.50), channel_id=1, source_target_pairs={{0,4},{4,0},{8,12},{12,8},{16,20},{20,16},{24,28},{28,24},{1,5},{5... | collective-permute-start | bytes 245768 | tf_op jit(solution)/shard_map/ppermute | solution.py:248
  21.9 5.6 %collective-permute-start.6 = (f32[40,512]{1,0:T(8,128)S(1)}, f32[40,512]{1,0:T(8,128)S(1)}, u32[]{:S(2)}, u32[]{:S(2)}) collective-permute-start(f32[40,512]{1,0:T(8,128)S(1)} %add.19.own_ref), channel_id=1, source_target_pairs={{0,16},{4,20},{8,24},{12,28},{16,0},{20,4},{24,8},{28,12},{1,17},{... | collective-permute-start | bytes 245768 | tf_op jit(solution)/shard_map/ppermute | solution.py:248
  27.6 5.4 %collective-permute-start.9 = (f32[40,512]{1,0:T(8,128)S(1)}, f32[40,512]{1,0:T(8,128)S(1)}, u32[]{:S(2)}, u32[]{:S(2)}) collective-permute-start(f32[40,512]{1,0:T(8,128)S(1)} %total.4.chunk_ref.mean_ref.refs_0_), channel_id=1, source_target_pairs={{0,12},{4,8},{8,4},{12,0},{16,28},{20,24},{24,20},{28,16},{1,13},{... | collective-permute-start | bytes 245768 | tf_op jit(solution)/shard_map/ppermute | solution.py:248
  30.1 4.5 %collective-permute-start.8 = (f32[40,512]{1,0:T(8,128)S(1)}, f32[40,512]{1,0:T(8,128)S(1)}, u32[]{:S(2)}, u32[]{:S(2)}) collective-permute-start(f32[40,512]{1,0:T(8,128)S(1)} %total.4.chunk_ref.mean_ref.refs_0_), channel_id=1, source_target_pairs={{0,4},{4,0},{8,12},{12,8},{16,20},{20,16},{24,28},{28,24},{1,5},{5... | collective-permute-start | bytes 245768 | tf_op jit(solution)/shard_map/ppermute | solution.py:248
  30.5 4.8 %collective-permute-start.7 = (f32[40,512]{1,0:T(8,128)S(1)}, f32[40,512]{1,0:T(8,128)S(1)}, u32[]{:S(2)}, u32[]{:S(2)}) collective-permute-start(f32[40,512]{1,0:T(8,128)S(1)} %total.4.chunk_ref.mean_ref.refs_0_), channel_id=1, source_target_pairs={{0,8},{4,12},{8,0},{12,4},{16,24},{20,28},{24,16},{28,20},{1,9},{5... | collective-permute-start | bytes 245768 | tf_op jit(solution)/shard_map/ppermute | solution.py:248
  37.0 4.9 %collective-permute-start.11 = (f32[32,768]{1,0:T(8,128)S(1)}, f32[32,768]{1,0:T(8,128)S(1)}, u32[]{:S(2)}, u32[]{:S(2)}) collective-permute-start(f32[32,768]{1,0:T(8,128)S(1)} %add.20.own_ref), channel_id=1, source_target_pairs={{0,2},{1,3},{2,0},{3,1},{4,6},{5,7},{6,4},{7,5},{8,10},{9,11},{10,... | collective-permute-start | bytes 294920 | tf_op jit(solution)/shard_map/ppermute | solution.py:248
  43.9 5.7 %collective-permute-start.14 = (f32[32,512]{1,0:T(8,128)S(1)}, f32[32,512]{1,0:T(8,128)S(1)}, u32[]{:S(2)}, u32[]{:S(2)}) collective-permute-start(f32[32,512]{1,0:T(8,128)S(1)} %get-tuple-element.57), channel_id=1, source_target_pairs={{0,12},{4,8},{8,4},{12,0},{16,28},{20,24},{24,20},{28,16},{1,13},{... | collective-permute-start | bytes 196616 | tf_op jit(solution)/shard_map/ppermute | solution.py:248
  46.2 4.4 %collective-permute-start.15 = (f32[32,512]{1,0:T(8,128)S(1)}, f32[32,512]{1,0:T(8,128)S(1)}, u32[]{:S(2)}, u32[]{:S(2)}) collective-permute-start(f32[32,512]{1,0:T(8,128)S(1)} %get-tuple-element.58), channel_id=1, source_target_pairs={{0,8},{4,12},{8,0},{12,4},{16,24},{20,28},{24,16},{28,20},{1,9},{5... | collective-permute-start | bytes 196616 | tf_op jit(solution)/shard_map/ppermute | solution.py:248
  47.4 7.0 %collective-permute-start.18 = (f32[32,128]{1,0:T(8,128)S(1)}, f32[32,128]{1,0:T(8,128)S(1)}, u32[]{:S(2)}, u32[]{:S(2)}) collective-permute-start(f32[32,128]{1,0:T(8,128)S(1)} %add.21.before_ref.own_ref), channel_id=1, source_target_pairs={{0,2},{1,3},{2,0},{3,1},{4,6},{5,7},{6,4},{7,5},{8,10},{9,11},{10,... | collective-permute-start | bytes 49160 | tf_op jit(solution)/shard_map/ppermute | solution.py:248
  51.3 6.0 %collective-permute-start.17 = (f32[32,512]{1,0:T(8,128)S(1)}, f32[32,512]{1,0:T(8,128)S(1)}, u32[]{:S(2)}, u32[]{:S(2)}) collective-permute-start(f32[32,512]{1,0:T(8,128)S(1)} %add.23.own_ref), channel_id=1, source_target_pairs={{0,16},{4,20},{8,24},{12,28},{16,0},{20,4},{24,8},{28,12},{1,17},{... | collective-permute-start | bytes 196616 | tf_op jit(solution)/shard_map/ppermute | solution.py:248
  57.5 5.4 %collective-permute-start.21 = (f32[32,512]{1,0:T(8,128)S(1)}, f32[32,512]{1,0:T(8,128)S(1)}, u32[]{:S(2)}, u32[]{:S(2)}) collective-permute-start(f32[32,512]{1,0:T(8,128)S(1)} %total.5.chunk_ref.refs_0_), channel_id=1, source_target_pairs={{0,12},{4,8},{8,4},{12,0},{16,28},{20,24},{24,20},{28,16},{1,13},{... | collective-permute-start | bytes 196616 | tf_op jit(solution)/shard_map/ppermute | solution.py:248
  58.9 4.6 %collective-permute-start.20 = (f32[32,512]{1,0:T(8,128)S(1)}, f32[32,512]{1,0:T(8,128)S(1)}, u32[]{:S(2)}, u32[]{:S(2)}) collective-permute-start(f32[32,512]{1,0:T(8,128)S(1)} %total.5.chunk_ref.refs_0_), channel_id=1, source_target_pairs={{0,4},{4,0},{8,12},{12,8},{16,20},{20,16},{24,28},{28,24},{1,5},{5... | collective-permute-start | bytes 196616 | tf_op jit(solution)/shard_map/ppermute | solution.py:248
  66.2 4.9 %collective-permute-start.23 = (f32[32,768]{1,0:T(8,128)S(1)}, f32[32,768]{1,0:T(8,128)S(1)}, u32[]{:S(2)}, u32[]{:S(2)}) collective-permute-start(f32[32,768]{1,0:T(8,128)S(1)} %add.24.own_ref), channel_id=1, source_target_pairs={{0,2},{1,3},{2,0},{3,1},{4,6},{5,7},{6,4},{7,5},{8,10},{9,11},{10,... | collective-permute-start | bytes 294920 | tf_op jit(solution)/shard_map/ppermute | solution.py:248
  73.0 5.8 %collective-permute-start.26 = (f32[32,512]{1,0:T(8,128)S(1)}, f32[32,512]{1,0:T(8,128)S(1)}, u32[]{:S(2)}, u32[]{:S(2)}) collective-permute-start(f32[32,512]{1,0:T(8,128)S(1)} %get-tuple-element.66), channel_id=1, source_target_pairs={{0,12},{4,8},{8,4},{12,0},{16,28},{20,24},{24,20},{28,16},{1,13},{... | collective-permute-start | bytes 196616 | tf_op jit(solution)/shard_map/ppermute | solution.py:248
  74.2 4.6 %collective-permute-start.27 = (f32[32,512]{1,0:T(8,128)S(1)}, f32[32,512]{1,0:T(8,128)S(1)}, u32[]{:S(2)}, u32[]{:S(2)}) collective-permute-start(f32[32,512]{1,0:T(8,128)S(1)} %get-tuple-element.67), channel_id=1, source_target_pairs={{0,8},{4,12},{8,0},{12,4},{16,24},{20,28},{24,16},{28,20},{1,9},{5... | collective-permute-start | bytes 196616 | tf_op jit(solution)/shard_map/ppermute | solution.py:248
  75.3 4.3 %collective-permute-start.28 = (f32[32,512]{1,0:T(8,128)S(1)}, f32[32,512]{1,0:T(8,128)S(1)}, u32[]{:S(2)}, u32[]{:S(2)}) collective-permute-start(f32[32,512]{1,0:T(8,128)S(1)} %get-tuple-element.68), channel_id=1, source_target_pairs={{0,4},{4,0},{8,12},{12,8},{16,20},{20,16},{24,28},{28,24},{1,5},{5... | collective-permute-start | bytes 196616 | tf_op jit(solution)/shard_map/ppermute | solution.py:248
  76.6 6.0 %collective-permute-start.30 = (f32[32,128]{1,0:T(8,128)S(1)}, f32[32,128]{1,0:T(8,128)S(1)}, u32[]{:S(2)}, u32[]{:S(2)}) collective-permute-start(f32[32,128]{1,0:T(8,128)S(1)} %add.25.before_ref.own_ref), channel_id=1, source_target_pairs={{0,2},{1,3},{2,0},{3,1},{4,6},{5,7},{6,4},{7,5},{8,10},{9,11},{10,... | collective-permute-start | bytes 49160 | tf_op jit(solution)/shard_map/ppermute | solution.py:248
  79.6 6.0 %collective-permute-start.29 = (f32[32,512]{1,0:T(8,128)S(1)}, f32[32,512]{1,0:T(8,128)S(1)}, u32[]{:S(2)}, u32[]{:S(2)}) collective-permute-start(f32[32,512]{1,0:T(8,128)S(1)} %add.27.own_ref), channel_id=1, source_target_pairs={{0,16},{4,20},{8,24},{12,28},{16,0},{20,4},{24,8},{28,12},{1,17},{... | collective-permute-start | bytes 196616 | tf_op jit(solution)/shard_map/ppermute | solution.py:248
  85.8 5.2 %collective-permute-start.33 = (f32[32,512]{1,0:T(8,128)S(1)}, f32[32,512]{1,0:T(8,128)S(1)}, u32[]{:S(2)}, u32[]{:S(2)}) collective-permute-start(f32[32,512]{1,0:T(8,128)S(1)} %total.6.chunk_ref.refs_0_), channel_id=1, source_target_pairs={{0,12},{4,8},{8,4},{12,0},{16,28},{20,24},{24,20},{28,16},{1,13},{... | collective-permute-start | bytes 196616 | tf_op jit(solution)/shard_map/ppermute | solution.py:248
  87.2 4.6 %collective-permute-start.32 = (f32[32,512]{1,0:T(8,128)S(1)}, f32[32,512]{1,0:T(8,128)S(1)}, u32[]{:S(2)}, u32[]{:S(2)}) collective-permute-start(f32[32,512]{1,0:T(8,128)S(1)} %total.6.chunk_ref.refs_0_), channel_id=1, source_target_pairs={{0,4},{4,0},{8,12},{12,8},{16,20},{20,16},{24,28},{28,24},{1,5},{5... | collective-permute-start | bytes 196616 | tf_op jit(solution)/shard_map/ppermute | solution.py:248
  87.9 4.5 %collective-permute-start.31 = (f32[32,512]{1,0:T(8,128)S(1)}, f32[32,512]{1,0:T(8,128)S(1)}, u32[]{:S(2)}, u32[]{:S(2)}) collective-permute-start(f32[32,512]{1,0:T(8,128)S(1)} %total.6.chunk_ref.refs_0_), channel_id=1, source_target_pairs={{0,8},{4,12},{8,0},{12,4},{16,24},{20,28},{24,16},{28,20},{1,9},{5... | collective-permute-start | bytes 196616 | tf_op jit(solution)/shard_map/ppermute | solution.py:248
  94.2 4.9 %collective-permute-start.35 = (f32[32,768]{1,0:T(8,128)S(1)}, f32[32,768]{1,0:T(8,128)S(1)}, u32[]{:S(2)}, u32[]{:S(2)}) collective-permute-start(f32[32,768]{1,0:T(8,128)S(1)} %add.28.own_ref), channel_id=1, source_target_pairs={{0,2},{1,3},{2,0},{3,1},{4,6},{5,7},{6,4},{7,5},{8,10},{9,11},{10,... | collective-permute-start | bytes 294920 | tf_op jit(solution)/shard_map/ppermute | solution.py:248
  101.0 5.7 %collective-permute-start.38 = (f32[32,512]{1,0:T(8,128)S(1)}, f32[32,512]{1,0:T(8,128)S(1)}, u32[]{:S(2)}, u32[]{:S(2)}) collective-permute-start(f32[32,512]{1,0:T(8,128)S(1)} %get-tuple-element.75), channel_id=1, source_target_pairs={{0,12},{4,8},{8,4},{12,0},{16,28},{20,24},{24,20},{28,16},{1,13},{... | collective-permute-start | bytes 196616 | tf_op jit(solution)/shard_map/ppermute | solution.py:248
  102.8 4.6 %collective-permute-start.39 = (f32[32,512]{1,0:T(8,128)S(1)}, f32[32,512]{1,0:T(8,128)S(1)}, u32[]{:S(2)}, u32[]{:S(2)}) collective-permute-start(f32[32,512]{1,0:T(8,128)S(1)} %get-tuple-element.76), channel_id=1, source_target_pairs={{0,8},{4,12},{8,0},{12,4},{16,24},{20,28},{24,16},{28,20},{1,9},{5... | collective-permute-start | bytes 196616 | tf_op jit(solution)/shard_map/ppermute | solution.py:248
  104.6 5.8 %collective-permute-start.42 = (f32[32,128]{1,0:T(8,128)S(1)}, f32[32,128]{1,0:T(8,128)S(1)}, u32[]{:S(2)}, u32[]{:S(2)}) collective-permute-start(f32[32,128]{1,0:T(8,128)S(1)} %add.29.before_ref.own_ref), channel_id=1, source_target_pairs={{0,2},{1,3},{2,0},{3,1},{4,6},{5,7},{6,4},{7,5},{8,10},{9,11},{10,... | collective-permute-start | bytes 49160 | tf_op jit(solution)/shard_map/ppermute | solution.py:248
  108.0 5.9 %collective-permute-start.41 = (f32[32,512]{1,0:T(8,128)S(1)}, f32[32,512]{1,0:T(8,128)S(1)}, u32[]{:S(2)}, u32[]{:S(2)}) collective-permute-start(f32[32,512]{1,0:T(8,128)S(1)} %add.31.own_ref), channel_id=1, source_target_pairs={{0,16},{4,20},{8,24},{12,28},{16,0},{20,4},{24,8},{28,12},{1,17},{... | collective-permute-start | bytes 196616 | tf_op jit(solution)/shard_map/ppermute | solution.py:248
  114.1 5.3 %collective-permute-start.45 = (f32[32,512]{1,0:T(8,128)S(1)}, f32[32,512]{1,0:T(8,128)S(1)}, u32[]{:S(2)}, u32[]{:S(2)}) collective-permute-start(f32[32,512]{1,0:T(8,128)S(1)} %total.7.chunk_ref.refs_0_), channel_id=1, source_target_pairs={{0,12},{4,8},{8,4},{12,0},{16,28},{20,24},{24,20},{28,16},{1,13},{... | collective-permute-start | bytes 196616 | tf_op jit(solution)/shard_map/ppermute | solution.py:248
  115.0 5.0 %collective-permute-start.44 = (f32[32,512]{1,0:T(8,128)S(1)}, f32[32,512]{1,0:T(8,128)S(1)}, u32[]{:S(2)}, u32[]{:S(2)}) collective-permute-start(f32[32,512]{1,0:T(8,128)S(1)} %total.7.chunk_ref.refs_0_), channel_id=1, source_target_pairs={{0,4},{4,0},{8,12},{12,8},{16,20},{20,16},{24,28},{28,24},{1,5},{5... | collective-permute-start | bytes 196616 | tf_op jit(solution)/shard_map/ppermute | solution.py:248
  124.8 5.1 %collective-permute-start.48 = (bf16[32,1536]{1,0:T(8,128)(2,1)S(1)}, bf16[32,1536]{1,0:T(8,128)(2,1)S(1)}, u32[]{:S(2)}, u32[]{:S(2)}) collective-permute-start(bf16[32,1536]{1,0:T(8,128)(2,1)S(1)} %add.33.own_ref), channel_id=1, source_target_pairs={{0,2},{1,3},{2,0},{3,1},{4,6},{5,7},{6,4},{7,5},{8,10},{9,11},{10,... | collective-permute-start | bytes 294920 | tf_op jit(solution)/shard_map/ppermute | solution.py:248
  (19 other events, 40.9 us)

commit v8 on v7

--- a/solution.py
+++ b/solution.py
@@ -11,7 +11,7 @@
 PEERS = 4
 LANES = 128
 EXTRA = 8
-SCATTER = (0, 3, 2, 1)
+SCATTER = (0, 3, 1, 2)
 GATHER = (0, 3, 1, 2)
 TERMS = 3
 LONG = pl.CostEstimate(flops=2**34, bytes_accessed=0, transcendentals=0)
@@ -229,6 +229,10 @@
 def normalised_total_kernel(own_ref, got_ref, lower_ref, out_ref):
     value = own_ref[...] + got_ref[...]
     out_ref[...] = jnp.dot(lower_ref[...], value, preferred_element_type=F32, precision=HIGHEST)
+
+
+def ordered_copy_kernel(value_ref, before_ref, out_ref):
+    out_ref[...] = value_ref[...]
 
 
 def ordered_add_kernel(own_ref, got_ref, before_ref, out_ref):
@@ -307,18 +311,21 @@
         images = share(image, "tok")
         means = means or images
         ranked = [means[GATHER.index(part)] for part in SCATTER]
-        gram = call(gram_kernel, [side], "gram")(*images)[0]
-        grams = (gram, swap(gram, "feat", 1))
         before = []
         for part, image, mean in zip(GATHER, images, means):
             operands = [image, mean, rows, *before]
             if part != GATHER[-1]:
                 kernel = functools.partial(projection_kernel, part, "all")
                 before = call(kernel, [whole], "projection", cost=SHORT)(*operands)
+            if part == GATHER[1]:
+                ready = before if last else []
+        gram = call(gram_kernel, [side], "gram")(*images, *ready)[0]
+        grams = (gram, swap(gram, "feat", 1))
         if last:
             gram = add(*grams)
             kernel = functools.partial(projection_kernel, part, "all")
-            own = call(kernel, [whole], "projection")(*operands, gram)[0]
+            own = call(kernel, [whole], "projection", cost=SHORT)(*operands)[0]
+            own = call(ordered_copy_kernel, [whole], "copy")(own, gram)[0]
             for distance in distances("feat", 1):
                 terms = (own, swap(own, "feat", distance))
                 if distance != last_feat:

time: 131 us -> 130 us (level)
  starting transfers between devices: 56.1 us -> 53.7 us
    ppermute x50, starting transfers between devices: 56.1 us -> 53.7 us  [swap(): return lax.ppermute(value, axis, [(i, i ^ distance) for i in range(size)])]
    ppermute x50, waiting for transfers between devices: 38.1 us -> 39.4 us  [swap(): return lax.ppermute(value, axis, [(i, i ^ distance) for i in range(size)])]
    pallas_call x65 -> x66, Pallas kernels: 35.7 us -> 35.7 us  [run(): pl.pallas_call(kernel, out_shape=[jax.ShapeDtypeStruct(shape, dtype) for...]
  transfers between devices with their start and end apart: 50 -> 50, of which waited for: 38 -> 34; matrix products, arithmetic and copies ran while one was open for 0% -> 0% of each run, Pallas kernels for 20% -> 20%
where the time goes in v8:
time: 130 us
  starting transfers between devices  53.7 us (41%)
  waiting for transfers between devices  39.4 us (30%)
  Pallas kernels  35.7 us (27%)
    ppermute x50, starting transfers between devices, swap(): return lax.ppermute(value, axis, [(i, i ^ distance) for i in range(size)])  53.7 us
    ppermute x50, waiting for transfers between devices, swap(): return lax.ppermute(value, axis, [(i, i ^ distance) for i in range(size)])  39.4 us
    pallas_call x66, Pallas kernels, run(): pl.pallas_call(kernel, out_shape=[jax.ShapeDtypeStruct(shape, dtype) for...  35.7 us
  transfers between devices with their start and end apart: 50, of which 34 were waited for; matrix products, arithmetic and copies ran while one was open for 0% of the time, Pallas kernels for 20%

profile of v8, /device:TPU:0, one launch (start us, length us, event | category | flops | bytes accessed | tf_op | source)
XLA Modules:
  0.0 129.9 jit_solution(15700036093188303292)
XLA Ops:
  0.6 2.0 %fetch.1.ready_ref = bf16[1536,2048]{1,0:T(8,128)(2,1)S(1)} custom-call(bf16[1536,2048]{1,0:T(8,128)(2,1)} %rows_hbm.3), custom_call_target="tpu_custom_call" | custom-call | tf_op jit(solution)/shard_map/fetch/pallas_call | solution.py:29
  2.6 1.9 %sent_projection.4 = (f32[32,768]{1,0:T(8,128)S(1)}, bf16[1536,2048]{1,0:T(8,128)(2,1)S(1)}) custom-call(f32[32,2048]{1,0:T(8,128)S(1)} %copy-done, bf16[1536,2048]{1,0:T(8,128)(2,1)} %rows_hbm.3, bf16[1536,2048]{1,0:T(8,128)(2,1)S(1)} %fetch.1.ready_ref), custom_call_target="tpu_custom_call", output_to_operand_aliasing={{1}: (2, {})} | custom-call | tf_op jit(solution)/shard_map/sent_projection/pallas_call | solution.py:29
  6.1 2.8 %collective-permute-start.1 = (f32[32,768]{1,0:T(8,128)S(1)}, f32[32,768]{1,0:T(8,128)S(1)}, u32[]{:S(2)}, u32[]{:S(2)}) collective-permute-start(f32[32,768]{1,0:T(8,128)S(1)} %add.17.refs_0_), channel_id=1, source_target_pairs={{0,2},{1,3},{2,0},{3,1},{4,6},{5,7},{6,4},{7,5},{8,10},{9,11},{10,... | collective-permute-start | bytes 294920 | tf_op jit(solution)/shard_map/ppermute | solution.py:252
  8.9 3.3 %collective-permute-done.1.refs_1_ = f32[32,768]{1,0:T(8,128)S(1)} collective-permute-done((f32[32,768]{1,0:T(8,128)S(1)}, f32[32,768]{1,0:T(8,128)S(1)}, u32[]{:S(2)}, u32[]{:S(2)}) %collective-permute-start.1) | collective-permute-done | bytes 98336 | tf_op jit(solution)/shard_map/ppermute | solution.py:252
  14.1 2.8 %collective-permute-start.3 = (f32[40,512]{1,0:T(8,128)S(1)}, f32[40,512]{1,0:T(8,128)S(1)}, u32[]{:S(2)}, u32[]{:S(2)}) collective-permute-start(f32[40,512]{1,0:T(8,128)S(1)} %get-tuple-element.48), channel_id=1, source_target_pairs={{0,12},{4,8},{8,4},{12,0},{16,28},{20,24},{24,20},{28,16},{1,13},{... | collective-permute-start | bytes 245768 | tf_op jit(solution)/shard_map/ppermute | solution.py:252
  18.0 1.9 %collective-permute-done.3.refs_1_ = f32[40,512]{1,0:T(8,128)S(1)} collective-permute-done((f32[40,512]{1,0:T(8,128)S(1)}, f32[40,512]{1,0:T(8,128)S(1)}, u32[]{:S(2)}, u32[]{:S(2)}) %collective-permute-start.3) | collective-permute-done | bytes 81952 | tf_op jit(solution)/shard_map/ppermute | solution.py:252
  19.8 1.7 %collective-permute-done.4.refs_2_ = f32[40,512]{1,0:T(8,128)S(1)} collective-permute-done((f32[40,512]{1,0:T(8,128)S(1)}, f32[40,512]{1,0:T(8,128)S(1)}, u32[]{:S(2)}, u32[]{:S(2)}) %collective-permute-start.4) | collective-permute-done | bytes 81952 | tf_op jit(solution)/shard_map/ppermute | solution.py:252
  22.0 2.6 %collective-permute-start.6 = (f32[40,512]{1,0:T(8,128)S(1)}, f32[40,512]{1,0:T(8,128)S(1)}, u32[]{:S(2)}, u32[]{:S(2)}) collective-permute-start(f32[40,512]{1,0:T(8,128)S(1)} %add.19.own_ref), channel_id=1, source_target_pairs={{0,16},{4,20},{8,24},{12,28},{16,0},{20,4},{24,8},{28,12},{1,17},{... | collective-permute-start | bytes 245768 | tf_op jit(solution)/shard_map/ppermute | solution.py:252
  24.6 4.3 %collective-permute-done.6.got_ref = f32[40,512]{1,0:T(8,128)S(1)} collective-permute-done((f32[40,512]{1,0:T(8,128)S(1)}, f32[40,512]{1,0:T(8,128)S(1)}, u32[]{:S(2)}, u32[]{:S(2)}) %collective-permute-start.6) | collective-permute-done | bytes 81952 | tf_op jit(solution)/shard_map/ppermute | solution.py:252
  30.3 2.1 %collective-permute-start.7 = (f32[40,512]{1,0:T(8,128)S(1)}, f32[40,512]{1,0:T(8,128)S(1)}, u32[]{:S(2)}, u32[]{:S(2)}) collective-permute-start(f32[40,512]{1,0:T(8,128)S(1)} %total.4.chunk_ref.mean_ref.refs_0_), channel_id=1, source_target_pairs={{0,8},{4,12},{8,0},{12,4},{16,24},{20,28},{24,16},{28,20},{1,9},{5... | collective-permute-start | bytes 245768 | tf_op jit(solution)/shard_map/ppermute | solution.py:252
  37.4 1.6 %collective-permute-start.11 = (f32[32,768]{1,0:T(8,128)S(1)}, f32[32,768]{1,0:T(8,128)S(1)}, u32[]{:S(2)}, u32[]{:S(2)}) collective-permute-start(f32[32,768]{1,0:T(8,128)S(1)} %add.20.own_ref), channel_id=1, source_target_pairs={{0,2},{1,3},{2,0},{3,1},{4,6},{5,7},{6,4},{7,5},{8,10},{9,11},{10,... | collective-permute-start | bytes 294920 | tf_op jit(solution)/shard_map/ppermute | solution.py:252
  40.5 1.8 %collective-permute-done.11.got_ref = f32[32,768]{1,0:T(8,128)S(1)} collective-permute-done((f32[32,768]{1,0:T(8,128)S(1)}, f32[32,768]{1,0:T(8,128)S(1)}, u32[]{:S(2)}, u32[]{:S(2)}) %collective-permute-start.11) | collective-permute-done | bytes 98336 | tf_op jit(solution)/shard_map/ppermute | solution.py:252
  44.2 1.5 %collective-permute-start.14 = (f32[32,512]{1,0:T(8,128)S(1)}, f32[32,512]{1,0:T(8,128)S(1)}, u32[]{:S(2)}, u32[]{:S(2)}) collective-permute-start(f32[32,512]{1,0:T(8,128)S(1)} %get-tuple-element.57), channel_id=1, source_target_pairs={{0,12},{4,8},{8,4},{12,0},{16,28},{20,24},{24,20},{28,16},{1,13},{... | collective-permute-start | bytes 196616 | tf_op jit(solution)/shard_map/ppermute | solution.py:252
  47.8 1.5 %collective-permute-start.18 = (f32[32,128]{1,0:T(8,128)S(1)}, f32[32,128]{1,0:T(8,128)S(1)}, u32[]{:S(2)}, u32[]{:S(2)}) collective-permute-start(f32[32,128]{1,0:T(8,128)S(1)} %add.21.before_ref.own_ref), channel_id=1, source_target_pairs={{0,2},{1,3},{2,0},{3,1},{4,6},{5,7},{6,4},{7,5},{8,10},{9,11},{10,... | collective-permute-start | bytes 49160 | tf_op jit(solution)/shard_map/ppermute | solution.py:252
  51.2 2.2 %collective-permute-start.17 = (f32[32,512]{1,0:T(8,128)S(1)}, f32[32,512]{1,0:T(8,128)S(1)}, u32[]{:S(2)}, u32[]{:S(2)}) collective-permute-start(f32[32,512]{1,0:T(8,128)S(1)} %add.23.own_ref), channel_id=1, source_target_pairs={{0,16},{4,20},{8,24},{12,28},{16,0},{20,4},{24,8},{28,12},{1,17},{... | collective-permute-start | bytes 196616 | tf_op jit(solution)/shard_map/ppermute | solution.py:252
  53.4 2.9 %inverse_factor.4.lower_ref = f32[32,32]{1,0:T(8,128)S(1)} custom-call(f32[32,128]{1,0:T(8,128)S(1)} %add.21.before_ref.own_ref, f32[32,128]{1,0:T(8,128)S(1)} %collective-permute-done.18.got_ref), custom_call_target="tpu_custom_call" | custom-call | flops 17179869184 | tf_op jit(solution)/shard_map/inverse_factor/pallas_call | solution.py:29
  59.2 1.7 %collective-permute-start.19 = (f32[32,512]{1,0:T(8,128)S(1)}, f32[32,512]{1,0:T(8,128)S(1)}, u32[]{:S(2)}, u32[]{:S(2)}) collective-permute-start(f32[32,512]{1,0:T(8,128)S(1)} %total.5.chunk_ref.refs_0_), channel_id=1, source_target_pairs={{0,8},{4,12},{8,0},{12,4},{16,24},{20,28},{24,16},{28,20},{1,9},{5... | collective-permute-start | bytes 196616 | tf_op jit(solution)/shard_map/ppermute | solution.py:252
  65.6 1.6 %collective-permute-start.23 = (f32[32,768]{1,0:T(8,128)S(1)}, f32[32,768]{1,0:T(8,128)S(1)}, u32[]{:S(2)}, u32[]{:S(2)}) collective-permute-start(f32[32,768]{1,0:T(8,128)S(1)} %add.24.own_ref), channel_id=1, source_target_pairs={{0,2},{1,3},{2,0},{3,1},{4,6},{5,7},{6,4},{7,5},{8,10},{9,11},{10,... | collective-permute-start | bytes 294920 | tf_op jit(solution)/shard_map/ppermute | solution.py:252
  68.7 1.8 %collective-permute-done.23.got_ref = f32[32,768]{1,0:T(8,128)S(1)} collective-permute-done((f32[32,768]{1,0:T(8,128)S(1)}, f32[32,768]{1,0:T(8,128)S(1)}, u32[]{:S(2)}, u32[]{:S(2)}) %collective-permute-start.23) | collective-permute-done | bytes 98336 | tf_op jit(solution)/shard_map/ppermute | solution.py:252
  72.4 1.6 %collective-permute-start.26 = (f32[32,512]{1,0:T(8,128)S(1)}, f32[32,512]{1,0:T(8,128)S(1)}, u32[]{:S(2)}, u32[]{:S(2)}) collective-permute-start(f32[32,512]{1,0:T(8,128)S(1)} %get-tuple-element.66), channel_id=1, source_target_pairs={{0,12},{4,8},{8,4},{12,0},{16,28},{20,24},{24,20},{28,16},{1,13},{... | collective-permute-start | bytes 196616 | tf_op jit(solution)/shard_map/ppermute | solution.py:252
  76.0 1.5 %collective-permute-start.30 = (f32[32,128]{1,0:T(8,128)S(1)}, f32[32,128]{1,0:T(8,128)S(1)}, u32[]{:S(2)}, u32[]{:S(2)}) collective-permute-start(f32[32,128]{1,0:T(8,128)S(1)} %add.25.before_ref.own_ref), channel_id=1, source_target_pairs={{0,2},{1,3},{2,0},{3,1},{4,6},{5,7},{6,4},{7,5},{8,10},{9,11},{10,... | collective-permute-start | bytes 49160 | tf_op jit(solution)/shard_map/ppermute | solution.py:252
  79.5 2.2 %collective-permute-start.29 = (f32[32,512]{1,0:T(8,128)S(1)}, f32[32,512]{1,0:T(8,128)S(1)}, u32[]{:S(2)}, u32[]{:S(2)}) collective-permute-start(f32[32,512]{1,0:T(8,128)S(1)} %add.27.own_ref), channel_id=1, source_target_pairs={{0,16},{4,20},{8,24},{12,28},{16,0},{20,4},{24,8},{28,12},{1,17},{... | collective-permute-start | bytes 196616 | tf_op jit(solution)/shard_map/ppermute | solution.py:252
  81.7 2.9 %inverse_factor.5.lower_ref = f32[32,32]{1,0:T(8,128)S(1)} custom-call(f32[32,128]{1,0:T(8,128)S(1)} %add.25.before_ref.own_ref, f32[32,128]{1,0:T(8,128)S(1)} %collective-permute-done.30.got_ref), custom_call_target="tpu_custom_call" | custom-call | flops 17179869184 | tf_op jit(solution)/shard_map/inverse_factor/pallas_call | solution.py:29
  87.5 1.7 %collective-permute-start.31 = (f32[32,512]{1,0:T(8,128)S(1)}, f32[32,512]{1,0:T(8,128)S(1)}, u32[]{:S(2)}, u32[]{:S(2)}) collective-permute-start(f32[32,512]{1,0:T(8,128)S(1)} %total.6.chunk_ref.refs_0_), channel_id=1, source_target_pairs={{0,8},{4,12},{8,0},{12,4},{16,24},{20,28},{24,16},{28,20},{1,9},{5... | collective-permute-start | bytes 196616 | tf_op jit(solution)/shard_map/ppermute | solution.py:252
  94.0 1.6 %collective-permute-start.35 = (f32[32,768]{1,0:T(8,128)S(1)}, f32[32,768]{1,0:T(8,128)S(1)}, u32[]{:S(2)}, u32[]{:S(2)}) collective-permute-start(f32[32,768]{1,0:T(8,128)S(1)} %add.28.own_ref), channel_id=1, source_target_pairs={{0,2},{1,3},{2,0},{3,1},{4,6},{5,7},{6,4},{7,5},{8,10},{9,11},{10,... | collective-permute-start | bytes 294920 | tf_op jit(solution)/shard_map/ppermute | solution.py:252
  97.1 1.8 %collective-permute-done.35.got_ref = f32[32,768]{1,0:T(8,128)S(1)} collective-permute-done((f32[32,768]{1,0:T(8,128)S(1)}, f32[32,768]{1,0:T(8,128)S(1)}, u32[]{:S(2)}, u32[]{:S(2)}) %collective-permute-start.35) | collective-permute-done | bytes 98336 | tf_op jit(solution)/shard_map/ppermute | solution.py:252
  104.4 1.5 %collective-permute-start.42 = (f32[32,128]{1,0:T(8,128)S(1)}, f32[32,128]{1,0:T(8,128)S(1)}, u32[]{:S(2)}, u32[]{:S(2)}) collective-permute-start(f32[32,128]{1,0:T(8,128)S(1)} %add.29.before_ref.own_ref), channel_id=1, source_target_pairs={{0,2},{1,3},{2,0},{3,1},{4,6},{5,7},{6,4},{7,5},{8,10},{9,11},{10,... | collective-permute-start | bytes 49160 | tf_op jit(solution)/shard_map/ppermute | solution.py:252
  107.7 2.3 %collective-permute-start.41 = (f32[32,512]{1,0:T(8,128)S(1)}, f32[32,512]{1,0:T(8,128)S(1)}, u32[]{:S(2)}, u32[]{:S(2)}) collective-permute-start(f32[32,512]{1,0:T(8,128)S(1)} %add.31.own_ref), channel_id=1, source_target_pairs={{0,16},{4,20},{8,24},{12,28},{16,0},{20,4},{24,8},{28,12},{1,17},{... | collective-permute-start | bytes 196616 | tf_op jit(solution)/shard_map/ppermute | solution.py:252
  110.1 2.9 %inverse_factor.6.lower_ref = f32[32,32]{1,0:T(8,128)S(1)} custom-call(f32[32,128]{1,0:T(8,128)S(1)} %add.29.before_ref.own_ref, f32[32,128]{1,0:T(8,128)S(1)} %collective-permute-done.42.got_ref), custom_call_target="tpu_custom_call" | custom-call | flops 17179869184 | tf_op jit(solution)/shard_map/inverse_factor/pallas_call | solution.py:29
  115.7 1.7 %collective-permute-start.43 = (f32[32,512]{1,0:T(8,128)S(1)}, f32[32,512]{1,0:T(8,128)S(1)}, u32[]{:S(2)}, u32[]{:S(2)}) collective-permute-start(f32[32,512]{1,0:T(8,128)S(1)} %total.7.chunk_ref.refs_0_), channel_id=1, source_target_pairs={{0,8},{4,12},{8,0},{12,4},{16,24},{20,28},{24,16},{28,20},{1,9},{5... | collective-permute-start | bytes 196616 | tf_op jit(solution)/shard_map/ppermute | solution.py:252
  122.2 1.5 %collective-permute-start.49 = (f32[32,128]{1,0:T(8,128)S(1)}, f32[32,128]{1,0:T(8,128)S(1)}, u32[]{:S(2)}, u32[]{:S(2)}) collective-permute-start(f32[32,128]{1,0:T(8,128)S(1)} %add.32.before_ref.own_ref), channel_id=1, source_target_pairs={{0,2},{1,3},{2,0},{3,1},{4,6},{5,7},{6,4},{7,5},{8,10},{9,11},{10,... | collective-permute-start | bytes 49160 | tf_op jit(solution)/shard_map/ppermute | solution.py:252
  125.9 2.9 %inverse_factor.7.lower_ref = f32[32,32]{1,0:T(8,128)S(1)} custom-call(f32[32,128]{1,0:T(8,128)S(1)} %add.32.before_ref.own_ref, f32[32,128]{1,0:T(8,128)S(1)} %collective-permute-done.49.got_ref), custom_call_target="tpu_custom_call" | custom-call | flops 17179869184 | tf_op jit(solution)/shard_map/inverse_factor/pallas_call | solution.py:29
  (136 shorter events, 61.3 us)
Async XLA Ops:
  6.1 6.0 %collective-permute-start.1 = (f32[32,768]{1,0:T(8,128)S(1)}, f32[32,768]{1,0:T(8,128)S(1)}, u32[]{:S(2)}, u32[]{:S(2)}) collective-permute-start(f32[32,768]{1,0:T(8,128)S(1)} %add.17.refs_0_), channel_id=1, source_target_pairs={{0,2},{1,3},{2,0},{3,1},{4,6},{5,7},{6,4},{7,5},{8,10},{9,11},{10,... | collective-permute-start | bytes 294920 | tf_op jit(solution)/shard_map/ppermute | solution.py:252
  14.1 5.7 %collective-permute-start.3 = (f32[40,512]{1,0:T(8,128)S(1)}, f32[40,512]{1,0:T(8,128)S(1)}, u32[]{:S(2)}, u32[]{:S(2)}) collective-permute-start(f32[40,512]{1,0:T(8,128)S(1)} %get-tuple-element.48), channel_id=1, source_target_pairs={{0,12},{4,8},{8,4},{12,0},{16,28},{20,24},{24,20},{28,16},{1,13},{... | collective-permute-start | bytes 245768 | tf_op jit(solution)/shard_map/ppermute | solution.py:252
  17.0 4.5 %collective-permute-start.4 = (f32[40,512]{1,0:T(8,128)S(1)}, f32[40,512]{1,0:T(8,128)S(1)}, u32[]{:S(2)}, u32[]{:S(2)}) collective-permute-start(f32[40,512]{1,0:T(8,128)S(1)} %get-tuple-element.49), channel_id=1, source_target_pairs={{0,4},{4,0},{8,12},{12,8},{16,20},{20,16},{24,28},{28,24},{1,5},{5... | collective-permute-start | bytes 245768 | tf_op jit(solution)/shard_map/ppermute | solution.py:252
  17.5 4.4 %collective-permute-start.5 = (f32[40,512]{1,0:T(8,128)S(1)}, f32[40,512]{1,0:T(8,128)S(1)}, u32[]{:S(2)}, u32[]{:S(2)}) collective-permute-start(f32[40,512]{1,0:T(8,128)S(1)} %get-tuple-element.50), channel_id=1, source_target_pairs={{0,8},{4,12},{8,0},{12,4},{16,24},{20,28},{24,16},{28,20},{1,9},{5... | collective-permute-start | bytes 245768 | tf_op jit(solution)/shard_map/ppermute | solution.py:252
  22.0 6.9 %collective-permute-start.6 = (f32[40,512]{1,0:T(8,128)S(1)}, f32[40,512]{1,0:T(8,128)S(1)}, u32[]{:S(2)}, u32[]{:S(2)}) collective-permute-start(f32[40,512]{1,0:T(8,128)S(1)} %add.19.own_ref), channel_id=1, source_target_pairs={{0,16},{4,20},{8,24},{12,28},{16,0},{20,4},{24,8},{28,12},{1,17},{... | collective-permute-start | bytes 245768 | tf_op jit(solution)/shard_map/ppermute | solution.py:252
  28.9 5.4 %collective-permute-start.9 = (f32[40,512]{1,0:T(8,128)S(1)}, f32[40,512]{1,0:T(8,128)S(1)}, u32[]{:S(2)}, u32[]{:S(2)}) collective-permute-start(f32[40,512]{1,0:T(8,128)S(1)} %total.4.chunk_ref.mean_ref.refs_0_), channel_id=1, source_target_pairs={{0,12},{4,8},{8,4},{12,0},{16,28},{20,24},{24,20},{28,16},{1,13},{... | collective-permute-start | bytes 245768 | tf_op jit(solution)/shard_map/ppermute | solution.py:252
  29.6 5.4 %collective-permute-start.8 = (f32[40,512]{1,0:T(8,128)S(1)}, f32[40,512]{1,0:T(8,128)S(1)}, u32[]{:S(2)}, u32[]{:S(2)}) collective-permute-start(f32[40,512]{1,0:T(8,128)S(1)} %total.4.chunk_ref.mean_ref.refs_0_), channel_id=1, source_target_pairs={{0,4},{4,0},{8,12},{12,8},{16,20},{20,16},{24,28},{28,24},{1,5},{5... | collective-permute-start | bytes 245768 | tf_op jit(solution)/shard_map/ppermute | solution.py:252
  30.3 5.3 %collective-permute-start.7 = (f32[40,512]{1,0:T(8,128)S(1)}, f32[40,512]{1,0:T(8,128)S(1)}, u32[]{:S(2)}, u32[]{:S(2)}) collective-permute-start(f32[40,512]{1,0:T(8,128)S(1)} %total.4.chunk_ref.mean_ref.refs_0_), channel_id=1, source_target_pairs={{0,8},{4,12},{8,0},{12,4},{16,24},{20,28},{24,16},{28,20},{1,9},{5... | collective-permute-start | bytes 245768 | tf_op jit(solution)/shard_map/ppermute | solution.py:252
  37.4 4.9 %collective-permute-start.11 = (f32[32,768]{1,0:T(8,128)S(1)}, f32[32,768]{1,0:T(8,128)S(1)}, u32[]{:S(2)}, u32[]{:S(2)}) collective-permute-start(f32[32,768]{1,0:T(8,128)S(1)} %add.20.own_ref), channel_id=1, source_target_pairs={{0,2},{1,3},{2,0},{3,1},{4,6},{5,7},{6,4},{7,5},{8,10},{9,11},{10,... | collective-permute-start | bytes 294920 | tf_op jit(solution)/shard_map/ppermute | solution.py:252
  44.2 5.3 %collective-permute-start.14 = (f32[32,512]{1,0:T(8,128)S(1)}, f32[32,512]{1,0:T(8,128)S(1)}, u32[]{:S(2)}, u32[]{:S(2)}) collective-permute-start(f32[32,512]{1,0:T(8,128)S(1)} %get-tuple-element.57), channel_id=1, source_target_pairs={{0,12},{4,8},{8,4},{12,0},{16,28},{20,24},{24,20},{28,16},{1,13},{... | collective-permute-start | bytes 196616 | tf_op jit(solution)/shard_map/ppermute | solution.py:252
  45.7 5.0 %collective-permute-start.15 = (f32[32,512]{1,0:T(8,128)S(1)}, f32[32,512]{1,0:T(8,128)S(1)}, u32[]{:S(2)}, u32[]{:S(2)}) collective-permute-start(f32[32,512]{1,0:T(8,128)S(1)} %get-tuple-element.58), channel_id=1, source_target_pairs={{0,4},{4,0},{8,12},{12,8},{16,20},{20,16},{24,28},{28,24},{1,5},{5... | collective-permute-start | bytes 196616 | tf_op jit(solution)/shard_map/ppermute | solution.py:252
  47.8 5.7 %collective-permute-start.18 = (f32[32,128]{1,0:T(8,128)S(1)}, f32[32,128]{1,0:T(8,128)S(1)}, u32[]{:S(2)}, u32[]{:S(2)}) collective-permute-start(f32[32,128]{1,0:T(8,128)S(1)} %add.21.before_ref.own_ref), channel_id=1, source_target_pairs={{0,2},{1,3},{2,0},{3,1},{4,6},{5,7},{6,4},{7,5},{8,10},{9,11},{10,... | collective-permute-start | bytes 49160 | tf_op jit(solution)/shard_map/ppermute | solution.py:252
  51.2 5.9 %collective-permute-start.17 = (f32[32,512]{1,0:T(8,128)S(1)}, f32[32,512]{1,0:T(8,128)S(1)}, u32[]{:S(2)}, u32[]{:S(2)}) collective-permute-start(f32[32,512]{1,0:T(8,128)S(1)} %add.23.own_ref), channel_id=1, source_target_pairs={{0,16},{4,20},{8,24},{12,28},{16,0},{20,4},{24,8},{28,12},{1,17},{... | collective-permute-start | bytes 196616 | tf_op jit(solution)/shard_map/ppermute | solution.py:252
  57.4 5.2 %collective-permute-start.21 = (f32[32,512]{1,0:T(8,128)S(1)}, f32[32,512]{1,0:T(8,128)S(1)}, u32[]{:S(2)}, u32[]{:S(2)}) collective-permute-start(f32[32,512]{1,0:T(8,128)S(1)} %total.5.chunk_ref.refs_0_), channel_id=1, source_target_pairs={{0,12},{4,8},{8,4},{12,0},{16,28},{20,24},{24,20},{28,16},{1,13},{... | collective-permute-start | bytes 196616 | tf_op jit(solution)/shard_map/ppermute | solution.py:252
  58.4 4.8 %collective-permute-start.20 = (f32[32,512]{1,0:T(8,128)S(1)}, f32[32,512]{1,0:T(8,128)S(1)}, u32[]{:S(2)}, u32[]{:S(2)}) collective-permute-start(f32[32,512]{1,0:T(8,128)S(1)} %total.5.chunk_ref.refs_0_), channel_id=1, source_target_pairs={{0,4},{4,0},{8,12},{12,8},{16,20},{20,16},{24,28},{28,24},{1,5},{5... | collective-permute-start | bytes 196616 | tf_op jit(solution)/shard_map/ppermute | solution.py:252
  59.2 4.6 %collective-permute-start.19 = (f32[32,512]{1,0:T(8,128)S(1)}, f32[32,512]{1,0:T(8,128)S(1)}, u32[]{:S(2)}, u32[]{:S(2)}) collective-permute-start(f32[32,512]{1,0:T(8,128)S(1)} %total.5.chunk_ref.refs_0_), channel_id=1, source_target_pairs={{0,8},{4,12},{8,0},{12,4},{16,24},{20,28},{24,16},{28,20},{1,9},{5... | collective-permute-start | bytes 196616 | tf_op jit(solution)/shard_map/ppermute | solution.py:252
  65.6 4.9 %collective-permute-start.23 = (f32[32,768]{1,0:T(8,128)S(1)}, f32[32,768]{1,0:T(8,128)S(1)}, u32[]{:S(2)}, u32[]{:S(2)}) collective-permute-start(f32[32,768]{1,0:T(8,128)S(1)} %add.24.own_ref), channel_id=1, source_target_pairs={{0,2},{1,3},{2,0},{3,1},{4,6},{5,7},{6,4},{7,5},{8,10},{9,11},{10,... | collective-permute-start | bytes 294920 | tf_op jit(solution)/shard_map/ppermute | solution.py:252
  72.4 5.3 %collective-permute-start.26 = (f32[32,512]{1,0:T(8,128)S(1)}, f32[32,512]{1,0:T(8,128)S(1)}, u32[]{:S(2)}, u32[]{:S(2)}) collective-permute-start(f32[32,512]{1,0:T(8,128)S(1)} %get-tuple-element.66), channel_id=1, source_target_pairs={{0,12},{4,8},{8,4},{12,0},{16,28},{20,24},{24,20},{28,16},{1,13},{... | collective-permute-start | bytes 196616 | tf_op jit(solution)/shard_map/ppermute | solution.py:252
  74.0 4.9 %collective-permute-start.27 = (f32[32,512]{1,0:T(8,128)S(1)}, f32[32,512]{1,0:T(8,128)S(1)}, u32[]{:S(2)}, u32[]{:S(2)}) collective-permute-start(f32[32,512]{1,0:T(8,128)S(1)} %get-tuple-element.67), channel_id=1, source_target_pairs={{0,4},{4,0},{8,12},{12,8},{16,20},{20,16},{24,28},{28,24},{1,5},{5... | collective-permute-start | bytes 196616 | tf_op jit(solution)/shard_map/ppermute | solution.py:252
  76.0 5.7 %collective-permute-start.30 = (f32[32,128]{1,0:T(8,128)S(1)}, f32[32,128]{1,0:T(8,128)S(1)}, u32[]{:S(2)}, u32[]{:S(2)}) collective-permute-start(f32[32,128]{1,0:T(8,128)S(1)} %add.25.before_ref.own_ref), channel_id=1, source_target_pairs={{0,2},{1,3},{2,0},{3,1},{4,6},{5,7},{6,4},{7,5},{8,10},{9,11},{10,... | collective-permute-start | bytes 49160 | tf_op jit(solution)/shard_map/ppermute | solution.py:252
  79.5 5.9 %collective-permute-start.29 = (f32[32,512]{1,0:T(8,128)S(1)}, f32[32,512]{1,0:T(8,128)S(1)}, u32[]{:S(2)}, u32[]{:S(2)}) collective-permute-start(f32[32,512]{1,0:T(8,128)S(1)} %add.27.own_ref), channel_id=1, source_target_pairs={{0,16},{4,20},{8,24},{12,28},{16,0},{20,4},{24,8},{28,12},{1,17},{... | collective-permute-start | bytes 196616 | tf_op jit(solution)/shard_map/ppermute | solution.py:252
  85.6 5.2 %collective-permute-start.33 = (f32[32,512]{1,0:T(8,128)S(1)}, f32[32,512]{1,0:T(8,128)S(1)}, u32[]{:S(2)}, u32[]{:S(2)}) collective-permute-start(f32[32,512]{1,0:T(8,128)S(1)} %total.6.chunk_ref.refs_0_), channel_id=1, source_target_pairs={{0,12},{4,8},{8,4},{12,0},{16,28},{20,24},{24,20},{28,16},{1,13},{... | collective-permute-start | bytes 196616 | tf_op jit(solution)/shard_map/ppermute | solution.py:252
  86.7 5.0 %collective-permute-start.32 = (f32[32,512]{1,0:T(8,128)S(1)}, f32[32,512]{1,0:T(8,128)S(1)}, u32[]{:S(2)}, u32[]{:S(2)}) collective-permute-start(f32[32,512]{1,0:T(8,128)S(1)} %total.6.chunk_ref.refs_0_), channel_id=1, source_target_pairs={{0,4},{4,0},{8,12},{12,8},{16,20},{20,16},{24,28},{28,24},{1,5},{5... | collective-permute-start | bytes 196616 | tf_op jit(solution)/shard_map/ppermute | solution.py:252
  87.5 4.8 %collective-permute-start.31 = (f32[32,512]{1,0:T(8,128)S(1)}, f32[32,512]{1,0:T(8,128)S(1)}, u32[]{:S(2)}, u32[]{:S(2)}) collective-permute-start(f32[32,512]{1,0:T(8,128)S(1)} %total.6.chunk_ref.refs_0_), channel_id=1, source_target_pairs={{0,8},{4,12},{8,0},{12,4},{16,24},{20,28},{24,16},{28,20},{1,9},{5... | collective-permute-start | bytes 196616 | tf_op jit(solution)/shard_map/ppermute | solution.py:252
  94.0 4.9 %collective-permute-start.35 = (f32[32,768]{1,0:T(8,128)S(1)}, f32[32,768]{1,0:T(8,128)S(1)}, u32[]{:S(2)}, u32[]{:S(2)}) collective-permute-start(f32[32,768]{1,0:T(8,128)S(1)} %add.28.own_ref), channel_id=1, source_target_pairs={{0,2},{1,3},{2,0},{3,1},{4,6},{5,7},{6,4},{7,5},{8,10},{9,11},{10,... | collective-permute-start | bytes 294920 | tf_op jit(solution)/shard_map/ppermute | solution.py:252
  100.8 5.4 %collective-permute-start.38 = (f32[32,512]{1,0:T(8,128)S(1)}, f32[32,512]{1,0:T(8,128)S(1)}, u32[]{:S(2)}, u32[]{:S(2)}) collective-permute-start(f32[32,512]{1,0:T(8,128)S(1)} %get-tuple-element.75), channel_id=1, source_target_pairs={{0,12},{4,8},{8,4},{12,0},{16,28},{20,24},{24,20},{28,16},{1,13},{... | collective-permute-start | bytes 196616 | tf_op jit(solution)/shard_map/ppermute | solution.py:252
  102.3 5.1 %collective-permute-start.39 = (f32[32,512]{1,0:T(8,128)S(1)}, f32[32,512]{1,0:T(8,128)S(1)}, u32[]{:S(2)}, u32[]{:S(2)}) collective-permute-start(f32[32,512]{1,0:T(8,128)S(1)} %get-tuple-element.76), channel_id=1, source_target_pairs={{0,4},{4,0},{8,12},{12,8},{16,20},{20,16},{24,28},{28,24},{1,5},{5... | collective-permute-start | bytes 196616 | tf_op jit(solution)/shard_map/ppermute | solution.py:252
  104.4 5.7 %collective-permute-start.42 = (f32[32,128]{1,0:T(8,128)S(1)}, f32[32,128]{1,0:T(8,128)S(1)}, u32[]{:S(2)}, u32[]{:S(2)}) collective-permute-start(f32[32,128]{1,0:T(8,128)S(1)} %add.29.before_ref.own_ref), channel_id=1, source_target_pairs={{0,2},{1,3},{2,0},{3,1},{4,6},{5,7},{6,4},{7,5},{8,10},{9,11},{10,... | collective-permute-start | bytes 49160 | tf_op jit(solution)/shard_map/ppermute | solution.py:252
  107.7 5.9 %collective-permute-start.41 = (f32[32,512]{1,0:T(8,128)S(1)}, f32[32,512]{1,0:T(8,128)S(1)}, u32[]{:S(2)}, u32[]{:S(2)}) collective-permute-start(f32[32,512]{1,0:T(8,128)S(1)} %add.31.own_ref), channel_id=1, source_target_pairs={{0,16},{4,20},{8,24},{12,28},{16,0},{20,4},{24,8},{28,12},{1,17},{... | collective-permute-start | bytes 196616 | tf_op jit(solution)/shard_map/ppermute | solution.py:252
  113.9 5.4 %collective-permute-start.45 = (f32[32,512]{1,0:T(8,128)S(1)}, f32[32,512]{1,0:T(8,128)S(1)}, u32[]{:S(2)}, u32[]{:S(2)}) collective-permute-start(f32[32,512]{1,0:T(8,128)S(1)} %total.7.chunk_ref.refs_0_), channel_id=1, source_target_pairs={{0,12},{4,8},{8,4},{12,0},{16,28},{20,24},{24,20},{28,16},{1,13},{... | collective-permute-start | bytes 196616 | tf_op jit(solution)/shard_map/ppermute | solution.py:252
  114.9 5.0 %collective-permute-start.44 = (f32[32,512]{1,0:T(8,128)S(1)}, f32[32,512]{1,0:T(8,128)S(1)}, u32[]{:S(2)}, u32[]{:S(2)}) collective-permute-start(f32[32,512]{1,0:T(8,128)S(1)} %total.7.chunk_ref.refs_0_), channel_id=1, source_target_pairs={{0,4},{4,0},{8,12},{12,8},{16,20},{20,16},{24,28},{28,24},{1,5},{5... | collective-permute-start | bytes 196616 | tf_op jit(solution)/shard_map/ppermute | solution.py:252
  123.8 5.1 %collective-permute-start.48 = (bf16[32,1536]{1,0:T(8,128)(2,1)S(1)}, bf16[32,1536]{1,0:T(8,128)(2,1)S(1)}, u32[]{:S(2)}, u32[]{:S(2)}) collective-permute-start(bf16[32,1536]{1,0:T(8,128)(2,1)S(1)} %add.33.own_ref), channel_id=1, source_target_pairs={{0,2},{1,3},{2,0},{3,1},{4,6},{5,7},{6,4},{7,5},{8,10},{9,11},{10,... | collective-permute-start | bytes 294920 | tf_op jit(solution)/shard_map/ppermute | solution.py:252
  (19 other events, 40.9 us)

commit v9 on v8

--- a/solution.py
+++ b/solution.py
@@ -64,6 +64,25 @@
     return terms[0]
 
 
+def terms_of(value):
+    parts = []
+    for _ in range(3):
+        parts.append(value.astype(BF16))
+        value = value - parts[-1].astype(F32)
+    return parts
+
+
+def stacked(value):
+    high, middle, low = terms_of(value)
+    return jnp.concatenate([high, middle, low, high, middle, high], axis=0)
+
+
+def product(left, right_stacked):
+    high, middle, low = terms_of(left)
+    left = jnp.concatenate([high, high, high, middle, middle, low], axis=1)
+    return jnp.dot(left, right_stacked, preferred_element_type=F32)
+
+
 def contract_last(left, right, precision=None):
     return lax.dot_general(
         left, right, (((1,), (1,)), ((), ())), preferred_element_type=F32, precision=precision
@@ -79,7 +98,11 @@
 
 
 def core():
-    return lax.rem(lax.axis_index("feat"), 2)
+    index, parity, shift = lax.axis_index("feat"), 0, 1
+    while shift < lax.axis_size("feat"):
+        parity = parity + lax.rem(index // shift, 2)
+        shift *= 2
+    return lax.rem(parity, 2)
 
 
 def aligned(index, size):
@@ -212,23 +235,21 @@
 
 def assemble_kernel(*refs):
     *chunks, out_ref = refs
-    n, width = out_ref.shape[0], chunks[0].shape[1]
+    width = chunks[0].shape[1]
     for part, chunk in zip(GATHER, chunks):
-        place = aligned(position() ^ part, width)
-        out_ref[:, place] = chunk[:n, :]
+        out_ref[:, aligned(position() ^ part, width)] = stacked(chunk[...])
 
 
 def last_kernel(own_ref, got_ref, lower_ref, image_ref, scores_ref, basis_ref):
     n, lower = lower_ref.shape[0], lower_ref[...]
-    basis_ref[...] = jnp.dot(lower, image_ref[...], preferred_element_type=F32, precision=HIGHEST)
-    projected = total(own_ref, got_ref)
-    projected = jnp.dot(lower, projected, preferred_element_type=F32, precision=HIGHEST)
+    basis_ref[...] = product(lower, image_ref[...])
+    projected = product(lower, stacked(total(own_ref, got_ref)))
     scores_ref[...] = jnp.sum(projected * projected, axis=0) / n
 
 
 def normalised_total_kernel(own_ref, got_ref, lower_ref, out_ref):
     value = own_ref[...] + got_ref[...]
-    out_ref[...] = jnp.dot(lower_ref[...], value, preferred_element_type=F32, precision=HIGHEST)
+    out_ref[...] = product(lower_ref[...], stacked(value))
 
 
 def ordered_copy_kernel(value_ref, before_ref, out_ref):
@@ -249,6 +270,8 @@
 
 def swap(value, axis, distance):
     size = lax.axis_size(axis)
+    if axis == "feat" and distance > 1:
+        distance += 1
     return lax.ppermute(value, axis, [(i, i ^ distance) for i in range(size)])
 
 
@@ -351,7 +374,7 @@
                     own = add(own, got)
             other = swap(own, "feat", 1)
         lower = call(inverse_factor_kernel, [((n, n), F32)], "inverse_factor", cost=LONG)(*grams)
-    image = call(assemble_kernel, [((n, features), F32)], "assemble")(*images)[0]
+    image = call(assemble_kernel, [((6 * n, features), BF16)], "assemble")(*images)[0]
     outputs = [((tokens,), F32), ((n, features), F32)]
     return tuple(call(last_kernel, outputs, "last")(own, other, *lower, image))
 

time: 130 us -> 129 us (level)
  starting transfers between devices: 53.7 us -> 51.4 us
  waiting for transfers between devices: 39.4 us -> 40.7 us
    ppermute x50, starting transfers between devices: 53.7 us -> 51.4 us  [swap(): return lax.ppermute(value, axis, [(i, i ^ distance) for i in range(size)])]
  transfers between devices with their start and end apart: 50 -> 50, of which waited for: 34 -> 36; matrix products, arithmetic and copies ran while one was open for 0% -> 0% of each run, Pallas kernels for 20% -> 20%
where the time goes in v9:
time: 129 us
  starting transfers between devices  51.4 us (40%)
  waiting for transfers between devices  40.7 us (32%)
  Pallas kernels  35.8 us (28%)
    ppermute x50, starting transfers between devices, swap(): return lax.ppermute(value, axis, [(i, i ^ distance) for i in range(size)])  51.4 us
    ppermute x50, waiting for transfers between devices, swap(): return lax.ppermute(value, axis, [(i, i ^ distance) for i in range(size)])  40.7 us
    pallas_call x66, Pallas kernels, run(): pl.pallas_call(kernel, out_shape=[jax.ShapeDtypeStruct(shape, dtype) for...  35.8 us
  transfers between devices with their start and end apart: 50, of which 36 were waited for; matrix products, arithmetic and copies ran while one was open for 0% of the time, Pallas kernels for 20%

profile of v9, /device:TPU:0, one launch (start us, length us, event | category | flops | bytes accessed | tf_op | source)
XLA Modules:
  0.0 128.9 jit_solution(1581233098515914945)
XLA Ops:
  0.6 2.0 %fetch.1.ready_ref = bf16[1536,2048]{1,0:T(8,128)(2,1)S(1)} custom-call(bf16[1536,2048]{1,0:T(8,128)(2,1)} %rows_hbm.3), custom_call_target="tpu_custom_call" | custom-call | tf_op jit(solution)/shard_map/fetch/pallas_call | solution.py:29
  2.6 1.9 %sent_projection.4 = (f32[32,768]{1,0:T(8,128)S(1)}, bf16[1536,2048]{1,0:T(8,128)(2,1)S(1)}) custom-call(f32[32,2048]{1,0:T(8,128)S(1)} %copy-done, bf16[1536,2048]{1,0:T(8,128)(2,1)} %rows_hbm.3, bf16[1536,2048]{1,0:T(8,128)(2,1)S(1)} %fetch.1.ready_ref), custom_call_target="tpu_custom_call", output_to_operand_aliasing={{1}: (2, {})} | custom-call | tf_op jit(solution)/shard_map/sent_projection/pallas_call | solution.py:29
  6.2 2.7 %collective-permute-start.1 = (f32[32,768]{1,0:T(8,128)S(1)}, f32[32,768]{1,0:T(8,128)S(1)}, u32[]{:S(2)}, u32[]{:S(2)}) collective-permute-start(f32[32,768]{1,0:T(8,128)S(1)} %add.17.refs_0_), channel_id=1, source_target_pairs={{0,3},{1,2},{2,1},{3,0},{4,7},{5,6},{6,5},{7,4},{8,11},{9,10},{10,... | collective-permute-start | bytes 294920 | tf_op jit(solution)/shard_map/ppermute | solution.py:275
  8.8 3.0 %collective-permute-done.1.refs_1_ = f32[32,768]{1,0:T(8,128)S(1)} collective-permute-done((f32[32,768]{1,0:T(8,128)S(1)}, f32[32,768]{1,0:T(8,128)S(1)}, u32[]{:S(2)}, u32[]{:S(2)}) %collective-permute-start.1) | collective-permute-done | bytes 98336 | tf_op jit(solution)/shard_map/ppermute | solution.py:275
  13.8 2.9 %collective-permute-start.3 = (f32[40,512]{1,0:T(8,128)S(1)}, f32[40,512]{1,0:T(8,128)S(1)}, u32[]{:S(2)}, u32[]{:S(2)}) collective-permute-start(f32[40,512]{1,0:T(8,128)S(1)} %get-tuple-element.48), channel_id=1, source_target_pairs={{0,12},{4,8},{8,4},{12,0},{16,28},{20,24},{24,20},{28,16},{1,13},{... | collective-permute-start | bytes 245768 | tf_op jit(solution)/shard_map/ppermute | solution.py:275
  17.7 1.9 %collective-permute-done.3.refs_1_ = f32[40,512]{1,0:T(8,128)S(1)} collective-permute-done((f32[40,512]{1,0:T(8,128)S(1)}, f32[40,512]{1,0:T(8,128)S(1)}, u32[]{:S(2)}, u32[]{:S(2)}) %collective-permute-start.3) | collective-permute-done | bytes 81952 | tf_op jit(solution)/shard_map/ppermute | solution.py:275
  19.6 1.7 %collective-permute-done.4.refs_2_ = f32[40,512]{1,0:T(8,128)S(1)} collective-permute-done((f32[40,512]{1,0:T(8,128)S(1)}, f32[40,512]{1,0:T(8,128)S(1)}, u32[]{:S(2)}, u32[]{:S(2)}) %collective-permute-start.4) | collective-permute-done | bytes 81952 | tf_op jit(solution)/shard_map/ppermute | solution.py:275
  21.7 2.7 %collective-permute-start.6 = (f32[40,512]{1,0:T(8,128)S(1)}, f32[40,512]{1,0:T(8,128)S(1)}, u32[]{:S(2)}, u32[]{:S(2)}) collective-permute-start(f32[40,512]{1,0:T(8,128)S(1)} %add.19.own_ref), channel_id=1, source_target_pairs={{0,16},{4,20},{8,24},{12,28},{16,0},{20,4},{24,8},{28,12},{1,17},{... | collective-permute-start | bytes 245768 | tf_op jit(solution)/shard_map/ppermute | solution.py:275
  24.3 4.3 %collective-permute-done.6.got_ref = f32[40,512]{1,0:T(8,128)S(1)} collective-permute-done((f32[40,512]{1,0:T(8,128)S(1)}, f32[40,512]{1,0:T(8,128)S(1)}, u32[]{:S(2)}, u32[]{:S(2)}) %collective-permute-start.6) | collective-permute-done | bytes 81952 | tf_op jit(solution)/shard_map/ppermute | solution.py:275
  30.2 2.0 %collective-permute-start.7 = (f32[40,512]{1,0:T(8,128)S(1)}, f32[40,512]{1,0:T(8,128)S(1)}, u32[]{:S(2)}, u32[]{:S(2)}) collective-permute-start(f32[40,512]{1,0:T(8,128)S(1)} %total.4.chunk_ref.mean_ref.refs_0_), channel_id=1, source_target_pairs={{0,8},{4,12},{8,0},{12,4},{16,24},{20,28},{24,16},{28,20},{1,9},{5... | collective-permute-start | bytes 245768 | tf_op jit(solution)/shard_map/ppermute | solution.py:275
  32.8 1.4 %collective-permute-done.9.chunk_ref.mean_ref.refs_1_.refs_0_ = f32[40,512]{1,0:T(8,128)S(1)} collective-permute-done((f32[40,512]{1,0:T(8,128)S(1)}, f32[40,512]{1,0:T(8,128)S(1)}, u32[]{:S(2)}, u32[]{:S(2)}) %collective-permute-start.9) | collective-permute-done | bytes 81952 | tf_op jit(solution)/shard_map/ppermute | solution.py:275
  37.2 1.3 %collective-permute-start.11 = (f32[32,768]{1,0:T(8,128)S(1)}, f32[32,768]{1,0:T(8,128)S(1)}, u32[]{:S(2)}, u32[]{:S(2)}) collective-permute-start(f32[32,768]{1,0:T(8,128)S(1)} %add.20.own_ref), channel_id=1, source_target_pairs={{0,3},{1,2},{2,1},{3,0},{4,7},{5,6},{6,5},{7,4},{8,11},{9,10},{10,... | collective-permute-start | bytes 294920 | tf_op jit(solution)/shard_map/ppermute | solution.py:275
  40.0 1.9 %collective-permute-done.11.got_ref = f32[32,768]{1,0:T(8,128)S(1)} collective-permute-done((f32[32,768]{1,0:T(8,128)S(1)}, f32[32,768]{1,0:T(8,128)S(1)}, u32[]{:S(2)}, u32[]{:S(2)}) %collective-permute-start.11) | collective-permute-done | bytes 98336 | tf_op jit(solution)/shard_map/ppermute | solution.py:275
  43.9 1.5 %collective-permute-start.14 = (f32[32,512]{1,0:T(8,128)S(1)}, f32[32,512]{1,0:T(8,128)S(1)}, u32[]{:S(2)}, u32[]{:S(2)}) collective-permute-start(f32[32,512]{1,0:T(8,128)S(1)} %get-tuple-element.57), channel_id=1, source_target_pairs={{0,12},{4,8},{8,4},{12,0},{16,28},{20,24},{24,20},{28,16},{1,13},{... | collective-permute-start | bytes 196616 | tf_op jit(solution)/shard_map/ppermute | solution.py:275
  50.9 2.2 %collective-permute-start.17 = (f32[32,512]{1,0:T(8,128)S(1)}, f32[32,512]{1,0:T(8,128)S(1)}, u32[]{:S(2)}, u32[]{:S(2)}) collective-permute-start(f32[32,512]{1,0:T(8,128)S(1)} %add.23.own_ref), channel_id=1, source_target_pairs={{0,16},{4,20},{8,24},{12,28},{16,0},{20,4},{24,8},{28,12},{1,17},{... | collective-permute-start | bytes 196616 | tf_op jit(solution)/shard_map/ppermute | solution.py:275
  53.2 2.9 %inverse_factor.4.lower_ref = f32[32,32]{1,0:T(8,128)S(1)} custom-call(f32[32,128]{1,0:T(8,128)S(1)} %add.21.before_ref.own_ref, f32[32,128]{1,0:T(8,128)S(1)} %collective-permute-done.18.got_ref), custom_call_target="tpu_custom_call" | custom-call | flops 17179869184 | tf_op jit(solution)/shard_map/inverse_factor/pallas_call | solution.py:29
  59.0 1.6 %collective-permute-start.19 = (f32[32,512]{1,0:T(8,128)S(1)}, f32[32,512]{1,0:T(8,128)S(1)}, u32[]{:S(2)}, u32[]{:S(2)}) collective-permute-start(f32[32,512]{1,0:T(8,128)S(1)} %total.5.chunk_ref.refs_0_), channel_id=1, source_target_pairs={{0,8},{4,12},{8,0},{12,4},{16,24},{20,28},{24,16},{28,20},{1,9},{5... | collective-permute-start | bytes 196616 | tf_op jit(solution)/shard_map/ppermute | solution.py:275
  65.3 1.3 %collective-permute-start.23 = (f32[32,768]{1,0:T(8,128)S(1)}, f32[32,768]{1,0:T(8,128)S(1)}, u32[]{:S(2)}, u32[]{:S(2)}) collective-permute-start(f32[32,768]{1,0:T(8,128)S(1)} %add.24.own_ref), channel_id=1, source_target_pairs={{0,3},{1,2},{2,1},{3,0},{4,7},{5,6},{6,5},{7,4},{8,11},{9,10},{10,... | collective-permute-start | bytes 294920 | tf_op jit(solution)/shard_map/ppermute | solution.py:275
  68.2 1.9 %collective-permute-done.23.got_ref = f32[32,768]{1,0:T(8,128)S(1)} collective-permute-done((f32[32,768]{1,0:T(8,128)S(1)}, f32[32,768]{1,0:T(8,128)S(1)}, u32[]{:S(2)}, u32[]{:S(2)}) %collective-permute-start.23) | collective-permute-done | bytes 98336 | tf_op jit(solution)/shard_map/ppermute | solution.py:275
  72.0 1.7 %collective-permute-start.26 = (f32[32,512]{1,0:T(8,128)S(1)}, f32[32,512]{1,0:T(8,128)S(1)}, u32[]{:S(2)}, u32[]{:S(2)}) collective-permute-start(f32[32,512]{1,0:T(8,128)S(1)} %get-tuple-element.66), channel_id=1, source_target_pairs={{0,12},{4,8},{8,4},{12,0},{16,28},{20,24},{24,20},{28,16},{1,13},{... | collective-permute-start | bytes 196616 | tf_op jit(solution)/shard_map/ppermute | solution.py:275
  79.1 2.2 %collective-permute-start.29 = (f32[32,512]{1,0:T(8,128)S(1)}, f32[32,512]{1,0:T(8,128)S(1)}, u32[]{:S(2)}, u32[]{:S(2)}) collective-permute-start(f32[32,512]{1,0:T(8,128)S(1)} %add.27.own_ref), channel_id=1, source_target_pairs={{0,16},{4,20},{8,24},{12,28},{16,0},{20,4},{24,8},{28,12},{1,17},{... | collective-permute-start | bytes 196616 | tf_op jit(solution)/shard_map/ppermute | solution.py:275
  81.4 2.9 %inverse_factor.5.lower_ref = f32[32,32]{1,0:T(8,128)S(1)} custom-call(f32[32,128]{1,0:T(8,128)S(1)} %add.25.before_ref.own_ref, f32[32,128]{1,0:T(8,128)S(1)} %collective-permute-done.30.got_ref), custom_call_target="tpu_custom_call" | custom-call | flops 17179869184 | tf_op jit(solution)/shard_map/inverse_factor/pallas_call | solution.py:29
  87.2 1.6 %collective-permute-start.31 = (f32[32,512]{1,0:T(8,128)S(1)}, f32[32,512]{1,0:T(8,128)S(1)}, u32[]{:S(2)}, u32[]{:S(2)}) collective-permute-start(f32[32,512]{1,0:T(8,128)S(1)} %total.6.chunk_ref.refs_0_), channel_id=1, source_target_pairs={{0,8},{4,12},{8,0},{12,4},{16,24},{20,28},{24,16},{28,20},{1,9},{5... | collective-permute-start | bytes 196616 | tf_op jit(solution)/shard_map/ppermute | solution.py:275
  93.6 1.3 %collective-permute-start.35 = (f32[32,768]{1,0:T(8,128)S(1)}, f32[32,768]{1,0:T(8,128)S(1)}, u32[]{:S(2)}, u32[]{:S(2)}) collective-permute-start(f32[32,768]{1,0:T(8,128)S(1)} %add.28.own_ref), channel_id=1, source_target_pairs={{0,3},{1,2},{2,1},{3,0},{4,7},{5,6},{6,5},{7,4},{8,11},{9,10},{10,... | collective-permute-start | bytes 294920 | tf_op jit(solution)/shard_map/ppermute | solution.py:275
  96.5 1.9 %collective-permute-done.35.got_ref = f32[32,768]{1,0:T(8,128)S(1)} collective-permute-done((f32[32,768]{1,0:T(8,128)S(1)}, f32[32,768]{1,0:T(8,128)S(1)}, u32[]{:S(2)}, u32[]{:S(2)}) %collective-permute-start.35) | collective-permute-done | bytes 98336 | tf_op jit(solution)/shard_map/ppermute | solution.py:275
  100.4 1.5 %collective-permute-start.38 = (f32[32,512]{1,0:T(8,128)S(1)}, f32[32,512]{1,0:T(8,128)S(1)}, u32[]{:S(2)}, u32[]{:S(2)}) collective-permute-start(f32[32,512]{1,0:T(8,128)S(1)} %get-tuple-element.75), channel_id=1, source_target_pairs={{0,12},{4,8},{8,4},{12,0},{16,28},{20,24},{24,20},{28,16},{1,13},{... | collective-permute-start | bytes 196616 | tf_op jit(solution)/shard_map/ppermute | solution.py:275
  107.3 2.4 %collective-permute-start.41 = (f32[32,512]{1,0:T(8,128)S(1)}, f32[32,512]{1,0:T(8,128)S(1)}, u32[]{:S(2)}, u32[]{:S(2)}) collective-permute-start(f32[32,512]{1,0:T(8,128)S(1)} %add.31.own_ref), channel_id=1, source_target_pairs={{0,16},{4,20},{8,24},{12,28},{16,0},{20,4},{24,8},{28,12},{1,17},{... | collective-permute-start | bytes 196616 | tf_op jit(solution)/shard_map/ppermute | solution.py:275
  109.7 2.9 %inverse_factor.6.lower_ref = f32[32,32]{1,0:T(8,128)S(1)} custom-call(f32[32,128]{1,0:T(8,128)S(1)} %add.29.before_ref.own_ref, f32[32,128]{1,0:T(8,128)S(1)} %collective-permute-done.42.got_ref), custom_call_target="tpu_custom_call" | custom-call | flops 17179869184 | tf_op jit(solution)/shard_map/inverse_factor/pallas_call | solution.py:29
  115.3 1.6 %collective-permute-start.43 = (f32[32,512]{1,0:T(8,128)S(1)}, f32[32,512]{1,0:T(8,128)S(1)}, u32[]{:S(2)}, u32[]{:S(2)}) collective-permute-start(f32[32,512]{1,0:T(8,128)S(1)} %total.7.chunk_ref.refs_0_), channel_id=1, source_target_pairs={{0,8},{4,12},{8,0},{12,4},{16,24},{20,28},{24,16},{28,20},{1,9},{5... | collective-permute-start | bytes 196616 | tf_op jit(solution)/shard_map/ppermute | solution.py:275
  117.5 1.3 %collective-permute-done.45.chunk_ref.refs_1_ = f32[32,512]{1,0:T(8,128)S(1)} collective-permute-done((f32[32,512]{1,0:T(8,128)S(1)}, f32[32,512]{1,0:T(8,128)S(1)}, u32[]{:S(2)}, u32[]{:S(2)}) %collective-permute-start.45) | collective-permute-done | bytes 65568 | tf_op jit(solution)/shard_map/ppermute | solution.py:275
  123.1 1.3 %collective-permute-start.48 = (bf16[32,1536]{1,0:T(8,128)(2,1)S(1)}, bf16[32,1536]{1,0:T(8,128)(2,1)S(1)}, u32[]{:S(2)}, u32[]{:S(2)}) collective-permute-start(bf16[32,1536]{1,0:T(8,128)(2,1)S(1)} %add.33.own_ref), channel_id=1, source_target_pairs={{0,3},{1,2},{2,1},{3,0},{4,7},{5,6},{6,5},{7,4},{8,11},{9,10},{10,... | collective-permute-start | bytes 294920 | tf_op jit(solution)/shard_map/ppermute | solution.py:275
  125.0 2.9 %inverse_factor.7.lower_ref = f32[32,32]{1,0:T(8,128)S(1)} custom-call(f32[32,128]{1,0:T(8,128)S(1)} %add.32.before_ref.own_ref, f32[32,128]{1,0:T(8,128)S(1)} %collective-permute-done.49.got_ref), custom_call_target="tpu_custom_call" | custom-call | flops 17179869184 | tf_op jit(solution)/shard_map/inverse_factor/pallas_call | solution.py:29
  (136 shorter events, 61.2 us)
Async XLA Ops:
  6.2 5.7 %collective-permute-start.1 = (f32[32,768]{1,0:T(8,128)S(1)}, f32[32,768]{1,0:T(8,128)S(1)}, u32[]{:S(2)}, u32[]{:S(2)}) collective-permute-start(f32[32,768]{1,0:T(8,128)S(1)} %add.17.refs_0_), channel_id=1, source_target_pairs={{0,3},{1,2},{2,1},{3,0},{4,7},{5,6},{6,5},{7,4},{8,11},{9,10},{10,... | collective-permute-start | bytes 294920 | tf_op jit(solution)/shard_map/ppermute | solution.py:275
  13.8 5.7 %collective-permute-start.3 = (f32[40,512]{1,0:T(8,128)S(1)}, f32[40,512]{1,0:T(8,128)S(1)}, u32[]{:S(2)}, u32[]{:S(2)}) collective-permute-start(f32[40,512]{1,0:T(8,128)S(1)} %get-tuple-element.48), channel_id=1, source_target_pairs={{0,12},{4,8},{8,4},{12,0},{16,28},{20,24},{24,20},{28,16},{1,13},{... | collective-permute-start | bytes 245768 | tf_op jit(solution)/shard_map/ppermute | solution.py:275
  16.7 4.6 %collective-permute-start.4 = (f32[40,512]{1,0:T(8,128)S(1)}, f32[40,512]{1,0:T(8,128)S(1)}, u32[]{:S(2)}, u32[]{:S(2)}) collective-permute-start(f32[40,512]{1,0:T(8,128)S(1)} %get-tuple-element.49), channel_id=1, source_target_pairs={{0,4},{4,0},{8,12},{12,8},{16,20},{20,16},{24,28},{28,24},{1,5},{5... | collective-permute-start | bytes 245768 | tf_op jit(solution)/shard_map/ppermute | solution.py:275
  17.2 4.4 %collective-permute-start.5 = (f32[40,512]{1,0:T(8,128)S(1)}, f32[40,512]{1,0:T(8,128)S(1)}, u32[]{:S(2)}, u32[]{:S(2)}) collective-permute-start(f32[40,512]{1,0:T(8,128)S(1)} %get-tuple-element.50), channel_id=1, source_target_pairs={{0,8},{4,12},{8,0},{12,4},{16,24},{20,28},{24,16},{28,20},{1,9},{5... | collective-permute-start | bytes 245768 | tf_op jit(solution)/shard_map/ppermute | solution.py:275
  21.7 7.0 %collective-permute-start.6 = (f32[40,512]{1,0:T(8,128)S(1)}, f32[40,512]{1,0:T(8,128)S(1)}, u32[]{:S(2)}, u32[]{:S(2)}) collective-permute-start(f32[40,512]{1,0:T(8,128)S(1)} %add.19.own_ref), channel_id=1, source_target_pairs={{0,16},{4,20},{8,24},{12,28},{16,0},{20,4},{24,8},{28,12},{1,17},{... | collective-permute-start | bytes 245768 | tf_op jit(solution)/shard_map/ppermute | solution.py:275
  28.7 5.4 %collective-permute-start.9 = (f32[40,512]{1,0:T(8,128)S(1)}, f32[40,512]{1,0:T(8,128)S(1)}, u32[]{:S(2)}, u32[]{:S(2)}) collective-permute-start(f32[40,512]{1,0:T(8,128)S(1)} %total.4.chunk_ref.mean_ref.refs_0_), channel_id=1, source_target_pairs={{0,12},{4,8},{8,4},{12,0},{16,28},{20,24},{24,20},{28,16},{1,13},{... | collective-permute-start | bytes 245768 | tf_op jit(solution)/shard_map/ppermute | solution.py:275
  29.4 5.4 %collective-permute-start.8 = (f32[40,512]{1,0:T(8,128)S(1)}, f32[40,512]{1,0:T(8,128)S(1)}, u32[]{:S(2)}, u32[]{:S(2)}) collective-permute-start(f32[40,512]{1,0:T(8,128)S(1)} %total.4.chunk_ref.mean_ref.refs_0_), channel_id=1, source_target_pairs={{0,4},{4,0},{8,12},{12,8},{16,20},{20,16},{24,28},{28,24},{1,5},{5... | collective-permute-start | bytes 245768 | tf_op jit(solution)/shard_map/ppermute | solution.py:275
  30.2 5.2 %collective-permute-start.7 = (f32[40,512]{1,0:T(8,128)S(1)}, f32[40,512]{1,0:T(8,128)S(1)}, u32[]{:S(2)}, u32[]{:S(2)}) collective-permute-start(f32[40,512]{1,0:T(8,128)S(1)} %total.4.chunk_ref.mean_ref.refs_0_), channel_id=1, source_target_pairs={{0,8},{4,12},{8,0},{12,4},{16,24},{20,28},{24,16},{28,20},{1,9},{5... | collective-permute-start | bytes 245768 | tf_op jit(solution)/shard_map/ppermute | solution.py:275
  37.2 4.8 %collective-permute-start.11 = (f32[32,768]{1,0:T(8,128)S(1)}, f32[32,768]{1,0:T(8,128)S(1)}, u32[]{:S(2)}, u32[]{:S(2)}) collective-permute-start(f32[32,768]{1,0:T(8,128)S(1)} %add.20.own_ref), channel_id=1, source_target_pairs={{0,3},{1,2},{2,1},{3,0},{4,7},{5,6},{6,5},{7,4},{8,11},{9,10},{10,... | collective-permute-start | bytes 294920 | tf_op jit(solution)/shard_map/ppermute | solution.py:275
  43.9 5.3 %collective-permute-start.14 = (f32[32,512]{1,0:T(8,128)S(1)}, f32[32,512]{1,0:T(8,128)S(1)}, u32[]{:S(2)}, u32[]{:S(2)}) collective-permute-start(f32[32,512]{1,0:T(8,128)S(1)} %get-tuple-element.57), channel_id=1, source_target_pairs={{0,12},{4,8},{8,4},{12,0},{16,28},{20,24},{24,20},{28,16},{1,13},{... | collective-permute-start | bytes 196616 | tf_op jit(solution)/shard_map/ppermute | solution.py:275
  45.4 5.0 %collective-permute-start.15 = (f32[32,512]{1,0:T(8,128)S(1)}, f32[32,512]{1,0:T(8,128)S(1)}, u32[]{:S(2)}, u32[]{:S(2)}) collective-permute-start(f32[32,512]{1,0:T(8,128)S(1)} %get-tuple-element.58), channel_id=1, source_target_pairs={{0,4},{4,0},{8,12},{12,8},{16,20},{20,16},{24,28},{28,24},{1,5},{5... | collective-permute-start | bytes 196616 | tf_op jit(solution)/shard_map/ppermute | solution.py:275
  47.5 5.7 %collective-permute-start.18 = (f32[32,128]{1,0:T(8,128)S(1)}, f32[32,128]{1,0:T(8,128)S(1)}, u32[]{:S(2)}, u32[]{:S(2)}) collective-permute-start(f32[32,128]{1,0:T(8,128)S(1)} %add.21.before_ref.own_ref), channel_id=1, source_target_pairs={{0,3},{1,2},{2,1},{3,0},{4,7},{5,6},{6,5},{7,4},{8,11},{9,10},{10,... | collective-permute-start | bytes 49160 | tf_op jit(solution)/shard_map/ppermute | solution.py:275
  50.9 5.9 %collective-permute-start.17 = (f32[32,512]{1,0:T(8,128)S(1)}, f32[32,512]{1,0:T(8,128)S(1)}, u32[]{:S(2)}, u32[]{:S(2)}) collective-permute-start(f32[32,512]{1,0:T(8,128)S(1)} %add.23.own_ref), channel_id=1, source_target_pairs={{0,16},{4,20},{8,24},{12,28},{16,0},{20,4},{24,8},{28,12},{1,17},{... | collective-permute-start | bytes 196616 | tf_op jit(solution)/shard_map/ppermute | solution.py:275
  57.1 5.2 %collective-permute-start.21 = (f32[32,512]{1,0:T(8,128)S(1)}, f32[32,512]{1,0:T(8,128)S(1)}, u32[]{:S(2)}, u32[]{:S(2)}) collective-permute-start(f32[32,512]{1,0:T(8,128)S(1)} %total.5.chunk_ref.refs_0_), channel_id=1, source_target_pairs={{0,12},{4,8},{8,4},{12,0},{16,28},{20,24},{24,20},{28,16},{1,13},{... | collective-permute-start | bytes 196616 | tf_op jit(solution)/shard_map/ppermute | solution.py:275
  58.1 4.8 %collective-permute-start.20 = (f32[32,512]{1,0:T(8,128)S(1)}, f32[32,512]{1,0:T(8,128)S(1)}, u32[]{:S(2)}, u32[]{:S(2)}) collective-permute-start(f32[32,512]{1,0:T(8,128)S(1)} %total.5.chunk_ref.refs_0_), channel_id=1, source_target_pairs={{0,4},{4,0},{8,12},{12,8},{16,20},{20,16},{24,28},{28,24},{1,5},{5... | collective-permute-start | bytes 196616 | tf_op jit(solution)/shard_map/ppermute | solution.py:275
  59.0 4.6 %collective-permute-start.19 = (f32[32,512]{1,0:T(8,128)S(1)}, f32[32,512]{1,0:T(8,128)S(1)}, u32[]{:S(2)}, u32[]{:S(2)}) collective-permute-start(f32[32,512]{1,0:T(8,128)S(1)} %total.5.chunk_ref.refs_0_), channel_id=1, source_target_pairs={{0,8},{4,12},{8,0},{12,4},{16,24},{20,28},{24,16},{28,20},{1,9},{5... | collective-permute-start | bytes 196616 | tf_op jit(solution)/shard_map/ppermute | solution.py:275
  65.3 4.8 %collective-permute-start.23 = (f32[32,768]{1,0:T(8,128)S(1)}, f32[32,768]{1,0:T(8,128)S(1)}, u32[]{:S(2)}, u32[]{:S(2)}) collective-permute-start(f32[32,768]{1,0:T(8,128)S(1)} %add.24.own_ref), channel_id=1, source_target_pairs={{0,3},{1,2},{2,1},{3,0},{4,7},{5,6},{6,5},{7,4},{8,11},{9,10},{10,... | collective-permute-start | bytes 294920 | tf_op jit(solution)/shard_map/ppermute | solution.py:275
  72.0 5.3 %collective-permute-start.26 = (f32[32,512]{1,0:T(8,128)S(1)}, f32[32,512]{1,0:T(8,128)S(1)}, u32[]{:S(2)}, u32[]{:S(2)}) collective-permute-start(f32[32,512]{1,0:T(8,128)S(1)} %get-tuple-element.66), channel_id=1, source_target_pairs={{0,12},{4,8},{8,4},{12,0},{16,28},{20,24},{24,20},{28,16},{1,13},{... | collective-permute-start | bytes 196616 | tf_op jit(solution)/shard_map/ppermute | solution.py:275
  73.7 4.8 %collective-permute-start.27 = (f32[32,512]{1,0:T(8,128)S(1)}, f32[32,512]{1,0:T(8,128)S(1)}, u32[]{:S(2)}, u32[]{:S(2)}) collective-permute-start(f32[32,512]{1,0:T(8,128)S(1)} %get-tuple-element.67), channel_id=1, source_target_pairs={{0,4},{4,0},{8,12},{12,8},{16,20},{20,16},{24,28},{28,24},{1,5},{5... | collective-permute-start | bytes 196616 | tf_op jit(solution)/shard_map/ppermute | solution.py:275
  75.6 5.8 %collective-permute-start.30 = (f32[32,128]{1,0:T(8,128)S(1)}, f32[32,128]{1,0:T(8,128)S(1)}, u32[]{:S(2)}, u32[]{:S(2)}) collective-permute-start(f32[32,128]{1,0:T(8,128)S(1)} %add.25.before_ref.own_ref), channel_id=1, source_target_pairs={{0,3},{1,2},{2,1},{3,0},{4,7},{5,6},{6,5},{7,4},{8,11},{9,10},{10,... | collective-permute-start | bytes 49160 | tf_op jit(solution)/shard_map/ppermute | solution.py:275
  79.1 5.9 %collective-permute-start.29 = (f32[32,512]{1,0:T(8,128)S(1)}, f32[32,512]{1,0:T(8,128)S(1)}, u32[]{:S(2)}, u32[]{:S(2)}) collective-permute-start(f32[32,512]{1,0:T(8,128)S(1)} %add.27.own_ref), channel_id=1, source_target_pairs={{0,16},{4,20},{8,24},{12,28},{16,0},{20,4},{24,8},{28,12},{1,17},{... | collective-permute-start | bytes 196616 | tf_op jit(solution)/shard_map/ppermute | solution.py:275
  85.2 5.2 %collective-permute-start.33 = (f32[32,512]{1,0:T(8,128)S(1)}, f32[32,512]{1,0:T(8,128)S(1)}, u32[]{:S(2)}, u32[]{:S(2)}) collective-permute-start(f32[32,512]{1,0:T(8,128)S(1)} %total.6.chunk_ref.refs_0_), channel_id=1, source_target_pairs={{0,12},{4,8},{8,4},{12,0},{16,28},{20,24},{24,20},{28,16},{1,13},{... | collective-permute-start | bytes 196616 | tf_op jit(solution)/shard_map/ppermute | solution.py:275
  86.3 5.0 %collective-permute-start.32 = (f32[32,512]{1,0:T(8,128)S(1)}, f32[32,512]{1,0:T(8,128)S(1)}, u32[]{:S(2)}, u32[]{:S(2)}) collective-permute-start(f32[32,512]{1,0:T(8,128)S(1)} %total.6.chunk_ref.refs_0_), channel_id=1, source_target_pairs={{0,4},{4,0},{8,12},{12,8},{16,20},{20,16},{24,28},{28,24},{1,5},{5... | collective-permute-start | bytes 196616 | tf_op jit(solution)/shard_map/ppermute | solution.py:275
  87.2 4.7 %collective-permute-start.31 = (f32[32,512]{1,0:T(8,128)S(1)}, f32[32,512]{1,0:T(8,128)S(1)}, u32[]{:S(2)}, u32[]{:S(2)}) collective-permute-start(f32[32,512]{1,0:T(8,128)S(1)} %total.6.chunk_ref.refs_0_), channel_id=1, source_target_pairs={{0,8},{4,12},{8,0},{12,4},{16,24},{20,28},{24,16},{28,20},{1,9},{5... | collective-permute-start | bytes 196616 | tf_op jit(solution)/shard_map/ppermute | solution.py:275
  93.6 4.8 %collective-permute-start.35 = (f32[32,768]{1,0:T(8,128)S(1)}, f32[32,768]{1,0:T(8,128)S(1)}, u32[]{:S(2)}, u32[]{:S(2)}) collective-permute-start(f32[32,768]{1,0:T(8,128)S(1)} %add.28.own_ref), channel_id=1, source_target_pairs={{0,3},{1,2},{2,1},{3,0},{4,7},{5,6},{6,5},{7,4},{8,11},{9,10},{10,... | collective-permute-start | bytes 294920 | tf_op jit(solution)/shard_map/ppermute | solution.py:275
  100.4 5.4 %collective-permute-start.38 = (f32[32,512]{1,0:T(8,128)S(1)}, f32[32,512]{1,0:T(8,128)S(1)}, u32[]{:S(2)}, u32[]{:S(2)}) collective-permute-start(f32[32,512]{1,0:T(8,128)S(1)} %get-tuple-element.75), channel_id=1, source_target_pairs={{0,12},{4,8},{8,4},{12,0},{16,28},{20,24},{24,20},{28,16},{1,13},{... | collective-permute-start | bytes 196616 | tf_op jit(solution)/shard_map/ppermute | solution.py:275
  101.9 5.0 %collective-permute-start.39 = (f32[32,512]{1,0:T(8,128)S(1)}, f32[32,512]{1,0:T(8,128)S(1)}, u32[]{:S(2)}, u32[]{:S(2)}) collective-permute-start(f32[32,512]{1,0:T(8,128)S(1)} %get-tuple-element.76), channel_id=1, source_target_pairs={{0,4},{4,0},{8,12},{12,8},{16,20},{20,16},{24,28},{28,24},{1,5},{5... | collective-permute-start | bytes 196616 | tf_op jit(solution)/shard_map/ppermute | solution.py:275
  103.9 5.8 %collective-permute-start.42 = (f32[32,128]{1,0:T(8,128)S(1)}, f32[32,128]{1,0:T(8,128)S(1)}, u32[]{:S(2)}, u32[]{:S(2)}) collective-permute-start(f32[32,128]{1,0:T(8,128)S(1)} %add.29.before_ref.own_ref), channel_id=1, source_target_pairs={{0,3},{1,2},{2,1},{3,0},{4,7},{5,6},{6,5},{7,4},{8,11},{9,10},{10,... | collective-permute-start | bytes 49160 | tf_op jit(solution)/shard_map/ppermute | solution.py:275
  107.3 5.9 %collective-permute-start.41 = (f32[32,512]{1,0:T(8,128)S(1)}, f32[32,512]{1,0:T(8,128)S(1)}, u32[]{:S(2)}, u32[]{:S(2)}) collective-permute-start(f32[32,512]{1,0:T(8,128)S(1)} %add.31.own_ref), channel_id=1, source_target_pairs={{0,16},{4,20},{8,24},{12,28},{16,0},{20,4},{24,8},{28,12},{1,17},{... | collective-permute-start | bytes 196616 | tf_op jit(solution)/shard_map/ppermute | solution.py:275
  113.4 5.4 %collective-permute-start.45 = (f32[32,512]{1,0:T(8,128)S(1)}, f32[32,512]{1,0:T(8,128)S(1)}, u32[]{:S(2)}, u32[]{:S(2)}) collective-permute-start(f32[32,512]{1,0:T(8,128)S(1)} %total.7.chunk_ref.refs_0_), channel_id=1, source_target_pairs={{0,12},{4,8},{8,4},{12,0},{16,28},{20,24},{24,20},{28,16},{1,13},{... | collective-permute-start | bytes 196616 | tf_op jit(solution)/shard_map/ppermute | solution.py:275
  114.5 5.0 %collective-permute-start.44 = (f32[32,512]{1,0:T(8,128)S(1)}, f32[32,512]{1,0:T(8,128)S(1)}, u32[]{:S(2)}, u32[]{:S(2)}) collective-permute-start(f32[32,512]{1,0:T(8,128)S(1)} %total.7.chunk_ref.refs_0_), channel_id=1, source_target_pairs={{0,4},{4,0},{8,12},{12,8},{16,20},{20,16},{24,28},{28,24},{1,5},{5... | collective-permute-start | bytes 196616 | tf_op jit(solution)/shard_map/ppermute | solution.py:275
  123.1 4.8 %collective-permute-start.48 = (bf16[32,1536]{1,0:T(8,128)(2,1)S(1)}, bf16[32,1536]{1,0:T(8,128)(2,1)S(1)}, u32[]{:S(2)}, u32[]{:S(2)}) collective-permute-start(bf16[32,1536]{1,0:T(8,128)(2,1)S(1)} %add.33.own_ref), channel_id=1, source_target_pairs={{0,3},{1,2},{2,1},{3,0},{4,7},{5,6},{6,5},{7,4},{8,11},{9,10},{10,... | collective-permute-start | bytes 294920 | tf_op jit(solution)/shard_map/ppermute | solution.py:275
  (19 other events, 40.1 us)

commit v10 on v9

--- a/solution.py
+++ b/solution.py
@@ -136,7 +136,7 @@
     n, tokens = out_ref.shape
     place = {"all": 0, "kept": core(), "sent": 1 - core()}[half]
     place = aligned(place, tokens) if half != "all" else slice(None)
-    chunk = chunk_ref[:n, :]
+    chunk = chunk_ref[:n, :].astype(F32)
     shift = jnp.sum(chunk * mean_ref[n : n + 1, :], axis=1, keepdims=True)
     rows = rows_ref[place, aligned(position() ^ part, chunk.shape[1])]
     value = join(contract_last(split(chunk), rows)) - shift
@@ -146,7 +146,7 @@
 def gram_kernel(*refs):
     *refs, out_ref = refs
     n = out_ref.shape[0]
-    chunks = {part: ref[:n, :] for part, ref in zip(GATHER, refs)}
+    chunks = {part: ref[:n, :].astype(F32) for part, ref in zip(GATHER, refs)}
     parts = [contract_last(chunks[part], chunks[part], HIGHEST) for part in range(PEERS)]
     out_ref[...] = jnp.zeros(out_ref.shape, F32)
     out_ref[:, :n] = (parts[0] + parts[1]) + (parts[2] + parts[3])
@@ -237,7 +237,7 @@
     *chunks, out_ref = refs
     width = chunks[0].shape[1]
     for part, chunk in zip(GATHER, chunks):
-        out_ref[:, aligned(position() ^ part, width)] = stacked(chunk[...])
+        out_ref[:, aligned(position() ^ part, width)] = stacked(chunk[...].astype(F32))
 
 
 def last_kernel(own_ref, got_ref, lower_ref, image_ref, scores_ref, basis_ref):
@@ -249,7 +249,7 @@
 
 def normalised_total_kernel(own_ref, got_ref, lower_ref, out_ref):
     value = own_ref[...] + got_ref[...]
-    out_ref[...] = product(lower_ref[...], stacked(value))
+    out_ref[...] = product(lower_ref[...], stacked(value)).astype(out_ref.dtype)
 
 
 def ordered_copy_kernel(value_ref, before_ref, out_ref):
@@ -330,7 +330,7 @@
         for distance in steps:
             image = add(image, swap(image, "tok", distance))
         kernel = functools.partial(first_total_kernel, rows_in_all) if first else normalised_total_kernel
-        image = call(kernel, [chunk], "total")(image, swap(image, "tok", last_step), *lower)[0]
+        image = call(kernel, [(chunk[0], BF16 if last else F32)], "total")(image, swap(image, "tok", last_step), *lower)[0]
         images = share(image, "tok")
         means = means or images
         ranked = [means[GATHER.index(part)] for part in SCATTER]

time: 129 us -> 129 us (level)
  transfers between devices with their start and end apart: 50 -> 50, of which waited for: 36 -> 36; matrix products, arithmetic and copies ran while one was open for 0% -> 0% of each run, Pallas kernels for 20% -> 21%
where the time goes in v10:
time: 129 us
  starting transfers between devices  51.4 us (40%)
  waiting for transfers between devices  40.3 us (31%)
  Pallas kernels  35.8 us (28%)
    ppermute x50, starting transfers between devices, swap(): return lax.ppermute(value, axis, [(i, i ^ distance) for i in range(size)])  51.4 us
    ppermute x50, waiting for transfers between devices, swap(): return lax.ppermute(value, axis, [(i, i ^ distance) for i in range(size)])  40.3 us
    pallas_call x66, Pallas kernels, run(): pl.pallas_call(kernel, out_shape=[jax.ShapeDtypeStruct(shape, dtype) for...  35.8 us
  transfers between devices with their start and end apart: 50, of which 36 were waited for; matrix products, arithmetic and copies ran while one was open for 0% of the time, Pallas kernels for 21%

profile of v10, /device:TPU:0, one launch (start us, length us, event | category | flops | bytes accessed | tf_op | source)
XLA Modules:
  0.0 128.5 jit_solution(311137291421125122)
XLA Ops:
  0.6 2.0 %fetch.1.ready_ref = bf16[1536,2048]{1,0:T(8,128)(2,1)S(1)} custom-call(bf16[1536,2048]{1,0:T(8,128)(2,1)} %rows_hbm.3), custom_call_target="tpu_custom_call" | custom-call | tf_op jit(solution)/shard_map/fetch/pallas_call | solution.py:29
  2.6 1.9 %sent_projection.4 = (f32[32,768]{1,0:T(8,128)S(1)}, bf16[1536,2048]{1,0:T(8,128)(2,1)S(1)}) custom-call(f32[32,2048]{1,0:T(8,128)S(1)} %copy-done, bf16[1536,2048]{1,0:T(8,128)(2,1)} %rows_hbm.3, bf16[1536,2048]{1,0:T(8,128)(2,1)S(1)} %fetch.1.ready_ref), custom_call_target="tpu_custom_call", output_to_operand_aliasing={{1}: (2, {})} | custom-call | tf_op jit(solution)/shard_map/sent_projection/pallas_call | solution.py:29
  6.2 2.7 %collective-permute-start.1 = (f32[32,768]{1,0:T(8,128)S(1)}, f32[32,768]{1,0:T(8,128)S(1)}, u32[]{:S(2)}, u32[]{:S(2)}) collective-permute-start(f32[32,768]{1,0:T(8,128)S(1)} %add.17.refs_0_), channel_id=1, source_target_pairs={{0,3},{1,2},{2,1},{3,0},{4,7},{5,6},{6,5},{7,4},{8,11},{9,10},{10,... | collective-permute-start | bytes 294920 | tf_op jit(solution)/shard_map/ppermute | solution.py:275
  8.8 3.0 %collective-permute-done.1.refs_1_ = f32[32,768]{1,0:T(8,128)S(1)} collective-permute-done((f32[32,768]{1,0:T(8,128)S(1)}, f32[32,768]{1,0:T(8,128)S(1)}, u32[]{:S(2)}, u32[]{:S(2)}) %collective-permute-start.1) | collective-permute-done | bytes 98336 | tf_op jit(solution)/shard_map/ppermute | solution.py:275
  13.8 2.9 %collective-permute-start.3 = (f32[40,512]{1,0:T(8,128)S(1)}, f32[40,512]{1,0:T(8,128)S(1)}, u32[]{:S(2)}, u32[]{:S(2)}) collective-permute-start(f32[40,512]{1,0:T(8,128)S(1)} %get-tuple-element.48), channel_id=1, source_target_pairs={{0,12},{4,8},{8,4},{12,0},{16,28},{20,24},{24,20},{28,16},{1,13},{... | collective-permute-start | bytes 245768 | tf_op jit(solution)/shard_map/ppermute | solution.py:275
  17.7 1.9 %collective-permute-done.3.refs_1_ = f32[40,512]{1,0:T(8,128)S(1)} collective-permute-done((f32[40,512]{1,0:T(8,128)S(1)}, f32[40,512]{1,0:T(8,128)S(1)}, u32[]{:S(2)}, u32[]{:S(2)}) %collective-permute-start.3) | collective-permute-done | bytes 81952 | tf_op jit(solution)/shard_map/ppermute | solution.py:275
  19.6 1.7 %collective-permute-done.4.refs_2_ = f32[40,512]{1,0:T(8,128)S(1)} collective-permute-done((f32[40,512]{1,0:T(8,128)S(1)}, f32[40,512]{1,0:T(8,128)S(1)}, u32[]{:S(2)}, u32[]{:S(2)}) %collective-permute-start.4) | collective-permute-done | bytes 81952 | tf_op jit(solution)/shard_map/ppermute | solution.py:275
  21.7 2.7 %collective-permute-start.6 = (f32[40,512]{1,0:T(8,128)S(1)}, f32[40,512]{1,0:T(8,128)S(1)}, u32[]{:S(2)}, u32[]{:S(2)}) collective-permute-start(f32[40,512]{1,0:T(8,128)S(1)} %add.19.own_ref), channel_id=1, source_target_pairs={{0,16},{4,20},{8,24},{12,28},{16,0},{20,4},{24,8},{28,12},{1,17},{... | collective-permute-start | bytes 245768 | tf_op jit(solution)/shard_map/ppermute | solution.py:275
  24.3 4.3 %collective-permute-done.6.got_ref = f32[40,512]{1,0:T(8,128)S(1)} collective-permute-done((f32[40,512]{1,0:T(8,128)S(1)}, f32[40,512]{1,0:T(8,128)S(1)}, u32[]{:S(2)}, u32[]{:S(2)}) %collective-permute-start.6) | collective-permute-done | bytes 81952 | tf_op jit(solution)/shard_map/ppermute | solution.py:275
  30.2 2.0 %collective-permute-start.7 = (f32[40,512]{1,0:T(8,128)S(1)}, f32[40,512]{1,0:T(8,128)S(1)}, u32[]{:S(2)}, u32[]{:S(2)}) collective-permute-start(f32[40,512]{1,0:T(8,128)S(1)} %total.4.chunk_ref.mean_ref.refs_0_), channel_id=1, source_target_pairs={{0,8},{4,12},{8,0},{12,4},{16,24},{20,28},{24,16},{28,20},{1,9},{5... | collective-permute-start | bytes 245768 | tf_op jit(solution)/shard_map/ppermute | solution.py:275
  32.8 1.4 %collective-permute-done.9.chunk_ref.mean_ref.refs_1_.refs_0_ = f32[40,512]{1,0:T(8,128)S(1)} collective-permute-done((f32[40,512]{1,0:T(8,128)S(1)}, f32[40,512]{1,0:T(8,128)S(1)}, u32[]{:S(2)}, u32[]{:S(2)}) %collective-permute-start.9) | collective-permute-done | bytes 81952 | tf_op jit(solution)/shard_map/ppermute | solution.py:275
  37.2 1.3 %collective-permute-start.11 = (f32[32,768]{1,0:T(8,128)S(1)}, f32[32,768]{1,0:T(8,128)S(1)}, u32[]{:S(2)}, u32[]{:S(2)}) collective-permute-start(f32[32,768]{1,0:T(8,128)S(1)} %add.20.own_ref), channel_id=1, source_target_pairs={{0,3},{1,2},{2,1},{3,0},{4,7},{5,6},{6,5},{7,4},{8,11},{9,10},{10,... | collective-permute-start | bytes 294920 | tf_op jit(solution)/shard_map/ppermute | solution.py:275
  40.0 1.9 %collective-permute-done.11.got_ref = f32[32,768]{1,0:T(8,128)S(1)} collective-permute-done((f32[32,768]{1,0:T(8,128)S(1)}, f32[32,768]{1,0:T(8,128)S(1)}, u32[]{:S(2)}, u32[]{:S(2)}) %collective-permute-start.11) | collective-permute-done | bytes 98336 | tf_op jit(solution)/shard_map/ppermute | solution.py:275
  43.9 1.5 %collective-permute-start.14 = (f32[32,512]{1,0:T(8,128)S(1)}, f32[32,512]{1,0:T(8,128)S(1)}, u32[]{:S(2)}, u32[]{:S(2)}) collective-permute-start(f32[32,512]{1,0:T(8,128)S(1)} %get-tuple-element.57), channel_id=1, source_target_pairs={{0,12},{4,8},{8,4},{12,0},{16,28},{20,24},{24,20},{28,16},{1,13},{... | collective-permute-start | bytes 196616 | tf_op jit(solution)/shard_map/ppermute | solution.py:275
  50.9 2.2 %collective-permute-start.17 = (f32[32,512]{1,0:T(8,128)S(1)}, f32[32,512]{1,0:T(8,128)S(1)}, u32[]{:S(2)}, u32[]{:S(2)}) collective-permute-start(f32[32,512]{1,0:T(8,128)S(1)} %add.23.own_ref), channel_id=1, source_target_pairs={{0,16},{4,20},{8,24},{12,28},{16,0},{20,4},{24,8},{28,12},{1,17},{... | collective-permute-start | bytes 196616 | tf_op jit(solution)/shard_map/ppermute | solution.py:275
  53.2 2.9 %inverse_factor.4.lower_ref = f32[32,32]{1,0:T(8,128)S(1)} custom-call(f32[32,128]{1,0:T(8,128)S(1)} %add.21.before_ref.own_ref, f32[32,128]{1,0:T(8,128)S(1)} %collective-permute-done.18.got_ref), custom_call_target="tpu_custom_call" | custom-call | flops 17179869184 | tf_op jit(solution)/shard_map/inverse_factor/pallas_call | solution.py:29
  59.0 1.6 %collective-permute-start.19 = (f32[32,512]{1,0:T(8,128)S(1)}, f32[32,512]{1,0:T(8,128)S(1)}, u32[]{:S(2)}, u32[]{:S(2)}) collective-permute-start(f32[32,512]{1,0:T(8,128)S(1)} %total.5.chunk_ref.refs_0_), channel_id=1, source_target_pairs={{0,8},{4,12},{8,0},{12,4},{16,24},{20,28},{24,16},{28,20},{1,9},{5... | collective-permute-start | bytes 196616 | tf_op jit(solution)/shard_map/ppermute | solution.py:275
  65.3 1.3 %collective-permute-start.23 = (f32[32,768]{1,0:T(8,128)S(1)}, f32[32,768]{1,0:T(8,128)S(1)}, u32[]{:S(2)}, u32[]{:S(2)}) collective-permute-start(f32[32,768]{1,0:T(8,128)S(1)} %add.24.own_ref), channel_id=1, source_target_pairs={{0,3},{1,2},{2,1},{3,0},{4,7},{5,6},{6,5},{7,4},{8,11},{9,10},{10,... | collective-permute-start | bytes 294920 | tf_op jit(solution)/shard_map/ppermute | solution.py:275
  68.2 1.9 %collective-permute-done.23.got_ref = f32[32,768]{1,0:T(8,128)S(1)} collective-permute-done((f32[32,768]{1,0:T(8,128)S(1)}, f32[32,768]{1,0:T(8,128)S(1)}, u32[]{:S(2)}, u32[]{:S(2)}) %collective-permute-start.23) | collective-permute-done | bytes 98336 | tf_op jit(solution)/shard_map/ppermute | solution.py:275
  72.0 1.7 %collective-permute-start.26 = (f32[32,512]{1,0:T(8,128)S(1)}, f32[32,512]{1,0:T(8,128)S(1)}, u32[]{:S(2)}, u32[]{:S(2)}) collective-permute-start(f32[32,512]{1,0:T(8,128)S(1)} %get-tuple-element.66), channel_id=1, source_target_pairs={{0,12},{4,8},{8,4},{12,0},{16,28},{20,24},{24,20},{28,16},{1,13},{... | collective-permute-start | bytes 196616 | tf_op jit(solution)/shard_map/ppermute | solution.py:275
  77.3 1.2 collective-permute-done.27.refs_2_
  79.1 2.2 %collective-permute-start.29 = (f32[32,512]{1,0:T(8,128)S(1)}, f32[32,512]{1,0:T(8,128)S(1)}, u32[]{:S(2)}, u32[]{:S(2)}) collective-permute-start(f32[32,512]{1,0:T(8,128)S(1)} %add.27.own_ref), channel_id=1, source_target_pairs={{0,16},{4,20},{8,24},{12,28},{16,0},{20,4},{24,8},{28,12},{1,17},{... | collective-permute-start | bytes 196616 | tf_op jit(solution)/shard_map/ppermute | solution.py:275
  81.4 2.9 %inverse_factor.5.lower_ref = f32[32,32]{1,0:T(8,128)S(1)} custom-call(f32[32,128]{1,0:T(8,128)S(1)} %add.25.before_ref.own_ref, f32[32,128]{1,0:T(8,128)S(1)} %collective-permute-done.30.got_ref), custom_call_target="tpu_custom_call" | custom-call | flops 17179869184 | tf_op jit(solution)/shard_map/inverse_factor/pallas_call | solution.py:29
  87.2 1.6 %collective-permute-start.31 = (f32[32,512]{1,0:T(8,128)S(1)}, f32[32,512]{1,0:T(8,128)S(1)}, u32[]{:S(2)}, u32[]{:S(2)}) collective-permute-start(f32[32,512]{1,0:T(8,128)S(1)} %total.6.chunk_ref.refs_0_), channel_id=1, source_target_pairs={{0,8},{4,12},{8,0},{12,4},{16,24},{20,28},{24,16},{28,20},{1,9},{5... | collective-permute-start | bytes 196616 | tf_op jit(solution)/shard_map/ppermute | solution.py:275
  93.6 1.3 %collective-permute-start.35 = (f32[32,768]{1,0:T(8,128)S(1)}, f32[32,768]{1,0:T(8,128)S(1)}, u32[]{:S(2)}, u32[]{:S(2)}) collective-permute-start(f32[32,768]{1,0:T(8,128)S(1)} %add.28.own_ref), channel_id=1, source_target_pairs={{0,3},{1,2},{2,1},{3,0},{4,7},{5,6},{6,5},{7,4},{8,11},{9,10},{10,... | collective-permute-start | bytes 294920 | tf_op jit(solution)/shard_map/ppermute | solution.py:275
  96.5 1.9 %collective-permute-done.35.got_ref = f32[32,768]{1,0:T(8,128)S(1)} collective-permute-done((f32[32,768]{1,0:T(8,128)S(1)}, f32[32,768]{1,0:T(8,128)S(1)}, u32[]{:S(2)}, u32[]{:S(2)}) %collective-permute-start.35) | collective-permute-done | bytes 98336 | tf_op jit(solution)/shard_map/ppermute | solution.py:275
  100.4 1.5 %collective-permute-start.38 = (f32[32,512]{1,0:T(8,128)S(1)}, f32[32,512]{1,0:T(8,128)S(1)}, u32[]{:S(2)}, u32[]{:S(2)}) collective-permute-start(f32[32,512]{1,0:T(8,128)S(1)} %get-tuple-element.75), channel_id=1, source_target_pairs={{0,12},{4,8},{8,4},{12,0},{16,28},{20,24},{24,20},{28,16},{1,13},{... | collective-permute-start | bytes 196616 | tf_op jit(solution)/shard_map/ppermute | solution.py:275
  107.3 2.4 %collective-permute-start.41 = (f32[32,512]{1,0:T(8,128)S(1)}, f32[32,512]{1,0:T(8,128)S(1)}, u32[]{:S(2)}, u32[]{:S(2)}) collective-permute-start(f32[32,512]{1,0:T(8,128)S(1)} %add.31.own_ref), channel_id=1, source_target_pairs={{0,16},{4,20},{8,24},{12,28},{16,0},{20,4},{24,8},{28,12},{1,17},{... | collective-permute-start | bytes 196616 | tf_op jit(solution)/shard_map/ppermute | solution.py:275
  109.7 2.9 %inverse_factor.6.lower_ref = f32[32,32]{1,0:T(8,128)S(1)} custom-call(f32[32,128]{1,0:T(8,128)S(1)} %add.29.before_ref.own_ref, f32[32,128]{1,0:T(8,128)S(1)} %collective-permute-done.42.got_ref), custom_call_target="tpu_custom_call" | custom-call | flops 17179869184 | tf_op jit(solution)/shard_map/inverse_factor/pallas_call | solution.py:29
  115.3 1.6 %collective-permute-start.43 = (bf16[32,512]{1,0:T(8,128)(2,1)S(1)}, bf16[32,512]{1,0:T(8,128)(2,1)S(1)}, u32[]{:S(2)}, u32[]{:S(2)}) collective-permute-start(bf16[32,512]{1,0:T(8,128)(2,1)S(1)} %total.7.chunk_ref.refs_0_), channel_id=1, source_target_pairs={{0,8},{4,12},{8,0},{12,4},{16,24},{20,28},{24,16},{28,20},{1,9},{5... | collective-permute-start | bytes 98312 | tf_op jit(solution)/shard_map/ppermute | solution.py:275
  122.7 1.3 %collective-permute-start.48 = (bf16[32,1536]{1,0:T(8,128)(2,1)S(1)}, bf16[32,1536]{1,0:T(8,128)(2,1)S(1)}, u32[]{:S(2)}, u32[]{:S(2)}) collective-permute-start(bf16[32,1536]{1,0:T(8,128)(2,1)S(1)} %add.33.own_ref), channel_id=1, source_target_pairs={{0,3},{1,2},{2,1},{3,0},{4,7},{5,6},{6,5},{7,4},{8,11},{9,10},{10,... | collective-permute-start | bytes 294920 | tf_op jit(solution)/shard_map/ppermute | solution.py:275
  124.6 2.9 %inverse_factor.7.lower_ref = f32[32,32]{1,0:T(8,128)S(1)} custom-call(f32[32,128]{1,0:T(8,128)S(1)} %add.32.before_ref.own_ref, f32[32,128]{1,0:T(8,128)S(1)} %collective-permute-done.49.got_ref), custom_call_target="tpu_custom_call" | custom-call | flops 17179869184 | tf_op jit(solution)/shard_map/inverse_factor/pallas_call | solution.py:29
  (136 shorter events, 60.9 us)
Async XLA Ops:
  6.2 5.7 %collective-permute-start.1 = (f32[32,768]{1,0:T(8,128)S(1)}, f32[32,768]{1,0:T(8,128)S(1)}, u32[]{:S(2)}, u32[]{:S(2)}) collective-permute-start(f32[32,768]{1,0:T(8,128)S(1)} %add.17.refs_0_), channel_id=1, source_target_pairs={{0,3},{1,2},{2,1},{3,0},{4,7},{5,6},{6,5},{7,4},{8,11},{9,10},{10,... | collective-permute-start | bytes 294920 | tf_op jit(solution)/shard_map/ppermute | solution.py:275
  13.8 5.7 %collective-permute-start.3 = (f32[40,512]{1,0:T(8,128)S(1)}, f32[40,512]{1,0:T(8,128)S(1)}, u32[]{:S(2)}, u32[]{:S(2)}) collective-permute-start(f32[40,512]{1,0:T(8,128)S(1)} %get-tuple-element.48), channel_id=1, source_target_pairs={{0,12},{4,8},{8,4},{12,0},{16,28},{20,24},{24,20},{28,16},{1,13},{... | collective-permute-start | bytes 245768 | tf_op jit(solution)/shard_map/ppermute | solution.py:275
  16.7 4.6 %collective-permute-start.4 = (f32[40,512]{1,0:T(8,128)S(1)}, f32[40,512]{1,0:T(8,128)S(1)}, u32[]{:S(2)}, u32[]{:S(2)}) collective-permute-start(f32[40,512]{1,0:T(8,128)S(1)} %get-tuple-element.49), channel_id=1, source_target_pairs={{0,4},{4,0},{8,12},{12,8},{16,20},{20,16},{24,28},{28,24},{1,5},{5... | collective-permute-start | bytes 245768 | tf_op jit(solution)/shard_map/ppermute | solution.py:275
  17.2 4.4 %collective-permute-start.5 = (f32[40,512]{1,0:T(8,128)S(1)}, f32[40,512]{1,0:T(8,128)S(1)}, u32[]{:S(2)}, u32[]{:S(2)}) collective-permute-start(f32[40,512]{1,0:T(8,128)S(1)} %get-tuple-element.50), channel_id=1, source_target_pairs={{0,8},{4,12},{8,0},{12,4},{16,24},{20,28},{24,16},{28,20},{1,9},{5... | collective-permute-start | bytes 245768 | tf_op jit(solution)/shard_map/ppermute | solution.py:275
  21.7 7.0 %collective-permute-start.6 = (f32[40,512]{1,0:T(8,128)S(1)}, f32[40,512]{1,0:T(8,128)S(1)}, u32[]{:S(2)}, u32[]{:S(2)}) collective-permute-start(f32[40,512]{1,0:T(8,128)S(1)} %add.19.own_ref), channel_id=1, source_target_pairs={{0,16},{4,20},{8,24},{12,28},{16,0},{20,4},{24,8},{28,12},{1,17},{... | collective-permute-start | bytes 245768 | tf_op jit(solution)/shard_map/ppermute | solution.py:275
  28.7 5.4 %collective-permute-start.9 = (f32[40,512]{1,0:T(8,128)S(1)}, f32[40,512]{1,0:T(8,128)S(1)}, u32[]{:S(2)}, u32[]{:S(2)}) collective-permute-start(f32[40,512]{1,0:T(8,128)S(1)} %total.4.chunk_ref.mean_ref.refs_0_), channel_id=1, source_target_pairs={{0,12},{4,8},{8,4},{12,0},{16,28},{20,24},{24,20},{28,16},{1,13},{... | collective-permute-start | bytes 245768 | tf_op jit(solution)/shard_map/ppermute | solution.py:275
  29.4 5.4 %collective-permute-start.8 = (f32[40,512]{1,0:T(8,128)S(1)}, f32[40,512]{1,0:T(8,128)S(1)}, u32[]{:S(2)}, u32[]{:S(2)}) collective-permute-start(f32[40,512]{1,0:T(8,128)S(1)} %total.4.chunk_ref.mean_ref.refs_0_), channel_id=1, source_target_pairs={{0,4},{4,0},{8,12},{12,8},{16,20},{20,16},{24,28},{28,24},{1,5},{5... | collective-permute-start | bytes 245768 | tf_op jit(solution)/shard_map/ppermute | solution.py:275
  30.2 5.2 %collective-permute-start.7 = (f32[40,512]{1,0:T(8,128)S(1)}, f32[40,512]{1,0:T(8,128)S(1)}, u32[]{:S(2)}, u32[]{:S(2)}) collective-permute-start(f32[40,512]{1,0:T(8,128)S(1)} %total.4.chunk_ref.mean_ref.refs_0_), channel_id=1, source_target_pairs={{0,8},{4,12},{8,0},{12,4},{16,24},{20,28},{24,16},{28,20},{1,9},{5... | collective-permute-start | bytes 245768 | tf_op jit(solution)/shard_map/ppermute | solution.py:275
  37.2 4.8 %collective-permute-start.11 = (f32[32,768]{1,0:T(8,128)S(1)}, f32[32,768]{1,0:T(8,128)S(1)}, u32[]{:S(2)}, u32[]{:S(2)}) collective-permute-start(f32[32,768]{1,0:T(8,128)S(1)} %add.20.own_ref), channel_id=1, source_target_pairs={{0,3},{1,2},{2,1},{3,0},{4,7},{5,6},{6,5},{7,4},{8,11},{9,10},{10,... | collective-permute-start | bytes 294920 | tf_op jit(solution)/shard_map/ppermute | solution.py:275
  43.9 5.3 %collective-permute-start.14 = (f32[32,512]{1,0:T(8,128)S(1)}, f32[32,512]{1,0:T(8,128)S(1)}, u32[]{:S(2)}, u32[]{:S(2)}) collective-permute-start(f32[32,512]{1,0:T(8,128)S(1)} %get-tuple-element.57), channel_id=1, source_target_pairs={{0,12},{4,8},{8,4},{12,0},{16,28},{20,24},{24,20},{28,16},{1,13},{... | collective-permute-start | bytes 196616 | tf_op jit(solution)/shard_map/ppermute | solution.py:275
  45.4 5.0 %collective-permute-start.15 = (f32[32,512]{1,0:T(8,128)S(1)}, f32[32,512]{1,0:T(8,128)S(1)}, u32[]{:S(2)}, u32[]{:S(2)}) collective-permute-start(f32[32,512]{1,0:T(8,128)S(1)} %get-tuple-element.58), channel_id=1, source_target_pairs={{0,4},{4,0},{8,12},{12,8},{16,20},{20,16},{24,28},{28,24},{1,5},{5... | collective-permute-start | bytes 196616 | tf_op jit(solution)/shard_map/ppermute | solution.py:275
  47.5 5.7 %collective-permute-start.18 = (f32[32,128]{1,0:T(8,128)S(1)}, f32[32,128]{1,0:T(8,128)S(1)}, u32[]{:S(2)}, u32[]{:S(2)}) collective-permute-start(f32[32,128]{1,0:T(8,128)S(1)} %add.21.before_ref.own_ref), channel_id=1, source_target_pairs={{0,3},{1,2},{2,1},{3,0},{4,7},{5,6},{6,5},{7,4},{8,11},{9,10},{10,... | collective-permute-start | bytes 49160 | tf_op jit(solution)/shard_map/ppermute | solution.py:275
  50.9 5.9 %collective-permute-start.17 = (f32[32,512]{1,0:T(8,128)S(1)}, f32[32,512]{1,0:T(8,128)S(1)}, u32[]{:S(2)}, u32[]{:S(2)}) collective-permute-start(f32[32,512]{1,0:T(8,128)S(1)} %add.23.own_ref), channel_id=1, source_target_pairs={{0,16},{4,20},{8,24},{12,28},{16,0},{20,4},{24,8},{28,12},{1,17},{... | collective-permute-start | bytes 196616 | tf_op jit(solution)/shard_map/ppermute | solution.py:275
  57.1 5.2 %collective-permute-start.21 = (f32[32,512]{1,0:T(8,128)S(1)}, f32[32,512]{1,0:T(8,128)S(1)}, u32[]{:S(2)}, u32[]{:S(2)}) collective-permute-start(f32[32,512]{1,0:T(8,128)S(1)} %total.5.chunk_ref.refs_0_), channel_id=1, source_target_pairs={{0,12},{4,8},{8,4},{12,0},{16,28},{20,24},{24,20},{28,16},{1,13},{... | collective-permute-start | bytes 196616 | tf_op jit(solution)/shard_map/ppermute | solution.py:275
  58.1 4.8 %collective-permute-start.20 = (f32[32,512]{1,0:T(8,128)S(1)}, f32[32,512]{1,0:T(8,128)S(1)}, u32[]{:S(2)}, u32[]{:S(2)}) collective-permute-start(f32[32,512]{1,0:T(8,128)S(1)} %total.5.chunk_ref.refs_0_), channel_id=1, source_target_pairs={{0,4},{4,0},{8,12},{12,8},{16,20},{20,16},{24,28},{28,24},{1,5},{5... | collective-permute-start | bytes 196616 | tf_op jit(solution)/shard_map/ppermute | solution.py:275
  59.0 4.6 %collective-permute-start.19 = (f32[32,512]{1,0:T(8,128)S(1)}, f32[32,512]{1,0:T(8,128)S(1)}, u32[]{:S(2)}, u32[]{:S(2)}) collective-permute-start(f32[32,512]{1,0:T(8,128)S(1)} %total.5.chunk_ref.refs_0_), channel_id=1, source_target_pairs={{0,8},{4,12},{8,0},{12,4},{16,24},{20,28},{24,16},{28,20},{1,9},{5... | collective-permute-start | bytes 196616 | tf_op jit(solution)/shard_map/ppermute | solution.py:275
  65.3 4.8 %collective-permute-start.23 = (f32[32,768]{1,0:T(8,128)S(1)}, f32[32,768]{1,0:T(8,128)S(1)}, u32[]{:S(2)}, u32[]{:S(2)}) collective-permute-start(f32[32,768]{1,0:T(8,128)S(1)} %add.24.own_ref), channel_id=1, source_target_pairs={{0,3},{1,2},{2,1},{3,0},{4,7},{5,6},{6,5},{7,4},{8,11},{9,10},{10,... | collective-permute-start | bytes 294920 | tf_op jit(solution)/shard_map/ppermute | solution.py:275
  72.0 5.3 %collective-permute-start.26 = (f32[32,512]{1,0:T(8,128)S(1)}, f32[32,512]{1,0:T(8,128)S(1)}, u32[]{:S(2)}, u32[]{:S(2)}) collective-permute-start(f32[32,512]{1,0:T(8,128)S(1)} %get-tuple-element.66), channel_id=1, source_target_pairs={{0,12},{4,8},{8,4},{12,0},{16,28},{20,24},{24,20},{28,16},{1,13},{... | collective-permute-start | bytes 196616 | tf_op jit(solution)/shard_map/ppermute | solution.py:275
  73.7 4.8 %collective-permute-start.27 = (f32[32,512]{1,0:T(8,128)S(1)}, f32[32,512]{1,0:T(8,128)S(1)}, u32[]{:S(2)}, u32[]{:S(2)}) collective-permute-start(f32[32,512]{1,0:T(8,128)S(1)} %get-tuple-element.67), channel_id=1, source_target_pairs={{0,4},{4,0},{8,12},{12,8},{16,20},{20,16},{24,28},{28,24},{1,5},{5... | collective-permute-start | bytes 196616 | tf_op jit(solution)/shard_map/ppermute | solution.py:275
  75.6 5.8 %collective-permute-start.30 = (f32[32,128]{1,0:T(8,128)S(1)}, f32[32,128]{1,0:T(8,128)S(1)}, u32[]{:S(2)}, u32[]{:S(2)}) collective-permute-start(f32[32,128]{1,0:T(8,128)S(1)} %add.25.before_ref.own_ref), channel_id=1, source_target_pairs={{0,3},{1,2},{2,1},{3,0},{4,7},{5,6},{6,5},{7,4},{8,11},{9,10},{10,... | collective-permute-start | bytes 49160 | tf_op jit(solution)/shard_map/ppermute | solution.py:275
  79.1 5.9 %collective-permute-start.29 = (f32[32,512]{1,0:T(8,128)S(1)}, f32[32,512]{1,0:T(8,128)S(1)}, u32[]{:S(2)}, u32[]{:S(2)}) collective-permute-start(f32[32,512]{1,0:T(8,128)S(1)} %add.27.own_ref), channel_id=1, source_target_pairs={{0,16},{4,20},{8,24},{12,28},{16,0},{20,4},{24,8},{28,12},{1,17},{... | collective-permute-start | bytes 196616 | tf_op jit(solution)/shard_map/ppermute | solution.py:275
  85.2 5.2 %collective-permute-start.33 = (f32[32,512]{1,0:T(8,128)S(1)}, f32[32,512]{1,0:T(8,128)S(1)}, u32[]{:S(2)}, u32[]{:S(2)}) collective-permute-start(f32[32,512]{1,0:T(8,128)S(1)} %total.6.chunk_ref.refs_0_), channel_id=1, source_target_pairs={{0,12},{4,8},{8,4},{12,0},{16,28},{20,24},{24,20},{28,16},{1,13},{... | collective-permute-start | bytes 196616 | tf_op jit(solution)/shard_map/ppermute | solution.py:275
  86.3 5.0 %collective-permute-start.32 = (f32[32,512]{1,0:T(8,128)S(1)}, f32[32,512]{1,0:T(8,128)S(1)}, u32[]{:S(2)}, u32[]{:S(2)}) collective-permute-start(f32[32,512]{1,0:T(8,128)S(1)} %total.6.chunk_ref.refs_0_), channel_id=1, source_target_pairs={{0,4},{4,0},{8,12},{12,8},{16,20},{20,16},{24,28},{28,24},{1,5},{5... | collective-permute-start | bytes 196616 | tf_op jit(solution)/shard_map/ppermute | solution.py:275
  87.2 4.7 %collective-permute-start.31 = (f32[32,512]{1,0:T(8,128)S(1)}, f32[32,512]{1,0:T(8,128)S(1)}, u32[]{:S(2)}, u32[]{:S(2)}) collective-permute-start(f32[32,512]{1,0:T(8,128)S(1)} %total.6.chunk_ref.refs_0_), channel_id=1, source_target_pairs={{0,8},{4,12},{8,0},{12,4},{16,24},{20,28},{24,16},{28,20},{1,9},{5... | collective-permute-start | bytes 196616 | tf_op jit(solution)/shard_map/ppermute | solution.py:275
  93.6 4.8 %collective-permute-start.35 = (f32[32,768]{1,0:T(8,128)S(1)}, f32[32,768]{1,0:T(8,128)S(1)}, u32[]{:S(2)}, u32[]{:S(2)}) collective-permute-start(f32[32,768]{1,0:T(8,128)S(1)} %add.28.own_ref), channel_id=1, source_target_pairs={{0,3},{1,2},{2,1},{3,0},{4,7},{5,6},{6,5},{7,4},{8,11},{9,10},{10,... | collective-permute-start | bytes 294920 | tf_op jit(solution)/shard_map/ppermute | solution.py:275
  100.4 5.4 %collective-permute-start.38 = (f32[32,512]{1,0:T(8,128)S(1)}, f32[32,512]{1,0:T(8,128)S(1)}, u32[]{:S(2)}, u32[]{:S(2)}) collective-permute-start(f32[32,512]{1,0:T(8,128)S(1)} %get-tuple-element.75), channel_id=1, source_target_pairs={{0,12},{4,8},{8,4},{12,0},{16,28},{20,24},{24,20},{28,16},{1,13},{... | collective-permute-start | bytes 196616 | tf_op jit(solution)/shard_map/ppermute | solution.py:275
  101.9 5.0 %collective-permute-start.39 = (f32[32,512]{1,0:T(8,128)S(1)}, f32[32,512]{1,0:T(8,128)S(1)}, u32[]{:S(2)}, u32[]{:S(2)}) collective-permute-start(f32[32,512]{1,0:T(8,128)S(1)} %get-tuple-element.76), channel_id=1, source_target_pairs={{0,4},{4,0},{8,12},{12,8},{16,20},{20,16},{24,28},{28,24},{1,5},{5... | collective-permute-start | bytes 196616 | tf_op jit(solution)/shard_map/ppermute | solution.py:275
  103.9 5.8 %collective-permute-start.42 = (f32[32,128]{1,0:T(8,128)S(1)}, f32[32,128]{1,0:T(8,128)S(1)}, u32[]{:S(2)}, u32[]{:S(2)}) collective-permute-start(f32[32,128]{1,0:T(8,128)S(1)} %add.29.before_ref.own_ref), channel_id=1, source_target_pairs={{0,3},{1,2},{2,1},{3,0},{4,7},{5,6},{6,5},{7,4},{8,11},{9,10},{10,... | collective-permute-start | bytes 49160 | tf_op jit(solution)/shard_map/ppermute | solution.py:275
  107.3 5.9 %collective-permute-start.41 = (f32[32,512]{1,0:T(8,128)S(1)}, f32[32,512]{1,0:T(8,128)S(1)}, u32[]{:S(2)}, u32[]{:S(2)}) collective-permute-start(f32[32,512]{1,0:T(8,128)S(1)} %add.31.own_ref), channel_id=1, source_target_pairs={{0,16},{4,20},{8,24},{12,28},{16,0},{20,4},{24,8},{28,12},{1,17},{... | collective-permute-start | bytes 196616 | tf_op jit(solution)/shard_map/ppermute | solution.py:275
  113.4 4.8 %collective-permute-start.45 = (bf16[32,512]{1,0:T(8,128)(2,1)S(1)}, bf16[32,512]{1,0:T(8,128)(2,1)S(1)}, u32[]{:S(2)}, u32[]{:S(2)}) collective-permute-start(bf16[32,512]{1,0:T(8,128)(2,1)S(1)} %total.7.chunk_ref.refs_0_), channel_id=1, source_target_pairs={{0,12},{4,8},{8,4},{12,0},{16,28},{20,24},{24,20},{28,16},{1,13},{... | collective-permute-start | bytes 98312 | tf_op jit(solution)/shard_map/ppermute | solution.py:275
  114.5 4.4 %collective-permute-start.44 = (bf16[32,512]{1,0:T(8,128)(2,1)S(1)}, bf16[32,512]{1,0:T(8,128)(2,1)S(1)}, u32[]{:S(2)}, u32[]{:S(2)}) collective-permute-start(bf16[32,512]{1,0:T(8,128)(2,1)S(1)} %total.7.chunk_ref.refs_0_), channel_id=1, source_target_pairs={{0,4},{4,0},{8,12},{12,8},{16,20},{20,16},{24,28},{28,24},{1,5},{5... | collective-permute-start | bytes 98312 | tf_op jit(solution)/shard_map/ppermute | solution.py:275
  122.7 4.8 %collective-permute-start.48 = (bf16[32,1536]{1,0:T(8,128)(2,1)S(1)}, bf16[32,1536]{1,0:T(8,128)(2,1)S(1)}, u32[]{:S(2)}, u32[]{:S(2)}) collective-permute-start(bf16[32,1536]{1,0:T(8,128)(2,1)S(1)} %add.33.own_ref), channel_id=1, source_target_pairs={{0,3},{1,2},{2,1},{3,0},{4,7},{5,6},{6,5},{7,4},{8,11},{9,10},{10,... | collective-permute-start | bytes 294920 | tf_op jit(solution)/shard_map/ppermute | solution.py:275
  (19 other events, 39.8 us)

commit v11 on v9

--- a/solution.py
+++ b/solution.py
@@ -12,7 +12,7 @@
 LANES = 128
 EXTRA = 8
 SCATTER = (0, 3, 1, 2)
-GATHER = (0, 3, 1, 2)
+GATHER = (0, 3, 2, 1)
 TERMS = 3
 LONG = pl.CostEstimate(flops=2**34, bytes_accessed=0, transcendentals=0)
 SHORT = pl.CostEstimate(flops=2**29, bytes_accessed=0, transcendentals=0)

time: 129 us -> 129 us (level)
  waiting for transfers between devices: 40.7 us -> 37.8 us
  starting transfers between devices: 51.4 us -> 54 us
    ppermute x50, waiting for transfers between devices: 40.7 us -> 37.8 us  [swap(): return lax.ppermute(value, axis, [(i, i ^ distance) for i in range(size)])]
    ppermute x50, starting transfers between devices: 51.4 us -> 54 us  [swap(): return lax.ppermute(value, axis, [(i, i ^ distance) for i in range(size)])]
  transfers between devices with their start and end apart: 50 -> 50, of which waited for: 36 -> 34; matrix products, arithmetic and copies ran while one was open for 0% -> 0% of each run, Pallas kernels for 20% -> 21%
where the time goes in v11:
time: 129 us
  starting transfers between devices  54 us (42%)
  waiting for transfers between devices  37.8 us (29%)
  Pallas kernels  35.8 us (28%)
    ppermute x50, starting transfers between devices, swap(): return lax.ppermute(value, axis, [(i, i ^ distance) for i in range(size)])  54 us
    ppermute x50, waiting for transfers between devices, swap(): return lax.ppermute(value, axis, [(i, i ^ distance) for i in range(size)])  37.8 us
    pallas_call x66, Pallas kernels, run(): pl.pallas_call(kernel, out_shape=[jax.ShapeDtypeStruct(shape, dtype) for...  35.8 us
  transfers between devices with their start and end apart: 50, of which 34 were waited for; matrix products, arithmetic and copies ran while one was open for 0% of the time, Pallas kernels for 21%

profile of v11, /device:TPU:0, one launch (start us, length us, event | category | flops | bytes accessed | tf_op | source)
XLA Modules:
  0.0 128.6 jit_solution(11951869059626647742)
XLA Ops:
  0.6 2.0 %fetch.1.ready_ref = bf16[1536,2048]{1,0:T(8,128)(2,1)S(1)} custom-call(bf16[1536,2048]{1,0:T(8,128)(2,1)} %rows_hbm.3), custom_call_target="tpu_custom_call" | custom-call | tf_op jit(solution)/shard_map/fetch/pallas_call | solution.py:29
  2.6 1.9 %sent_projection.4 = (f32[32,768]{1,0:T(8,128)S(1)}, bf16[1536,2048]{1,0:T(8,128)(2,1)S(1)}) custom-call(f32[32,2048]{1,0:T(8,128)S(1)} %copy-done, bf16[1536,2048]{1,0:T(8,128)(2,1)} %rows_hbm.3, bf16[1536,2048]{1,0:T(8,128)(2,1)S(1)} %fetch.1.ready_ref), custom_call_target="tpu_custom_call", output_to_operand_aliasing={{1}: (2, {})} | custom-call | tf_op jit(solution)/shard_map/sent_projection/pallas_call | solution.py:29
  6.2 2.7 %collective-permute-start.1 = (f32[32,768]{1,0:T(8,128)S(1)}, f32[32,768]{1,0:T(8,128)S(1)}, u32[]{:S(2)}, u32[]{:S(2)}) collective-permute-start(f32[32,768]{1,0:T(8,128)S(1)} %add.17.refs_0_), channel_id=1, source_target_pairs={{0,3},{1,2},{2,1},{3,0},{4,7},{5,6},{6,5},{7,4},{8,11},{9,10},{10,... | collective-permute-start | bytes 294920 | tf_op jit(solution)/shard_map/ppermute | solution.py:275
  8.8 3.0 %collective-permute-done.1.refs_1_ = f32[32,768]{1,0:T(8,128)S(1)} collective-permute-done((f32[32,768]{1,0:T(8,128)S(1)}, f32[32,768]{1,0:T(8,128)S(1)}, u32[]{:S(2)}, u32[]{:S(2)}) %collective-permute-start.1) | collective-permute-done | bytes 98336 | tf_op jit(solution)/shard_map/ppermute | solution.py:275
  13.8 2.9 %collective-permute-start.3 = (f32[40,512]{1,0:T(8,128)S(1)}, f32[40,512]{1,0:T(8,128)S(1)}, u32[]{:S(2)}, u32[]{:S(2)}) collective-permute-start(f32[40,512]{1,0:T(8,128)S(1)} %get-tuple-element.48), channel_id=1, source_target_pairs={{0,12},{4,8},{8,4},{12,0},{16,28},{20,24},{24,20},{28,16},{1,13},{... | collective-permute-start | bytes 245768 | tf_op jit(solution)/shard_map/ppermute | solution.py:275
  17.7 1.9 %collective-permute-done.3.refs_1_ = f32[40,512]{1,0:T(8,128)S(1)} collective-permute-done((f32[40,512]{1,0:T(8,128)S(1)}, f32[40,512]{1,0:T(8,128)S(1)}, u32[]{:S(2)}, u32[]{:S(2)}) %collective-permute-start.3) | collective-permute-done | bytes 81952 | tf_op jit(solution)/shard_map/ppermute | solution.py:275
  19.6 1.7 %collective-permute-done.4.refs_2_ = f32[40,512]{1,0:T(8,128)S(1)} collective-permute-done((f32[40,512]{1,0:T(8,128)S(1)}, f32[40,512]{1,0:T(8,128)S(1)}, u32[]{:S(2)}, u32[]{:S(2)}) %collective-permute-start.4) | collective-permute-done | bytes 81952 | tf_op jit(solution)/shard_map/ppermute | solution.py:275
  21.7 2.7 %collective-permute-start.6 = (f32[40,512]{1,0:T(8,128)S(1)}, f32[40,512]{1,0:T(8,128)S(1)}, u32[]{:S(2)}, u32[]{:S(2)}) collective-permute-start(f32[40,512]{1,0:T(8,128)S(1)} %add.19.own_ref), channel_id=1, source_target_pairs={{0,16},{4,20},{8,24},{12,28},{16,0},{20,4},{24,8},{28,12},{1,17},{... | collective-permute-start | bytes 245768 | tf_op jit(solution)/shard_map/ppermute | solution.py:275
  24.3 4.3 %collective-permute-done.6.got_ref = f32[40,512]{1,0:T(8,128)S(1)} collective-permute-done((f32[40,512]{1,0:T(8,128)S(1)}, f32[40,512]{1,0:T(8,128)S(1)}, u32[]{:S(2)}, u32[]{:S(2)}) %collective-permute-start.6) | collective-permute-done | bytes 81952 | tf_op jit(solution)/shard_map/ppermute | solution.py:275
  29.4 1.6 %collective-permute-start.8 = (f32[40,512]{1,0:T(8,128)S(1)}, f32[40,512]{1,0:T(8,128)S(1)}, u32[]{:S(2)}, u32[]{:S(2)}) collective-permute-start(f32[40,512]{1,0:T(8,128)S(1)} %total.4.chunk_ref.mean_ref.refs_0_), channel_id=1, source_target_pairs={{0,8},{4,12},{8,0},{12,4},{16,24},{20,28},{24,16},{28,20},{1,9},{5... | collective-permute-start | bytes 245768 | tf_op jit(solution)/shard_map/ppermute | solution.py:275
  37.1 1.3 %collective-permute-start.11 = (f32[32,768]{1,0:T(8,128)S(1)}, f32[32,768]{1,0:T(8,128)S(1)}, u32[]{:S(2)}, u32[]{:S(2)}) collective-permute-start(f32[32,768]{1,0:T(8,128)S(1)} %add.20.own_ref), channel_id=1, source_target_pairs={{0,3},{1,2},{2,1},{3,0},{4,7},{5,6},{6,5},{7,4},{8,11},{9,10},{10,... | collective-permute-start | bytes 294920 | tf_op jit(solution)/shard_map/ppermute | solution.py:275
  40.1 1.9 %collective-permute-done.11.got_ref = f32[32,768]{1,0:T(8,128)S(1)} collective-permute-done((f32[32,768]{1,0:T(8,128)S(1)}, f32[32,768]{1,0:T(8,128)S(1)}, u32[]{:S(2)}, u32[]{:S(2)}) %collective-permute-start.11) | collective-permute-done | bytes 98336 | tf_op jit(solution)/shard_map/ppermute | solution.py:275
  43.9 1.4 %collective-permute-start.14 = (f32[32,512]{1,0:T(8,128)S(1)}, f32[32,512]{1,0:T(8,128)S(1)}, u32[]{:S(2)}, u32[]{:S(2)}) collective-permute-start(f32[32,512]{1,0:T(8,128)S(1)} %get-tuple-element.57), channel_id=1, source_target_pairs={{0,12},{4,8},{8,4},{12,0},{16,28},{20,24},{24,20},{28,16},{1,13},{... | collective-permute-start | bytes 196616 | tf_op jit(solution)/shard_map/ppermute | solution.py:275
  46.1 1.4 %collective-permute-start.16 = (f32[32,512]{1,0:T(8,128)S(1)}, f32[32,512]{1,0:T(8,128)S(1)}, u32[]{:S(2)}, u32[]{:S(2)}) collective-permute-start(f32[32,512]{1,0:T(8,128)S(1)} %get-tuple-element.59), channel_id=1, source_target_pairs={{0,8},{4,12},{8,0},{12,4},{16,24},{20,28},{24,16},{28,20},{1,9},{5... | collective-permute-start | bytes 196616 | tf_op jit(solution)/shard_map/ppermute | solution.py:275
  50.4 3.1 %collective-permute-start.17 = (f32[32,512]{1,0:T(8,128)S(1)}, f32[32,512]{1,0:T(8,128)S(1)}, u32[]{:S(2)}, u32[]{:S(2)}) collective-permute-start(f32[32,512]{1,0:T(8,128)S(1)} %add.23.own_ref), channel_id=1, source_target_pairs={{0,16},{4,20},{8,24},{12,28},{16,0},{20,4},{24,8},{28,12},{1,17},{... | collective-permute-start | bytes 196616 | tf_op jit(solution)/shard_map/ppermute | solution.py:275
  53.5 2.9 %inverse_factor.4.lower_ref = f32[32,32]{1,0:T(8,128)S(1)} custom-call(f32[32,128]{1,0:T(8,128)S(1)} %add.21.before_ref.own_ref, f32[32,128]{1,0:T(8,128)S(1)} %collective-permute-done.18.got_ref), custom_call_target="tpu_custom_call" | custom-call | flops 17179869184 | tf_op jit(solution)/shard_map/inverse_factor/pallas_call | solution.py:29
  59.0 1.5 %collective-permute-start.19 = (f32[32,512]{1,0:T(8,128)S(1)}, f32[32,512]{1,0:T(8,128)S(1)}, u32[]{:S(2)}, u32[]{:S(2)}) collective-permute-start(f32[32,512]{1,0:T(8,128)S(1)} %total.5.chunk_ref.refs_0_), channel_id=1, source_target_pairs={{0,4},{4,0},{8,12},{12,8},{16,20},{20,16},{24,28},{28,24},{1,5},{5... | collective-permute-start | bytes 196616 | tf_op jit(solution)/shard_map/ppermute | solution.py:275
  65.1 1.3 %collective-permute-start.23 = (f32[32,768]{1,0:T(8,128)S(1)}, f32[32,768]{1,0:T(8,128)S(1)}, u32[]{:S(2)}, u32[]{:S(2)}) collective-permute-start(f32[32,768]{1,0:T(8,128)S(1)} %add.24.own_ref), channel_id=1, source_target_pairs={{0,3},{1,2},{2,1},{3,0},{4,7},{5,6},{6,5},{7,4},{8,11},{9,10},{10,... | collective-permute-start | bytes 294920 | tf_op jit(solution)/shard_map/ppermute | solution.py:275
  68.0 1.9 %collective-permute-done.23.got_ref = f32[32,768]{1,0:T(8,128)S(1)} collective-permute-done((f32[32,768]{1,0:T(8,128)S(1)}, f32[32,768]{1,0:T(8,128)S(1)}, u32[]{:S(2)}, u32[]{:S(2)}) %collective-permute-start.23) | collective-permute-done | bytes 98336 | tf_op jit(solution)/shard_map/ppermute | solution.py:275
  71.9 1.5 %collective-permute-start.26 = (f32[32,512]{1,0:T(8,128)S(1)}, f32[32,512]{1,0:T(8,128)S(1)}, u32[]{:S(2)}, u32[]{:S(2)}) collective-permute-start(f32[32,512]{1,0:T(8,128)S(1)} %get-tuple-element.66), channel_id=1, source_target_pairs={{0,12},{4,8},{8,4},{12,0},{16,28},{20,24},{24,20},{28,16},{1,13},{... | collective-permute-start | bytes 196616 | tf_op jit(solution)/shard_map/ppermute | solution.py:275
  78.4 3.2 %collective-permute-start.29 = (f32[32,512]{1,0:T(8,128)S(1)}, f32[32,512]{1,0:T(8,128)S(1)}, u32[]{:S(2)}, u32[]{:S(2)}) collective-permute-start(f32[32,512]{1,0:T(8,128)S(1)} %add.27.own_ref), channel_id=1, source_target_pairs={{0,16},{4,20},{8,24},{12,28},{16,0},{20,4},{24,8},{28,12},{1,17},{... | collective-permute-start | bytes 196616 | tf_op jit(solution)/shard_map/ppermute | solution.py:275
  81.6 2.9 %inverse_factor.5.lower_ref = f32[32,32]{1,0:T(8,128)S(1)} custom-call(f32[32,128]{1,0:T(8,128)S(1)} %add.25.before_ref.own_ref, f32[32,128]{1,0:T(8,128)S(1)} %collective-permute-done.30.got_ref), custom_call_target="tpu_custom_call" | custom-call | flops 17179869184 | tf_op jit(solution)/shard_map/inverse_factor/pallas_call | solution.py:29
  86.9 1.5 %collective-permute-start.31 = (f32[32,512]{1,0:T(8,128)S(1)}, f32[32,512]{1,0:T(8,128)S(1)}, u32[]{:S(2)}, u32[]{:S(2)}) collective-permute-start(f32[32,512]{1,0:T(8,128)S(1)} %total.6.chunk_ref.refs_0_), channel_id=1, source_target_pairs={{0,4},{4,0},{8,12},{12,8},{16,20},{20,16},{24,28},{28,24},{1,5},{5... | collective-permute-start | bytes 196616 | tf_op jit(solution)/shard_map/ppermute | solution.py:275
  93.2 1.3 %collective-permute-start.35 = (f32[32,768]{1,0:T(8,128)S(1)}, f32[32,768]{1,0:T(8,128)S(1)}, u32[]{:S(2)}, u32[]{:S(2)}) collective-permute-start(f32[32,768]{1,0:T(8,128)S(1)} %add.28.own_ref), channel_id=1, source_target_pairs={{0,3},{1,2},{2,1},{3,0},{4,7},{5,6},{6,5},{7,4},{8,11},{9,10},{10,... | collective-permute-start | bytes 294920 | tf_op jit(solution)/shard_map/ppermute | solution.py:275
  96.1 1.9 %collective-permute-done.35.got_ref = f32[32,768]{1,0:T(8,128)S(1)} collective-permute-done((f32[32,768]{1,0:T(8,128)S(1)}, f32[32,768]{1,0:T(8,128)S(1)}, u32[]{:S(2)}, u32[]{:S(2)}) %collective-permute-start.35) | collective-permute-done | bytes 98336 | tf_op jit(solution)/shard_map/ppermute | solution.py:275
  102.2 1.3 %collective-permute-start.40 = (f32[32,512]{1,0:T(8,128)S(1)}, f32[32,512]{1,0:T(8,128)S(1)}, u32[]{:S(2)}, u32[]{:S(2)}) collective-permute-start(f32[32,512]{1,0:T(8,128)S(1)} %get-tuple-element.77), channel_id=1, source_target_pairs={{0,8},{4,12},{8,0},{12,4},{16,24},{20,28},{24,16},{28,20},{1,9},{5... | collective-permute-start | bytes 196616 | tf_op jit(solution)/shard_map/ppermute | solution.py:275
  104.2 1.4 %collective-permute-done.38.refs_1_ = f32[32,512]{1,0:T(8,128)S(1)} collective-permute-done((f32[32,512]{1,0:T(8,128)S(1)}, f32[32,512]{1,0:T(8,128)S(1)}, u32[]{:S(2)}, u32[]{:S(2)}) %collective-permute-start.38) | collective-permute-done | bytes 65568 | tf_op jit(solution)/shard_map/ppermute | solution.py:275
  106.5 3.0 %collective-permute-start.41 = (f32[32,512]{1,0:T(8,128)S(1)}, f32[32,512]{1,0:T(8,128)S(1)}, u32[]{:S(2)}, u32[]{:S(2)}) collective-permute-start(f32[32,512]{1,0:T(8,128)S(1)} %add.31.own_ref), channel_id=1, source_target_pairs={{0,16},{4,20},{8,24},{12,28},{16,0},{20,4},{24,8},{28,12},{1,17},{... | collective-permute-start | bytes 196616 | tf_op jit(solution)/shard_map/ppermute | solution.py:275
  109.5 2.9 %inverse_factor.6.lower_ref = f32[32,32]{1,0:T(8,128)S(1)} custom-call(f32[32,128]{1,0:T(8,128)S(1)} %add.29.before_ref.own_ref, f32[32,128]{1,0:T(8,128)S(1)} %collective-permute-done.42.got_ref), custom_call_target="tpu_custom_call" | custom-call | flops 17179869184 | tf_op jit(solution)/shard_map/inverse_factor/pallas_call | solution.py:29
  115.0 1.6 %collective-permute-start.43 = (f32[32,512]{1,0:T(8,128)S(1)}, f32[32,512]{1,0:T(8,128)S(1)}, u32[]{:S(2)}, u32[]{:S(2)}) collective-permute-start(f32[32,512]{1,0:T(8,128)S(1)} %total.7.chunk_ref.refs_0_), channel_id=1, source_target_pairs={{0,4},{4,0},{8,12},{12,8},{16,20},{20,16},{24,28},{28,24},{1,5},{5... | collective-permute-start | bytes 196616 | tf_op jit(solution)/shard_map/ppermute | solution.py:275
  122.8 1.3 %collective-permute-start.48 = (bf16[32,1536]{1,0:T(8,128)(2,1)S(1)}, bf16[32,1536]{1,0:T(8,128)(2,1)S(1)}, u32[]{:S(2)}, u32[]{:S(2)}) collective-permute-start(bf16[32,1536]{1,0:T(8,128)(2,1)S(1)} %add.33.own_ref), channel_id=1, source_target_pairs={{0,3},{1,2},{2,1},{3,0},{4,7},{5,6},{6,5},{7,4},{8,11},{9,10},{10,... | collective-permute-start | bytes 294920 | tf_op jit(solution)/shard_map/ppermute | solution.py:275
  124.6 2.9 %inverse_factor.7.lower_ref = f32[32,32]{1,0:T(8,128)S(1)} custom-call(f32[32,128]{1,0:T(8,128)S(1)} %add.32.before_ref.own_ref, f32[32,128]{1,0:T(8,128)S(1)} %collective-permute-done.49.got_ref), custom_call_target="tpu_custom_call" | custom-call | flops 17179869184 | tf_op jit(solution)/shard_map/inverse_factor/pallas_call | solution.py:29
  (136 shorter events, 59.5 us)
Async XLA Ops:
  6.2 5.7 %collective-permute-start.1 = (f32[32,768]{1,0:T(8,128)S(1)}, f32[32,768]{1,0:T(8,128)S(1)}, u32[]{:S(2)}, u32[]{:S(2)}) collective-permute-start(f32[32,768]{1,0:T(8,128)S(1)} %add.17.refs_0_), channel_id=1, source_target_pairs={{0,3},{1,2},{2,1},{3,0},{4,7},{5,6},{6,5},{7,4},{8,11},{9,10},{10,... | collective-permute-start | bytes 294920 | tf_op jit(solution)/shard_map/ppermute | solution.py:275
  13.8 5.7 %collective-permute-start.3 = (f32[40,512]{1,0:T(8,128)S(1)}, f32[40,512]{1,0:T(8,128)S(1)}, u32[]{:S(2)}, u32[]{:S(2)}) collective-permute-start(f32[40,512]{1,0:T(8,128)S(1)} %get-tuple-element.48), channel_id=1, source_target_pairs={{0,12},{4,8},{8,4},{12,0},{16,28},{20,24},{24,20},{28,16},{1,13},{... | collective-permute-start | bytes 245768 | tf_op jit(solution)/shard_map/ppermute | solution.py:275
  16.7 4.6 %collective-permute-start.4 = (f32[40,512]{1,0:T(8,128)S(1)}, f32[40,512]{1,0:T(8,128)S(1)}, u32[]{:S(2)}, u32[]{:S(2)}) collective-permute-start(f32[40,512]{1,0:T(8,128)S(1)} %get-tuple-element.49), channel_id=1, source_target_pairs={{0,4},{4,0},{8,12},{12,8},{16,20},{20,16},{24,28},{28,24},{1,5},{5... | collective-permute-start | bytes 245768 | tf_op jit(solution)/shard_map/ppermute | solution.py:275
  17.2 4.4 %collective-permute-start.5 = (f32[40,512]{1,0:T(8,128)S(1)}, f32[40,512]{1,0:T(8,128)S(1)}, u32[]{:S(2)}, u32[]{:S(2)}) collective-permute-start(f32[40,512]{1,0:T(8,128)S(1)} %get-tuple-element.50), channel_id=1, source_target_pairs={{0,8},{4,12},{8,0},{12,4},{16,24},{20,28},{24,16},{28,20},{1,9},{5... | collective-permute-start | bytes 245768 | tf_op jit(solution)/shard_map/ppermute | solution.py:275
  21.7 7.0 %collective-permute-start.6 = (f32[40,512]{1,0:T(8,128)S(1)}, f32[40,512]{1,0:T(8,128)S(1)}, u32[]{:S(2)}, u32[]{:S(2)}) collective-permute-start(f32[40,512]{1,0:T(8,128)S(1)} %add.19.own_ref), channel_id=1, source_target_pairs={{0,16},{4,20},{8,24},{12,28},{16,0},{20,4},{24,8},{28,12},{1,17},{... | collective-permute-start | bytes 245768 | tf_op jit(solution)/shard_map/ppermute | solution.py:275
  28.7 5.3 %collective-permute-start.9 = (f32[40,512]{1,0:T(8,128)S(1)}, f32[40,512]{1,0:T(8,128)S(1)}, u32[]{:S(2)}, u32[]{:S(2)}) collective-permute-start(f32[40,512]{1,0:T(8,128)S(1)} %total.4.chunk_ref.mean_ref.refs_0_), channel_id=1, source_target_pairs={{0,12},{4,8},{8,4},{12,0},{16,28},{20,24},{24,20},{28,16},{1,13},{... | collective-permute-start | bytes 245768 | tf_op jit(solution)/shard_map/ppermute | solution.py:275
  29.4 5.3 %collective-permute-start.8 = (f32[40,512]{1,0:T(8,128)S(1)}, f32[40,512]{1,0:T(8,128)S(1)}, u32[]{:S(2)}, u32[]{:S(2)}) collective-permute-start(f32[40,512]{1,0:T(8,128)S(1)} %total.4.chunk_ref.mean_ref.refs_0_), channel_id=1, source_target_pairs={{0,8},{4,12},{8,0},{12,4},{16,24},{20,28},{24,16},{28,20},{1,9},{5... | collective-permute-start | bytes 245768 | tf_op jit(solution)/shard_map/ppermute | solution.py:275
  31.0 4.4 %collective-permute-start.7 = (f32[40,512]{1,0:T(8,128)S(1)}, f32[40,512]{1,0:T(8,128)S(1)}, u32[]{:S(2)}, u32[]{:S(2)}) collective-permute-start(f32[40,512]{1,0:T(8,128)S(1)} %total.4.chunk_ref.mean_ref.refs_0_), channel_id=1, source_target_pairs={{0,4},{4,0},{8,12},{12,8},{16,20},{20,16},{24,28},{28,24},{1,5},{5... | collective-permute-start | bytes 245768 | tf_op jit(solution)/shard_map/ppermute | solution.py:275
  37.1 4.8 %collective-permute-start.11 = (f32[32,768]{1,0:T(8,128)S(1)}, f32[32,768]{1,0:T(8,128)S(1)}, u32[]{:S(2)}, u32[]{:S(2)}) collective-permute-start(f32[32,768]{1,0:T(8,128)S(1)} %add.20.own_ref), channel_id=1, source_target_pairs={{0,3},{1,2},{2,1},{3,0},{4,7},{5,6},{6,5},{7,4},{8,11},{9,10},{10,... | collective-permute-start | bytes 294920 | tf_op jit(solution)/shard_map/ppermute | solution.py:275
  43.9 5.5 %collective-permute-start.14 = (f32[32,512]{1,0:T(8,128)S(1)}, f32[32,512]{1,0:T(8,128)S(1)}, u32[]{:S(2)}, u32[]{:S(2)}) collective-permute-start(f32[32,512]{1,0:T(8,128)S(1)} %get-tuple-element.57), channel_id=1, source_target_pairs={{0,12},{4,8},{8,4},{12,0},{16,28},{20,24},{24,20},{28,16},{1,13},{... | collective-permute-start | bytes 196616 | tf_op jit(solution)/shard_map/ppermute | solution.py:275
  45.3 5.2 %collective-permute-start.15 = (f32[32,512]{1,0:T(8,128)S(1)}, f32[32,512]{1,0:T(8,128)S(1)}, u32[]{:S(2)}, u32[]{:S(2)}) collective-permute-start(f32[32,512]{1,0:T(8,128)S(1)} %get-tuple-element.58), channel_id=1, source_target_pairs={{0,4},{4,0},{8,12},{12,8},{16,20},{20,16},{24,28},{28,24},{1,5},{5... | collective-permute-start | bytes 196616 | tf_op jit(solution)/shard_map/ppermute | solution.py:275
  47.5 6.1 %collective-permute-start.18 = (f32[32,128]{1,0:T(8,128)S(1)}, f32[32,128]{1,0:T(8,128)S(1)}, u32[]{:S(2)}, u32[]{:S(2)}) collective-permute-start(f32[32,128]{1,0:T(8,128)S(1)} %add.21.before_ref.own_ref), channel_id=1, source_target_pairs={{0,3},{1,2},{2,1},{3,0},{4,7},{5,6},{6,5},{7,4},{8,11},{9,10},{10,... | collective-permute-start | bytes 49160 | tf_op jit(solution)/shard_map/ppermute | solution.py:275
  50.4 6.3 %collective-permute-start.17 = (f32[32,512]{1,0:T(8,128)S(1)}, f32[32,512]{1,0:T(8,128)S(1)}, u32[]{:S(2)}, u32[]{:S(2)}) collective-permute-start(f32[32,512]{1,0:T(8,128)S(1)} %add.23.own_ref), channel_id=1, source_target_pairs={{0,16},{4,20},{8,24},{12,28},{16,0},{20,4},{24,8},{28,12},{1,17},{... | collective-permute-start | bytes 196616 | tf_op jit(solution)/shard_map/ppermute | solution.py:275
  57.0 5.2 %collective-permute-start.21 = (f32[32,512]{1,0:T(8,128)S(1)}, f32[32,512]{1,0:T(8,128)S(1)}, u32[]{:S(2)}, u32[]{:S(2)}) collective-permute-start(f32[32,512]{1,0:T(8,128)S(1)} %total.5.chunk_ref.refs_0_), channel_id=1, source_target_pairs={{0,12},{4,8},{8,4},{12,0},{16,28},{20,24},{24,20},{28,16},{1,13},{... | collective-permute-start | bytes 196616 | tf_op jit(solution)/shard_map/ppermute | solution.py:275
  57.8 4.9 %collective-permute-start.20 = (f32[32,512]{1,0:T(8,128)S(1)}, f32[32,512]{1,0:T(8,128)S(1)}, u32[]{:S(2)}, u32[]{:S(2)}) collective-permute-start(f32[32,512]{1,0:T(8,128)S(1)} %total.5.chunk_ref.refs_0_), channel_id=1, source_target_pairs={{0,8},{4,12},{8,0},{12,4},{16,24},{20,28},{24,16},{28,20},{1,9},{5... | collective-permute-start | bytes 196616 | tf_op jit(solution)/shard_map/ppermute | solution.py:275
  59.0 4.4 %collective-permute-start.19 = (f32[32,512]{1,0:T(8,128)S(1)}, f32[32,512]{1,0:T(8,128)S(1)}, u32[]{:S(2)}, u32[]{:S(2)}) collective-permute-start(f32[32,512]{1,0:T(8,128)S(1)} %total.5.chunk_ref.refs_0_), channel_id=1, source_target_pairs={{0,4},{4,0},{8,12},{12,8},{16,20},{20,16},{24,28},{28,24},{1,5},{5... | collective-permute-start | bytes 196616 | tf_op jit(solution)/shard_map/ppermute | solution.py:275
  65.1 4.8 %collective-permute-start.23 = (f32[32,768]{1,0:T(8,128)S(1)}, f32[32,768]{1,0:T(8,128)S(1)}, u32[]{:S(2)}, u32[]{:S(2)}) collective-permute-start(f32[32,768]{1,0:T(8,128)S(1)} %add.24.own_ref), channel_id=1, source_target_pairs={{0,3},{1,2},{2,1},{3,0},{4,7},{5,6},{6,5},{7,4},{8,11},{9,10},{10,... | collective-permute-start | bytes 294920 | tf_op jit(solution)/shard_map/ppermute | solution.py:275
  71.9 5.4 %collective-permute-start.26 = (f32[32,512]{1,0:T(8,128)S(1)}, f32[32,512]{1,0:T(8,128)S(1)}, u32[]{:S(2)}, u32[]{:S(2)}) collective-permute-start(f32[32,512]{1,0:T(8,128)S(1)} %get-tuple-element.66), channel_id=1, source_target_pairs={{0,12},{4,8},{8,4},{12,0},{16,28},{20,24},{24,20},{28,16},{1,13},{... | collective-permute-start | bytes 196616 | tf_op jit(solution)/shard_map/ppermute | solution.py:275
  73.3 5.1 %collective-permute-start.27 = (f32[32,512]{1,0:T(8,128)S(1)}, f32[32,512]{1,0:T(8,128)S(1)}, u32[]{:S(2)}, u32[]{:S(2)}) collective-permute-start(f32[32,512]{1,0:T(8,128)S(1)} %get-tuple-element.67), channel_id=1, source_target_pairs={{0,4},{4,0},{8,12},{12,8},{16,20},{20,16},{24,28},{28,24},{1,5},{5... | collective-permute-start | bytes 196616 | tf_op jit(solution)/shard_map/ppermute | solution.py:275
  75.4 6.2 %collective-permute-start.30 = (f32[32,128]{1,0:T(8,128)S(1)}, f32[32,128]{1,0:T(8,128)S(1)}, u32[]{:S(2)}, u32[]{:S(2)}) collective-permute-start(f32[32,128]{1,0:T(8,128)S(1)} %add.25.before_ref.own_ref), channel_id=1, source_target_pairs={{0,3},{1,2},{2,1},{3,0},{4,7},{5,6},{6,5},{7,4},{8,11},{9,10},{10,... | collective-permute-start | bytes 49160 | tf_op jit(solution)/shard_map/ppermute | solution.py:275
  78.4 6.3 %collective-permute-start.29 = (f32[32,512]{1,0:T(8,128)S(1)}, f32[32,512]{1,0:T(8,128)S(1)}, u32[]{:S(2)}, u32[]{:S(2)}) collective-permute-start(f32[32,512]{1,0:T(8,128)S(1)} %add.27.own_ref), channel_id=1, source_target_pairs={{0,16},{4,20},{8,24},{12,28},{16,0},{20,4},{24,8},{28,12},{1,17},{... | collective-permute-start | bytes 196616 | tf_op jit(solution)/shard_map/ppermute | solution.py:275
  84.9 5.2 %collective-permute-start.33 = (f32[32,512]{1,0:T(8,128)S(1)}, f32[32,512]{1,0:T(8,128)S(1)}, u32[]{:S(2)}, u32[]{:S(2)}) collective-permute-start(f32[32,512]{1,0:T(8,128)S(1)} %total.6.chunk_ref.refs_0_), channel_id=1, source_target_pairs={{0,12},{4,8},{8,4},{12,0},{16,28},{20,24},{24,20},{28,16},{1,13},{... | collective-permute-start | bytes 196616 | tf_op jit(solution)/shard_map/ppermute | solution.py:275
  85.9 4.9 %collective-permute-start.32 = (f32[32,512]{1,0:T(8,128)S(1)}, f32[32,512]{1,0:T(8,128)S(1)}, u32[]{:S(2)}, u32[]{:S(2)}) collective-permute-start(f32[32,512]{1,0:T(8,128)S(1)} %total.6.chunk_ref.refs_0_), channel_id=1, source_target_pairs={{0,8},{4,12},{8,0},{12,4},{16,24},{20,28},{24,16},{28,20},{1,9},{5... | collective-permute-start | bytes 196616 | tf_op jit(solution)/shard_map/ppermute | solution.py:275
  86.9 4.6 %collective-permute-start.31 = (f32[32,512]{1,0:T(8,128)S(1)}, f32[32,512]{1,0:T(8,128)S(1)}, u32[]{:S(2)}, u32[]{:S(2)}) collective-permute-start(f32[32,512]{1,0:T(8,128)S(1)} %total.6.chunk_ref.refs_0_), channel_id=1, source_target_pairs={{0,4},{4,0},{8,12},{12,8},{16,20},{20,16},{24,28},{28,24},{1,5},{5... | collective-permute-start | bytes 196616 | tf_op jit(solution)/shard_map/ppermute | solution.py:275
  93.2 4.8 %collective-permute-start.35 = (f32[32,768]{1,0:T(8,128)S(1)}, f32[32,768]{1,0:T(8,128)S(1)}, u32[]{:S(2)}, u32[]{:S(2)}) collective-permute-start(f32[32,768]{1,0:T(8,128)S(1)} %add.28.own_ref), channel_id=1, source_target_pairs={{0,3},{1,2},{2,1},{3,0},{4,7},{5,6},{6,5},{7,4},{8,11},{9,10},{10,... | collective-permute-start | bytes 294920 | tf_op jit(solution)/shard_map/ppermute | solution.py:275
  100.0 5.6 %collective-permute-start.38 = (f32[32,512]{1,0:T(8,128)S(1)}, f32[32,512]{1,0:T(8,128)S(1)}, u32[]{:S(2)}, u32[]{:S(2)}) collective-permute-start(f32[32,512]{1,0:T(8,128)S(1)} %get-tuple-element.75), channel_id=1, source_target_pairs={{0,12},{4,8},{8,4},{12,0},{16,28},{20,24},{24,20},{28,16},{1,13},{... | collective-permute-start | bytes 196616 | tf_op jit(solution)/shard_map/ppermute | solution.py:275
  101.3 5.2 %collective-permute-start.39 = (f32[32,512]{1,0:T(8,128)S(1)}, f32[32,512]{1,0:T(8,128)S(1)}, u32[]{:S(2)}, u32[]{:S(2)}) collective-permute-start(f32[32,512]{1,0:T(8,128)S(1)} %get-tuple-element.76), channel_id=1, source_target_pairs={{0,4},{4,0},{8,12},{12,8},{16,20},{20,16},{24,28},{28,24},{1,5},{5... | collective-permute-start | bytes 196616 | tf_op jit(solution)/shard_map/ppermute | solution.py:275
  103.5 6.0 %collective-permute-start.42 = (f32[32,128]{1,0:T(8,128)S(1)}, f32[32,128]{1,0:T(8,128)S(1)}, u32[]{:S(2)}, u32[]{:S(2)}) collective-permute-start(f32[32,128]{1,0:T(8,128)S(1)} %add.29.before_ref.own_ref), channel_id=1, source_target_pairs={{0,3},{1,2},{2,1},{3,0},{4,7},{5,6},{6,5},{7,4},{8,11},{9,10},{10,... | collective-permute-start | bytes 49160 | tf_op jit(solution)/shard_map/ppermute | solution.py:275
  106.5 6.3 %collective-permute-start.41 = (f32[32,512]{1,0:T(8,128)S(1)}, f32[32,512]{1,0:T(8,128)S(1)}, u32[]{:S(2)}, u32[]{:S(2)}) collective-permute-start(f32[32,512]{1,0:T(8,128)S(1)} %add.31.own_ref), channel_id=1, source_target_pairs={{0,16},{4,20},{8,24},{12,28},{16,0},{20,4},{24,8},{28,12},{1,17},{... | collective-permute-start | bytes 196616 | tf_op jit(solution)/shard_map/ppermute | solution.py:275
  113.0 5.2 %collective-permute-start.45 = (f32[32,512]{1,0:T(8,128)S(1)}, f32[32,512]{1,0:T(8,128)S(1)}, u32[]{:S(2)}, u32[]{:S(2)}) collective-permute-start(f32[32,512]{1,0:T(8,128)S(1)} %total.7.chunk_ref.refs_0_), channel_id=1, source_target_pairs={{0,12},{4,8},{8,4},{12,0},{16,28},{20,24},{24,20},{28,16},{1,13},{... | collective-permute-start | bytes 196616 | tf_op jit(solution)/shard_map/ppermute | solution.py:275
  113.9 4.9 %collective-permute-start.44 = (f32[32,512]{1,0:T(8,128)S(1)}, f32[32,512]{1,0:T(8,128)S(1)}, u32[]{:S(2)}, u32[]{:S(2)}) collective-permute-start(f32[32,512]{1,0:T(8,128)S(1)} %total.7.chunk_ref.refs_0_), channel_id=1, source_target_pairs={{0,8},{4,12},{8,0},{12,4},{16,24},{20,28},{24,16},{28,20},{1,9},{5... | collective-permute-start | bytes 196616 | tf_op jit(solution)/shard_map/ppermute | solution.py:275
  122.8 4.8 %collective-permute-start.48 = (bf16[32,1536]{1,0:T(8,128)(2,1)S(1)}, bf16[32,1536]{1,0:T(8,128)(2,1)S(1)}, u32[]{:S(2)}, u32[]{:S(2)}) collective-permute-start(bf16[32,1536]{1,0:T(8,128)(2,1)S(1)} %add.33.own_ref), channel_id=1, source_target_pairs={{0,3},{1,2},{2,1},{3,0},{4,7},{5,6},{6,5},{7,4},{8,11},{9,10},{10,... | collective-permute-start | bytes 294920 | tf_op jit(solution)/shard_map/ppermute | solution.py:275
  (19 other events, 40.3 us)

commit v12 on v11

--- a/solution.py
+++ b/solution.py
@@ -317,7 +317,7 @@
         chunk = ((n + EXTRA if first else n, width), F32)
         weights = ((TERMS * n + 2 * EXTRA if first else TERMS * n, tokens // 2), BF16)
         kernel = functools.partial(half_image_kernel, first)
-        kept, *halves = call(kernel, [chunk] * PEERS, "half_image", cost=SHORT)(own, rows, *ranked)
+        kept, *halves = call(kernel, [chunk] * PEERS, "half_image", cost=LONG)(own, rows, *ranked)
         kernel = functools.partial(image_kernel, first)
         *terms, weights, sums = call(kernel, [chunk] * (PEERS - 1) + [weights, side], "image")(
             other, rows, *ranked[1:], *halves

time: 129 us -> 129 us (level)
  no operation moved by 1% of the time
where the time goes in v12:
time: 129 us
  starting transfers between devices  54 us (42%)
  waiting for transfers between devices  37.8 us (29%)
  Pallas kernels  35.8 us (28%)
    ppermute x50, starting transfers between devices, swap(): return lax.ppermute(value, axis, [(i, i ^ distance) for i in range(size)])  54 us
    ppermute x50, waiting for transfers between devices, swap(): return lax.ppermute(value, axis, [(i, i ^ distance) for i in range(size)])  37.8 us
    pallas_call x66, Pallas kernels, run(): pl.pallas_call(kernel, out_shape=[jax.ShapeDtypeStruct(shape, dtype) for...  35.8 us
  transfers between devices with their start and end apart: 50, of which 34 were waited for; matrix products, arithmetic and copies ran while one was open for 0% of the time, Pallas kernels for 21%

profile of v12, /device:TPU:0, one launch (start us, length us, event | category | flops | bytes accessed | tf_op | source)
XLA Modules:
  0.0 128.6 jit_solution(9069686431762326640)
XLA Ops:
  0.6 2.0 %fetch.1.ready_ref = bf16[1536,2048]{1,0:T(8,128)(2,1)S(1)} custom-call(bf16[1536,2048]{1,0:T(8,128)(2,1)} %rows_hbm.3), custom_call_target="tpu_custom_call" | custom-call | tf_op jit(solution)/shard_map/fetch/pallas_call | solution.py:29
  2.6 1.9 %sent_projection.4 = (f32[32,768]{1,0:T(8,128)S(1)}, bf16[1536,2048]{1,0:T(8,128)(2,1)S(1)}) custom-call(f32[32,2048]{1,0:T(8,128)S(1)} %copy-done, bf16[1536,2048]{1,0:T(8,128)(2,1)} %rows_hbm.3, bf16[1536,2048]{1,0:T(8,128)(2,1)S(1)} %fetch.1.ready_ref), custom_call_target="tpu_custom_call", output_to_operand_aliasing={{1}: (2, {})} | custom-call | tf_op jit(solution)/shard_map/sent_projection/pallas_call | solution.py:29
  6.2 2.7 %collective-permute-start.1 = (f32[32,768]{1,0:T(8,128)S(1)}, f32[32,768]{1,0:T(8,128)S(1)}, u32[]{:S(2)}, u32[]{:S(2)}) collective-permute-start(f32[32,768]{1,0:T(8,128)S(1)} %add.17.refs_0_), channel_id=1, source_target_pairs={{0,3},{1,2},{2,1},{3,0},{4,7},{5,6},{6,5},{7,4},{8,11},{9,10},{10,... | collective-permute-start | bytes 294920 | tf_op jit(solution)/shard_map/ppermute | solution.py:275
  8.8 3.0 %collective-permute-done.1.refs_1_ = f32[32,768]{1,0:T(8,128)S(1)} collective-permute-done((f32[32,768]{1,0:T(8,128)S(1)}, f32[32,768]{1,0:T(8,128)S(1)}, u32[]{:S(2)}, u32[]{:S(2)}) %collective-permute-start.1) | collective-permute-done | bytes 98336 | tf_op jit(solution)/shard_map/ppermute | solution.py:275
  13.8 2.9 %collective-permute-start.3 = (f32[40,512]{1,0:T(8,128)S(1)}, f32[40,512]{1,0:T(8,128)S(1)}, u32[]{:S(2)}, u32[]{:S(2)}) collective-permute-start(f32[40,512]{1,0:T(8,128)S(1)} %get-tuple-element.48), channel_id=1, source_target_pairs={{0,12},{4,8},{8,4},{12,0},{16,28},{20,24},{24,20},{28,16},{1,13},{... | collective-permute-start | bytes 245768 | tf_op jit(solution)/shard_map/ppermute | solution.py:275
  17.7 1.9 %collective-permute-done.3.refs_1_ = f32[40,512]{1,0:T(8,128)S(1)} collective-permute-done((f32[40,512]{1,0:T(8,128)S(1)}, f32[40,512]{1,0:T(8,128)S(1)}, u32[]{:S(2)}, u32[]{:S(2)}) %collective-permute-start.3) | collective-permute-done | bytes 81952 | tf_op jit(solution)/shard_map/ppermute | solution.py:275
  19.6 1.7 %collective-permute-done.4.refs_2_ = f32[40,512]{1,0:T(8,128)S(1)} collective-permute-done((f32[40,512]{1,0:T(8,128)S(1)}, f32[40,512]{1,0:T(8,128)S(1)}, u32[]{:S(2)}, u32[]{:S(2)}) %collective-permute-start.4) | collective-permute-done | bytes 81952 | tf_op jit(solution)/shard_map/ppermute | solution.py:275
  21.7 2.7 %collective-permute-start.6 = (f32[40,512]{1,0:T(8,128)S(1)}, f32[40,512]{1,0:T(8,128)S(1)}, u32[]{:S(2)}, u32[]{:S(2)}) collective-permute-start(f32[40,512]{1,0:T(8,128)S(1)} %add.19.own_ref), channel_id=1, source_target_pairs={{0,16},{4,20},{8,24},{12,28},{16,0},{20,4},{24,8},{28,12},{1,17},{... | collective-permute-start | bytes 245768 | tf_op jit(solution)/shard_map/ppermute | solution.py:275
  24.3 4.3 %collective-permute-done.6.got_ref = f32[40,512]{1,0:T(8,128)S(1)} collective-permute-done((f32[40,512]{1,0:T(8,128)S(1)}, f32[40,512]{1,0:T(8,128)S(1)}, u32[]{:S(2)}, u32[]{:S(2)}) %collective-permute-start.6) | collective-permute-done | bytes 81952 | tf_op jit(solution)/shard_map/ppermute | solution.py:275
  29.4 1.6 %collective-permute-start.8 = (f32[40,512]{1,0:T(8,128)S(1)}, f32[40,512]{1,0:T(8,128)S(1)}, u32[]{:S(2)}, u32[]{:S(2)}) collective-permute-start(f32[40,512]{1,0:T(8,128)S(1)} %total.4.chunk_ref.mean_ref.refs_0_), channel_id=1, source_target_pairs={{0,8},{4,12},{8,0},{12,4},{16,24},{20,28},{24,16},{28,20},{1,9},{5... | collective-permute-start | bytes 245768 | tf_op jit(solution)/shard_map/ppermute | solution.py:275
  37.1 1.3 %collective-permute-start.11 = (f32[32,768]{1,0:T(8,128)S(1)}, f32[32,768]{1,0:T(8,128)S(1)}, u32[]{:S(2)}, u32[]{:S(2)}) collective-permute-start(f32[32,768]{1,0:T(8,128)S(1)} %add.20.own_ref), channel_id=1, source_target_pairs={{0,3},{1,2},{2,1},{3,0},{4,7},{5,6},{6,5},{7,4},{8,11},{9,10},{10,... | collective-permute-start | bytes 294920 | tf_op jit(solution)/shard_map/ppermute | solution.py:275
  40.1 1.9 %collective-permute-done.11.got_ref = f32[32,768]{1,0:T(8,128)S(1)} collective-permute-done((f32[32,768]{1,0:T(8,128)S(1)}, f32[32,768]{1,0:T(8,128)S(1)}, u32[]{:S(2)}, u32[]{:S(2)}) %collective-permute-start.11) | collective-permute-done | bytes 98336 | tf_op jit(solution)/shard_map/ppermute | solution.py:275
  43.9 1.4 %collective-permute-start.14 = (f32[32,512]{1,0:T(8,128)S(1)}, f32[32,512]{1,0:T(8,128)S(1)}, u32[]{:S(2)}, u32[]{:S(2)}) collective-permute-start(f32[32,512]{1,0:T(8,128)S(1)} %get-tuple-element.57), channel_id=1, source_target_pairs={{0,12},{4,8},{8,4},{12,0},{16,28},{20,24},{24,20},{28,16},{1,13},{... | collective-permute-start | bytes 196616 | tf_op jit(solution)/shard_map/ppermute | solution.py:275
  46.1 1.4 %collective-permute-start.16 = (f32[32,512]{1,0:T(8,128)S(1)}, f32[32,512]{1,0:T(8,128)S(1)}, u32[]{:S(2)}, u32[]{:S(2)}) collective-permute-start(f32[32,512]{1,0:T(8,128)S(1)} %get-tuple-element.59), channel_id=1, source_target_pairs={{0,8},{4,12},{8,0},{12,4},{16,24},{20,28},{24,16},{28,20},{1,9},{5... | collective-permute-start | bytes 196616 | tf_op jit(solution)/shard_map/ppermute | solution.py:275
  50.4 3.1 %collective-permute-start.17 = (f32[32,512]{1,0:T(8,128)S(1)}, f32[32,512]{1,0:T(8,128)S(1)}, u32[]{:S(2)}, u32[]{:S(2)}) collective-permute-start(f32[32,512]{1,0:T(8,128)S(1)} %add.23.own_ref), channel_id=1, source_target_pairs={{0,16},{4,20},{8,24},{12,28},{16,0},{20,4},{24,8},{28,12},{1,17},{... | collective-permute-start | bytes 196616 | tf_op jit(solution)/shard_map/ppermute | solution.py:275
  53.5 2.9 %inverse_factor.4.lower_ref = f32[32,32]{1,0:T(8,128)S(1)} custom-call(f32[32,128]{1,0:T(8,128)S(1)} %add.21.before_ref.own_ref, f32[32,128]{1,0:T(8,128)S(1)} %collective-permute-done.18.got_ref), custom_call_target="tpu_custom_call" | custom-call | flops 17179869184 | tf_op jit(solution)/shard_map/inverse_factor/pallas_call | solution.py:29
  59.0 1.5 %collective-permute-start.19 = (f32[32,512]{1,0:T(8,128)S(1)}, f32[32,512]{1,0:T(8,128)S(1)}, u32[]{:S(2)}, u32[]{:S(2)}) collective-permute-start(f32[32,512]{1,0:T(8,128)S(1)} %total.5.chunk_ref.refs_0_), channel_id=1, source_target_pairs={{0,4},{4,0},{8,12},{12,8},{16,20},{20,16},{24,28},{28,24},{1,5},{5... | collective-permute-start | bytes 196616 | tf_op jit(solution)/shard_map/ppermute | solution.py:275
  65.1 1.3 %collective-permute-start.23 = (f32[32,768]{1,0:T(8,128)S(1)}, f32[32,768]{1,0:T(8,128)S(1)}, u32[]{:S(2)}, u32[]{:S(2)}) collective-permute-start(f32[32,768]{1,0:T(8,128)S(1)} %add.24.own_ref), channel_id=1, source_target_pairs={{0,3},{1,2},{2,1},{3,0},{4,7},{5,6},{6,5},{7,4},{8,11},{9,10},{10,... | collective-permute-start | bytes 294920 | tf_op jit(solution)/shard_map/ppermute | solution.py:275
  68.0 1.9 %collective-permute-done.23.got_ref = f32[32,768]{1,0:T(8,128)S(1)} collective-permute-done((f32[32,768]{1,0:T(8,128)S(1)}, f32[32,768]{1,0:T(8,128)S(1)}, u32[]{:S(2)}, u32[]{:S(2)}) %collective-permute-start.23) | collective-permute-done | bytes 98336 | tf_op jit(solution)/shard_map/ppermute | solution.py:275
  71.9 1.5 %collective-permute-start.26 = (f32[32,512]{1,0:T(8,128)S(1)}, f32[32,512]{1,0:T(8,128)S(1)}, u32[]{:S(2)}, u32[]{:S(2)}) collective-permute-start(f32[32,512]{1,0:T(8,128)S(1)} %get-tuple-element.66), channel_id=1, source_target_pairs={{0,12},{4,8},{8,4},{12,0},{16,28},{20,24},{24,20},{28,16},{1,13},{... | collective-permute-start | bytes 196616 | tf_op jit(solution)/shard_map/ppermute | solution.py:275
  78.4 3.2 %collective-permute-start.29 = (f32[32,512]{1,0:T(8,128)S(1)}, f32[32,512]{1,0:T(8,128)S(1)}, u32[]{:S(2)}, u32[]{:S(2)}) collective-permute-start(f32[32,512]{1,0:T(8,128)S(1)} %add.27.own_ref), channel_id=1, source_target_pairs={{0,16},{4,20},{8,24},{12,28},{16,0},{20,4},{24,8},{28,12},{1,17},{... | collective-permute-start | bytes 196616 | tf_op jit(solution)/shard_map/ppermute | solution.py:275
  81.6 2.9 %inverse_factor.5.lower_ref = f32[32,32]{1,0:T(8,128)S(1)} custom-call(f32[32,128]{1,0:T(8,128)S(1)} %add.25.before_ref.own_ref, f32[32,128]{1,0:T(8,128)S(1)} %collective-permute-done.30.got_ref), custom_call_target="tpu_custom_call" | custom-call | flops 17179869184 | tf_op jit(solution)/shard_map/inverse_factor/pallas_call | solution.py:29
  86.9 1.5 %collective-permute-start.31 = (f32[32,512]{1,0:T(8,128)S(1)}, f32[32,512]{1,0:T(8,128)S(1)}, u32[]{:S(2)}, u32[]{:S(2)}) collective-permute-start(f32[32,512]{1,0:T(8,128)S(1)} %total.6.chunk_ref.refs_0_), channel_id=1, source_target_pairs={{0,4},{4,0},{8,12},{12,8},{16,20},{20,16},{24,28},{28,24},{1,5},{5... | collective-permute-start | bytes 196616 | tf_op jit(solution)/shard_map/ppermute | solution.py:275
  93.2 1.3 %collective-permute-start.35 = (f32[32,768]{1,0:T(8,128)S(1)}, f32[32,768]{1,0:T(8,128)S(1)}, u32[]{:S(2)}, u32[]{:S(2)}) collective-permute-start(f32[32,768]{1,0:T(8,128)S(1)} %add.28.own_ref), channel_id=1, source_target_pairs={{0,3},{1,2},{2,1},{3,0},{4,7},{5,6},{6,5},{7,4},{8,11},{9,10},{10,... | collective-permute-start | bytes 294920 | tf_op jit(solution)/shard_map/ppermute | solution.py:275
  96.1 1.9 %collective-permute-done.35.got_ref = f32[32,768]{1,0:T(8,128)S(1)} collective-permute-done((f32[32,768]{1,0:T(8,128)S(1)}, f32[32,768]{1,0:T(8,128)S(1)}, u32[]{:S(2)}, u32[]{:S(2)}) %collective-permute-start.35) | collective-permute-done | bytes 98336 | tf_op jit(solution)/shard_map/ppermute | solution.py:275
  102.2 1.3 %collective-permute-start.40 = (f32[32,512]{1,0:T(8,128)S(1)}, f32[32,512]{1,0:T(8,128)S(1)}, u32[]{:S(2)}, u32[]{:S(2)}) collective-permute-start(f32[32,512]{1,0:T(8,128)S(1)} %get-tuple-element.77), channel_id=1, source_target_pairs={{0,8},{4,12},{8,0},{12,4},{16,24},{20,28},{24,16},{28,20},{1,9},{5... | collective-permute-start | bytes 196616 | tf_op jit(solution)/shard_map/ppermute | solution.py:275
  104.2 1.4 %collective-permute-done.38.refs_1_ = f32[32,512]{1,0:T(8,128)S(1)} collective-permute-done((f32[32,512]{1,0:T(8,128)S(1)}, f32[32,512]{1,0:T(8,128)S(1)}, u32[]{:S(2)}, u32[]{:S(2)}) %collective-permute-start.38) | collective-permute-done | bytes 65568 | tf_op jit(solution)/shard_map/ppermute | solution.py:275
  106.5 3.0 %collective-permute-start.41 = (f32[32,512]{1,0:T(8,128)S(1)}, f32[32,512]{1,0:T(8,128)S(1)}, u32[]{:S(2)}, u32[]{:S(2)}) collective-permute-start(f32[32,512]{1,0:T(8,128)S(1)} %add.31.own_ref), channel_id=1, source_target_pairs={{0,16},{4,20},{8,24},{12,28},{16,0},{20,4},{24,8},{28,12},{1,17},{... | collective-permute-start | bytes 196616 | tf_op jit(solution)/shard_map/ppermute | solution.py:275
  109.5 2.9 %inverse_factor.6.lower_ref = f32[32,32]{1,0:T(8,128)S(1)} custom-call(f32[32,128]{1,0:T(8,128)S(1)} %add.29.before_ref.own_ref, f32[32,128]{1,0:T(8,128)S(1)} %collective-permute-done.42.got_ref), custom_call_target="tpu_custom_call" | custom-call | flops 17179869184 | tf_op jit(solution)/shard_map/inverse_factor/pallas_call | solution.py:29
  115.0 1.6 %collective-permute-start.43 = (f32[32,512]{1,0:T(8,128)S(1)}, f32[32,512]{1,0:T(8,128)S(1)}, u32[]{:S(2)}, u32[]{:S(2)}) collective-permute-start(f32[32,512]{1,0:T(8,128)S(1)} %total.7.chunk_ref.refs_0_), channel_id=1, source_target_pairs={{0,4},{4,0},{8,12},{12,8},{16,20},{20,16},{24,28},{28,24},{1,5},{5... | collective-permute-start | bytes 196616 | tf_op jit(solution)/shard_map/ppermute | solution.py:275
  122.8 1.3 %collective-permute-start.48 = (bf16[32,1536]{1,0:T(8,128)(2,1)S(1)}, bf16[32,1536]{1,0:T(8,128)(2,1)S(1)}, u32[]{:S(2)}, u32[]{:S(2)}) collective-permute-start(bf16[32,1536]{1,0:T(8,128)(2,1)S(1)} %add.33.own_ref), channel_id=1, source_target_pairs={{0,3},{1,2},{2,1},{3,0},{4,7},{5,6},{6,5},{7,4},{8,11},{9,10},{10,... | collective-permute-start | bytes 294920 | tf_op jit(solution)/shard_map/ppermute | solution.py:275
  124.6 2.9 %inverse_factor.7.lower_ref = f32[32,32]{1,0:T(8,128)S(1)} custom-call(f32[32,128]{1,0:T(8,128)S(1)} %add.32.before_ref.own_ref, f32[32,128]{1,0:T(8,128)S(1)} %collective-permute-done.49.got_ref), custom_call_target="tpu_custom_call" | custom-call | flops 17179869184 | tf_op jit(solution)/shard_map/inverse_factor/pallas_call | solution.py:29
  (136 shorter events, 59.5 us)
Async XLA Ops:
  6.2 5.7 %collective-permute-start.1 = (f32[32,768]{1,0:T(8,128)S(1)}, f32[32,768]{1,0:T(8,128)S(1)}, u32[]{:S(2)}, u32[]{:S(2)}) collective-permute-start(f32[32,768]{1,0:T(8,128)S(1)} %add.17.refs_0_), channel_id=1, source_target_pairs={{0,3},{1,2},{2,1},{3,0},{4,7},{5,6},{6,5},{7,4},{8,11},{9,10},{10,... | collective-permute-start | bytes 294920 | tf_op jit(solution)/shard_map/ppermute | solution.py:275
  13.8 5.7 %collective-permute-start.3 = (f32[40,512]{1,0:T(8,128)S(1)}, f32[40,512]{1,0:T(8,128)S(1)}, u32[]{:S(2)}, u32[]{:S(2)}) collective-permute-start(f32[40,512]{1,0:T(8,128)S(1)} %get-tuple-element.48), channel_id=1, source_target_pairs={{0,12},{4,8},{8,4},{12,0},{16,28},{20,24},{24,20},{28,16},{1,13},{... | collective-permute-start | bytes 245768 | tf_op jit(solution)/shard_map/ppermute | solution.py:275
  16.7 4.6 %collective-permute-start.4 = (f32[40,512]{1,0:T(8,128)S(1)}, f32[40,512]{1,0:T(8,128)S(1)}, u32[]{:S(2)}, u32[]{:S(2)}) collective-permute-start(f32[40,512]{1,0:T(8,128)S(1)} %get-tuple-element.49), channel_id=1, source_target_pairs={{0,4},{4,0},{8,12},{12,8},{16,20},{20,16},{24,28},{28,24},{1,5},{5... | collective-permute-start | bytes 245768 | tf_op jit(solution)/shard_map/ppermute | solution.py:275
  17.2 4.4 %collective-permute-start.5 = (f32[40,512]{1,0:T(8,128)S(1)}, f32[40,512]{1,0:T(8,128)S(1)}, u32[]{:S(2)}, u32[]{:S(2)}) collective-permute-start(f32[40,512]{1,0:T(8,128)S(1)} %get-tuple-element.50), channel_id=1, source_target_pairs={{0,8},{4,12},{8,0},{12,4},{16,24},{20,28},{24,16},{28,20},{1,9},{5... | collective-permute-start | bytes 245768 | tf_op jit(solution)/shard_map/ppermute | solution.py:275
  21.7 7.0 %collective-permute-start.6 = (f32[40,512]{1,0:T(8,128)S(1)}, f32[40,512]{1,0:T(8,128)S(1)}, u32[]{:S(2)}, u32[]{:S(2)}) collective-permute-start(f32[40,512]{1,0:T(8,128)S(1)} %add.19.own_ref), channel_id=1, source_target_pairs={{0,16},{4,20},{8,24},{12,28},{16,0},{20,4},{24,8},{28,12},{1,17},{... | collective-permute-start | bytes 245768 | tf_op jit(solution)/shard_map/ppermute | solution.py:275
  28.7 5.3 %collective-permute-start.9 = (f32[40,512]{1,0:T(8,128)S(1)}, f32[40,512]{1,0:T(8,128)S(1)}, u32[]{:S(2)}, u32[]{:S(2)}) collective-permute-start(f32[40,512]{1,0:T(8,128)S(1)} %total.4.chunk_ref.mean_ref.refs_0_), channel_id=1, source_target_pairs={{0,12},{4,8},{8,4},{12,0},{16,28},{20,24},{24,20},{28,16},{1,13},{... | collective-permute-start | bytes 245768 | tf_op jit(solution)/shard_map/ppermute | solution.py:275
  29.4 5.3 %collective-permute-start.8 = (f32[40,512]{1,0:T(8,128)S(1)}, f32[40,512]{1,0:T(8,128)S(1)}, u32[]{:S(2)}, u32[]{:S(2)}) collective-permute-start(f32[40,512]{1,0:T(8,128)S(1)} %total.4.chunk_ref.mean_ref.refs_0_), channel_id=1, source_target_pairs={{0,8},{4,12},{8,0},{12,4},{16,24},{20,28},{24,16},{28,20},{1,9},{5... | collective-permute-start | bytes 245768 | tf_op jit(solution)/shard_map/ppermute | solution.py:275
  31.0 4.4 %collective-permute-start.7 = (f32[40,512]{1,0:T(8,128)S(1)}, f32[40,512]{1,0:T(8,128)S(1)}, u32[]{:S(2)}, u32[]{:S(2)}) collective-permute-start(f32[40,512]{1,0:T(8,128)S(1)} %total.4.chunk_ref.mean_ref.refs_0_), channel_id=1, source_target_pairs={{0,4},{4,0},{8,12},{12,8},{16,20},{20,16},{24,28},{28,24},{1,5},{5... | collective-permute-start | bytes 245768 | tf_op jit(solution)/shard_map/ppermute | solution.py:275
  37.1 4.8 %collective-permute-start.11 = (f32[32,768]{1,0:T(8,128)S(1)}, f32[32,768]{1,0:T(8,128)S(1)}, u32[]{:S(2)}, u32[]{:S(2)}) collective-permute-start(f32[32,768]{1,0:T(8,128)S(1)} %add.20.own_ref), channel_id=1, source_target_pairs={{0,3},{1,2},{2,1},{3,0},{4,7},{5,6},{6,5},{7,4},{8,11},{9,10},{10,... | collective-permute-start | bytes 294920 | tf_op jit(solution)/shard_map/ppermute | solution.py:275
  43.9 5.5 %collective-permute-start.14 = (f32[32,512]{1,0:T(8,128)S(1)}, f32[32,512]{1,0:T(8,128)S(1)}, u32[]{:S(2)}, u32[]{:S(2)}) collective-permute-start(f32[32,512]{1,0:T(8,128)S(1)} %get-tuple-element.57), channel_id=1, source_target_pairs={{0,12},{4,8},{8,4},{12,0},{16,28},{20,24},{24,20},{28,16},{1,13},{... | collective-permute-start | bytes 196616 | tf_op jit(solution)/shard_map/ppermute | solution.py:275
  45.3 5.2 %collective-permute-start.15 = (f32[32,512]{1,0:T(8,128)S(1)}, f32[32,512]{1,0:T(8,128)S(1)}, u32[]{:S(2)}, u32[]{:S(2)}) collective-permute-start(f32[32,512]{1,0:T(8,128)S(1)} %get-tuple-element.58), channel_id=1, source_target_pairs={{0,4},{4,0},{8,12},{12,8},{16,20},{20,16},{24,28},{28,24},{1,5},{5... | collective-permute-start | bytes 196616 | tf_op jit(solution)/shard_map/ppermute | solution.py:275
  47.5 6.1 %collective-permute-start.18 = (f32[32,128]{1,0:T(8,128)S(1)}, f32[32,128]{1,0:T(8,128)S(1)}, u32[]{:S(2)}, u32[]{:S(2)}) collective-permute-start(f32[32,128]{1,0:T(8,128)S(1)} %add.21.before_ref.own_ref), channel_id=1, source_target_pairs={{0,3},{1,2},{2,1},{3,0},{4,7},{5,6},{6,5},{7,4},{8,11},{9,10},{10,... | collective-permute-start | bytes 49160 | tf_op jit(solution)/shard_map/ppermute | solution.py:275
  50.4 6.3 %collective-permute-start.17 = (f32[32,512]{1,0:T(8,128)S(1)}, f32[32,512]{1,0:T(8,128)S(1)}, u32[]{:S(2)}, u32[]{:S(2)}) collective-permute-start(f32[32,512]{1,0:T(8,128)S(1)} %add.23.own_ref), channel_id=1, source_target_pairs={{0,16},{4,20},{8,24},{12,28},{16,0},{20,4},{24,8},{28,12},{1,17},{... | collective-permute-start | bytes 196616 | tf_op jit(solution)/shard_map/ppermute | solution.py:275
  57.0 5.2 %collective-permute-start.21 = (f32[32,512]{1,0:T(8,128)S(1)}, f32[32,512]{1,0:T(8,128)S(1)}, u32[]{:S(2)}, u32[]{:S(2)}) collective-permute-start(f32[32,512]{1,0:T(8,128)S(1)} %total.5.chunk_ref.refs_0_), channel_id=1, source_target_pairs={{0,12},{4,8},{8,4},{12,0},{16,28},{20,24},{24,20},{28,16},{1,13},{... | collective-permute-start | bytes 196616 | tf_op jit(solution)/shard_map/ppermute | solution.py:275
  57.8 4.9 %collective-permute-start.20 = (f32[32,512]{1,0:T(8,128)S(1)}, f32[32,512]{1,0:T(8,128)S(1)}, u32[]{:S(2)}, u32[]{:S(2)}) collective-permute-start(f32[32,512]{1,0:T(8,128)S(1)} %total.5.chunk_ref.refs_0_), channel_id=1, source_target_pairs={{0,8},{4,12},{8,0},{12,4},{16,24},{20,28},{24,16},{28,20},{1,9},{5... | collective-permute-start | bytes 196616 | tf_op jit(solution)/shard_map/ppermute | solution.py:275
  59.0 4.4 %collective-permute-start.19 = (f32[32,512]{1,0:T(8,128)S(1)}, f32[32,512]{1,0:T(8,128)S(1)}, u32[]{:S(2)}, u32[]{:S(2)}) collective-permute-start(f32[32,512]{1,0:T(8,128)S(1)} %total.5.chunk_ref.refs_0_), channel_id=1, source_target_pairs={{0,4},{4,0},{8,12},{12,8},{16,20},{20,16},{24,28},{28,24},{1,5},{5... | collective-permute-start | bytes 196616 | tf_op jit(solution)/shard_map/ppermute | solution.py:275
  65.1 4.8 %collective-permute-start.23 = (f32[32,768]{1,0:T(8,128)S(1)}, f32[32,768]{1,0:T(8,128)S(1)}, u32[]{:S(2)}, u32[]{:S(2)}) collective-permute-start(f32[32,768]{1,0:T(8,128)S(1)} %add.24.own_ref), channel_id=1, source_target_pairs={{0,3},{1,2},{2,1},{3,0},{4,7},{5,6},{6,5},{7,4},{8,11},{9,10},{10,... | collective-permute-start | bytes 294920 | tf_op jit(solution)/shard_map/ppermute | solution.py:275
  71.9 5.4 %collective-permute-start.26 = (f32[32,512]{1,0:T(8,128)S(1)}, f32[32,512]{1,0:T(8,128)S(1)}, u32[]{:S(2)}, u32[]{:S(2)}) collective-permute-start(f32[32,512]{1,0:T(8,128)S(1)} %get-tuple-element.66), channel_id=1, source_target_pairs={{0,12},{4,8},{8,4},{12,0},{16,28},{20,24},{24,20},{28,16},{1,13},{... | collective-permute-start | bytes 196616 | tf_op jit(solution)/shard_map/ppermute | solution.py:275
  73.3 5.1 %collective-permute-start.27 = (f32[32,512]{1,0:T(8,128)S(1)}, f32[32,512]{1,0:T(8,128)S(1)}, u32[]{:S(2)}, u32[]{:S(2)}) collective-permute-start(f32[32,512]{1,0:T(8,128)S(1)} %get-tuple-element.67), channel_id=1, source_target_pairs={{0,4},{4,0},{8,12},{12,8},{16,20},{20,16},{24,28},{28,24},{1,5},{5... | collective-permute-start | bytes 196616 | tf_op jit(solution)/shard_map/ppermute | solution.py:275
  75.4 6.2 %collective-permute-start.30 = (f32[32,128]{1,0:T(8,128)S(1)}, f32[32,128]{1,0:T(8,128)S(1)}, u32[]{:S(2)}, u32[]{:S(2)}) collective-permute-start(f32[32,128]{1,0:T(8,128)S(1)} %add.25.before_ref.own_ref), channel_id=1, source_target_pairs={{0,3},{1,2},{2,1},{3,0},{4,7},{5,6},{6,5},{7,4},{8,11},{9,10},{10,... | collective-permute-start | bytes 49160 | tf_op jit(solution)/shard_map/ppermute | solution.py:275
  78.4 6.3 %collective-permute-start.29 = (f32[32,512]{1,0:T(8,128)S(1)}, f32[32,512]{1,0:T(8,128)S(1)}, u32[]{:S(2)}, u32[]{:S(2)}) collective-permute-start(f32[32,512]{1,0:T(8,128)S(1)} %add.27.own_ref), channel_id=1, source_target_pairs={{0,16},{4,20},{8,24},{12,28},{16,0},{20,4},{24,8},{28,12},{1,17},{... | collective-permute-start | bytes 196616 | tf_op jit(solution)/shard_map/ppermute | solution.py:275
  84.9 5.2 %collective-permute-start.33 = (f32[32,512]{1,0:T(8,128)S(1)}, f32[32,512]{1,0:T(8,128)S(1)}, u32[]{:S(2)}, u32[]{:S(2)}) collective-permute-start(f32[32,512]{1,0:T(8,128)S(1)} %total.6.chunk_ref.refs_0_), channel_id=1, source_target_pairs={{0,12},{4,8},{8,4},{12,0},{16,28},{20,24},{24,20},{28,16},{1,13},{... | collective-permute-start | bytes 196616 | tf_op jit(solution)/shard_map/ppermute | solution.py:275
  85.9 4.9 %collective-permute-start.32 = (f32[32,512]{1,0:T(8,128)S(1)}, f32[32,512]{1,0:T(8,128)S(1)}, u32[]{:S(2)}, u32[]{:S(2)}) collective-permute-start(f32[32,512]{1,0:T(8,128)S(1)} %total.6.chunk_ref.refs_0_), channel_id=1, source_target_pairs={{0,8},{4,12},{8,0},{12,4},{16,24},{20,28},{24,16},{28,20},{1,9},{5... | collective-permute-start | bytes 196616 | tf_op jit(solution)/shard_map/ppermute | solution.py:275
  86.9 4.6 %collective-permute-start.31 = (f32[32,512]{1,0:T(8,128)S(1)}, f32[32,512]{1,0:T(8,128)S(1)}, u32[]{:S(2)}, u32[]{:S(2)}) collective-permute-start(f32[32,512]{1,0:T(8,128)S(1)} %total.6.chunk_ref.refs_0_), channel_id=1, source_target_pairs={{0,4},{4,0},{8,12},{12,8},{16,20},{20,16},{24,28},{28,24},{1,5},{5... | collective-permute-start | bytes 196616 | tf_op jit(solution)/shard_map/ppermute | solution.py:275
  93.2 4.8 %collective-permute-start.35 = (f32[32,768]{1,0:T(8,128)S(1)}, f32[32,768]{1,0:T(8,128)S(1)}, u32[]{:S(2)}, u32[]{:S(2)}) collective-permute-start(f32[32,768]{1,0:T(8,128)S(1)} %add.28.own_ref), channel_id=1, source_target_pairs={{0,3},{1,2},{2,1},{3,0},{4,7},{5,6},{6,5},{7,4},{8,11},{9,10},{10,... | collective-permute-start | bytes 294920 | tf_op jit(solution)/shard_map/ppermute | solution.py:275
  100.0 5.6 %collective-permute-start.38 = (f32[32,512]{1,0:T(8,128)S(1)}, f32[32,512]{1,0:T(8,128)S(1)}, u32[]{:S(2)}, u32[]{:S(2)}) collective-permute-start(f32[32,512]{1,0:T(8,128)S(1)} %get-tuple-element.75), channel_id=1, source_target_pairs={{0,12},{4,8},{8,4},{12,0},{16,28},{20,24},{24,20},{28,16},{1,13},{... | collective-permute-start | bytes 196616 | tf_op jit(solution)/shard_map/ppermute | solution.py:275
  101.3 5.2 %collective-permute-start.39 = (f32[32,512]{1,0:T(8,128)S(1)}, f32[32,512]{1,0:T(8,128)S(1)}, u32[]{:S(2)}, u32[]{:S(2)}) collective-permute-start(f32[32,512]{1,0:T(8,128)S(1)} %get-tuple-element.76), channel_id=1, source_target_pairs={{0,4},{4,0},{8,12},{12,8},{16,20},{20,16},{24,28},{28,24},{1,5},{5... | collective-permute-start | bytes 196616 | tf_op jit(solution)/shard_map/ppermute | solution.py:275
  103.5 6.0 %collective-permute-start.42 = (f32[32,128]{1,0:T(8,128)S(1)}, f32[32,128]{1,0:T(8,128)S(1)}, u32[]{:S(2)}, u32[]{:S(2)}) collective-permute-start(f32[32,128]{1,0:T(8,128)S(1)} %add.29.before_ref.own_ref), channel_id=1, source_target_pairs={{0,3},{1,2},{2,1},{3,0},{4,7},{5,6},{6,5},{7,4},{8,11},{9,10},{10,... | collective-permute-start | bytes 49160 | tf_op jit(solution)/shard_map/ppermute | solution.py:275
  106.5 6.3 %collective-permute-start.41 = (f32[32,512]{1,0:T(8,128)S(1)}, f32[32,512]{1,0:T(8,128)S(1)}, u32[]{:S(2)}, u32[]{:S(2)}) collective-permute-start(f32[32,512]{1,0:T(8,128)S(1)} %add.31.own_ref), channel_id=1, source_target_pairs={{0,16},{4,20},{8,24},{12,28},{16,0},{20,4},{24,8},{28,12},{1,17},{... | collective-permute-start | bytes 196616 | tf_op jit(solution)/shard_map/ppermute | solution.py:275
  113.0 5.2 %collective-permute-start.45 = (f32[32,512]{1,0:T(8,128)S(1)}, f32[32,512]{1,0:T(8,128)S(1)}, u32[]{:S(2)}, u32[]{:S(2)}) collective-permute-start(f32[32,512]{1,0:T(8,128)S(1)} %total.7.chunk_ref.refs_0_), channel_id=1, source_target_pairs={{0,12},{4,8},{8,4},{12,0},{16,28},{20,24},{24,20},{28,16},{1,13},{... | collective-permute-start | bytes 196616 | tf_op jit(solution)/shard_map/ppermute | solution.py:275
  113.9 4.9 %collective-permute-start.44 = (f32[32,512]{1,0:T(8,128)S(1)}, f32[32,512]{1,0:T(8,128)S(1)}, u32[]{:S(2)}, u32[]{:S(2)}) collective-permute-start(f32[32,512]{1,0:T(8,128)S(1)} %total.7.chunk_ref.refs_0_), channel_id=1, source_target_pairs={{0,8},{4,12},{8,0},{12,4},{16,24},{20,28},{24,16},{28,20},{1,9},{5... | collective-permute-start | bytes 196616 | tf_op jit(solution)/shard_map/ppermute | solution.py:275
  122.8 4.8 %collective-permute-start.48 = (bf16[32,1536]{1,0:T(8,128)(2,1)S(1)}, bf16[32,1536]{1,0:T(8,128)(2,1)S(1)}, u32[]{:S(2)}, u32[]{:S(2)}) collective-permute-start(bf16[32,1536]{1,0:T(8,128)(2,1)S(1)} %add.33.own_ref), channel_id=1, source_target_pairs={{0,3},{1,2},{2,1},{3,0},{4,7},{5,6},{6,5},{7,4},{8,11},{9,10},{10,... | collective-permute-start | bytes 294920 | tf_op jit(solution)/shard_map/ppermute | solution.py:275
  (19 other events, 40.3 us)
